TPU v7x, 128 devices: a whole 4x4x4 slice. The times are simulated.
128 devices in a mesh: seq: 64 (over z_hi, y, x, core), ch: 2 (over z_lo).
Axes of the slice: x: 4, y: 4, z: 4 (z_hi: 2, z_lo: 2; z = z_hi * 2 + z_lo), core: 2. Of those that a mesh axis runs over, the one named last changes fastest.
Arguments:
- tokens: bfloat16 [512, 64, 4096], P(None, 'seq'), may hold values from -6 to 6
- in_weight: bfloat16 [4096, 3, 2048], P('seq', None, 'ch'), may hold values from -0.09375 to 0.09375
- filter_spectrum: float32 [2, 1024, 64, 8], P(None, 'seq', None, 'ch'), may hold values from -6 to 6
- skip_bias: float32 [2048], P('ch'), may hold values from -1 to 1
- out_weight: bfloat16 [2048, 4096], P('ch'), may hold values from -0.125 to 0.125
Outputs:
- mixed: bfloat16 [512, 64, 4096], P('ch', 'seq')
All inputs are finite; a program needn't handle non-finite values.
Results may differ from a plain program's by a relative error of at most 0.018.
Values may be sent and summed in bfloat16 or wider, within the bound.
No kernel may reach another device: no remote copies, remote signals or barrier semaphores. Data moves between devices by JAX's collectives and lax.ppermute only.
A program may use at most 128 MiB of HBM per device.

v0:
```python
import math

import jax
import jax.numpy as jnp
from jax import lax
from jax.sharding import PartitionSpec as P

HIGH = lax.Precision.HIGHEST


def angle_table(left, right, modulus):
    product = left * right % modulus
    phase = product.astype(jnp.float32) * (2.0 * math.pi / modulus)
    return (jnp.cos(phase), jnp.sin(phase))


def split_table(table):
    upper = table.astype(jnp.bfloat16)
    lower = (table - upper.astype(jnp.float32)).astype(jnp.bfloat16)
    return (upper, lower)


def per_device(tokens, in_weight, filter_spectrum, skip_bias, out_weight):
    rows, cols_dev, width = tokens.shape
    ch_dev = in_weight.shape[2]
    seq_count = lax.axis_size("seq")
    seq_index = lax.axis_index("seq")
    points = 2 * rows
    cols_all = cols_dev * seq_count
    padded = points * cols_all
    kappa = points // seq_count
    filters_dev = filter_spectrum.shape[3]
    group = ch_dev // filters_dev
    flat = tokens.reshape(rows * cols_dev, width)
    whole_weight = lax.all_gather(in_weight, "seq", axis=0, tiled=True)
    projected = jnp.einsum("td,dsc->stc", flat, whole_weight, preferred_element_type=jnp.float32)
    projected = projected.astype(jnp.bfloat16)
    gate = projected[0].reshape(rows, cols_dev, ch_dev)
    source = (projected[1].astype(jnp.float32) * projected[2].astype(jnp.float32)).reshape(
        rows, cols_dev, ch_dev
    )
    freq_all = lax.iota(jnp.int32, points)[:, None]
    row_cos, row_sin = angle_table(freq_all, lax.iota(jnp.int32, rows)[None, :], points)
    row_table = jnp.concatenate([row_cos, -row_sin], axis=0)
    both_rows = jnp.einsum("ka,atc->ktc", row_table, source, precision=HIGH)
    rowwise_re = both_rows[:points]
    rowwise_im = both_rows[points:]
    my_cols = (seq_index * cols_dev + lax.iota(jnp.int32, cols_dev))[None, :]
    turn_cos, turn_sin = angle_table(freq_all, my_cols, padded)
    turn_cos = turn_cos[:, :, None]
    turn_sin = turn_sin[:, :, None]
    turned = jnp.stack(
        [
            rowwise_re * turn_cos + rowwise_im * turn_sin,
            rowwise_im * turn_cos - rowwise_re * turn_sin,
        ]
    ).astype(jnp.bfloat16)
    middle = lax.all_to_all(turned, "seq", split_axis=1, concat_axis=2, tiled=True)
    col_index = lax.iota(jnp.int32, cols_all)
    col_cos, col_sin = angle_table(col_index[:, None], col_index[None, :], cols_all)
    forward_cols = jnp.stack([jnp.stack([col_cos, col_sin]), jnp.stack([-col_sin, col_cos])])
    forward_upper, forward_lower = split_table(forward_cols)
    spectrum = jnp.einsum(
        "opkb,pjbc->ojkc", forward_upper, middle, preferred_element_type=jnp.float32
    ) + jnp.einsum("opkb,pjbc->ojkc", forward_lower, middle, preferred_element_type=jnp.float32)
    spec_re = spectrum[0].reshape(kappa, cols_all, filters_dev, group)
    spec_im = spectrum[1].reshape(kappa, cols_all, filters_dev, group)
    filt_re = filter_spectrum[0][:, :, :, None]
    filt_im = filter_spectrum[1][:, :, :, None]
    filtered = jnp.stack(
        [
            (spec_re * filt_re - spec_im * filt_im).reshape(kappa, cols_all, ch_dev),
            (spec_re * filt_im + spec_im * filt_re).reshape(kappa, cols_all, ch_dev),
        ]
    )
    backward_cols = jnp.stack([jnp.stack([col_cos, -col_sin]), jnp.stack([col_sin, col_cos])])
    back = jnp.einsum("opkb,pjkc->ojbc", backward_cols, filtered, precision=HIGH)
    back_re = back[0]
    back_im = back[1]
    my_freq = (seq_index * kappa + lax.iota(jnp.int32, kappa))[:, None]
    ret_cos, ret_sin = angle_table(my_freq, col_index[None, :], padded)
    ret_cos = ret_cos[:, :, None]
    ret_sin = ret_sin[:, :, None]
    returned = jnp.stack(
        [back_re * ret_cos - back_im * ret_sin, back_im * ret_cos + back_re * ret_sin]
    ).astype(jnp.bfloat16)
    arrived = lax.all_to_all(returned, "seq", split_axis=2, concat_axis=1, tiled=True)
    arrived_flat = arrived.reshape(2 * points, cols_dev, ch_dev)
    inverse_upper, inverse_lower = split_table(row_table)
    conv = (
        jnp.einsum("ka,ktc->atc", inverse_upper, arrived_flat, preferred_element_type=jnp.float32)
        + jnp.einsum("ka,ktc->atc", inverse_lower, arrived_flat, preferred_element_type=jnp.float32)
    ) / padded
    gated = (gate.astype(jnp.float32) * (conv + skip_bias * source)).astype(jnp.bfloat16)
    gated_flat = gated.reshape(rows * cols_dev, ch_dev)
    ch_count = lax.axis_size("ch")
    kept = rows * cols_dev // ch_count
    summed = lax.psum(
        jnp.dot(gated_flat, out_weight, preferred_element_type=jnp.float32).astype(jnp.bfloat16),
        "ch",
    ).astype(jnp.float32)
    mine = lax.dynamic_slice_in_dim(summed, lax.axis_index("ch") * kept, kept, 0)
    return mine.astype(jnp.bfloat16).reshape(rows // ch_count, cols_dev, width)


def solution(mesh):
    in_specs = (
        P(None, "seq", None),
        P("seq", None, "ch"),
        P(None, "seq", None, "ch"),
        P("ch"),
        P("ch", None),
    )
    out_specs = P("ch", "seq", None)
    return jax.shard_map(
        per_device, mesh=mesh, in_specs=in_specs, out_specs=out_specs, check_vma=False
    )
```

profile of v0, /device:TPU:1, one launch (start us, length us, event | category | flops | bytes accessed | tf_op | source)
XLA Modules:
  0.0 494.6 jit_solution(7548741234227609527)
XLA Ops:
  6.5 0.0 all-gather.2.cloned.1.call-start
  6.5 0.7 all-gather.2.cloned.1.call-update
  7.3 0.1 fusion.75
  7.3 9.1 %sine_negate_fusion = (f32[1024,512]{1,0:T(8,128)S(1)}, f32[1024,512]{1,0:T(8,128)}) fusion(), kind=kLoop, calls=%fused_computation.47 | loop fusion | flops 7864320 | bytes 4194304 | tf_op jit(solution)/shard_map/neg | solution.py:44
  16.4 0.0 copy-start.2
  16.4 129.9 %all-gather.2.cloned.1.call-done = bf16[4096,3,1024]{2,0,1:T(8,128)(2,1)} async-done(((bf16[64,3,1024]{2,0,1:T(8,128)(2,1)}), bf16[4096,3,1024]{2,0,1:T(8,128)(2,1)}) %all-gather.2.cloned.1.call-update) | async-done | bytes 25165840 | tf_op jit(solution)/shard_map/all_gather | solution.py:35
  146.3 0.0 copy-start.4
  146.3 18.9 %convert_bitcast_fusion = bf16[3,512,1024]{1,2,0:T(8,128)(2,1)S(1)} fusion(bf16[4096,3,1024]{2,0,1:T(8,128)(2,1)} %all-gather.2.cloned.1.call-done, bf16[512,1,4096]{2,0,1:T(8,128)(2,1)} %param.5), kind=kOutput, calls=%fused_computation.30 | convolution fusion | flops 12886474752 | bytes 32505856 | tf_op jit(solution)/shard_map/td,dsc->stc/dot_general | solution.py:36
  165.2 0.0 copy-start.7
  165.2 0.0 copy-done.2
  165.2 0.0 copy-done.4
  165.2 13.9 %fusion.15 = f32[2048,1024]{1,0:T(8,128)S(1)} fusion(f32[1024,512]{1,0:T(8,128)S(1)} %get-tuple-element.21, f32[1024,512]{1,0:T(8,128)S(1)} %copy-done.4, bf16[3,512,1024]{1,2,0:T(8,128)(2,1)S(1)} %convert_bitcast_fusion), kind=kOutput, calls=%fused_computation.31 | convolution fusion | flops 12887523328 | bytes 14680064 | tf_op jit(solution)/shard_map/ka,atc->ktc/dot_general | solution.py:45
  179.1 0.0 copy-done.7
  179.1 1.3 fusion.24
  180.4 0.4 pad_maximum_fusion.1
  180.8 6.3 %copy.33 = bf16[2,1024,1,1024]{3,0,2,1:T(2,128)(2,1)} copy(bf16[2,1024,1,1024]{3,1,2,0:T(8,128)(2,1)S(1)} %pad_maximum_fusion.1) | data formatting | bytes 8388608 | tf_op jit(solution)/shard_map/stack | solution.py:52
  187.1 0.0 copy-start.8
  187.1 6.2 %all-to-all-start = ((bf16[2,1024,1,1024]{3,0,2,1:T(2,128)(2,1)}), bf16[2,1024,1,1024]{3,0,2,1:T(2,128)(2,1)}, u32[]{:S(2)}, u32[]{:S(2)}) async-start(bf16[2,1024,1,1024]{3,0,2,1:T(2,128)(2,1)} %copy.33), calls=%async_computation | async-start | bytes 8388608 | tf_op jit(solution)/shard_map/all_to_all | solution.py:58
  193.3 0.0 all-reduce.2.cloned.1.call-start
  193.4 0.0 copy-done.8
  193.4 0.2 copy.37
  193.7 0.2 copy.36
  193.9 2.6 mul.352
  196.5 5.8 %mul.353 = f32[1,16,64,1024]{3,2,0,1:T(8,128)} reshape(f32[16,64,4,256]{3,2,1,0:T(4,128)} %mul.352) | data formatting | bytes 8388608 | tf_op jit(solution)/shard_map/mul | solution.py:72
  202.3 2.6 mul.356
  204.8 6.2 %mul.357 = f32[1,16,64,1024]{3,2,0,1:T(8,128)} reshape(f32[16,64,4,256]{3,2,1,0:T(4,128)} %mul.356) | data formatting | bytes 8388608 | tf_op jit(solution)/shard_map/mul | solution.py:72
  211.0 0.1 fusion.60
  211.2 0.1 fusion.58
  211.3 0.1 fusion.71
  211.5 35.2 %all-to-all-done = bf16[2,1024,1,1024]{3,0,2,1:T(2,128)(2,1)} async-done(((bf16[2,1024,1,1024]{3,0,2,1:T(2,128)(2,1)}), bf16[2,1024,1,1024]{3,0,2,1:T(2,128)(2,1)}, u32[]{:S(2)}, u32[]{:S(2)}) %all-to-all-start) | async-done | bytes 4194336 | tf_op jit(solution)/shard_map/all_to_all | solution.py:58
  246.6 7.6 %fusion.4 = f32[16,1024,2,64,1]{1,3,4,2,0:T(8,128)S(1)} fusion(bf16[2,64,16,1,1024]{4,0,2,1,3:T(2,128)(2,1)} %bitcast.7, f32[1,2,64,64]{3,2,1,0:T(8,128)S(1)} %get-tuple-element.12, f32[1,2,64,64]{3,2,1,0:T(8,128)S(1)} %get-tuple-element.17), kind=kOutput, calls=%fused_computation.10 | convolution fusion | flops 536952832 | bytes 12648448 | tf_op jit(solution)/shard_map/opkb,pjbc->ojkc/dot_general | solution.py:65
  254.2 0.0 copy-start
  254.3 0.0 copy-start.1
  254.3 8.4 %fusion.3 = f32[2,16,64,1024]{3,2,0,1:T(8,128)S(1)} fusion(f32[16,1024,2,64,1]{1,3,4,2,0:T(8,128)S(1)} %fusion.4, bf16[2,64,16,1,1024]{4,0,2,1,3:T(2,128)(2,1)} %bitcast.7, f32[1,2,64,64]{3,2,1,0:T(8,128)S(1)} %get-tuple-element.12, f32[1,2,64,64]{3,2,1,0:T(8,128)S(1)} %get-tuple-element.17), kind=kOutput, calls=%fused_computation.5 | convolution fusion | flops 539033600 | bytes 21037056 | tf_op jit(solution)/shard_map/opkb,pjbc->ojkc/dot_general | solution.py:63
  262.7 0.0 copy-done
  262.7 0.0 copy-done.1
  262.7 2.6 multiply_subtract_fusion
  265.3 12.6 %fusion.12 = f32[2,16,64,1024]{3,2,0,1:T(8,128)S(1)} fusion(f32[1,16,64,1024]{3,2,0,1:T(8,128)S(1)} %get-tuple-element.6, f32[1,16,64,1024]{3,2,0,1:T(8,128)S(1)} %get-tuple-element.5, f32[1,2,64,64]{3,2,1,0:T(8,128)S(1)} %get-tuple-element.18, f32[1,2,64,64]{3,2,1,0:T(8,128)S(1)} %get-tuple-element.11), kind=kOutput, calls=%fused_computation.26 | convolution fusion | flops 3223339008 | bytes 16842752 | tf_op jit(solution)/shard_map/opkb,pjkc->ojbc/dot_general | solution.py:77
  278.0 1.2 subtract_convert_fusion.1
  279.1 0.4 pad_maximum_fusion.2
  279.5 6.3 %copy.39 = bf16[2,16,64,1024]{3,0,1,2:T(2,128)(2,1)} copy(bf16[2,16,64,1024]{3,2,0,1:T(8,128)(2,1)S(1)} %pad_maximum_fusion.2) | data formatting | bytes 8388608 | tf_op jit(solution)/shard_map/stack | solution.py:84
  285.8 64.0 %all_to_all.33 = bf16[2,16,64,1024]{3,0,1,2:T(2,128)(2,1)S(1)} all-to-all(bf16[2,16,64,1024]{3,0,1,2:T(2,128)(2,1)} %copy.39), channel_id=1, replica_groups=mesh['seq'=64,'ch'=2] {'seq'}, dimensions={2} | all-to-all | bytes 8388608 | tf_op jit(solution)/shard_map/all_to_all | solution.py:87
  349.8 0.0 copy-start.3
  349.8 0.0 copy-start.5
  349.8 1.4 copy.40
  351.2 0.0 copy-start.6
  351.2 1.9 copy-done.6
  353.2 0.0 copy-done.3
  353.2 0.0 copy-done.5
  353.2 0.0 copy-start.9
  353.2 3.8 fusion.17
  357.0 0.0 copy-done.9
  357.0 15.8 %convolution_convert_fusion = bf16[512,4096]{1,0:T(8,128)(2,1)} fusion(bf16[1024,4096]{1,0:T(8,128)(2,1)} %param.9, f32[512,1024]{0,1:T(8,128)} %fusion.17, bf16[2048,1024]{1,0:T(8,128)(2,1)} %bitcast.97, f32[1024,512]{1,0:T(8,128)S(1)} %copy-done.3, f32[1024,512]{1,0:T(8,128)} %get-tuple-element.22, bf16[3,512,1024]{1,2,0:T(8,128)(2,1)} %copy-done.7, ...), kind=kOutput, calls=%fused_computation.6 | convolution fusion | flops 6455033856 | bytes 26218496 | tf_op jit(solution)/shard_map/dot_general | solution.py:99
  372.8 0.0 all-reduce.2.cloned.1.call-update
  372.8 111.6 %all-reduce.2.cloned.1.call-done = bf16[512,4096]{1,0:T(8,128)(2,1)} async-done(((bf16[512,4096]{1,0:T(8,128)(2,1)}), bf16[512,4096]{1,0:T(8,128)(2,1)}) %all-reduce.2.cloned.1.call-update) | async-done | bytes 4194320 | tf_op jit(solution)/shard_map/psum | solution.py:98
  484.4 3.1 fusion.27
  (3 shorter events, 0.0 us)
Async XLA Ops:
  6.5 139.8 %all-gather.2.cloned.1.call-start = ((), (), s32[]{:S(2)}) async-start(), calls=%async_computation.2 | async-start | bytes 25559040 | tf_op jit(solution)/shard_map/all_gather | solution.py:35
  16.4 148.8 %copy-start.2 = (f32[1024,512]{1,0:T(8,128)}, f32[1024,512]{1,0:T(8,128)S(1)}, u32[]{:S(2)}) copy-start(f32[1024,512]{1,0:T(8,128)S(1)} %get-tuple-element.21) | copy-start | bytes 6291460
  146.3 18.9 %copy-start.4 = (f32[1024,512]{1,0:T(8,128)S(1)}, f32[1024,512]{1,0:T(8,128)}, u32[]{:S(2)}) copy-start(f32[1024,512]{1,0:T(8,128)} %get-tuple-element.22) | copy-start | bytes 6291460
  165.2 13.9 %copy-start.7 = (bf16[3,512,1024]{1,2,0:T(8,128)(2,1)}, bf16[3,512,1024]{1,2,0:T(8,128)(2,1)S(1)}, u32[]{:S(2)}) copy-start(bf16[3,512,1024]{1,2,0:T(8,128)(2,1)S(1)} %convert_bitcast_fusion) | copy-start | bytes 9437188
  187.1 6.3 %copy-start.8 = (f32[2,16,64,4]{2,3,1,0:T(4,128)S(1)}, f32[2,16,64,4]{2,3,1,0:T(4,128)}, u32[]{:S(2)}) copy-start(f32[2,16,64,4]{2,3,1,0:T(4,128)} %param.7) | copy-start | bytes 98308
  187.1 59.5 %all-to-all-start = ((bf16[2,1024,1,1024]{3,0,2,1:T(2,128)(2,1)}), bf16[2,1024,1,1024]{3,0,2,1:T(2,128)(2,1)}, u32[]{:S(2)}, u32[]{:S(2)}) async-start(bf16[2,1024,1,1024]{3,0,2,1:T(2,128)(2,1)} %copy.33), calls=%async_computation | async-start | bytes 8388608 | tf_op jit(solution)/shard_map/all_to_all | solution.py:58
  193.3 291.0 %all-reduce.2.cloned.1.call-start = ((), (), s32[]{:S(2)}) async-start(), calls=%async_computation.3 | async-start | bytes 8388608 | tf_op jit(solution)/shard_map/psum | solution.py:98
  254.2 8.4 %copy-start = (f32[1,16,64,1024]{3,2,0,1:T(8,128)S(1)}, f32[1,16,64,1024]{3,2,0,1:T(8,128)}, u32[]{:S(2)}) copy-start(f32[1,16,64,1024]{3,2,0,1:T(8,128)} %mul.353) | copy-start | bytes 12582916
  254.3 8.4 %copy-start.1 = (f32[1,16,64,1024]{3,2,0,1:T(8,128)S(1)}, f32[1,16,64,1024]{3,2,0,1:T(8,128)}, u32[]{:S(2)}) copy-start(f32[1,16,64,1024]{3,2,0,1:T(8,128)} %mul.357) | copy-start | bytes 12582916
  349.8 3.3 copy-start.3
  349.8 3.3 copy-start.5
  351.2 1.9 copy-start.6
  353.2 3.8 copy-start.9
Sparse Core Ops, SparseCore 0:
  10.7 135.6 all-gather.1
  373.0 111.3 all-reduce.1
where the time goes:
time: 500 us; the launch traced here: 495 us
  waiting for transfers between devices  277 us (55%)
  matrix products  81 us (16%)
  blocking collectives  64 us (13%)
  local copies, waits for them, and re-layouts  33.5 us (7%)
  other arithmetic  18.6 us (4%)
  between operations  13.9 us (3%)
  starting transfers between devices  6.26 us (1%)
    all_gather x1, waiting for transfers between devices, per_device(): whole_weight = lax.all_gather(in_weight, 'seq', axis=0, tiled=True)  130 us
    psum x1, waiting for transfers between devices, per_device(): lax.psum(jnp.dot(gated_flat, out_weight, preferred_element_type=jnp.float...  112 us
    all_to_all x1, blocking collectives, per_device(): lax.all_to_all(returned, 'seq', split_axis=2, concat_axis=1, tiled=True)  64 us
    all_to_all x1, waiting for transfers between devices, per_device(): lax.all_to_all(turned, 'seq', split_axis=1, concat_axis=2, tiled=True)  35.2 us
    dot_general x1, matrix products, per_device(): jnp.einsum('td,dsc->stc', flat, whole_weight, preferred_element_type=jnp....  18.9 us
    dot_general x1, matrix products, per_device(): jnp.dot(gated_flat, out_weight, preferred_element_type=jnp.float32)  15.8 us
    dot_general x1, matrix products, per_device(): both_rows = jnp.einsum('ka,atc->ktc', row_table, source, precision=HIGH)  13.9 us
    dot_general x1, matrix products, per_device(): jnp.einsum('opkb,pjkc->ojbc', backward_cols, filtered, precision=HIGH)  12.6 us
  transfers between devices with their start and end apart: 3, of which 3 were waited for; matrix products, arithmetic and copies ran while one was open for 5% of the time, Pallas kernels for 0%

commit v1 on v0

v1 whole, which is shorter than its diff:
```python
import functools
import math

import jax
import jax.numpy as jnp
import ml_dtypes
import numpy as np
from jax import lax
from jax.experimental import pallas as pl
from jax.experimental.pallas import tpu as pltpu
from jax.sharding import PartitionSpec as P

BF16 = jnp.bfloat16
F32 = jnp.float32
SEQ = 64
CHIPS = 32
SAME_CORE = [[2 * p + j for p in range(CHIPS)] for j in range(2)]


def coords(s):
    return s // 32, (s // 8) % 4, (s // 2) % 4, s % 2


def index_of(z, y, x, c):
    return ((z * 4 + y) * 4 + x) * 2 + c


def send(value, dz=0, dy=0, dx=0, dc=0):
    perm = []
    for s in range(SEQ):
        z, y, x, c = coords(s)
        perm.append((s, index_of((z + dz) % 2, (y + dy) % 4, (x + dx) % 4, c ^ dc)))
    return lax.ppermute(value, "seq", perm)


def split_np(table):
    upper = table.astype(np.float32).astype(ml_dtypes.bfloat16)
    lower = (table - upper.astype(np.float64)).astype(np.float32).astype(ml_dtypes.bfloat16)
    return upper, lower


def split_table(table):
    upper = table.astype(BF16)
    lower = (table - upper.astype(F32)).astype(BF16)
    return upper, lower


def row_tables(rows, padded):
    points = 2 * rows
    a = np.arange(rows)
    k = np.arange(rows)
    phase = 2.0 * np.pi * ((a[:, None] * k[None, :]) % points) / points
    re, im = np.cos(phase), -np.sin(phase)
    im[:, 0] = np.where(a % 2 == 0, 1.0, -1.0)
    forward = np.concatenate([re, im], axis=1)
    scale = np.full((rows,), 2.0)
    scale[0] = 1.0
    inverse = np.concatenate([re * scale, im * scale], axis=1).T / padded
    return forward, inverse


def reorder_kernel(order_ref, a0, a1, b0, b1, out_a, out_b):
    rows = a0.shape[0]
    out_a[:rows, :] = a0[...]
    out_a[rows:, :] = a1[...]
    out_b[:rows, :] = b0[...]
    out_b[rows:, :] = b1[...]


def reorder(order, mine, other):
    rows, width = mine.shape
    blocks = width // 128
    return pl.pallas_call(
        reorder_kernel,
        grid_spec=pltpu.PrefetchScalarGridSpec(
            num_scalar_prefetch=1,
            grid=(blocks,),
            in_specs=[
                pl.BlockSpec((rows, 128), lambda i, o: (0, o[0, i])),
                pl.BlockSpec((rows, 128), lambda i, o: (0, o[0, i])),
                pl.BlockSpec((rows, 128), lambda i, o: (0, o[1, i])),
                pl.BlockSpec((rows, 128), lambda i, o: (0, o[1, i])),
            ],
            out_specs=[
                pl.BlockSpec((2 * rows, 128), lambda i, o: (0, i)),
                pl.BlockSpec((2 * rows, 128), lambda i, o: (0, i)),
            ],
        ),
        out_shape=[jax.ShapeDtypeStruct((2 * rows, width), BF16)] * 2,
        cost_estimate=pl.CostEstimate(flops=0, bytes_accessed=8 * rows * width * 2, transcendentals=0),
        name="reorder_tokens",
    )(order, mine, other, mine, other)


def conv_kernel(x_ref, fwd_ref, inv_ref, tw_ref, a_ref, ai_ref, m_ref, f_ref, y_ref, r_ref, q_ref):
    chips, chans, both = x_ref.shape
    rows = both // 2
    blocks = rows // 128
    for col in range(2):
        x = x_ref[:, :, col * rows : (col + 1) * rows].reshape(chips * chans, rows)
        r = jnp.dot(x, fwd_ref[0], preferred_element_type=F32)
        r += jnp.dot(x, fwd_ref[1], preferred_element_type=F32)
        r = r.reshape(chips, chans, 2 * rows)
        tw = tw_ref[col * chips : (col + 1) * chips, :]
        cos = tw[:, None, :rows]
        sin = tw[:, None, rows:]
        re, im = r[:, :, :rows], r[:, :, rows:]
        turned_re = (re * cos + im * sin).reshape(chips * chans, rows)
        turned_im = (im * cos - re * sin).reshape(chips * chans, rows)
        for k in range(blocks):
            r_ref[col, k] = turned_re[:, k * 128 : (k + 1) * 128]
            r_ref[col, blocks + k] = turned_im[:, k * 128 : (k + 1) * 128]
    half = 2 * chips
    lane = lax.broadcasted_iota(jnp.int32, (2 * half, 128), 1)

    def channel(c, carry):
        pick = pl.ds(c, chips, stride=chans)
        parts = [
            jnp.concatenate([r_ref[col, part * blocks + k, pick, :] for k in range(blocks)], axis=1)
            for part in range(2)
            for col in range(2)
        ]
        turned = jnp.concatenate(parts, axis=0).astype(BF16)
        s = jnp.dot(a_ref[...], turned, preferred_element_type=F32)
        s = s[: 2 * half] + s[2 * half :]
        s_re, s_im = s[:half], s[half:]
        f_re, f_im = f_ref[:, :rows], f_ref[:, rows:]
        filtered = jnp.concatenate(
            [s_re * f_re - s_im * f_im, s_re * f_im + s_im * f_re], axis=0
        ).astype(BF16)
        back = jnp.dot(ai_ref[...], filtered, preferred_element_type=F32)
        back = back[: 2 * half] + back[2 * half :]
        edge = jnp.dot(m_ref[...], turned[:, :128], preferred_element_type=F32)
        edge = edge[: 2 * half] + edge[2 * half :]
        head = jnp.where(lane == 0, edge, back[:, :128])
        back = jnp.concatenate([head, back[:, 128:]], axis=1)
        b_re, b_im = back[:half], back[half:]
        cos, sin = tw_ref[:, :rows], tw_ref[:, rows:]
        out_re = b_re * cos - b_im * sin
        out_im = b_im * cos + b_re * sin
        for col in range(2):
            part = slice(col * chips, (col + 1) * chips)
            for k in range(blocks):
                q_ref[col, k, pick, :] = out_re[part, k * 128 : (k + 1) * 128]
                q_ref[col, blocks + k, pick, :] = out_im[part, k * 128 : (k + 1) * 128]
        return carry

    lax.fori_loop(0, chans, channel, 0)
    for col in range(2):
        q = jnp.concatenate([q_ref[col, k].astype(BF16) for k in range(2 * blocks)], axis=1)
        y = jnp.dot(q, inv_ref[0], preferred_element_type=F32)
        y += jnp.dot(q, inv_ref[1], preferred_element_type=F32)
        y_ref[:, :, col * rows : (col + 1) * rows] = y.astype(BF16).reshape(chips, chans, rows)


def long_conv(x, fwd, inv, tw, a, ai, m, f):
    chips, chans, both = x.shape
    vmem = pl.BlockSpec(memory_space=pltpu.VMEM)
    return pl.pallas_call(
        conv_kernel,
        in_specs=[vmem] * 8,
        out_specs=vmem,
        out_shape=jax.ShapeDtypeStruct(x.shape, BF16),
        scratch_shapes=[
            pltpu.VMEM((2, both // 128, chips * chans, 128), F32),
            pltpu.VMEM((2, both // 128, chips * chans, 128), F32),
        ],
        compiler_params=pltpu.CompilerParams(vmem_limit_bytes=48 * 2**20),
        cost_estimate=pl.CostEstimate(flops=8 * 10**9, bytes_accessed=8 * 2**20, transcendentals=0),
        name="long_conv",
    )(x, fwd, inv, tw, a, ai, m, f)


def cos_sin(product, modulus):
    phase = (product % modulus).astype(F32) * (2.0 * math.pi / modulus)
    return jnp.cos(phase), jnp.sin(phase)


def column_tables(core, filt, rows, cols, padded):
    points = 2 * rows
    i = lax.iota(jnp.int32, cols)
    b = 2 * (i % CHIPS) + ((i // CHIPS) ^ core)
    k1 = lax.iota(jnp.int32, rows)
    tw = jnp.concatenate(cos_sin(b[:, None] * k1[None, :], padded), axis=1)
    k2 = lax.iota(jnp.int32, cols)
    c, s = cos_sin(k2[:, None] * b[None, :], cols)
    a = jnp.block([[c, s], [-s, c]])
    ai = a.T
    f_re, f_im = filt[0], filt[1]
    back_re = jnp.flip(f_re, (0, 1))[rows - 1 : points - 1]
    back_im = jnp.flip(f_im, (0, 1))[rows - 1 : points - 1]
    back_re = jnp.concatenate([back_re[:1], jnp.flip(f_re, (0, 1))[: rows - 1]], axis=0)
    back_im = jnp.concatenate([back_im[:1], jnp.flip(f_im, (0, 1))[: rows - 1]], axis=0)
    h_re = (0.5 * (f_re[:rows] + back_re)).T
    h_im = (0.5 * (f_im[:rows] - back_im)).T
    f = jnp.concatenate([h_re, h_im], axis=1)

    def edge(k):
        d = jnp.mod(b[:, None] - b[None, :], cols)
        dd = b[:, None] - b[None, :]
        ec, es = cos_sin(d[:, :, None] * k2[None, None, :], cols)
        g_re = jnp.sum(ec * f_re[k] - es * f_im[k], axis=-1)
        g_im = jnp.sum(es * f_re[k] + ec * f_im[k], axis=-1)
        tc, ts = cos_sin(jnp.mod(dd * k, padded), padded)
        return g_re * tc - g_im * ts

    zero = jnp.zeros((cols, cols), F32)
    m = jnp.block([[edge(0), zero], [zero, edge(rows)]])

    def stacked(t):
        return jnp.concatenate(split_table(t), axis=0)

    return tw, stacked(a), stacked(ai), stacked(m), f


def dot_t(weight, tokens):
    return lax.dot_general(weight, tokens, (((0,), (1,)), ((), ())), preferred_element_type=F32)


def gather_two(block, first, second):
    d1 = send(block, **{first: -1})
    d3 = send(block, **{first: 1})
    d2 = send(block, **{first: 2})
    line = jnp.concatenate([block, d1, d2, d3], axis=0)
    e1 = send(line, **{second: -1})
    e3 = send(line, **{second: 1})
    half = line.shape[0] // 2
    e2a = send(e1[:half], **{second: -1})
    e2b = send(e3[half:], **{second: 1})
    return line, e1, e2a, e2b, e3


def project(pieces, tokens):
    line, e1, e2a, e2b, e3 = pieces
    n = line.shape[0]
    out = dot_t(line, tokens[:, :n])
    out += dot_t(e1, tokens[:, n : 2 * n])
    out += dot_t(e3, tokens[:, 3 * n :])
    out += dot_t(e2a, tokens[:, 2 * n : 2 * n + n // 2])
    out += dot_t(e2b, tokens[:, 2 * n + n // 2 : 3 * n])
    return out.astype(BF16).astype(F32)


def per_device(tokens, in_weight, filter_spectrum, skip_bias, out_weight):
    rows, _, width = tokens.shape
    cols = SEQ
    padded = 2 * rows * cols
    s = lax.axis_index("seq")
    h = lax.axis_index("ch")
    z, y, x, core = coords(s)
    chan = in_weight.shape[2] // 2
    depth = in_weight.shape[0]

    mine = tokens.reshape(rows, width)
    keep = lax.dynamic_slice_in_dim(in_weight, core * chan, chan, 2)
    give = lax.dynamic_slice_in_dim(in_weight, (1 - core) * chan, chan, 2)
    keep = jnp.concatenate([keep[:, 1], keep[:, 2], keep[:, 0]], axis=1)
    give = jnp.concatenate([give[:, 1], give[:, 2], give[:, 0]], axis=1)
    near = send(give, dc=1)
    far = send(keep[:, : 2 * chan], dz=1)
    far_near = send(give[:, : 2 * chan], dz=1, dc=1)

    def ordered(own, partner):
        return jnp.concatenate(
            [jnp.where(core == 0, own, partner), jnp.where(core == 0, partner, own)], axis=0
        )

    own_z = ordered(keep, near)
    oth_z = ordered(far, far_near)
    block = jnp.concatenate([own_z[:, : 2 * chan], oth_z], axis=0)
    gate_weight = lax.all_gather(
        own_z[:, 2 * chan :], "seq", axis=0, tiled=True, axis_index_groups=SAME_CORE
    )
    key_pieces = gather_two(block[:, :chan], "dx", "dy")
    value_pieces = gather_two(block[:, chan:], "dy", "dx")

    other = send(mine, dc=1)
    order = np.arange(32)
    p_, q_, dz = order // 8, (order // 2) % 4, order % 2
    key_order = ((z ^ dz) * 4 + (y + p_) % 4) * 4 + (x + q_) % 4
    value_order = ((z ^ dz) * 4 + (y + q_) % 4) * 4 + (x + p_) % 4
    tokens_key, tokens_value = reorder(jnp.stack([key_order, value_order]), mine, other)

    half_ow = out_weight.shape[0] // 2
    perm = []
    for t in range(SEQ):
        tz, ty, tx, tc = coords(t)
        for th in range(2):
            perm.append((t * 2 + th, index_of(tz ^ tc, ty, tx, tc) * 2 + 1 - th))
    ow_part = lax.dynamic_slice_in_dim(out_weight, core * half_ow, half_ow, 0)
    ow_same = lax.ppermute(ow_part, ("seq", "ch"), perm)
    ow_cross = send(ow_same, dc=1)

    filt = jnp.transpose(filter_spectrum, (3, 0, 2, 1)).reshape(4, -1)
    filt = lax.all_gather(filt, "seq", axis=0)
    filt = lax.dynamic_index_in_dim(filt, 2 * core + z, 1, keepdims=False)
    filt = filt.reshape(SEQ, 2, cols, 2 * rows // SEQ)
    filt = jnp.transpose(filt, (1, 0, 3, 2)).reshape(2, 2 * rows, cols)
    tw, a, ai, m, f = column_tables(core, filt, rows, cols, padded)
    forward, inverse = row_tables(rows, padded)
    fwd = jnp.asarray(np.stack(split_np(forward)))
    inv = jnp.asarray(np.stack(split_np(inverse)))

    source = project(key_pieces, tokens_key) * project(value_pieces, tokens_value)
    packed = source.astype(BF16).reshape(CHIPS, chan // CHIPS, 2 * rows)
    mine_ch = lax.all_to_all(packed, "seq", 0, 0, axis_index_groups=SAME_CORE)
    conv = long_conv(mine_ch, fwd, inv, tw, a, ai, m, f)
    conv = lax.all_to_all(conv, "seq", 0, 0, axis_index_groups=SAME_CORE)
    conv = conv.reshape(chan, 2 * rows).astype(F32)

    gate = jnp.concatenate([dot_t(gate_weight, mine), dot_t(gate_weight, other)], axis=1)
    gate = gate.astype(BF16).astype(F32)
    skip = lax.dynamic_slice_in_dim(skip_bias, core * chan, chan, 0)[:, None]
    gated = (gate * (conv + skip * source)).astype(BF16)

    kept = rows // 2
    own_here = lax.dynamic_slice(gated, (0, h * kept), (chan, kept))
    own_there = lax.dynamic_slice(gated, (0, (1 - h) * kept), (chan, kept))
    oth_here = lax.dynamic_slice(gated, (0, rows + h * kept), (chan, kept))
    oth_there = lax.dynamic_slice(gated, (0, rows + (1 - h) * kept), (chan, kept))
    swap_ch = [(0, 1), (1, 0)]
    from_h = lax.ppermute(own_there, "ch", swap_ch)
    perm2 = []
    for t in range(SEQ):
        for th in range(2):
            perm2.append((t * 2 + th, (t ^ 1) * 2 + 1 - th))
    from_hc = lax.ppermute(oth_there, ("seq", "ch"), perm2)
    from_c = send(oth_here, dc=1)
    here = ordered(own_here, from_c)

    def out_dot(g, w):
        return lax.dot_general(g, w, (((0,), (0,)), ((), ())), preferred_element_type=F32)

    mixed = out_dot(here, out_weight) + out_dot(from_h, ow_same) + out_dot(from_hc, ow_cross)
    return mixed.astype(BF16).reshape(kept, 1, out_weight.shape[1])


def solution(mesh):
    in_specs = (
        P(None, "seq", None),
        P("seq", None, "ch"),
        P(None, "seq", None, "ch"),
        P("ch"),
        P("ch", None),
    )
    return jax.shard_map(
        per_device, mesh=mesh, in_specs=in_specs, out_specs=P("ch", "seq", None), check_vma=False
    )
```

time: 500 us -> 269 us (0.54)
  waiting for transfers between devices: 277 us -> 73.9 us
  blocking collectives: 64 us -> 0 us
  starting transfers between devices: 6.26 us -> 48.3 us
  Pallas kernels: 0 us -> 41.3 us
  matrix products: 81 us -> 44.5 us
  local copies, waits for them, and re-layouts: 33.5 us -> 26.6 us
    all_gather x1 -> x2, waiting for transfers between devices: 130 us -> 3.91 us  [the longest x1 3.91 us: per_device(): filt = lax.all_gather(filt, 'seq', axis=0)]
    psum x1 -> x0, waiting for transfers between devices: 112 us -> none  [per_device(): lax.psum(jnp.dot(gated_flat, out_weight, preferred_element_type=jnp.float...]
    all_to_all x1 -> x0, blocking collectives: 64 us -> none  [per_device(): lax.all_to_all(returned, 'seq', split_axis=2, concat_axis=1, tiled=True)]
    pallas_call x0 -> x2, Pallas kernels: none -> 41.3 us  [the longest x1 23.3 us: reorder(): pl.pallas_call(reorder_kernel, grid_spec=pltpu.PrefetchScalarGridSpec(num...]
    ppermute x0 -> x23, starting transfers between devices: none -> 37.8 us  [the longest x20 31.8 us: send(): return lax.ppermute(value, 'seq', perm)]
    dot_general x7 -> x15, matrix products: 81 us -> 44.5 us  [the longest x12 30.1 us: dot_t(): lax.dot_general(weight, tokens, (((0,), (1,)), ((), ())), preferred_eleme...]
    ppermute x0 -> x23, waiting for transfers between devices: none -> 36.2 us  [the longest x20 30.2 us: send(): return lax.ppermute(value, 'seq', perm)]
    mul x7 -> x0, local copies, waits for them, and re-layouts: 17.6 us -> none  [the longest x4 8.95 us: per_device(): spec_im * filt_im]
  transfers between devices with their start and end apart: 3 -> 27, of which waited for: 3 -> 11; matrix products, arithmetic and copies ran while one was open for 5% -> 30% of each run, Pallas kernels for 0% -> 15%
where the time goes in v1:
time: 269 us; the launch traced here: 267 us
  waiting for transfers between devices  73.9 us (27%)
  starting transfers between devices  48.3 us (18%)
  matrix products  44.5 us (17%)
  Pallas kernels  41.3 us (15%)
  local copies, waits for them, and re-layouts  26.6 us (10%)
  other arithmetic  18.2 us (7%)
  between operations  14.3 us (5%)
    ppermute x20, starting transfers between devices, send(): return lax.ppermute(value, 'seq', perm)  31.8 us
    ppermute x20, waiting for transfers between devices, send(): return lax.ppermute(value, 'seq', perm)  30.2 us
    dot_general x12, matrix products, dot_t(): lax.dot_general(weight, tokens, (((0,), (1,)), ((), ())), preferred_eleme...  30.1 us
    pallas_call x1, Pallas kernels, reorder(): pl.pallas_call(reorder_kernel, grid_spec=pltpu.PrefetchScalarGridSpec(num...  23.3 us
    all_to_all x1, waiting for transfers between devices, per_device(): mine_ch = lax.all_to_all(packed, 'seq', 0, 0, axis_index_groups=SAME_CORE)  19.7 us
    pallas_call x1, Pallas kernels, long_conv(): pl.pallas_call(conv_kernel, in_specs=[vmem] * 8, out_specs=vmem, out_shap...  18 us
    dot_general x3, matrix products, out_dot(): lax.dot_general(g, w, (((0,), (0,)), ((), ())), preferred_element_type=F32)  14.4 us
    all_to_all x1, waiting for transfers between devices, per_device(): conv = lax.all_to_all(conv, 'seq', 0, 0, axis_index_groups=SAME_CORE)  14 us
  transfers between devices with their start and end apart: 27, of which 11 were waited for; matrix products, arithmetic and copies ran while one was open for 30% of the time, Pallas kernels for 15%

profile of v1, /device:TPU:1, one launch (start us, length us, event | category | flops | bytes accessed | tf_op | source)
XLA Modules:
  0.0 267.1 jit_solution(6814180565220224714)
XLA Ops:
  6.5 1.0 copy.85
  7.5 0.8 all_gather_reshape.3
  8.4 1.0 dynamic-slice_bitcast_fusion.5
  9.4 4.5 %collective-permute-start.2 = (bf16[64,1024]{1,0:T(8,128)(2,1)S(1)}, bf16[64,1024]{1,0:T(8,128)(2,1)S(1)}, u32[]{:S(2)}, u32[]{:S(2)}) collective-permute-start(bf16[64,1024]{1,0:T(8,128)(2,1)S(1)} %pad_maximum_fusion.8), channel_id=1, source_target_pairs={{0,64},{2,66},{4,68},{6,70},{8,72},{10,74},{12,76},{14,78},{16,80}... | collective-permute-start | bytes 393224 | tf_op jit(solution)/shard_map/ppermute | solution.py:33
  14.0 0.7 collective-permute-start.3
  15.2 1.9 collective-permute-done.2
  17.2 4.2 %collective-permute-done.3 = bf16[64,1024]{1,0:T(8,128)(2,1)S(1)} collective-permute-done((bf16[64,1024]{1,0:T(8,128)(2,1)S(1)}, bf16[64,1024]{1,0:T(8,128)(2,1)S(1)}, u32[]{:S(2)}, u32[]{:S(2)}) %collective-permute-start.3) | collective-permute-done | bytes 131104 | tf_op jit(solution)/shard_map/ppermute | solution.py:33
  21.6 1.3 collective-permute-start.6
  22.9 2.5 collective-permute-start.5
  25.3 1.2 collective-permute-start.4
  26.5 0.6 fusion.52
  27.1 1.4 collective-permute-start.13
  28.5 1.7 collective-permute-done.6
  30.2 2.9 %collective-permute-start.12 = (bf16[256,512]{1,0:T(8,128)(2,1)S(1)}, bf16[256,512]{1,0:T(8,128)(2,1)S(1)}, u32[]{:S(2)}, u32[]{:S(2)}) collective-permute-start(bf16[256,512]{1,0:T(8,128)(2,1)S(1)} %get-tuple-element.31), channel_id=1, source_target_pairs={{0,32},{2,34},{4,36},{6,38},{8,40},{10,42},{12,44},{14,46},{16,48}... | collective-permute-start | bytes 786440 | tf_op jit(solution)/shard_map/ppermute | solution.py:33
  33.1 3.9 %collective-permute-done.5 = bf16[256,512]{1,0:T(8,128)(2,1)S(1)} collective-permute-done((bf16[256,512]{1,0:T(8,128)(2,1)S(1)}, bf16[256,512]{1,0:T(8,128)(2,1)S(1)}, u32[]{:S(2)}, u32[]{:S(2)}) %collective-permute-start.5) | collective-permute-done | bytes 262176 | tf_op jit(solution)/shard_map/ppermute | solution.py:33
  37.0 2.8 %collective-permute-start.11 = (bf16[256,512]{1,0:T(8,128)(2,1)S(1)}, bf16[256,512]{1,0:T(8,128)(2,1)S(1)}, u32[]{:S(2)}, u32[]{:S(2)}) collective-permute-start(bf16[256,512]{1,0:T(8,128)(2,1)S(1)} %get-tuple-element.31), channel_id=1, source_target_pairs={{0,48},{2,50},{4,52},{6,54},{8,56},{10,58},{12,60},{14,62},{16,0},... | collective-permute-start | bytes 786440 | tf_op jit(solution)/shard_map/ppermute | solution.py:33
  40.4 1.0 collective-permute-start.8
  41.9 2.8 %collective-permute-done.11 = bf16[256,512]{1,0:T(8,128)(2,1)S(1)} collective-permute-done((bf16[256,512]{1,0:T(8,128)(2,1)S(1)}, bf16[256,512]{1,0:T(8,128)(2,1)S(1)}, u32[]{:S(2)}, u32[]{:S(2)}) %collective-permute-start.11) | collective-permute-done | bytes 262176 | tf_op jit(solution)/shard_map/ppermute | solution.py:33
  44.9 2.7 collective-permute-start.14
  48.3 4.6 %constant_dynamic-slice_fusion.1 = bf16[512,4096]{1,0:T(8,128)(2,1)} fusion(bf16[1024,4096]{1,0:T(8,128)(2,1)} %param.14, s32[]{:T(128)S(6)} %select_n.177), kind=kLoop, calls=%fused_computation.138 | loop fusion | bytes 8388612 | tf_op jit(solution)/shard_map/dynamic_slice | solution.py:290
  52.9 0.7 pad_maximum_fusion.7
  53.6 15.2 %collective-permute-done.7 = bf16[1024,512]{1,0:T(8,128)(2,1)} collective-permute-done((bf16[1024,512]{1,0:T(8,128)(2,1)S(1)}, bf16[1024,512]{1,0:T(8,128)(2,1)}, u32[]{:S(2)}, u32[]{:S(2)}) %collective-permute-start.7) | collective-permute-done | bytes 1048608 | tf_op jit(solution)/shard_map/ppermute | solution.py:33
  68.8 4.3 %collective-permute-start.20 = (bf16[512,4096]{1,0:T(8,128)(2,1)}, bf16[512,4096]{1,0:T(8,128)(2,1)}, u32[]{:S(2)}, u32[]{:S(2)}) collective-permute-start(bf16[512,4096]{1,0:T(8,128)(2,1)} %constant_dynamic-slice_fusion.1), channel_id=1, source_target_pairs={{0,1},{1,0},{2,67},{3,66},{4,5},{5,4},{6,71},{7,70},{8,9},{9,8},{1... | collective-permute-start | bytes 12582920 | tf_op jit(solution)/shard_map/ppermute | solution.py:291
  73.1 1.9 slice.181
  74.9 3.5 %collective-permute-start.9 = (bf16[512,512]{1,0:T(8,128)(2,1)}, bf16[512,512]{1,0:T(8,128)(2,1)}, u32[]{:S(2)}, u32[]{:S(2)}) collective-permute-start(bf16[512,512]{1,0:T(8,128)(2,1)} %slice.181), channel_id=1, source_target_pairs={{0,48},{2,50},{4,52},{6,54},{8,56},{10,58},{12,60},{14,62},{16,0},... | collective-permute-start | bytes 1572872 | tf_op jit(solution)/shard_map/ppermute | solution.py:33
  78.5 1.9 slice.182
  80.3 1.9 slice.185
  82.2 1.9 slice.184
  84.1 3.9 %all-gather.5.cloned.1.call-done = f32[64,4,2048]{2,1,0:T(4,128)} async-done(((f32[1,4,2048]{2,1,0:T(4,128)}), f32[64,4,2048]{2,1,0:T(4,128)}) %all-gather.5.cloned.1.call-update) | async-done | bytes 2097168 | tf_op jit(solution)/shard_map/all_gather | solution.py:295
  88.0 2.1 constant_dynamic-slice_fusion.4
  91.5 12.1 %add_reduce_fusion.1 = (f32[64,64]{1,0:T(8,128)}, f32[64,64]{1,0:T(8,128)}, f32[64,64]{1,0:T(8,128)S(1)}, f32[64,64]{1,0:T(8,128)S(1)}) fusion(f32[64]{0:T(128)S(1)} %get-tuple-element.54, f32[64]{0:T(128)S(1)} %get-tuple-element.26, s32[64,64]{1,0:T(8,128)S(1)} %add_select_fusion.4, f32[64]{0:T(128)S(1)} %get-tuple-element.55, f32[64]{0:T(128)S(1)} %get-tuple-element.25), kind=kLoop, calls=%fused_computation.13 | loop fusion | flops 7847936 | bytes 82944 | tf_op jit(solution)/shard_map/reduce_sum | solution.py:203
  103.6 0.9 multiply_subtract_fusion
  107.8 1.4 collective-permute-start.16
  109.3 23.3 %reorder_tokens.1 = (bf16[1024,4096]{1,0:T(8,128)(2,1)}, bf16[1024,4096]{1,0:T(8,128)(2,1)}) custom-call(s32[2,32]{1,0:T(2,128)} %pad_add_fusion.order_ref, bf16[512,4096]{1,0:T(8,128)(2,1)} %bitcast.73, bf16[512,4096]{1,0:T(8,128)(2,1)} %collective-permute-done.1.a1.b1, bf16[512,4096]{1,0:T(8,128)(2,1)} %bitcast.74, ...), custom_call_target="tpu_custom_call" | custom-call | bytes 33554432 | tf_op jit(solution)/shard_map/reorder_tokens/pallas_call | solution.py:73
  132.5 3.3 %fusion.13 = f32[512,1024]{0,1:T(8,128)S(1)} fusion(bf16[1024,512]{1,0:T(8,128)(2,1)} %collective-permute-done.8, bf16[1024,4096]{1,0:T(8,128)(2,1)} %get-tuple-element.7), kind=kOutput, calls=%fused_computation.26 | convolution fusion | flops 1073741824 | bytes 5242880 | tf_op jit(solution)/shard_map/dot_general | solution.py:217
  135.8 3.3 %fusion.15 = f32[512,1024]{0,1:T(8,128)S(1)} fusion(bf16[1024,512]{1,0:T(8,128)(2,1)} %collective-permute-done.7, bf16[1024,4096]{1,0:T(8,128)(2,1)} %get-tuple-element.7), kind=kOutput, calls=%fused_computation.28 | convolution fusion | flops 1073741824 | bytes 5242880 | tf_op jit(solution)/shard_map/dot_general | solution.py:217
  139.1 2.6 fusion.7
  141.7 2.6 fusion.9
  144.4 1.8 fusion.33
  146.3 1.3 fusion.17
  147.6 0.7 fusion.27
  148.8 1.2 fusion.11
  150.0 1.9 add_convert_fusion.1
  152.0 3.1 %fusion.20 = (bf16[512,1024]{0,1:T(8,128)(2,1)S(1)}, bf16[512,1024]{0,1:T(8,128)(2,1)}) fusion(bf16[512,1024]{0,1:T(8,128)(2,1)S(1)} %add_convert_fusion.1, bf16[512,512]{1,0:T(8,128)(2,1)} %collective-permute-done.17, bf16[1024,4096]{1,0:T(8,128)(2,1)S(1)} %bitcast.84, f32[512,1024]{0,1:T(8,128)S(1)} %fusion.27, f32[512,1024]{0,1:T(8,128)S(1)} %fusion.7, ...), kind=kOutput, calls=%fused_computation.33 | convolution fusion | flops 541589504 | bytes 13107200 | tf_op jit(solution)/shard_map/dot_general | solution.py:217
  155.1 1.3 copy.84
  156.4 4.9 %all-to-all-start = ((bf16[32,16,1024]{2,1,0:T(8,128)(2,1)}), bf16[32,16,1024]{2,1,0:T(8,128)(2,1)S(1)}, u32[]{:S(2)}, u32[]{:S(2)}) async-start(bf16[32,16,1024]{2,1,0:T(8,128)(2,1)} %bitcast.9), calls=%async_computation | async-start | bytes 2097152 | tf_op jit(solution)/shard_map/all_to_all | solution.py:306
  161.7 19.7 %all-to-all-done.x_ref = bf16[32,16,1024]{2,1,0:T(8,128)(2,1)S(1)} async-done(((bf16[32,16,1024]{2,1,0:T(8,128)(2,1)}), bf16[32,16,1024]{2,1,0:T(8,128)(2,1)S(1)}, u32[]{:S(2)}, u32[]{:S(2)}) %all-to-all-start) | async-done | bytes 1048608 | tf_op jit(solution)/shard_map/all_to_all | solution.py:306
  181.4 1.6 copy-done
  183.0 18.0 %long_conv.1 = bf16[32,16,1024]{2,1,0:T(8,128)(2,1)} custom-call(bf16[32,16,1024]{2,1,0:T(8,128)(2,1)S(1)} %all-to-all-done.x_ref, bf16[2,512,1024]{2,1,0:T(8,128)(2,1)S(1)} %copy-done, bf16[2,1024,512]{2,1,0:T(8,128)(2,1)} %constant.242.clone.inv_ref, f32[64,1024]{1,0:T(8,128)S(1)} %pad_maximum_fusion.3.tw_ref, ...), custom_call_target="tpu_custom_call" | custom-call | flops 8000000000 | bytes 8388608 | tf_op jit(solution)/shard_map/long_conv/pallas_call | solution.py:159
  201.0 5.6 %all-to-all-start.1 = ((bf16[32,16,1024]{2,1,0:T(8,128)(2,1)}), bf16[32,16,1024]{2,1,0:T(8,128)(2,1)}, u32[]{:S(2)}, u32[]{:S(2)}) async-start(bf16[32,16,1024]{2,1,0:T(8,128)(2,1)} %long_conv.1), calls=%async_computation.1 | async-start | bytes 2097152 | tf_op jit(solution)/shard_map/all_to_all | solution.py:308
  206.7 2.0 collective-permute-start.22
  208.8 14.0 %all-to-all-done.1 = bf16[32,16,1024]{2,1,0:T(8,128)(2,1)} async-done(((bf16[32,16,1024]{2,1,0:T(8,128)(2,1)}), bf16[32,16,1024]{2,1,0:T(8,128)(2,1)}, u32[]{:S(2)}, u32[]{:S(2)}) %all-to-all-start.1) | async-done | bytes 1048608 | tf_op jit(solution)/shard_map/all_to_all | solution.py:308
  222.7 1.5 bitcast_convert_fusion
  224.2 1.8 copy.98
  226.0 5.9 %convolution_convert_fusion = bf16[512,512]{0,1:T(8,128)(2,1)S(1)} fusion(bf16[512,4096]{1,0:T(8,128)(2,1)} %collective-permute-done.1.a1.b1, bf16[4096,512]{1,0:T(8,128)(2,1)} %all-gather.3.cloned.1.call-done), kind=kOutput, calls=%fused_computation.34 | convolution fusion | flops 2147745792 | bytes 8912896 | tf_op jit(solution)/shard_map/dot_general | solution.py:217
  232.0 2.3 convolution_convert_fusion.1
  234.4 0.7 multiply_convert_fusion
  235.1 2.9 %collective-permute-start.18 = (bf16[512,256]{0,1:T(8,128)(2,1)S(1)}, bf16[512,256]{0,1:T(8,128)(2,1)S(1)}, u32[]{:S(2)}, u32[]{:S(2)}) collective-permute-start(bf16[512,256]{0,1:T(8,128)(2,1)S(1)} %get-tuple-element.19), channel_id=1, source_target_pairs={{0,2},{2,0},{4,6},{6,4},{8,10},{10,8},{12,14},{14,12},{16,18},{18,... | collective-permute-start | bytes 786440 | tf_op jit(solution)/shard_map/ppermute | solution.py:33
  238.0 0.7 collective-permute-start.19
  238.7 1.0 collective-permute-start.21
  239.9 6.0 %collective-permute-done.19 = bf16[512,256]{0,1:T(8,128)(2,1)S(1)} collective-permute-done((bf16[512,256]{0,1:T(8,128)(2,1)S(1)}, bf16[512,256]{0,1:T(8,128)(2,1)S(1)}, u32[]{:S(2)}, u32[]{:S(2)}) %collective-permute-start.19) | collective-permute-done | bytes 262176 | tf_op jit(solution)/shard_map/ppermute | solution.py:322
  245.9 3.4 %fusion.94 = f32[256,4096]{1,0:T(8,128)S(1)} fusion(bf16[512,256]{0,1:T(8,128)(2,1)S(1)} %collective-permute-done.19, bf16[512,4096]{1,0:T(8,128)(2,1)} %collective-permute-done.20), kind=kOutput, calls=%fused_computation.187 | convolution fusion | flops 1073741824 | bytes 8650752 | tf_op jit(solution)/shard_map/dot_general | solution.py:332
  249.3 6.0 %convolution_add_fusion.1 = f32[256,4096]{1,0:T(8,128)S(1)} fusion(f32[256,4096]{1,0:T(8,128)S(1)} %fusion.94, bf16[1024,4096]{1,0:T(8,128)(2,1)} %param.14, bf16[512,256]{0,1:T(8,128)(2,1)S(1)} %get-tuple-element.16, bf16[512,256]{0,1:T(8,128)(2,1)S(1)} %get-tuple-element.15), kind=kOutput, calls=%fused_computation.1 | convolution fusion | flops 2149580800 | bytes 17301504 | tf_op jit(solution)/shard_map/dot_general | solution.py:332
  255.4 4.9 %fusion.1 = bf16[256,1,4096]{2,0,1:T(8,128)(2,1)} fusion(f32[256,4096]{1,0:T(8,128)S(1)} %convolution_add_fusion.1, bf16[512,256]{0,1:T(8,128)(2,1)S(1)} %collective-permute-done.21, bf16[512,4096]{1,0:T(8,128)(2,1)} %collective-permute-done.22), kind=kOutput, calls=%fused_computation.3 | convolution fusion | flops 1075838976 | bytes 10747904 | tf_op jit(solution)/shard_map/dot_general | solution.py:332
  (150 shorter events, 8.6 us)
Async XLA Ops:
  6.5 81.5 %all-gather.5.cloned.1.call-start = ((), (), s32[]{:S(2)}) async-start(), calls=%async_computation.3 | async-start | bytes 2129920 | tf_op jit(solution)/shard_map/all_gather | solution.py:295
  8.3 217.7 %all-gather.3.cloned.1.call-start = ((), (), s32[]{:S(2)}) async-start(), calls=%async_computation.2 | async-start | bytes 4325376 | tf_op jit(solution)/shard_map/all_gather | solution.py:271
  9.4 7.7 %collective-permute-start.2 = (bf16[64,1024]{1,0:T(8,128)(2,1)S(1)}, bf16[64,1024]{1,0:T(8,128)(2,1)S(1)}, u32[]{:S(2)}, u32[]{:S(2)}) collective-permute-start(bf16[64,1024]{1,0:T(8,128)(2,1)S(1)} %pad_maximum_fusion.8), channel_id=1, source_target_pairs={{0,64},{2,66},{4,68},{6,70},{8,72},{10,74},{12,76},{14,78},{16,80}... | collective-permute-start | bytes 393224 | tf_op jit(solution)/shard_map/ppermute | solution.py:33
  14.0 7.4 %collective-permute-start.3 = (bf16[64,1024]{1,0:T(8,128)(2,1)S(1)}, bf16[64,1024]{1,0:T(8,128)(2,1)S(1)}, u32[]{:S(2)}, u32[]{:S(2)}) collective-permute-start(bf16[64,1024]{1,0:T(8,128)(2,1)S(1)} %pad_maximum_fusion.9), channel_id=1, source_target_pairs={{0,66},{2,64},{4,70},{6,68},{8,74},{10,72},{12,78},{14,76},{16,82}... | collective-permute-start | bytes 393224 | tf_op jit(solution)/shard_map/ppermute | solution.py:33
  14.6 25.1 %copy-start.27 = (s32[32]{0:T(128)S(1)}, s32[32]{0:T(128)}, u32[]{:S(2)}) copy-start(s32[32]{0:T(128)} %constant.240.clone) | copy-start | bytes 388
  14.6 25.1 %copy-start.28 = (s32[32]{0:T(128)S(1)}, s32[32]{0:T(128)}, u32[]{:S(2)}) copy-start(s32[32]{0:T(128)} %constant.239.clone) | copy-start | bytes 388
  14.6 25.1 %copy-start.29 = (s32[32]{0:T(128)S(1)}, s32[32]{0:T(128)}, u32[]{:S(2)}) copy-start(s32[32]{0:T(128)} %constant.238.clone) | copy-start | bytes 388
  14.6 6.8 %collective-permute-start = (bf16[64,1536]{1,0:T(8,128)(2,1)S(1)}, bf16[64,1536]{1,0:T(8,128)(2,1)S(1)}, u32[]{:S(2)}, u32[]{:S(2)}) collective-permute-start(bf16[64,1536]{1,0:T(8,128)(2,1)S(1)} %pad_maximum_fusion.6), channel_id=1, source_target_pairs={{0,2},{2,0},{4,6},{6,4},{8,10},{10,8},{12,14},{14,12},{16,18},{18,... | collective-permute-start | bytes 589832 | tf_op jit(solution)/shard_map/ppermute | solution.py:33
  15.1 92.7 %collective-permute-start.1 = (bf16[512,4096]{1,0:T(8,128)(2,1)}, bf16[512,4096]{1,0:T(8,128)(2,1)}, u32[]{:S(2)}, u32[]{:S(2)}) collective-permute-start(bf16[512,4096]{1,0:T(8,128)(2,1)} %bitcast.72), channel_id=1, source_target_pairs={{0,2},{2,0},{4,6},{6,4},{8,10},{10,8},{12,14},{14,12},{16,18},{18,... | collective-permute-start | bytes 12582920 | tf_op jit(solution)/shard_map/ppermute | solution.py:33
  21.6 20.3 %copy-start.6 = (bf16[256,512]{1,0:T(8,128)(2,1)}, bf16[256,512]{1,0:T(8,128)(2,1)S(1)}, u32[]{:S(2)}) copy-start(bf16[256,512]{1,0:T(8,128)(2,1)S(1)} %get-tuple-element.30) | copy-start | bytes 786436
  21.6 23.3 %copy-start.4 = (bf16[256,512]{1,0:T(8,128)(2,1)}, bf16[256,512]{1,0:T(8,128)(2,1)S(1)}, u32[]{:S(2)}) copy-start(bf16[256,512]{1,0:T(8,128)(2,1)S(1)} %get-tuple-element.31) | copy-start | bytes 786436
  21.6 8.6 %collective-permute-start.6 = (bf16[256,512]{1,0:T(8,128)(2,1)S(1)}, bf16[256,512]{1,0:T(8,128)(2,1)S(1)}, u32[]{:S(2)}, u32[]{:S(2)}) collective-permute-start(bf16[256,512]{1,0:T(8,128)(2,1)S(1)} %get-tuple-element.30), channel_id=1, source_target_pairs={{0,4},{2,6},{4,8},{6,10},{8,12},{10,14},{12,0},{14,2},{16,20},{18,... | collective-permute-start | bytes 786440 | tf_op jit(solution)/shard_map/ppermute | solution.py:33
  22.9 14.1 %collective-permute-start.5 = (bf16[256,512]{1,0:T(8,128)(2,1)S(1)}, bf16[256,512]{1,0:T(8,128)(2,1)S(1)}, u32[]{:S(2)}, u32[]{:S(2)}) collective-permute-start(bf16[256,512]{1,0:T(8,128)(2,1)S(1)} %get-tuple-element.30), channel_id=1, source_target_pairs={{0,8},{2,10},{4,12},{6,14},{8,0},{10,2},{12,4},{14,6},{16,24},{18,... | collective-permute-start | bytes 786440 | tf_op jit(solution)/shard_map/ppermute | solution.py:33
  25.3 14.4 %collective-permute-start.4 = (bf16[256,512]{1,0:T(8,128)(2,1)S(1)}, bf16[256,512]{1,0:T(8,128)(2,1)S(1)}, u32[]{:S(2)}, u32[]{:S(2)}) collective-permute-start(bf16[256,512]{1,0:T(8,128)(2,1)S(1)} %get-tuple-element.30), channel_id=1, source_target_pairs={{0,12},{2,14},{4,0},{6,2},{8,4},{10,6},{12,8},{14,10},{16,28},{18,... | collective-permute-start | bytes 786440 | tf_op jit(solution)/shard_map/ppermute | solution.py:33
  27.1 13.3 %collective-permute-start.13 = (bf16[256,512]{1,0:T(8,128)(2,1)S(1)}, bf16[256,512]{1,0:T(8,128)(2,1)S(1)}, u32[]{:S(2)}, u32[]{:S(2)}) collective-permute-start(bf16[256,512]{1,0:T(8,128)(2,1)S(1)} %get-tuple-element.31), channel_id=1, source_target_pairs={{0,16},{2,18},{4,20},{6,22},{8,24},{10,26},{12,28},{14,30},{16,32}... | collective-permute-start | bytes 786440 | tf_op jit(solution)/shard_map/ppermute | solution.py:33
  30.2 11.7 %copy-start.12 = (bf16[256,512]{1,0:T(8,128)(2,1)}, bf16[256,512]{1,0:T(8,128)(2,1)S(1)}, u32[]{:S(2)}) copy-start(bf16[256,512]{1,0:T(8,128)(2,1)S(1)} %collective-permute-done.6) | copy-start | bytes 786436
  30.2 11.7 %collective-permute-start.12 = (bf16[256,512]{1,0:T(8,128)(2,1)S(1)}, bf16[256,512]{1,0:T(8,128)(2,1)S(1)}, u32[]{:S(2)}, u32[]{:S(2)}) collective-permute-start(bf16[256,512]{1,0:T(8,128)(2,1)S(1)} %get-tuple-element.31), channel_id=1, source_target_pairs={{0,32},{2,34},{4,36},{6,38},{8,40},{10,42},{12,44},{14,46},{16,48}... | collective-permute-start | bytes 786440 | tf_op jit(solution)/shard_map/ppermute | solution.py:33
  37.0 5.0 %copy-start.14 = (bf16[256,512]{1,0:T(8,128)(2,1)}, bf16[256,512]{1,0:T(8,128)(2,1)S(1)}, u32[]{:S(2)}) copy-start(bf16[256,512]{1,0:T(8,128)(2,1)S(1)} %collective-permute-done.5) | copy-start | bytes 786436
  37.0 7.8 %collective-permute-start.11 = (bf16[256,512]{1,0:T(8,128)(2,1)S(1)}, bf16[256,512]{1,0:T(8,128)(2,1)S(1)}, u32[]{:S(2)}, u32[]{:S(2)}) collective-permute-start(bf16[256,512]{1,0:T(8,128)(2,1)S(1)} %get-tuple-element.31), channel_id=1, source_target_pairs={{0,48},{2,50},{4,52},{6,54},{8,56},{10,58},{12,60},{14,62},{16,0},... | collective-permute-start | bytes 786440 | tf_op jit(solution)/shard_map/ppermute | solution.py:33
  39.8 2.2 copy-start.16
  39.9 28.9 %collective-permute-start.7 = (bf16[1024,512]{1,0:T(8,128)(2,1)S(1)}, bf16[1024,512]{1,0:T(8,128)(2,1)}, u32[]{:S(2)}, u32[]{:S(2)}) collective-permute-start(bf16[1024,512]{1,0:T(8,128)(2,1)S(1)} %pad_maximum_fusion), channel_id=1, source_target_pairs={{0,48},{2,50},{4,52},{6,54},{8,56},{10,58},{12,60},{14,62},{16,0},... | collective-permute-start | bytes 3145736 | tf_op jit(solution)/shard_map/ppermute | solution.py:33
  40.4 7.2 %copy-start.18 = (bf16[256,512]{1,0:T(8,128)(2,1)}, bf16[256,512]{1,0:T(8,128)(2,1)S(1)}, u32[]{:S(2)}) copy-start(bf16[256,512]{1,0:T(8,128)(2,1)S(1)} %collective-permute-done.13) | copy-start | bytes 786436
  40.4 34.6 %collective-permute-start.8 = (bf16[1024,512]{1,0:T(8,128)(2,1)S(1)}, bf16[1024,512]{1,0:T(8,128)(2,1)}, u32[]{:S(2)}, u32[]{:S(2)}) collective-permute-start(bf16[1024,512]{1,0:T(8,128)(2,1)S(1)} %pad_maximum_fusion), channel_id=1, source_target_pairs={{0,16},{2,18},{4,20},{6,22},{8,24},{10,26},{12,28},{14,30},{16,32}... | collective-permute-start | bytes 3145736 | tf_op jit(solution)/shard_map/ppermute | solution.py:33
  41.9 5.7 %copy-start.20 = (bf16[256,512]{1,0:T(8,128)(2,1)}, bf16[256,512]{1,0:T(8,128)(2,1)S(1)}, u32[]{:S(2)}) copy-start(bf16[256,512]{1,0:T(8,128)(2,1)S(1)} %collective-permute-done.12) | copy-start | bytes 786436
  44.8 2.8 %copy-start.22 = (bf16[256,512]{1,0:T(8,128)(2,1)}, bf16[256,512]{1,0:T(8,128)(2,1)S(1)}, u32[]{:S(2)}) copy-start(bf16[256,512]{1,0:T(8,128)(2,1)S(1)} %collective-permute-done.11) | copy-start | bytes 786436
  44.8 35.5 %collective-permute-start.15 = (bf16[1024,512]{1,0:T(8,128)(2,1)S(1)}, bf16[1024,512]{1,0:T(8,128)(2,1)}, u32[]{:S(2)}, u32[]{:S(2)}) collective-permute-start(bf16[1024,512]{1,0:T(8,128)(2,1)S(1)} %pad_maximum_fusion.1), channel_id=1, source_target_pairs={{0,4},{2,6},{4,8},{6,10},{8,12},{10,14},{12,0},{14,2},{16,20},{18,... | collective-permute-start | bytes 3145736 | tf_op jit(solution)/shard_map/ppermute | solution.py:33
  44.9 37.3 %collective-permute-start.14 = (bf16[1024,512]{1,0:T(8,128)(2,1)S(1)}, bf16[1024,512]{1,0:T(8,128)(2,1)}, u32[]{:S(2)}, u32[]{:S(2)}) collective-permute-start(bf16[1024,512]{1,0:T(8,128)(2,1)S(1)} %pad_maximum_fusion.1), channel_id=1, source_target_pairs={{0,12},{2,14},{4,0},{6,2},{8,4},{10,6},{12,8},{14,10},{16,28},{18,... | collective-permute-start | bytes 3145736 | tf_op jit(solution)/shard_map/ppermute | solution.py:33
  68.8 137.9 %collective-permute-start.20 = (bf16[512,4096]{1,0:T(8,128)(2,1)}, bf16[512,4096]{1,0:T(8,128)(2,1)}, u32[]{:S(2)}, u32[]{:S(2)}) collective-permute-start(bf16[512,4096]{1,0:T(8,128)(2,1)} %constant_dynamic-slice_fusion.1), channel_id=1, source_target_pairs={{0,1},{1,0},{2,67},{3,66},{4,5},{5,4},{6,71},{7,70},{8,9},{9,8},{1... | collective-permute-start | bytes 12582920 | tf_op jit(solution)/shard_map/ppermute | solution.py:291
  74.9 69.5 %collective-permute-start.9 = (bf16[512,512]{1,0:T(8,128)(2,1)}, bf16[512,512]{1,0:T(8,128)(2,1)}, u32[]{:S(2)}, u32[]{:S(2)}) collective-permute-start(bf16[512,512]{1,0:T(8,128)(2,1)} %slice.181), channel_id=1, source_target_pairs={{0,48},{2,50},{4,52},{6,54},{8,56},{10,58},{12,60},{14,62},{16,0},... | collective-permute-start | bytes 1572872 | tf_op jit(solution)/shard_map/ppermute | solution.py:33
  80.3 69.7 %collective-permute-start.10 = (bf16[512,512]{1,0:T(8,128)(2,1)}, bf16[512,512]{1,0:T(8,128)(2,1)}, u32[]{:S(2)}, u32[]{:S(2)}) collective-permute-start(bf16[512,512]{1,0:T(8,128)(2,1)} %slice.182), channel_id=1, source_target_pairs={{0,16},{2,18},{4,20},{6,22},{8,24},{10,26},{12,28},{14,30},{16,32}... | collective-permute-start | bytes 1572872 | tf_op jit(solution)/shard_map/ppermute | solution.py:33
  82.2 69.7 %collective-permute-start.17 = (bf16[512,512]{1,0:T(8,128)(2,1)}, bf16[512,512]{1,0:T(8,128)(2,1)}, u32[]{:S(2)}, u32[]{:S(2)}) collective-permute-start(bf16[512,512]{1,0:T(8,128)(2,1)} %slice.185), channel_id=1, source_target_pairs={{0,4},{2,6},{4,8},{6,10},{8,12},{10,14},{12,0},{14,2},{16,20},{18,... | collective-permute-start | bytes 1572872 | tf_op jit(solution)/shard_map/ppermute | solution.py:33
  104.5 0.6 copy-start.9
  105.3 2.4 copy-start.10
  105.3 2.5 copy-start.24
  105.3 2.5 copy-start.25
  105.6 2.2 copy-start.8
  107.8 39.8 %collective-permute-start.16 = (bf16[512,512]{1,0:T(8,128)(2,1)S(1)}, bf16[512,512]{1,0:T(8,128)(2,1)S(1)}, u32[]{:S(2)}, u32[]{:S(2)}) collective-permute-start(bf16[512,512]{1,0:T(8,128)(2,1)S(1)} %copy-done.8), channel_id=1, source_target_pairs={{0,12},{2,14},{4,0},{6,2},{8,4},{10,6},{12,8},{14,10},{16,28},{18,... | collective-permute-start | bytes 1572872 | tf_op jit(solution)/shard_map/ppermute | solution.py:33
  132.5 6.5 %slice-start = ((s8[8388608]{0:T(1024)(128)(4,1)}), s8[4194304]{0:T(1024)(128)(4,1)S(1)}, s32[]{:S(2)}) async-start(s8[8388608]{0:T(1024)(128)(4,1)} %bitcast.83), calls=%async_computation.4 | async-start | bytes 8388608
  135.8 3.3 %slice-start.1 = ((s8[8388608]{0:T(1024)(128)(4,1)}), s8[4194304]{0:T(1024)(128)(4,1)S(1)}, s32[]{:S(2)}) async-start(s8[8388608]{0:T(1024)(128)(4,1)} %bitcast.83), calls=%async_computation.5 | async-start | bytes 8388608
  139.1 5.3 %slice-start.2 = ((s8[8388608]{0:T(1024)(128)(4,1)}), s8[4194304]{0:T(1024)(128)(4,1)S(1)}, s32[]{:S(2)}) async-start(s8[8388608]{0:T(1024)(128)(4,1)} %bitcast.87), calls=%async_computation.6 | async-start | bytes 8388608
  141.7 2.7 %slice-start.3 = ((s8[8388608]{0:T(1024)(128)(4,1)}), s8[4194304]{0:T(1024)(128)(4,1)S(1)}, s32[]{:S(2)}) async-start(s8[8388608]{0:T(1024)(128)(4,1)} %bitcast.87), calls=%async_computation.7 | async-start | bytes 8388608
  144.4 1.9 copy-start.7
  144.4 1.9 copy-start.13
  144.4 1.9 copy-start.15
  144.4 1.9 copy-start.17
  147.6 1.0 copy-start.5
  147.6 1.0 copy-start.19
  147.6 1.1 copy-start.21
  147.6 1.2 copy-start.23
  155.1 6.2 %copy-start.11 = (f32[64,64]{1,0:T(8,128)S(1)}, f32[64,64]{1,0:T(8,128)}, u32[]{:S(2)}) copy-start(f32[64,64]{1,0:T(8,128)} %get-tuple-element.46) | copy-start | bytes 49156
  156.4 25.0 %all-to-all-start = ((bf16[32,16,1024]{2,1,0:T(8,128)(2,1)}), bf16[32,16,1024]{2,1,0:T(8,128)(2,1)S(1)}, u32[]{:S(2)}, u32[]{:S(2)}) async-start(bf16[32,16,1024]{2,1,0:T(8,128)(2,1)} %bitcast.9), calls=%async_computation | async-start | bytes 2097152 | tf_op jit(solution)/shard_map/all_to_all | solution.py:306
  181.4 1.6 copy-start
  201.0 7.7 %copy-start.26 = (f32[1024]{0:T(1024)S(1)}, f32[1024]{0:T(1024)}, u32[]{:S(2)}) copy-start(f32[1024]{0:T(1024)} %param.13) | copy-start | bytes 12292
  201.0 21.7 %all-to-all-start.1 = ((bf16[32,16,1024]{2,1,0:T(8,128)(2,1)}), bf16[32,16,1024]{2,1,0:T(8,128)(2,1)}, u32[]{:S(2)}, u32[]{:S(2)}) async-start(bf16[32,16,1024]{2,1,0:T(8,128)(2,1)} %long_conv.1), calls=%async_computation.1 | async-start | bytes 2097152 | tf_op jit(solution)/shard_map/all_to_all | solution.py:308
  206.7 48.7 %collective-permute-start.22 = (bf16[512,4096]{1,0:T(8,128)(2,1)}, bf16[512,4096]{1,0:T(8,128)(2,1)}, u32[]{:S(2)}, u32[]{:S(2)}) collective-permute-start(bf16[512,4096]{1,0:T(8,128)(2,1)} %collective-permute-done.20), channel_id=1, source_target_pairs={{0,2},{2,0},{4,6},{6,4},{8,10},{10,8},{12,14},{14,12},{16,18},{18,... | collective-permute-start | bytes 12582920 | tf_op jit(solution)/shard_map/ppermute | solution.py:33
  226.0 5.9 %copy-start.1 = (bf16[512,1,4096]{2,0,1:T(8,128)(2,1)S(1)}, bf16[512,1,4096]{2,0,1:T(8,128)(2,1)}, u32[]{:S(2)}) copy-start(bf16[512,1,4096]{2,0,1:T(8,128)(2,1)} %param.10) | copy-start | bytes 12582916
  226.0 5.9 %copy-start.30 = (bf16[4096,512]{1,0:T(8,128)(2,1)S(1)}, bf16[4096,512]{1,0:T(8,128)(2,1)}, u32[]{:S(2)}) copy-start(bf16[4096,512]{1,0:T(8,128)(2,1)} %all-gather.3.cloned.1.call-done) | copy-start | bytes 12582916
  232.0 2.4 copy-start.2
  232.0 2.4 copy-start.3
  235.1 4.6 %collective-permute-start.18 = (bf16[512,256]{0,1:T(8,128)(2,1)S(1)}, bf16[512,256]{0,1:T(8,128)(2,1)S(1)}, u32[]{:S(2)}, u32[]{:S(2)}) collective-permute-start(bf16[512,256]{0,1:T(8,128)(2,1)S(1)} %get-tuple-element.19), channel_id=1, source_target_pairs={{0,2},{2,0},{4,6},{6,4},{8,10},{10,8},{12,14},{14,12},{16,18},{18,... | collective-permute-start | bytes 786440 | tf_op jit(solution)/shard_map/ppermute | solution.py:33
  238.0 7.9 %collective-permute-start.19 = (bf16[512,256]{0,1:T(8,128)(2,1)S(1)}, bf16[512,256]{0,1:T(8,128)(2,1)S(1)}, u32[]{:S(2)}, u32[]{:S(2)}) collective-permute-start(bf16[512,256]{0,1:T(8,128)(2,1)S(1)} %get-tuple-element.18), channel_id=1, source_target_pairs={{0,1},{1,0},{2,3},{3,2},{4,5},{5,4},{6,7},{7,6},{8,9},{9,8},{10,11... | collective-permute-start | bytes 786440 | tf_op jit(solution)/shard_map/ppermute | solution.py:322
  238.7 16.7 %collective-permute-start.21 = (bf16[512,256]{0,1:T(8,128)(2,1)S(1)}, bf16[512,256]{0,1:T(8,128)(2,1)S(1)}, u32[]{:S(2)}, u32[]{:S(2)}) collective-permute-start(bf16[512,256]{0,1:T(8,128)(2,1)S(1)} %get-tuple-element.17), channel_id=1, source_target_pairs={{0,3},{1,2},{2,1},{3,0},{4,7},{5,6},{6,5},{7,4},{8,11},{9,10},{10,... | collective-permute-start | bytes 786440 | tf_op jit(solution)/shard_map/ppermute | solution.py:327
Sparse Core Ops, SparseCore 0:
  10.6 77.3 all-gather.4
  91.0 83.2 all-gather.2

commit v2 on v1

--- a/solution.py
+++ b/solution.py
@@ -12,6 +12,7 @@
 
 BF16 = jnp.bfloat16
 F32 = jnp.float32
+HIGH = lax.Precision.HIGHEST
 SEQ = 64
 CHIPS = 32
 SAME_CORE = [[2 * p + j for p in range(CHIPS)] for j in range(2)]
@@ -59,37 +60,272 @@
     return forward, inverse
 
 
-def reorder_kernel(order_ref, a0, a1, b0, b1, out_a, out_b):
-    rows = a0.shape[0]
-    out_a[:rows, :] = a0[...]
-    out_a[rows:, :] = a1[...]
-    out_b[:rows, :] = b0[...]
-    out_b[rows:, :] = b1[...]
-
-
-def reorder(order, mine, other):
+def picked(order_ref, row, group, tok_ref):
+    blocks = [
+        tok_ref[:, pl.ds(pl.multiple_of(order_ref[row, group * 8 + i] * 128, 128), 128)]
+        for i in range(8)
+    ]
+    return jnp.concatenate(blocks, axis=1)
+
+
+def first_kernel(order_ref, mine_ref, other_ref, *refs):
+    weights, (key_ref, value_ref, key_tok_ref, value_tok_ref) = refs[:6], refs[6:]
+
+    def run(tok_ref):
+        for row, total_ref, last_ref in ((0, key_ref, key_tok_ref), (1, value_ref, value_tok_ref)):
+            line, e1, e3 = weights[3 * row : 3 * row + 3]
+            total = jnp.dot(picked(order_ref, row, 0, tok_ref), line[...], preferred_element_type=F32)
+            total += jnp.dot(picked(order_ref, row, 1, tok_ref), e1[...], preferred_element_type=F32)
+            total += jnp.dot(picked(order_ref, row, 3, tok_ref), e3[...], preferred_element_type=F32)
+            total_ref[...] = total
+            last_ref[...] = picked(order_ref, row, 2, tok_ref)
+
+    step = pl.program_id(0)
+
+    @pl.when(step < 2)
+    def _():
+        run(mine_ref)
+
+    @pl.when(step >= 2)
+    def _():
+        run(other_ref)
+
+
+def first_part(order, mine, other, key_pieces, value_pieces):
     rows, width = mine.shape
-    blocks = width // 128
+    chan = key_pieces[0].shape[1]
+    tile = rows // 2
+    weights = [key_pieces[0], key_pieces[1], key_pieces[4]]
+    weights += [value_pieces[0], value_pieces[1], value_pieces[4]]
+    quarter = width // 4
     return pl.pallas_call(
-        reorder_kernel,
+        first_kernel,
         grid_spec=pltpu.PrefetchScalarGridSpec(
             num_scalar_prefetch=1,
-            grid=(blocks,),
+            grid=(4,),
             in_specs=[
-                pl.BlockSpec((rows, 128), lambda i, o: (0, o[0, i])),
-                pl.BlockSpec((rows, 128), lambda i, o: (0, o[0, i])),
-                pl.BlockSpec((rows, 128), lambda i, o: (0, o[1, i])),
-                pl.BlockSpec((rows, 128), lambda i, o: (0, o[1, i])),
+                pl.BlockSpec((tile, width), lambda i, o: (jnp.minimum(i, 1), 0)),
+                pl.BlockSpec((tile, width), lambda i, o: (jnp.maximum(i - 2, 0), 0)),
+            ]
+            + [pl.BlockSpec((quarter, chan), lambda i, o: (0, 0))] * 6,
+            out_specs=[
+                pl.BlockSpec((tile, chan), lambda i, o: (i, 0)),
+                pl.BlockSpec((tile, chan), lambda i, o: (i, 0)),
+                pl.BlockSpec((tile, quarter), lambda i, o: (i, 0)),
+                pl.BlockSpec((tile, quarter), lambda i, o: (i, 0)),
+            ],
+        ),
+        out_shape=[jax.ShapeDtypeStruct((2 * rows, chan), F32)] * 2
+        + [jax.ShapeDtypeStruct((2 * rows, quarter), BF16)] * 2,
+        compiler_params=pltpu.CompilerParams(vmem_limit_bytes=48 * 2**20),
+        cost_estimate=pl.CostEstimate(
+            flops=2 * 2 * 2 * rows * 3 * quarter * chan, bytes_accessed=22 * 2**20, transcendentals=0
+        ),
+        name="first_part",
+    )(order, mine, other, *weights)
+
+
+def last_kernel(key_ref, value_ref, key_tok_ref, value_tok_ref, ka, kb, va, vb, out_ref, send_ref):
+    half = ka.shape[0]
+
+    def finish(total_ref, tok_ref, wa, wb):
+        total = total_ref[...]
+        total += jnp.dot(tok_ref[:, :half], wa[...], preferred_element_type=F32)
+        total += jnp.dot(tok_ref[:, half:], wb[...], preferred_element_type=F32)
+        return total.astype(BF16).astype(F32)
+
+    source = finish(key_ref, key_tok_ref, ka, kb) * finish(value_ref, value_tok_ref, va, vb)
+    source = source.T
+    out_ref[...] = source
+    send_ref[...] = source.astype(BF16)
+
+
+def last_part(first, key_pieces, value_pieces):
+    total, chan = first[0].shape
+    quarter = first[2].shape[1]
+    tile = total // 4
+    weights = [*key_pieces[2:4], *value_pieces[2:4]]
+    return pl.pallas_call(
+        last_kernel,
+        grid=(4,),
+        in_specs=[pl.BlockSpec((tile, chan), lambda i: (i, 0))] * 2
+        + [pl.BlockSpec((tile, quarter), lambda i: (i, 0))] * 2
+        + [pl.BlockSpec((quarter // 2, chan), lambda i: (0, 0))] * 4,
+        out_specs=[pl.BlockSpec((chan, tile), lambda i: (0, i))] * 2,
+        out_shape=[
+            jax.ShapeDtypeStruct((chan, total), F32),
+            jax.ShapeDtypeStruct((chan, total), BF16),
+        ],
+        compiler_params=pltpu.CompilerParams(vmem_limit_bytes=48 * 2**20),
+        cost_estimate=pl.CostEstimate(
+            flops=2 * 2 * total * quarter * chan, bytes_accessed=13 * 2**20, transcendentals=0
+        ),
+        name="last_part",
+    )(*first, *weights)
+
+
+def gate_kernel(mine_ref, other_ref, weight_ref, out_ref):
+    step = pl.program_id(0)
+    chips, deep, _ = weight_ref.shape
+    depth = deep // 4
+
+    def run(tok_ref):
+        for k in range(0, 4, 2):
+            parts = [
+                weight_ref[:, i * depth : (i + 1) * depth, :].reshape(chips * depth, 128)
+                for i in (k, k + 1)
+            ]
+            weight = jnp.concatenate(parts, axis=1)
+            gate = jnp.dot(tok_ref[...], weight, preferred_element_type=F32)
+            out_ref[k * 128 : (k + 2) * 128, :] = gate.T.astype(BF16)
+
+    @pl.when(step < 2)
+    def _():
+        run(mine_ref)
+
+    @pl.when(step >= 2)
+    def _():
+        run(other_ref)
+
+
+def gate_part(mine, other, gathered):
+    rows, width = mine.shape
+    chips = gathered.shape[0]
+    depth = width // chips
+    chan = 4 * 128
+    tile = rows // 2
+    return pl.pallas_call(
+        gate_kernel,
+        grid=(4,),
+        in_specs=[
+            pl.BlockSpec((tile, width), lambda i: (jnp.minimum(i, 1), 0)),
+            pl.BlockSpec((tile, width), lambda i: (jnp.maximum(i - 2, 0), 0)),
+            pl.BlockSpec((chips, 4 * depth, 128), lambda i: (0, 0, 0)),
+        ],
+        out_specs=pl.BlockSpec((chan, tile), lambda i: (0, i)),
+        out_shape=jax.ShapeDtypeStruct((chan, 2 * rows), BF16),
+        compiler_params=pltpu.CompilerParams(vmem_limit_bytes=48 * 2**20),
+        cost_estimate=pl.CostEstimate(
+            flops=2 * 2 * rows * width * chan, bytes_accessed=13 * 2**20, transcendentals=0
+        ),
+        name="gate_part",
+    )(mine, other, gathered)
+
+
+def mix_kernel(here, near_h, far_h, w_here, w_near, w_far, out_ref, lhs_ref):
+    @pl.when(pl.program_id(0) == 0)
+    def _():
+        n, m = here.shape[0], near_h.shape[0]
+        lhs_ref[:, :n] = here[...].astype(F32).T.astype(BF16)
+        lhs_ref[:, n : n + m] = near_h[...].astype(F32).T.astype(BF16)
+        lhs_ref[:, n + m :] = far_h[...].astype(F32).T.astype(BF16)
+
+    n, m = here.shape[0], near_h.shape[0]
+    total = jnp.dot(lhs_ref[:, :n], w_here[...], preferred_element_type=F32)
+    total += jnp.dot(lhs_ref[:, n : n + m], w_near[...], preferred_element_type=F32)
+    total += jnp.dot(lhs_ref[:, n + m :], w_far[...], preferred_element_type=F32)
+    out_ref[...] = total.astype(BF16)
+
+
+def mix_part(here, near_h, far_h, w_here, w_near, w_far):
+    rows = here.shape[1]
+    width = w_here.shape[1]
+    tile = width // 8
+
+    def whole(g):
+        return pl.BlockSpec(g.shape, lambda i: (0, 0))
+
+    def tiled(w):
+        return pl.BlockSpec((w.shape[0], tile), lambda i: (0, i))
+
+    depth = here.shape[0] + near_h.shape[0] + far_h.shape[0]
+    return pl.pallas_call(
+        mix_kernel,
+        grid=(8,),
+        in_specs=[whole(here), whole(near_h), whole(far_h), tiled(w_here), tiled(w_near), tiled(w_far)],
+        out_specs=pl.BlockSpec((rows, tile), lambda i: (0, i)),
+        out_shape=jax.ShapeDtypeStruct((rows, width), BF16),
+        scratch_shapes=[pltpu.VMEM((rows, depth), BF16)],
+        compiler_params=pltpu.CompilerParams(vmem_limit_bytes=48 * 2**20),
+        cost_estimate=pl.CostEstimate(
+            flops=2 * rows * depth * width, bytes_accessed=19 * 2**20, transcendentals=0
+        ),
+        name="mix_part",
+    )(here, near_h, far_h, w_here, w_near, w_far)
+
+
+def filter_kernel(z_ref, x_ref, cs_ref, twist_ref, f_ref, m_ref):
+    chips, _, lanes = x_ref.shape
+    x = x_ref[...].reshape(2 * chips, 2, 16, lanes)
+    points = 2 * chips * 16
+    rows, cols = points // 2, lanes // 2
+    upper = x[:, 0].reshape(points, lanes)
+    lower = x[:, 1].reshape(points, lanes)
+    whole = (upper.astype(F32) + lower.astype(F32)).T
+    i = lax.broadcasted_iota(jnp.int32, (rows, rows), 0)
+    j = lax.broadcasted_iota(jnp.int32, (rows, rows), 1)
+    mirror = (i + j == rows).astype(F32).astype(BF16)
+    i = lax.broadcasted_iota(jnp.int32, (lanes, lanes), 0)
+    j = lax.broadcasted_iota(jnp.int32, (lanes, lanes), 1)
+    flip = ((i // cols == j // cols) & (i % cols + j % cols == cols - 1)).astype(F32).astype(BF16)
+
+    def mirrored(part):
+        turned = jnp.dot(flip, part[:, rows:], preferred_element_type=F32).astype(BF16)
+        return jnp.dot(turned, mirror, preferred_element_type=F32)
+
+    other = mirrored(upper.astype(F32).T.astype(BF16)) + mirrored(lower.astype(F32).T.astype(BF16))
+    f_ref[:, :rows] = 0.5 * (whole[:cols, :rows] + other[:cols])
+    f_ref[:, rows:] = 0.5 * (whole[cols:, :rows] - other[cols:])
+    c, s = cs_ref[0], cs_ref[1]
+
+    def contract(left, right):
+        return lax.dot_general(
+            left, right, (((0,), (0,)), ((), ())), precision=HIGH, preferred_element_type=F32
+        )
+
+    m_ref[...] = jnp.zeros_like(m_ref)
+    for n, k in enumerate((0, rows)):
+        e_re, e_im = whole[:cols, k : k + 1], whole[cols:, k : k + 1]
+        u = c * e_re - s * e_im
+        v = s * e_re + c * e_im
+        g = contract(u, c) + contract(v, s)
+        if n:
+            g = g * twist_ref[0] - (contract(v, c) - contract(u, s)) * twist_ref[1]
+        g_upper = g.astype(BF16)
+        g_lower = (g - g_upper.astype(F32)).astype(BF16)
+        spot = slice(n * cols, (n + 1) * cols)
+        m_ref[0, spot, spot] = g_upper
+        m_ref[1, spot, spot] = g_lower
+
+
+def filter_part(z, gathered, cs, twist):
+    chips = gathered.shape[0]
+    cols = cs.shape[1]
+    rows = chips * 16
+    lanes = 2 * cols
+    return pl.pallas_call(
+        filter_kernel,
+        grid_spec=pltpu.PrefetchScalarGridSpec(
+            num_scalar_prefetch=1,
+            grid=(1,),
+            in_specs=[
+                pl.BlockSpec((chips, 64, lanes), lambda i, z: (0, 8 + z[0], 0)),
+                pl.BlockSpec(cs.shape, lambda i, z: (0, 0, 0)),
+                pl.BlockSpec(twist.shape, lambda i, z: (0, 0, 0)),
             ],
             out_specs=[
-                pl.BlockSpec((2 * rows, 128), lambda i, o: (0, i)),
-                pl.BlockSpec((2 * rows, 128), lambda i, o: (0, i)),
+                pl.BlockSpec((cols, 2 * rows), lambda i, z: (0, 0)),
+                pl.BlockSpec((2, lanes, lanes), lambda i, z: (0, 0, 0)),
             ],
         ),
-        out_shape=[jax.ShapeDtypeStruct((2 * rows, width), BF16)] * 2,
-        cost_estimate=pl.CostEstimate(flops=0, bytes_accessed=8 * rows * width * 2, transcendentals=0),
-        name="reorder_tokens",
-    )(order, mine, other, mine, other)
+        out_shape=[
+            jax.ShapeDtypeStruct((cols, 2 * rows), F32),
+            jax.ShapeDtypeStruct((2, lanes, lanes), BF16),
+        ],
+        compiler_params=pltpu.CompilerParams(vmem_limit_bytes=32 * 2**20),
+        cost_estimate=pl.CostEstimate(flops=10**9, bytes_accessed=2**20, transcendentals=0),
+        name="filter_part",
+    )(z.reshape(1), gathered, cs, twist)
 
 
 def conv_kernel(x_ref, fwd_ref, inv_ref, tw_ref, a_ref, ai_ref, m_ref, f_ref, y_ref, r_ref, q_ref):
@@ -176,8 +412,7 @@
     return jnp.cos(phase), jnp.sin(phase)
 
 
-def column_tables(core, filt, rows, cols, padded):
-    points = 2 * rows
+def column_tables(core, rows, cols, padded):
     i = lax.iota(jnp.int32, cols)
     b = 2 * (i % CHIPS) + ((i // CHIPS) ^ core)
     k1 = lax.iota(jnp.int32, rows)
@@ -185,36 +420,12 @@
     k2 = lax.iota(jnp.int32, cols)
     c, s = cos_sin(k2[:, None] * b[None, :], cols)
     a = jnp.block([[c, s], [-s, c]])
-    ai = a.T
-    f_re, f_im = filt[0], filt[1]
-    back_re = jnp.flip(f_re, (0, 1))[rows - 1 : points - 1]
-    back_im = jnp.flip(f_im, (0, 1))[rows - 1 : points - 1]
-    back_re = jnp.concatenate([back_re[:1], jnp.flip(f_re, (0, 1))[: rows - 1]], axis=0)
-    back_im = jnp.concatenate([back_im[:1], jnp.flip(f_im, (0, 1))[: rows - 1]], axis=0)
-    h_re = (0.5 * (f_re[:rows] + back_re)).T
-    h_im = (0.5 * (f_im[:rows] - back_im)).T
-    f = jnp.concatenate([h_re, h_im], axis=1)
-
-    def edge(k):
-        d = jnp.mod(b[:, None] - b[None, :], cols)
-        dd = b[:, None] - b[None, :]
-        ec, es = cos_sin(d[:, :, None] * k2[None, None, :], cols)
-        g_re = jnp.sum(ec * f_re[k] - es * f_im[k], axis=-1)
-        g_im = jnp.sum(es * f_re[k] + ec * f_im[k], axis=-1)
-        tc, ts = cos_sin(jnp.mod(dd * k, padded), padded)
-        return g_re * tc - g_im * ts
-
-    zero = jnp.zeros((cols, cols), F32)
-    m = jnp.block([[edge(0), zero], [zero, edge(rows)]])
+    twist = jnp.stack(cos_sin(jnp.mod((b[:, None] - b[None, :]) * rows, padded), padded))
 
     def stacked(t):
         return jnp.concatenate(split_table(t), axis=0)
 
-    return tw, stacked(a), stacked(ai), stacked(m), f
-
-
-def dot_t(weight, tokens):
-    return lax.dot_general(weight, tokens, (((0,), (1,)), ((), ())), preferred_element_type=F32)
+    return tw, stacked(a), stacked(a.T), jnp.stack([c, s]), twist
 
 
 def gather_two(block, first, second):
@@ -230,17 +441,6 @@
     return line, e1, e2a, e2b, e3
 
 
-def project(pieces, tokens):
-    line, e1, e2a, e2b, e3 = pieces
-    n = line.shape[0]
-    out = dot_t(line, tokens[:, :n])
-    out += dot_t(e1, tokens[:, n : 2 * n])
-    out += dot_t(e3, tokens[:, 3 * n :])
-    out += dot_t(e2a, tokens[:, 2 * n : 2 * n + n // 2])
-    out += dot_t(e2b, tokens[:, 2 * n + n // 2 : 3 * n])
-    return out.astype(BF16).astype(F32)
-
-
 def per_device(tokens, in_weight, filter_spectrum, skip_bias, out_weight):
     rows, _, width = tokens.shape
     cols = SEQ
@@ -252,64 +452,79 @@
     depth = in_weight.shape[0]
 
     mine = tokens.reshape(rows, width)
-    keep = lax.dynamic_slice_in_dim(in_weight, core * chan, chan, 2)
-    give = lax.dynamic_slice_in_dim(in_weight, (1 - core) * chan, chan, 2)
-    keep = jnp.concatenate([keep[:, 1], keep[:, 2], keep[:, 0]], axis=1)
-    give = jnp.concatenate([give[:, 1], give[:, 2], give[:, 0]], axis=1)
+    filt = jnp.transpose(filter_spectrum, (3, 1, 0, 2)).reshape(4, 1, -1, 2 * cols)
+    filt = jnp.concatenate(split_table(filt), axis=1).reshape(4, -1, 2 * cols)
+
+    def half_for(c):
+        w = lax.dynamic_slice_in_dim(in_weight, c * chan, chan, 2)
+        f = lax.dynamic_slice_in_dim(filt, 2 * c, 2, 0)
+        g = jnp.concatenate([w[:, 0, i * 128 : (i + 1) * 128] for i in range(chan // 128)], axis=0)
+        return jnp.concatenate([w[:, 1], w[:, 2]], axis=0), g.reshape(-1, depth, 128), f
+
+    keep, keep_g, keep_f = half_for(core)
+    give, give_g, give_f = half_for(1 - core)
+    near_g = send(jnp.concatenate([give_g.reshape(-1, 128), give_f.reshape(-1, 128)], axis=0), dc=1)
     near = send(give, dc=1)
-    far = send(keep[:, : 2 * chan], dz=1)
-    far_near = send(give[:, : 2 * chan], dz=1, dc=1)
-
-    def ordered(own, partner):
+    far = send(keep, dz=1)
+    far_near = send(give, dz=1, dc=1)
+    other = send(mine, dc=1)
+
+    def ordered(own, partner, axis=0):
         return jnp.concatenate(
-            [jnp.where(core == 0, own, partner), jnp.where(core == 0, partner, own)], axis=0
+            [jnp.where(core == 0, own, partner), jnp.where(core == 0, partner, own)], axis=axis
         )
 
-    own_z = ordered(keep, near)
-    oth_z = ordered(far, far_near)
-    block = jnp.concatenate([own_z[:, : 2 * chan], oth_z], axis=0)
-    gate_weight = lax.all_gather(
-        own_z[:, 2 * chan :], "seq", axis=0, tiled=True, axis_index_groups=SAME_CORE
+    key_block = jnp.concatenate(
+        [ordered(keep[:depth], near[:depth]), ordered(far[:depth], far_near[:depth])], axis=0
     )
-    key_pieces = gather_two(block[:, :chan], "dx", "dy")
-    value_pieces = gather_two(block[:, chan:], "dy", "dx")
-
-    other = send(mine, dc=1)
+    value_block = jnp.concatenate(
+        [ordered(keep[depth:], near[depth:]), ordered(far[depth:], far_near[depth:])], axis=0
+    )
+    cut = 4 * depth
+    gate_block = jnp.concatenate(
+        [
+            ordered(keep_g, near_g[:cut].reshape(keep_g.shape), 1).reshape(-1, 128),
+            ordered(keep_f, near_g[cut:].reshape(keep_f.shape), 1).reshape(-1, 128),
+        ],
+        axis=0,
+    )
+    gathered = lax.all_gather(gate_block, "seq", axis=0, axis_index_groups=SAME_CORE)
+    ow_part = lax.dynamic_slice_in_dim(
+        out_weight, core * (out_weight.shape[0] // 2), out_weight.shape[0] // 2, 0
+    )
+    key_block, value_block, ow_part = lax.optimization_barrier((key_block, value_block, ow_part))
+    key_pieces = gather_two(key_block, "dx", "dy")
+    value_pieces = gather_two(value_block, "dy", "dx")
+
     order = np.arange(32)
     p_, q_, dz = order // 8, (order // 2) % 4, order % 2
     key_order = ((z ^ dz) * 4 + (y + p_) % 4) * 4 + (x + q_) % 4
     value_order = ((z ^ dz) * 4 + (y + q_) % 4) * 4 + (x + p_) % 4
-    tokens_key, tokens_value = reorder(jnp.stack([key_order, value_order]), mine, other)
-
-    half_ow = out_weight.shape[0] // 2
+    first = first_part(jnp.stack([key_order, value_order]), mine, other, key_pieces, value_pieces)
+
     perm = []
     for t in range(SEQ):
         tz, ty, tx, tc = coords(t)
         for th in range(2):
             perm.append((t * 2 + th, index_of(tz ^ tc, ty, tx, tc) * 2 + 1 - th))
-    ow_part = lax.dynamic_slice_in_dim(out_weight, core * half_ow, half_ow, 0)
     ow_same = lax.ppermute(ow_part, ("seq", "ch"), perm)
     ow_cross = send(ow_same, dc=1)
 
-    filt = jnp.transpose(filter_spectrum, (3, 0, 2, 1)).reshape(4, -1)
-    filt = lax.all_gather(filt, "seq", axis=0)
-    filt = lax.dynamic_index_in_dim(filt, 2 * core + z, 1, keepdims=False)
-    filt = filt.reshape(SEQ, 2, cols, 2 * rows // SEQ)
-    filt = jnp.transpose(filt, (1, 0, 3, 2)).reshape(2, 2 * rows, cols)
-    tw, a, ai, m, f = column_tables(core, filt, rows, cols, padded)
+    source, packed = last_part(first, key_pieces, value_pieces)
+    packed = packed.reshape(CHIPS, chan // CHIPS, 2 * rows)
+    mine_ch = lax.all_to_all(packed, "seq", 0, 0, axis_index_groups=SAME_CORE)
+
+    tw, a, ai, cs, twist = column_tables(core, rows, cols, padded)
+    f, m = filter_part(z, gathered, cs, twist)
+    m = m.reshape(-1, 2 * cols)
     forward, inverse = row_tables(rows, padded)
     fwd = jnp.asarray(np.stack(split_np(forward)))
     inv = jnp.asarray(np.stack(split_np(inverse)))
-
-    source = project(key_pieces, tokens_key) * project(value_pieces, tokens_value)
-    packed = source.astype(BF16).reshape(CHIPS, chan // CHIPS, 2 * rows)
-    mine_ch = lax.all_to_all(packed, "seq", 0, 0, axis_index_groups=SAME_CORE)
     conv = long_conv(mine_ch, fwd, inv, tw, a, ai, m, f)
     conv = lax.all_to_all(conv, "seq", 0, 0, axis_index_groups=SAME_CORE)
     conv = conv.reshape(chan, 2 * rows).astype(F32)
 
-    gate = jnp.concatenate([dot_t(gate_weight, mine), dot_t(gate_weight, other)], axis=1)
-    gate = gate.astype(BF16).astype(F32)
+    gate = gate_part(mine, other, gathered).astype(F32)
     skip = lax.dynamic_slice_in_dim(skip_bias, core * chan, chan, 0)[:, None]
     gated = (gate * (conv + skip * source)).astype(BF16)
 
@@ -328,11 +543,8 @@
     from_c = send(oth_here, dc=1)
     here = ordered(own_here, from_c)
 
-    def out_dot(g, w):
-        return lax.dot_general(g, w, (((0,), (0,)), ((), ())), preferred_element_type=F32)
-
-    mixed = out_dot(here, out_weight) + out_dot(from_h, ow_same) + out_dot(from_hc, ow_cross)
-    return mixed.astype(BF16).reshape(kept, 1, out_weight.shape[1])
+    mixed = mix_part(here, from_h, from_hc, out_weight, ow_same, ow_cross)
+    return mixed.reshape(kept, 1, width)
 
 
 def solution(mesh):

time: 269 us -> 269 us (level)
  matrix products: 44.5 us -> 0 us
  waiting for transfers between devices: 73.9 us -> 108 us
  Pallas kernels: 41.3 us -> 58.4 us
  other arithmetic: 18.2 us -> 5.74 us
  local copies, waits for them, and re-layouts: 26.6 us -> 30.3 us
    ppermute x20 -> x21, waiting for transfers between devices: 30.2 us -> 81.5 us  [send(): return lax.ppermute(value, 'seq', perm)]
    dot_general x15 -> x0, matrix products: 44.5 us -> none  [the longest x12 30.1 us: dot_t(): lax.dot_general(weight, tokens, (((0,), (1,)), ((), ())), preferred_eleme...]
    pallas_call x1 -> x5, Pallas kernels: 23.3 us -> 41.3 us  [the longest x1 13.6 us: first_part(): pl.pallas_call(first_kernel, grid_spec=pltpu.PrefetchScalarGridSpec(num_s...]
    unnamed x79 -> x42, local copies, waits for them, and re-layouts: 4.28 us -> 20.4 us
    reduce_sum x1 -> x0, other arithmetic: 12.1 us -> none  [edge(): g_im = jnp.sum(es * f_re[k] + ec * f_im[k], axis=-1)]
    all_to_all x1, waiting for transfers between devices: 19.7 us -> 10.5 us  [per_device(): mine_ch = lax.all_to_all(packed, 'seq', 0, 0, axis_index_groups=SAME_CORE)]
    all_to_all x1, waiting for transfers between devices: 14 us -> 5.3 us  [per_device(): conv = lax.all_to_all(conv, 'seq', 0, 0, axis_index_groups=SAME_CORE)]
    all_to_all x1, starting transfers between devices: 4.88 us -> 12 us  [per_device(): mine_ch = lax.all_to_all(packed, 'seq', 0, 0, axis_index_groups=SAME_CORE)]
  transfers between devices with their start and end apart: 27 -> 27, of which waited for: 11 -> 11; matrix products, arithmetic and copies ran while one was open for 30% -> 7% of each run, Pallas kernels for 15% -> 18%
where the time goes in v2:
time: 269 us; the launch traced here: 267 us
  waiting for transfers between devices  108 us (40%)
  Pallas kernels  58.4 us (22%)
  starting transfers between devices  50.9 us (19%)
  local copies, waits for them, and re-layouts  30.3 us (11%)
  between operations  13.8 us (5%)
  other arithmetic  5.74 us (2%)
    ppermute x21, waiting for transfers between devices, send(): return lax.ppermute(value, 'seq', perm)  81.5 us
    ppermute x21, starting transfers between devices, send(): return lax.ppermute(value, 'seq', perm)  31.9 us
    unnamed x42, local copies, waits for them, and re-layouts  20.4 us
    pallas_call x1, Pallas kernels, long_conv(): pl.pallas_call(conv_kernel, in_specs=[vmem] * 8, out_specs=vmem, out_shap...  17.1 us
    pallas_call x1, Pallas kernels, first_part(): pl.pallas_call(first_kernel, grid_spec=pltpu.PrefetchScalarGridSpec(num_s...  13.6 us
    all_to_all x1, starting transfers between devices, per_device(): mine_ch = lax.all_to_all(packed, 'seq', 0, 0, axis_index_groups=SAME_CORE)  12 us
    pallas_call x1, Pallas kernels, mix_part(): pl.pallas_call(mix_kernel, grid=(8,), in_specs=[whole(here), whole(near_h...  11.5 us
    all_to_all x1, waiting for transfers between devices, per_device(): mine_ch = lax.all_to_all(packed, 'seq', 0, 0, axis_index_groups=SAME_CORE)  10.5 us
  transfers between devices with their start and end apart: 27, of which 11 were waited for; matrix products, arithmetic and copies ran while one was open for 7% of the time, Pallas kernels for 18%

profile of v2, /device:TPU:1, one launch (start us, length us, event | category | flops | bytes accessed | tf_op | source)
XLA Modules:
  0.0 267.4 jit_solution(5278509895693639100)
XLA Ops:
  6.5 0.8 constant_dynamic-update-slice_fusion.4
  7.3 0.9 copy.14
  8.4 0.7 constant_dynamic-update-slice_fusion.3
  9.1 0.7 constant_dynamic-update-slice_fusion.2
  9.8 0.7 constant_dynamic-update-slice_fusion.1
  10.6 1.5 collective-permute-start.1
  12.1 0.8 dynamic-slice_bitcast_fusion.11
  13.1 0.7 pad_maximum_fusion.4
  14.3 3.7 %collective-permute-start.4 = (bf16[128,512]{1,0:T(8,128)(2,1)S(1)}, bf16[128,512]{1,0:T(8,128)(2,1)S(1)}, u32[]{:S(2)}, u32[]{:S(2)}) collective-permute-start(bf16[128,512]{1,0:T(8,128)(2,1)S(1)} %pad_maximum_fusion.6), channel_id=1, source_target_pairs={{0,66},{2,64},{4,70},{6,68},{8,74},{10,72},{12,78},{14,76},{16,82}... | collective-permute-start | bytes 393224 | tf_op jit(solution)/shard_map/ppermute | solution.py:34
  18.3 4.6 %constant_dynamic-slice_fusion.3 = bf16[512,4096]{1,0:T(8,128)(2,1)} fusion(bf16[1024,4096]{1,0:T(8,128)(2,1)} %w_here.1, s32[]{:T(128)S(6)} %select_n.232), kind=kLoop, calls=%fused_computation.112 | loop fusion | bytes 8388612 | tf_op jit(solution)/shard_map/dynamic_slice | solution.py:492
  23.2 6.4 %collective-permute-done.3 = bf16[128,512]{1,0:T(8,128)(2,1)S(1)} collective-permute-done((bf16[128,512]{1,0:T(8,128)(2,1)S(1)}, bf16[128,512]{1,0:T(8,128)(2,1)S(1)}, u32[]{:S(2)}, u32[]{:S(2)}) %collective-permute-start.3) | collective-permute-done | bytes 131104 | tf_op jit(solution)/shard_map/ppermute | solution.py:34
  30.2 2.7 %collective-permute-start.10 = (bf16[256,512]{1,0:T(8,128)(2,1)S(1)}, bf16[256,512]{1,0:T(8,128)(2,1)S(1)}, u32[]{:S(2)}, u32[]{:S(2)}) collective-permute-start(bf16[256,512]{1,0:T(8,128)(2,1)S(1)} %get-tuple-element.17), channel_id=1, source_target_pairs={{0,48},{2,50},{4,52},{6,54},{8,56},{10,58},{12,60},{14,62},{16,0},... | collective-permute-start | bytes 786440 | tf_op jit(solution)/shard_map/ppermute | solution.py:34
  33.3 0.7 collective-permute-start.12
  34.0 0.7 constant_dynamic-update-slice_fusion.12
  34.7 3.5 %collective-permute-done.10 = bf16[256,512]{1,0:T(8,128)(2,1)S(1)} collective-permute-done((bf16[256,512]{1,0:T(8,128)(2,1)S(1)}, bf16[256,512]{1,0:T(8,128)(2,1)S(1)}, u32[]{:S(2)}, u32[]{:S(2)}) %collective-permute-start.10) | collective-permute-done | bytes 262176 | tf_op jit(solution)/shard_map/ppermute | solution.py:34
  38.3 0.7 constant_dynamic-update-slice_fusion.11
  39.0 2.2 collective-permute-done.11
  41.2 0.7 constant_dynamic-update-slice_fusion.10
  41.9 6.8 %collective-permute-done.12 = bf16[256,512]{1,0:T(8,128)(2,1)S(1)} collective-permute-done((bf16[256,512]{1,0:T(8,128)(2,1)S(1)}, bf16[256,512]{1,0:T(8,128)(2,1)S(1)}, u32[]{:S(2)}, u32[]{:S(2)}) %collective-permute-start.12) | collective-permute-done | bytes 262176 | tf_op jit(solution)/shard_map/ppermute | solution.py:34
  48.8 0.7 constant_dynamic-update-slice_fusion.9.refs_3_
  49.5 2.4 collective-permute-start.13
  52.7 33.6 %collective-permute-done.5 = bf16[256,512]{1,0:T(8,128)(2,1)S(1)} collective-permute-done((bf16[256,512]{1,0:T(8,128)(2,1)S(1)}, bf16[256,512]{1,0:T(8,128)(2,1)S(1)}, u32[]{:S(2)}, u32[]{:S(2)}) %collective-permute-start.5) | collective-permute-done | bytes 262176 | tf_op jit(solution)/shard_map/ppermute | solution.py:34
  86.4 1.0 collective-permute-start.7
  87.4 0.7 constant_dynamic-update-slice_fusion.8
  88.1 0.7 constant_dynamic-update-slice_fusion.7
  88.8 7.6 %collective-permute-start.14 = (bf16[1024,512]{1,0:T(8,128)(2,1)}, bf16[1024,512]{1,0:T(8,128)(2,1)}, u32[]{:S(2)}, u32[]{:S(2)}) collective-permute-start(bf16[1024,512]{1,0:T(8,128)(2,1)} %constant_dynamic-update-slice_fusion.9.refs_3_), channel_id=1, source_target_pairs={{0,4},{2,6},{4,8},{6,10},{8,12},{10,14},{12,0},{14,2},{16,20},{18,... | collective-permute-start | bytes 3145736 | tf_op jit(solution)/shard_map/ppermute | solution.py:34
  96.5 0.7 constant_dynamic-update-slice_fusion.6
  97.2 0.7 constant_dynamic-update-slice_fusion.5.refs_0_
  97.9 1.5 collective-permute-start.9
  99.9 28.7 %collective-permute-done.14.refs_5_ = bf16[1024,512]{1,0:T(8,128)(2,1)} collective-permute-done((bf16[1024,512]{1,0:T(8,128)(2,1)}, bf16[1024,512]{1,0:T(8,128)(2,1)}, u32[]{:S(2)}, u32[]{:S(2)}) %collective-permute-start.14) | collective-permute-done | bytes 1048608 | tf_op jit(solution)/shard_map/ppermute | solution.py:34
  128.6 0.9 collective-permute-start.17
  129.4 1.1 slice.107
  130.5 0.7 collective-permute-start.18
  131.4 1.5 collective-permute-start.16
  132.9 13.6 %first_part.1 = (f32[1024,512]{1,0:T(8,128)}, f32[1024,512]{1,0:T(8,128)}, bf16[1024,1024]{1,0:T(8,128)(2,1)}, bf16[1024,1024]{1,0:T(8,128)(2,1)}) custom-call(s32[2,32]{1,0:T(2,128)S(1)} %pad_add_fusion.order_ref, bf16[512,4096]{1,0:T(8,128)(2,1)} %bitcast.65, bf16[512,4096]{1,0:T(8,128)(2,1)} %collective-permute-done.other_ref, ...), custom_call_target="tpu_custom_call" | custom-call | flops 6442450944 | bytes 23068672 | tf_op jit(solution)/shard_map/first_part/pallas_call | solution.py:101
  146.5 2.7 %collective-permute-start.23 = (bf16[512,4096]{1,0:T(8,128)(2,1)}, bf16[512,4096]{1,0:T(8,128)(2,1)}, u32[]{:S(2)}, u32[]{:S(2)}) collective-permute-start(bf16[512,4096]{1,0:T(8,128)(2,1)} %collective-permute-done.22.w_near), channel_id=1, source_target_pairs={{0,2},{2,0},{4,6},{6,4},{8,10},{10,8},{12,14},{14,12},{16,18},{18,... | collective-permute-start | bytes 12582920 | tf_op jit(solution)/shard_map/ppermute | solution.py:34
  149.2 6.8 %last_part.1 = (f32[512,1024]{1,0:T(8,128)S(1)}, bf16[512,1024]{1,0:T(8,128)(2,1)}) custom-call(f32[1024,512]{1,0:T(8,128)} %get-tuple-element.18.key_ref, f32[1024,512]{1,0:T(8,128)} %get-tuple-element.19.value_ref, bf16[1024,1024]{1,0:T(8,128)(2,1)} %get-tuple-element.20.key_tok_ref, bf16[1024,1024]{1,0:T(8,128)(2,1)} %get-tuple-element.21.value_tok_ref, ...), custom_call_target="tpu_custom_call" | custom-call | flops 2147483648 | bytes 13631488 | tf_op jit(solution)/shard_map/last_part/pallas_call | solution.py:148
  156.0 12.0 %all-to-all-start = ((bf16[32,16,1024]{2,1,0:T(8,128)(2,1)}), bf16[32,16,1024]{2,1,0:T(8,128)(2,1)S(1)}, u32[]{:S(2)}, u32[]{:S(2)}) async-start(bf16[32,16,1024]{2,1,0:T(8,128)(2,1)} %bitcast.24), calls=%async_computation | async-start | bytes 2097152 | tf_op jit(solution)/shard_map/all_to_all | solution.py:515
  168.1 0.7 copy.16.a_ref
  168.9 0.6 pad_maximum_fusion.10.ai_ref
  170.5 2.5 copy-done
  173.0 0.8 filter_part.1
  173.8 0.7 copy-done.5
  174.5 0.6 copy-done.7
  175.1 10.5 %all-to-all-done.x_ref = bf16[32,16,1024]{2,1,0:T(8,128)(2,1)S(1)} async-done(((bf16[32,16,1024]{2,1,0:T(8,128)(2,1)}), bf16[32,16,1024]{2,1,0:T(8,128)(2,1)S(1)}, u32[]{:S(2)}, u32[]{:S(2)}) %all-to-all-start) | async-done | bytes 1048608 | tf_op jit(solution)/shard_map/all_to_all | solution.py:515
  185.7 0.8 copy-done.2
  186.5 0.8 copy-done.3
  187.4 0.9 copy-done.6
  188.3 0.8 copy-done.8
  189.2 1.6 copy-done.9
  190.7 17.1 %long_conv.1 = bf16[32,16,1024]{2,1,0:T(8,128)(2,1)S(1)} custom-call(bf16[32,16,1024]{2,1,0:T(8,128)(2,1)S(1)} %all-to-all-done.x_ref, bf16[2,512,1024]{2,1,0:T(8,128)(2,1)S(1)} %copy-done.9, bf16[2,1024,512]{2,1,0:T(8,128)(2,1)} %constant.192.clone.inv_ref, f32[64,1024]{1,0:T(8,128)S(1)} %pad_maximum_fusion.3.tw_ref, bf16[256,128]{1,0:T(8,128)(2,1)S(1)} %copy-done.2, ...), custom_call_target="tpu_custom_call" | custom-call | flops 8000000000 | bytes 8388608 | tf_op jit(solution)/shard_map/long_conv/pallas_call | solution.py:395
  207.8 1.0 copy-done.1
  208.8 4.8 %all-to-all-start.1 = ((bf16[32,16,1024]{2,1,0:T(8,128)(2,1)}), bf16[32,16,1024]{2,1,0:T(8,128)(2,1)}, u32[]{:S(2)}, u32[]{:S(2)}) async-start(bf16[32,16,1024]{2,1,0:T(8,128)(2,1)} %copy-done.1), calls=%async_computation.1 | async-start | bytes 2097152 | tf_op jit(solution)/shard_map/all_to_all | solution.py:524
  213.7 2.2 copy-done.4
  215.9 8.6 %gate_part.1 = bf16[512,1024]{1,0:T(8,128)(2,1)S(1)} custom-call(bf16[512,4096]{1,0:T(8,128)(2,1)S(1)} %bitcast.66, bf16[512,4096]{1,0:T(8,128)(2,1)} %collective-permute-done.other_ref, bf16[32,640,128]{2,1,0:T(8,128)(2,1)} %bitcast.62), custom_call_target="tpu_custom_call" | custom-call | flops 4294967296 | bytes 13631488 | tf_op jit(solution)/shard_map/gate_part/pallas_call | solution.py:197
  224.5 5.3 %all-to-all-done.1 = bf16[32,16,1024]{2,1,0:T(8,128)(2,1)} async-done(((bf16[32,16,1024]{2,1,0:T(8,128)(2,1)}), bf16[32,16,1024]{2,1,0:T(8,128)(2,1)}, u32[]{:S(2)}, u32[]{:S(2)}) %all-to-all-start.1) | async-done | bytes 1048608 | tf_op jit(solution)/shard_map/all_to_all | solution.py:524
  229.8 1.7 fusion.1
  231.5 1.0 copy-done.10
  232.6 2.8 %collective-permute-start.19 = (bf16[512,256]{1,0:T(8,128)(2,1)S(1)}, bf16[512,256]{1,0:T(8,128)(2,1)S(1)}, u32[]{:S(2)}, u32[]{:S(2)}) collective-permute-start(bf16[512,256]{1,0:T(8,128)(2,1)S(1)} %get-tuple-element.37), channel_id=1, source_target_pairs={{0,2},{2,0},{4,6},{6,4},{8,10},{10,8},{12,14},{14,12},{16,18},{18,... | collective-permute-start | bytes 786440 | tf_op jit(solution)/shard_map/ppermute | solution.py:34
  235.8 1.3 collective-permute-start.21
  237.1 1.0 broadcast_select_fusion.1
  238.2 5.0 %collective-permute-done.20.near_h = bf16[512,256]{1,0:T(8,128)(2,1)S(1)} collective-permute-done((bf16[512,256]{1,0:T(8,128)(2,1)S(1)}, bf16[512,256]{1,0:T(8,128)(2,1)S(1)}, u32[]{:S(2)}, u32[]{:S(2)}) %collective-permute-start.20) | collective-permute-done | bytes 262176 | tf_op jit(solution)/shard_map/ppermute | solution.py:537
  243.2 5.8 %collective-permute-done.21.far_h = bf16[512,256]{1,0:T(8,128)(2,1)S(1)} collective-permute-done((bf16[512,256]{1,0:T(8,128)(2,1)S(1)}, bf16[512,256]{1,0:T(8,128)(2,1)S(1)}, u32[]{:S(2)}, u32[]{:S(2)}) %collective-permute-start.21) | collective-permute-done | bytes 262176 | tf_op jit(solution)/shard_map/ppermute | solution.py:542
  249.0 11.5 %mix_part.1 = bf16[256,4096]{1,0:T(8,128)(2,1)} custom-call(bf16[1024,256]{1,0:T(8,128)(2,1)S(1)} %pad_maximum_fusion.here, bf16[512,256]{1,0:T(8,128)(2,1)S(1)} %collective-permute-done.20.near_h, bf16[512,256]{1,0:T(8,128)(2,1)S(1)} %collective-permute-done.21.far_h, bf16[1024,4096]{1,0:T(8,128)(2,1)} %w_here.1, ...), custom_call_target="tpu_custom_call" | custom-call | flops 4294967296 | bytes 19922944 | tf_op jit(solution)/shard_map/mix_part/pallas_call | solution.py:242
  (86 shorter events, 5.5 us)
Async XLA Ops:
  6.5 7.2 %copy-start.11 = (bf16[64,3,1024]{2,0,1:T(8,128)(2,1)S(1)}, bf16[64,3,1024]{2,0,1:T(8,128)(2,1)}, u32[]{:S(2)}) copy-start(bf16[64,3,1024]{2,0,1:T(8,128)(2,1)} %param.11) | copy-start | bytes 1179652
  6.5 164.0 %all-gather.3.cloned.1.call-start = ((), (), s32[]{:S(2)}) async-start(), calls=%async_computation.2 | async-start | bytes 5406720 | tf_op jit(solution)/shard_map/all_gather | solution.py:491
  10.6 2.4 collective-permute-start.1
  13.8 9.2 %collective-permute-start.2 = (bf16[128,512]{1,0:T(8,128)(2,1)S(1)}, bf16[128,512]{1,0:T(8,128)(2,1)S(1)}, u32[]{:S(2)}, u32[]{:S(2)}) collective-permute-start(bf16[128,512]{1,0:T(8,128)(2,1)S(1)} %pad_maximum_fusion.6), channel_id=1, source_target_pairs={{0,2},{2,0},{4,6},{6,4},{8,10},{10,8},{12,14},{14,12},{16,18},{18,... | collective-permute-start | bytes 393224 | tf_op jit(solution)/shard_map/ppermute | solution.py:34
  14.3 8.9 %collective-permute-start.4 = (bf16[128,512]{1,0:T(8,128)(2,1)S(1)}, bf16[128,512]{1,0:T(8,128)(2,1)S(1)}, u32[]{:S(2)}, u32[]{:S(2)}) collective-permute-start(bf16[128,512]{1,0:T(8,128)(2,1)S(1)} %pad_maximum_fusion.6), channel_id=1, source_target_pairs={{0,66},{2,64},{4,70},{6,68},{8,74},{10,72},{12,78},{14,76},{16,82}... | collective-permute-start | bytes 393224 | tf_op jit(solution)/shard_map/ppermute | solution.py:34
  18.0 113.4 %collective-permute-start = (bf16[512,4096]{1,0:T(8,128)(2,1)}, bf16[512,4096]{1,0:T(8,128)(2,1)}, u32[]{:S(2)}, u32[]{:S(2)}) collective-permute-start(bf16[512,4096]{1,0:T(8,128)(2,1)} %bitcast.64), channel_id=1, source_target_pairs={{0,2},{2,0},{4,6},{6,4},{8,10},{10,8},{12,14},{14,12},{16,18},{18,... | collective-permute-start | bytes 12582920 | tf_op jit(solution)/shard_map/ppermute | solution.py:34
  23.0 6.5 %collective-permute-start.3 = (bf16[128,512]{1,0:T(8,128)(2,1)S(1)}, bf16[128,512]{1,0:T(8,128)(2,1)S(1)}, u32[]{:S(2)}, u32[]{:S(2)}) collective-permute-start(bf16[128,512]{1,0:T(8,128)(2,1)S(1)} %pad_maximum_fusion.7), channel_id=1, source_target_pairs={{0,64},{2,66},{4,68},{6,70},{8,72},{10,74},{12,76},{14,78},{16,80}... | collective-permute-start | bytes 393224 | tf_op jit(solution)/shard_map/ppermute | solution.py:34
  29.7 69.7 %copy-start.13 = (s32[32]{0:T(128)S(1)}, s32[32]{0:T(128)}, u32[]{:S(2)}) copy-start(s32[32]{0:T(128)} %constant.188.clone) | copy-start | bytes 388
  29.7 69.7 %copy-start.14 = (s32[32]{0:T(128)S(1)}, s32[32]{0:T(128)}, u32[]{:S(2)}) copy-start(s32[32]{0:T(128)} %constant.189.clone) | copy-start | bytes 388
  29.7 69.7 %copy-start.15 = (s32[32]{0:T(128)S(1)}, s32[32]{0:T(128)}, u32[]{:S(2)}) copy-start(s32[32]{0:T(128)} %constant.190.clone) | copy-start | bytes 388
  29.7 116.8 %collective-permute-start.22 = (bf16[512,4096]{1,0:T(8,128)(2,1)}, bf16[512,4096]{1,0:T(8,128)(2,1)}, u32[]{:S(2)}, u32[]{:S(2)}) collective-permute-start(bf16[512,4096]{1,0:T(8,128)(2,1)} %constant_dynamic-slice_fusion.3), channel_id=1, source_target_pairs={{0,1},{1,0},{2,67},{3,66},{4,5},{5,4},{6,71},{7,70},{8,9},{9,8},{1... | collective-permute-start | bytes 12582920 | tf_op jit(solution)/shard_map/ppermute | solution.py:510
  30.2 8.1 %collective-permute-start.10 = (bf16[256,512]{1,0:T(8,128)(2,1)S(1)}, bf16[256,512]{1,0:T(8,128)(2,1)S(1)}, u32[]{:S(2)}, u32[]{:S(2)}) collective-permute-start(bf16[256,512]{1,0:T(8,128)(2,1)S(1)} %get-tuple-element.17), channel_id=1, source_target_pairs={{0,48},{2,50},{4,52},{6,54},{8,56},{10,58},{12,60},{14,62},{16,0},... | collective-permute-start | bytes 786440 | tf_op jit(solution)/shard_map/ppermute | solution.py:34
  32.9 8.3 %collective-permute-start.11 = (bf16[256,512]{1,0:T(8,128)(2,1)S(1)}, bf16[256,512]{1,0:T(8,128)(2,1)S(1)}, u32[]{:S(2)}, u32[]{:S(2)}) collective-permute-start(bf16[256,512]{1,0:T(8,128)(2,1)S(1)} %get-tuple-element.17), channel_id=1, source_target_pairs={{0,32},{2,34},{4,36},{6,38},{8,40},{10,42},{12,44},{14,46},{16,48}... | collective-permute-start | bytes 786440 | tf_op jit(solution)/shard_map/ppermute | solution.py:34
  33.3 15.5 %collective-permute-start.12 = (bf16[256,512]{1,0:T(8,128)(2,1)S(1)}, bf16[256,512]{1,0:T(8,128)(2,1)S(1)}, u32[]{:S(2)}, u32[]{:S(2)}) collective-permute-start(bf16[256,512]{1,0:T(8,128)(2,1)S(1)} %get-tuple-element.17), channel_id=1, source_target_pairs={{0,16},{2,18},{4,20},{6,22},{8,24},{10,26},{12,28},{14,30},{16,32}... | collective-permute-start | bytes 786440 | tf_op jit(solution)/shard_map/ppermute | solution.py:34
  49.5 48.4 %collective-permute-start.13 = (bf16[1024,512]{1,0:T(8,128)(2,1)}, bf16[1024,512]{1,0:T(8,128)(2,1)S(1)}, u32[]{:S(2)}, u32[]{:S(2)}) collective-permute-start(bf16[1024,512]{1,0:T(8,128)(2,1)} %constant_dynamic-update-slice_fusion.9.refs_3_), channel_id=1, source_target_pairs={{0,12},{2,14},{4,0},{6,2},{8,4},{10,6},{12,8},{14,10},{16,28},{18,... | collective-permute-start | bytes 3145736 | tf_op jit(solution)/shard_map/ppermute | solution.py:34
  51.9 34.4 %collective-permute-start.5 = (bf16[256,512]{1,0:T(8,128)(2,1)S(1)}, bf16[256,512]{1,0:T(8,128)(2,1)S(1)}, u32[]{:S(2)}, u32[]{:S(2)}) collective-permute-start(bf16[256,512]{1,0:T(8,128)(2,1)S(1)} %get-tuple-element.16), channel_id=1, source_target_pairs={{0,12},{2,14},{4,0},{6,2},{8,4},{10,6},{12,8},{14,10},{16,28},{18,... | collective-permute-start | bytes 786440 | tf_op jit(solution)/shard_map/ppermute | solution.py:34
  52.3 36.5 %collective-permute-start.6 = (bf16[256,512]{1,0:T(8,128)(2,1)S(1)}, bf16[256,512]{1,0:T(8,128)(2,1)S(1)}, u32[]{:S(2)}, u32[]{:S(2)}) collective-permute-start(bf16[256,512]{1,0:T(8,128)(2,1)S(1)} %get-tuple-element.16), channel_id=1, source_target_pairs={{0,8},{2,10},{4,12},{6,14},{8,0},{10,2},{12,4},{14,6},{16,24},{18,... | collective-permute-start | bytes 786440 | tf_op jit(solution)/shard_map/ppermute | solution.py:34
  86.4 10.8 %collective-permute-start.7 = (bf16[256,512]{1,0:T(8,128)(2,1)S(1)}, bf16[256,512]{1,0:T(8,128)(2,1)S(1)}, u32[]{:S(2)}, u32[]{:S(2)}) collective-permute-start(bf16[256,512]{1,0:T(8,128)(2,1)S(1)} %get-tuple-element.16), channel_id=1, source_target_pairs={{0,4},{2,6},{4,8},{6,10},{8,12},{10,14},{12,0},{14,2},{16,20},{18,... | collective-permute-start | bytes 786440 | tf_op jit(solution)/shard_map/ppermute | solution.py:34
  88.8 39.8 %collective-permute-start.14 = (bf16[1024,512]{1,0:T(8,128)(2,1)}, bf16[1024,512]{1,0:T(8,128)(2,1)}, u32[]{:S(2)}, u32[]{:S(2)}) collective-permute-start(bf16[1024,512]{1,0:T(8,128)(2,1)} %constant_dynamic-update-slice_fusion.9.refs_3_), channel_id=1, source_target_pairs={{0,4},{2,6},{4,8},{6,10},{8,12},{10,14},{12,0},{14,2},{16,20},{18,... | collective-permute-start | bytes 3145736 | tf_op jit(solution)/shard_map/ppermute | solution.py:34
  97.9 32.6 %collective-permute-start.8 = (bf16[1024,512]{1,0:T(8,128)(2,1)}, bf16[1024,512]{1,0:T(8,128)(2,1)S(1)}, u32[]{:S(2)}, u32[]{:S(2)}) collective-permute-start(bf16[1024,512]{1,0:T(8,128)(2,1)} %constant_dynamic-update-slice_fusion.5.refs_0_), channel_id=1, source_target_pairs={{0,48},{2,50},{4,52},{6,54},{8,56},{10,58},{12,60},{14,62},{16,0},... | collective-permute-start | bytes 3145736 | tf_op jit(solution)/shard_map/ppermute | solution.py:34
  97.9 33.3 %collective-permute-start.9 = (bf16[1024,512]{1,0:T(8,128)(2,1)}, bf16[1024,512]{1,0:T(8,128)(2,1)S(1)}, u32[]{:S(2)}, u32[]{:S(2)}) collective-permute-start(bf16[1024,512]{1,0:T(8,128)(2,1)} %constant_dynamic-update-slice_fusion.5.refs_0_), channel_id=1, source_target_pairs={{0,16},{2,18},{4,20},{6,22},{8,24},{10,26},{12,28},{14,30},{16,32}... | collective-permute-start | bytes 3145736 | tf_op jit(solution)/shard_map/ppermute | solution.py:34
  128.6 20.6 %collective-permute-start.17 = (bf16[512,512]{1,0:T(8,128)(2,1)S(1)}, bf16[512,512]{1,0:T(8,128)(2,1)S(1)}, u32[]{:S(2)}, u32[]{:S(2)}) collective-permute-start(bf16[512,512]{1,0:T(8,128)(2,1)S(1)} %slice.106), channel_id=1, source_target_pairs={{0,12},{2,14},{4,0},{6,2},{8,4},{10,6},{12,8},{14,10},{16,28},{18,... | collective-permute-start | bytes 1572872 | tf_op jit(solution)/shard_map/ppermute | solution.py:34
  130.5 18.7 %collective-permute-start.18 = (bf16[512,512]{1,0:T(8,128)(2,1)S(1)}, bf16[512,512]{1,0:T(8,128)(2,1)S(1)}, u32[]{:S(2)}, u32[]{:S(2)}) collective-permute-start(bf16[512,512]{1,0:T(8,128)(2,1)S(1)} %slice.107), channel_id=1, source_target_pairs={{0,4},{2,6},{4,8},{6,10},{8,12},{10,14},{12,0},{14,2},{16,20},{18,... | collective-permute-start | bytes 1572872 | tf_op jit(solution)/shard_map/ppermute | solution.py:34
  131.3 17.9 %collective-permute-start.15 = (bf16[512,512]{1,0:T(8,128)(2,1)S(1)}, bf16[512,512]{1,0:T(8,128)(2,1)S(1)}, u32[]{:S(2)}, u32[]{:S(2)}) collective-permute-start(bf16[512,512]{1,0:T(8,128)(2,1)S(1)} %slice.104), channel_id=1, source_target_pairs={{0,48},{2,50},{4,52},{6,54},{8,56},{10,58},{12,60},{14,62},{16,0},... | collective-permute-start | bytes 1572872 | tf_op jit(solution)/shard_map/ppermute | solution.py:34
  131.4 17.8 %collective-permute-start.16 = (bf16[512,512]{1,0:T(8,128)(2,1)S(1)}, bf16[512,512]{1,0:T(8,128)(2,1)S(1)}, u32[]{:S(2)}, u32[]{:S(2)}) collective-permute-start(bf16[512,512]{1,0:T(8,128)(2,1)S(1)} %slice.105), channel_id=1, source_target_pairs={{0,16},{2,18},{4,20},{6,22},{8,24},{10,26},{12,28},{14,30},{16,32}... | collective-permute-start | bytes 1572872 | tf_op jit(solution)/shard_map/ppermute | solution.py:34
  146.5 91.7 %collective-permute-start.23 = (bf16[512,4096]{1,0:T(8,128)(2,1)}, bf16[512,4096]{1,0:T(8,128)(2,1)}, u32[]{:S(2)}, u32[]{:S(2)}) collective-permute-start(bf16[512,4096]{1,0:T(8,128)(2,1)} %collective-permute-done.22.w_near), channel_id=1, source_target_pairs={{0,2},{2,0},{4,6},{6,4},{8,10},{10,8},{12,14},{14,12},{16,18},{18,... | collective-permute-start | bytes 12582920 | tf_op jit(solution)/shard_map/ppermute | solution.py:34
  156.0 29.6 %all-to-all-start = ((bf16[32,16,1024]{2,1,0:T(8,128)(2,1)}), bf16[32,16,1024]{2,1,0:T(8,128)(2,1)S(1)}, u32[]{:S(2)}, u32[]{:S(2)}) async-start(bf16[32,16,1024]{2,1,0:T(8,128)(2,1)} %bitcast.24), calls=%async_computation | async-start | bytes 2097152 | tf_op jit(solution)/shard_map/all_to_all | solution.py:515
  170.5 2.5 copy-start
  173.8 0.7 copy-start.5
  174.5 0.6 copy-start.7
  185.7 0.8 copy-start.2
  186.5 0.8 copy-start.3
  187.4 0.9 copy-start.6
  188.3 0.8 copy-start.8
  189.2 1.6 copy-start.9
  207.8 1.0 copy-start.1
  208.8 4.8 %copy-start.12 = (f32[1024]{0:T(1024)S(1)}, f32[1024]{0:T(1024)}, u32[]{:S(2)}) copy-start(f32[1024]{0:T(1024)} %param.13) | copy-start | bytes 12292
  208.8 21.0 %all-to-all-start.1 = ((bf16[32,16,1024]{2,1,0:T(8,128)(2,1)}), bf16[32,16,1024]{2,1,0:T(8,128)(2,1)}, u32[]{:S(2)}, u32[]{:S(2)}) async-start(bf16[32,16,1024]{2,1,0:T(8,128)(2,1)} %copy-done.1), calls=%async_computation.1 | async-start | bytes 2097152 | tf_op jit(solution)/shard_map/all_to_all | solution.py:524
  213.7 2.2 copy-start.4
  231.5 1.0 copy-start.10
  232.6 4.5 %collective-permute-start.19 = (bf16[512,256]{1,0:T(8,128)(2,1)S(1)}, bf16[512,256]{1,0:T(8,128)(2,1)S(1)}, u32[]{:S(2)}, u32[]{:S(2)}) collective-permute-start(bf16[512,256]{1,0:T(8,128)(2,1)S(1)} %get-tuple-element.37), channel_id=1, source_target_pairs={{0,2},{2,0},{4,6},{6,4},{8,10},{10,8},{12,14},{14,12},{16,18},{18,... | collective-permute-start | bytes 786440 | tf_op jit(solution)/shard_map/ppermute | solution.py:34
  235.3 7.9 %collective-permute-start.20 = (bf16[512,256]{1,0:T(8,128)(2,1)S(1)}, bf16[512,256]{1,0:T(8,128)(2,1)S(1)}, u32[]{:S(2)}, u32[]{:S(2)}) collective-permute-start(bf16[512,256]{1,0:T(8,128)(2,1)S(1)} %get-tuple-element.36), channel_id=1, source_target_pairs={{0,1},{1,0},{2,3},{3,2},{4,5},{5,4},{6,7},{7,6},{8,9},{9,8},{10,11... | collective-permute-start | bytes 786440 | tf_op jit(solution)/shard_map/ppermute | solution.py:537
  235.8 13.2 %collective-permute-start.21 = (bf16[512,256]{1,0:T(8,128)(2,1)S(1)}, bf16[512,256]{1,0:T(8,128)(2,1)S(1)}, u32[]{:S(2)}, u32[]{:S(2)}) collective-permute-start(bf16[512,256]{1,0:T(8,128)(2,1)S(1)} %get-tuple-element.35), channel_id=1, source_target_pairs={{0,3},{1,2},{2,1},{3,0},{4,7},{5,6},{6,5},{7,4},{8,11},{9,10},{10,... | collective-permute-start | bytes 786440 | tf_op jit(solution)/shard_map/ppermute | solution.py:542
Sparse Core Ops, SparseCore 0:
  13.9 105.2 all-gather.2

commit v3 on v2

--- a/solution.py
+++ b/solution.py
@@ -212,25 +212,38 @@
     )(mine, other, gathered)
 
 
-def mix_kernel(here, near_h, far_h, w_here, w_near, w_far, out_ref, lhs_ref):
+def turn(ref):
+    return ref[...].astype(F32).T.astype(BF16)
+
+
+def mix_kernel(here, w_here, out_ref, lhs_ref):
     @pl.when(pl.program_id(0) == 0)
     def _():
-        n, m = here.shape[0], near_h.shape[0]
-        lhs_ref[:, :n] = here[...].astype(F32).T.astype(BF16)
-        lhs_ref[:, n : n + m] = near_h[...].astype(F32).T.astype(BF16)
-        lhs_ref[:, n + m :] = far_h[...].astype(F32).T.astype(BF16)
-
-    n, m = here.shape[0], near_h.shape[0]
-    total = jnp.dot(lhs_ref[:, :n], w_here[...], preferred_element_type=F32)
-    total += jnp.dot(lhs_ref[:, n : n + m], w_near[...], preferred_element_type=F32)
-    total += jnp.dot(lhs_ref[:, n + m :], w_far[...], preferred_element_type=F32)
+        lhs_ref[...] = turn(here)
+
+    out_ref[...] = jnp.dot(lhs_ref[...], w_here[...], preferred_element_type=F32)
+
+
+def mix_more_kernel(total_ref, near_h, far_h, w_near, w_far, out_ref, lhs_ref):
+    m = near_h.shape[0]
+
+    @pl.when(pl.program_id(0) == 0)
+    def _():
+        lhs_ref[:, :m] = turn(near_h)
+        lhs_ref[:, m:] = turn(far_h)
+
+    total = total_ref[...]
+    total += jnp.dot(lhs_ref[:, :m], w_near[...], preferred_element_type=F32)
+    total += jnp.dot(lhs_ref[:, m:], w_far[...], preferred_element_type=F32)
     out_ref[...] = total.astype(BF16)
 
 
-def mix_part(here, near_h, far_h, w_here, w_near, w_far):
-    rows = here.shape[1]
-    width = w_here.shape[1]
-    tile = width // 8
+def mix_part(total, parts, weights):
+    rows = parts[0].shape[1]
+    width = weights[0].shape[1]
+    tile = width // 4
+    depth = sum(p.shape[0] for p in parts)
+    totals = [] if total is None else [total]
 
     def whole(g):
         return pl.BlockSpec(g.shape, lambda i: (0, 0))
@@ -238,20 +251,19 @@
     def tiled(w):
         return pl.BlockSpec((w.shape[0], tile), lambda i: (0, i))
 
-    depth = here.shape[0] + near_h.shape[0] + far_h.shape[0]
     return pl.pallas_call(
-        mix_kernel,
-        grid=(8,),
-        in_specs=[whole(here), whole(near_h), whole(far_h), tiled(w_here), tiled(w_near), tiled(w_far)],
+        mix_kernel if total is None else mix_more_kernel,
+        grid=(4,),
+        in_specs=[tiled(t) for t in totals] + [whole(p) for p in parts] + [tiled(w) for w in weights],
         out_specs=pl.BlockSpec((rows, tile), lambda i: (0, i)),
-        out_shape=jax.ShapeDtypeStruct((rows, width), BF16),
+        out_shape=jax.ShapeDtypeStruct((rows, width), F32 if total is None else BF16),
         scratch_shapes=[pltpu.VMEM((rows, depth), BF16)],
         compiler_params=pltpu.CompilerParams(vmem_limit_bytes=48 * 2**20),
         cost_estimate=pl.CostEstimate(
-            flops=2 * rows * depth * width, bytes_accessed=19 * 2**20, transcendentals=0
+            flops=2 * rows * depth * width, bytes_accessed=12 * 2**20, transcendentals=0
         ),
-        name="mix_part",
-    )(here, near_h, far_h, w_here, w_near, w_far)
+        name="mix_part" if total is None else "mix_more",
+    )(*totals, *parts, *weights)
 
 
 def filter_kernel(z_ref, x_ref, cs_ref, twist_ref, f_ref, m_ref):
@@ -291,11 +303,9 @@
         g = contract(u, c) + contract(v, s)
         if n:
             g = g * twist_ref[0] - (contract(v, c) - contract(u, s)) * twist_ref[1]
-        g_upper = g.astype(BF16)
-        g_lower = (g - g_upper.astype(F32)).astype(BF16)
-        spot = slice(n * cols, (n + 1) * cols)
-        m_ref[0, spot, spot] = g_upper
-        m_ref[1, spot, spot] = g_lower
+        for start in (n * cols, lanes + n * cols):
+            spot = slice(start, start + cols)
+            m_ref[spot, spot] = g.astype(BF16)
 
 
 def filter_part(z, gathered, cs, twist):
@@ -315,12 +325,12 @@
             ],
             out_specs=[
                 pl.BlockSpec((cols, 2 * rows), lambda i, z: (0, 0)),
-                pl.BlockSpec((2, lanes, lanes), lambda i, z: (0, 0, 0)),
+                pl.BlockSpec((2 * lanes, 2 * lanes), lambda i, z: (0, 0)),
             ],
         ),
         out_shape=[
             jax.ShapeDtypeStruct((cols, 2 * rows), F32),
-            jax.ShapeDtypeStruct((2, lanes, lanes), BF16),
+            jax.ShapeDtypeStruct((2 * lanes, 2 * lanes), BF16),
         ],
         compiler_params=pltpu.CompilerParams(vmem_limit_bytes=32 * 2**20),
         cost_estimate=pl.CostEstimate(flops=10**9, bytes_accessed=2**20, transcendentals=0),
@@ -328,15 +338,27 @@
     )(z.reshape(1), gathered, cs, twist)
 
 
-def conv_kernel(x_ref, fwd_ref, inv_ref, tw_ref, a_ref, ai_ref, m_ref, f_ref, y_ref, r_ref, q_ref):
+def conv_kernel(
+    x_ref, fwd_hbm, inv_hbm, tw_hbm, a_ref, ai_ref, m_ref, f_ref, y_ref, fwd_ref, inv_ref, tw_ref, r_ref, q_ref, sems
+):
+    copies = [
+        pltpu.make_async_copy(src, dst, sems.at[i])
+        for i, (src, dst) in enumerate(((fwd_hbm, fwd_ref), (tw_hbm, tw_ref), (inv_hbm, inv_ref)))
+    ]
+    for copy in copies:
+        copy.start()
     chips, chans, both = x_ref.shape
     rows = both // 2
     blocks = rows // 128
+    half = 2 * chips
+    copies[0].wait()
     for col in range(2):
         x = x_ref[:, :, col * rows : (col + 1) * rows].reshape(chips * chans, rows)
         r = jnp.dot(x, fwd_ref[0], preferred_element_type=F32)
         r += jnp.dot(x, fwd_ref[1], preferred_element_type=F32)
         r = r.reshape(chips, chans, 2 * rows)
+        if col == 0:
+            copies[1].wait()
         tw = tw_ref[col * chips : (col + 1) * chips, :]
         cos = tw[:, None, :rows]
         sin = tw[:, None, rows:]
@@ -346,42 +368,44 @@
         for k in range(blocks):
             r_ref[col, k] = turned_re[:, k * 128 : (k + 1) * 128]
             r_ref[col, blocks + k] = turned_im[:, k * 128 : (k + 1) * 128]
-    half = 2 * chips
-    lane = lax.broadcasted_iota(jnp.int32, (2 * half, 128), 1)
-
-    def channel(c, carry):
-        pick = pl.ds(c, chips, stride=chans)
+    lane = lax.broadcasted_iota(jnp.int32, (4 * half, 128), 1)
+
+    def pair(n, carry):
+        picks = [pl.ds(2 * n + i, chips, stride=chans) for i in range(2)]
         parts = [
             jnp.concatenate([r_ref[col, part * blocks + k, pick, :] for k in range(blocks)], axis=1)
+            for pick in picks
             for part in range(2)
             for col in range(2)
         ]
         turned = jnp.concatenate(parts, axis=0).astype(BF16)
         s = jnp.dot(a_ref[...], turned, preferred_element_type=F32)
-        s = s[: 2 * half] + s[2 * half :]
-        s_re, s_im = s[:half], s[half:]
         f_re, f_im = f_ref[:, :rows], f_ref[:, rows:]
-        filtered = jnp.concatenate(
-            [s_re * f_re - s_im * f_im, s_re * f_im + s_im * f_re], axis=0
-        ).astype(BF16)
+        filtered = []
+        for i in range(2):
+            s_re = s[2 * i * half : (2 * i + 1) * half]
+            s_im = s[(2 * i + 1) * half : (2 * i + 2) * half]
+            filtered += [s_re * f_re - s_im * f_im, s_re * f_im + s_im * f_re]
+        filtered = jnp.concatenate(filtered, axis=0).astype(BF16)
         back = jnp.dot(ai_ref[...], filtered, preferred_element_type=F32)
-        back = back[: 2 * half] + back[2 * half :]
         edge = jnp.dot(m_ref[...], turned[:, :128], preferred_element_type=F32)
-        edge = edge[: 2 * half] + edge[2 * half :]
         head = jnp.where(lane == 0, edge, back[:, :128])
         back = jnp.concatenate([head, back[:, 128:]], axis=1)
-        b_re, b_im = back[:half], back[half:]
         cos, sin = tw_ref[:, :rows], tw_ref[:, rows:]
-        out_re = b_re * cos - b_im * sin
-        out_im = b_im * cos + b_re * sin
-        for col in range(2):
-            part = slice(col * chips, (col + 1) * chips)
-            for k in range(blocks):
-                q_ref[col, k, pick, :] = out_re[part, k * 128 : (k + 1) * 128]
-                q_ref[col, blocks + k, pick, :] = out_im[part, k * 128 : (k + 1) * 128]
+        for i, pick in enumerate(picks):
+            b_re = back[2 * i * half : (2 * i + 1) * half]
+            b_im = back[(2 * i + 1) * half : (2 * i + 2) * half]
+            out_re = b_re * cos - b_im * sin
+            out_im = b_im * cos + b_re * sin
+            for col in range(2):
+                part = slice(col * chips, (col + 1) * chips)
+                for k in range(blocks):
+                    q_ref[col, k, pick, :] = out_re[part, k * 128 : (k + 1) * 128]
+                    q_ref[col, blocks + k, pick, :] = out_im[part, k * 128 : (k + 1) * 128]
         return carry
 
-    lax.fori_loop(0, chans, channel, 0)
+    lax.fori_loop(0, chans // 2, pair, 0, unroll=2)
+    copies[2].wait()
     for col in range(2):
         q = jnp.concatenate([q_ref[col, k].astype(BF16) for k in range(2 * blocks)], axis=1)
         y = jnp.dot(q, inv_ref[0], preferred_element_type=F32)
@@ -392,14 +416,19 @@
 def long_conv(x, fwd, inv, tw, a, ai, m, f):
     chips, chans, both = x.shape
     vmem = pl.BlockSpec(memory_space=pltpu.VMEM)
+    hbm = pl.BlockSpec(memory_space=pl.ANY)
     return pl.pallas_call(
         conv_kernel,
-        in_specs=[vmem] * 8,
+        in_specs=[vmem, hbm, hbm, hbm, vmem, vmem, vmem, vmem],
         out_specs=vmem,
         out_shape=jax.ShapeDtypeStruct(x.shape, BF16),
         scratch_shapes=[
+            pltpu.VMEM(fwd.shape, BF16),
+            pltpu.VMEM(inv.shape, BF16),
+            pltpu.VMEM(tw.shape, F32),
             pltpu.VMEM((2, both // 128, chips * chans, 128), F32),
             pltpu.VMEM((2, both // 128, chips * chans, 128), F32),
+            pltpu.SemaphoreType.DMA((3,)),
         ],
         compiler_params=pltpu.CompilerParams(vmem_limit_bytes=48 * 2**20),
         cost_estimate=pl.CostEstimate(flops=8 * 10**9, bytes_accessed=8 * 2**20, transcendentals=0),
@@ -410,6 +439,11 @@
 def cos_sin(product, modulus):
     phase = (product % modulus).astype(F32) * (2.0 * math.pi / modulus)
     return jnp.cos(phase), jnp.sin(phase)
+
+
+def twice(t):
+    zero = jnp.zeros_like(t)
+    return jnp.block([[t, zero], [zero, t]])
 
 
 def column_tables(core, rows, cols, padded):
@@ -422,22 +456,22 @@
     a = jnp.block([[c, s], [-s, c]])
     twist = jnp.stack(cos_sin(jnp.mod((b[:, None] - b[None, :]) * rows, padded), padded))
 
-    def stacked(t):
-        return jnp.concatenate(split_table(t), axis=0)
-
-    return tw, stacked(a), stacked(a.T), jnp.stack([c, s]), twist
-
-
-def gather_two(block, first, second):
-    d1 = send(block, **{first: -1})
-    d3 = send(block, **{first: 1})
-    d2 = send(block, **{first: 2})
-    line = jnp.concatenate([block, d1, d2, d3], axis=0)
-    e1 = send(line, **{second: -1})
-    e3 = send(line, **{second: 1})
+    return tw, twice(a.astype(BF16)), twice(a.T.astype(BF16)), jnp.stack([c, s]), twist
+
+
+def gather_line(block, axis):
+    d1 = send(block, **{axis: -1})
+    d3 = send(block, **{axis: 1})
+    d2 = send(block, **{axis: 2})
+    return jnp.concatenate([block, d1, d2, d3], axis=0)
+
+
+def gather_lines(line, axis):
+    e1 = send(line, **{axis: -1})
+    e3 = send(line, **{axis: 1})
     half = line.shape[0] // 2
-    e2a = send(e1[:half], **{second: -1})
-    e2b = send(e3[half:], **{second: 1})
+    e2a = send(e1[:half], **{axis: -1})
+    e2b = send(e3[half:], **{axis: 1})
     return line, e1, e2a, e2b, e3
 
 
@@ -489,12 +523,13 @@
         axis=0,
     )
     gathered = lax.all_gather(gate_block, "seq", axis=0, axis_index_groups=SAME_CORE)
-    ow_part = lax.dynamic_slice_in_dim(
-        out_weight, core * (out_weight.shape[0] // 2), out_weight.shape[0] // 2, 0
+    key_line, value_line, late = lax.optimization_barrier(
+        (gather_line(key_block, "dx"), gather_line(value_block, "dy"), core)
     )
-    key_block, value_block, ow_part = lax.optimization_barrier((key_block, value_block, ow_part))
-    key_pieces = gather_two(key_block, "dx", "dy")
-    value_pieces = gather_two(value_block, "dy", "dx")
+    half_ow = out_weight.shape[0] // 2
+    ow_part = lax.dynamic_slice_in_dim(out_weight, late * half_ow, half_ow, 0)
+    key_pieces = gather_lines(key_line, "dy")
+    value_pieces = gather_lines(value_line, "dx")
 
     order = np.arange(32)
     p_, q_, dz = order // 8, (order // 2) % 4, order % 2
@@ -516,7 +551,6 @@
 
     tw, a, ai, cs, twist = column_tables(core, rows, cols, padded)
     f, m = filter_part(z, gathered, cs, twist)
-    m = m.reshape(-1, 2 * cols)
     forward, inverse = row_tables(rows, padded)
     fwd = jnp.asarray(np.stack(split_np(forward)))
     inv = jnp.asarray(np.stack(split_np(inverse)))
@@ -543,7 +577,8 @@
     from_c = send(oth_here, dc=1)
     here = ordered(own_here, from_c)
 
-    mixed = mix_part(here, from_h, from_hc, out_weight, ow_same, ow_cross)
+    mixed = mix_part(None, [here], [out_weight])
+    mixed = mix_part(mixed, [from_h, from_hc], [ow_same, ow_cross])
     return mixed.reshape(kept, 1, width)
 
 

time: 269 us -> 246 us (0.914)
  waiting for transfers between devices: 108 us -> 82.8 us
  starting transfers between devices: 50.9 us -> 56.4 us
  Pallas kernels: 58.4 us -> 54.5 us
    ppermute x21, waiting for transfers between devices: 81.5 us -> 65.5 us  [send(): return lax.ppermute(value, 'seq', perm)]
    ppermute x21, starting transfers between devices: 31.9 us -> 38.7 us  [send(): return lax.ppermute(value, 'seq', perm)]
    ppermute x1, waiting for transfers between devices: 5.03 us -> 0.01 us  [per_device(): from_h = lax.ppermute(own_there, 'ch', swap_ch)]
    pallas_call x2 -> x3, Pallas kernels: 28.6 us -> 24.7 us  [the longest x2 12.7 us: mix_part(): pl.pallas_call(mix_kernel if total is None else mix_more_kernel, grid=(4,...]
    all_to_all x1, starting transfers between devices: 12 us -> 8.35 us  [per_device(): mine_ch = lax.all_to_all(packed, 'seq', 0, 0, axis_index_groups=SAME_CORE)]
    unnamed x0 -> x4, other arithmetic: none -> 2.73 us
    unnamed x42 -> x40, local copies, waits for them, and re-layouts: 20.4 us -> 19.1 us
  transfers between devices with their start and end apart: 27 -> 27, of which waited for: 11 -> 9; matrix products, arithmetic and copies ran while one was open for 7% -> 8% of each run, Pallas kernels for 18% -> 19%
where the time goes in v3:
time: 246 us; the launch traced here: 245 us
  waiting for transfers between devices  82.8 us (34%)
  starting transfers between devices  56.4 us (23%)
  Pallas kernels  54.5 us (22%)
  local copies, waits for them, and re-layouts  29.2 us (12%)
  between operations  13.8 us (6%)
  other arithmetic  8.32 us (3%)
    ppermute x21, waiting for transfers between devices, send(): return lax.ppermute(value, 'seq', perm)  65.5 us
    ppermute x21, starting transfers between devices, send(): return lax.ppermute(value, 'seq', perm)  38.7 us
    unnamed x40, local copies, waits for them, and re-layouts  19.1 us
    pallas_call x1, Pallas kernels, first_part(): pl.pallas_call(first_kernel, grid_spec=pltpu.PrefetchScalarGridSpec(num_s...  13.5 us
    pallas_call x2, Pallas kernels, mix_part(): pl.pallas_call(mix_kernel if total is None else mix_more_kernel, grid=(4,...  12.7 us
    pallas_call x1, Pallas kernels, long_conv(): pl.pallas_call(conv_kernel, in_specs=[vmem, hbm, hbm, hbm, vmem, vmem, vm...  12 us
    pallas_call x1, Pallas kernels, gate_part(): pl.pallas_call(gate_kernel, grid=(4,), in_specs=[pl.BlockSpec((tile, widt...  8.62 us
    all_to_all x1, starting transfers between devices, per_device(): mine_ch = lax.all_to_all(packed, 'seq', 0, 0, axis_index_groups=SAME_CORE)  8.35 us
  transfers between devices with their start and end apart: 27, of which 9 were waited for; matrix products, arithmetic and copies ran while one was open for 8% of the time, Pallas kernels for 19%

profile of v3, /device:TPU:1, one launch (start us, length us, event | category | flops | bytes accessed | tf_op | source)
XLA Modules:
  0.0 244.9 jit_solution(782463520702372424)
XLA Ops:
  6.5 0.8 constant_dynamic-update-slice_fusion.4
  7.3 0.9 copy.14
  8.4 0.7 constant_dynamic-update-slice_fusion.3
  9.1 0.7 constant_dynamic-update-slice_fusion.2
  9.8 0.7 constant_dynamic-update-slice_fusion.1
  10.6 1.5 collective-permute-start.1
  12.1 0.8 dynamic-slice_bitcast_fusion.11
  14.2 3.7 %collective-permute-start.4 = (bf16[128,512]{1,0:T(8,128)(2,1)S(1)}, bf16[128,512]{1,0:T(8,128)(2,1)S(1)}, u32[]{:S(2)}, u32[]{:S(2)}) collective-permute-start(bf16[128,512]{1,0:T(8,128)(2,1)S(1)} %pad_maximum_fusion.6), channel_id=1, source_target_pairs={{0,66},{2,64},{4,70},{6,68},{8,74},{10,72},{12,78},{14,76},{16,82}... | collective-permute-start | bytes 393224 | tf_op jit(solution)/shard_map/ppermute | solution.py:34
  18.0 0.7 constant_dynamic-update-slice_fusion.18
  18.7 1.0 collective-permute-start.3
  19.7 0.7 constant_dynamic-update-slice_fusion.17
  20.4 1.3 collective-permute-done.4
  21.7 3.3 %collective-permute-done.3 = bf16[128,512]{1,0:T(8,128)(2,1)S(1)} collective-permute-done((bf16[128,512]{1,0:T(8,128)(2,1)S(1)}, bf16[128,512]{1,0:T(8,128)(2,1)S(1)}, u32[]{:S(2)}, u32[]{:S(2)}) %collective-permute-start.3) | collective-permute-done | bytes 131104 | tf_op jit(solution)/shard_map/ppermute | solution.py:34
  25.0 0.7 constant_dynamic-update-slice_fusion.16
  25.7 0.7 constant_dynamic-update-slice_fusion.15
  26.4 2.5 %collective-permute-start.5 = (bf16[256,512]{1,0:T(8,128)(2,1)S(1)}, bf16[256,512]{1,0:T(8,128)(2,1)S(1)}, u32[]{:S(2)}, u32[]{:S(2)}) collective-permute-start(bf16[256,512]{1,0:T(8,128)(2,1)S(1)} %pad_maximum_fusion.1), channel_id=1, source_target_pairs={{0,12},{2,14},{4,0},{6,2},{8,4},{10,6},{12,8},{14,10},{16,28},{18,... | collective-permute-start | bytes 786440 | tf_op jit(solution)/shard_map/ppermute | solution.py:34
  29.4 1.7 collective-permute-start
  31.8 2.8 %collective-permute-start.8 = (bf16[256,512]{1,0:T(8,128)(2,1)S(1)}, bf16[256,512]{1,0:T(8,128)(2,1)S(1)}, u32[]{:S(2)}, u32[]{:S(2)}) collective-permute-start(bf16[256,512]{1,0:T(8,128)(2,1)S(1)} %pad_maximum_fusion.2), channel_id=1, source_target_pairs={{0,48},{2,50},{4,52},{6,54},{8,56},{10,58},{12,60},{14,62},{16,0},... | collective-permute-start | bytes 786440 | tf_op jit(solution)/shard_map/ppermute | solution.py:34
  34.6 2.9 %collective-permute-start.9 = (bf16[256,512]{1,0:T(8,128)(2,1)S(1)}, bf16[256,512]{1,0:T(8,128)(2,1)S(1)}, u32[]{:S(2)}, u32[]{:S(2)}) collective-permute-start(bf16[256,512]{1,0:T(8,128)(2,1)S(1)} %pad_maximum_fusion.2), channel_id=1, source_target_pairs={{0,32},{2,34},{4,36},{6,38},{8,40},{10,42},{12,44},{14,46},{16,48}... | collective-permute-start | bytes 786440 | tf_op jit(solution)/shard_map/ppermute | solution.py:34
  37.5 0.7 constant_dynamic-update-slice_fusion.7
  38.7 0.7 constant_dynamic-update-slice_fusion.6
  39.4 6.0 %collective-permute-done.7 = bf16[256,512]{1,0:T(8,128)(2,1)S(1)} collective-permute-done((bf16[256,512]{1,0:T(8,128)(2,1)S(1)}, bf16[256,512]{1,0:T(8,128)(2,1)S(1)}, u32[]{:S(2)}, u32[]{:S(2)}) %collective-permute-start.7) | collective-permute-done | bytes 262176 | tf_op jit(solution)/shard_map/ppermute | solution.py:34
  45.5 0.7 constant_dynamic-update-slice_fusion.5.refs_0_
  46.2 0.7 constant_dynamic-update-slice_fusion.14
  46.9 0.7 constant_dynamic-update-slice_fusion.13
  47.6 0.7 constant_dynamic-update-slice_fusion.12.refs_3_
  48.4 4.7 %constant_dynamic-slice_fusion = bf16[512,4096]{1,0:T(8,128)(2,1)} fusion(bf16[1024,4096]{1,0:T(8,128)(2,1)} %w_here.1, s32[]{:T(128)S(6)} %select_n.276), kind=kLoop, calls=%fused_computation.119 | loop fusion | bytes 8388612 | tf_op jit(solution)/shard_map/dynamic_slice | solution.py:530
  53.1 2.5 %collective-permute-start.22 = (bf16[512,4096]{1,0:T(8,128)(2,1)}, bf16[512,4096]{1,0:T(8,128)(2,1)}, u32[]{:S(2)}, u32[]{:S(2)}) collective-permute-start(bf16[512,4096]{1,0:T(8,128)(2,1)} %constant_dynamic-slice_fusion), channel_id=1, source_target_pairs={{0,1},{1,0},{2,67},{3,66},{4,5},{5,4},{6,71},{7,70},{8,9},{9,8},{1... | collective-permute-start | bytes 12582920 | tf_op jit(solution)/shard_map/ppermute | solution.py:545
  55.6 2.7 %collective-permute-start.11 = (bf16[1024,512]{1,0:T(8,128)(2,1)}, bf16[1024,512]{1,0:T(8,128)(2,1)S(1)}, u32[]{:S(2)}, u32[]{:S(2)}) collective-permute-start(bf16[1024,512]{1,0:T(8,128)(2,1)} %constant_dynamic-update-slice_fusion.5.refs_0_), channel_id=1, source_target_pairs={{0,48},{2,50},{4,52},{6,54},{8,56},{10,58},{12,60},{14,62},{16,0},... | collective-permute-start | bytes 3145736 | tf_op jit(solution)/shard_map/ppermute | solution.py:34
  58.3 3.0 %collective-permute-start.13 = (bf16[1024,512]{1,0:T(8,128)(2,1)}, bf16[1024,512]{1,0:T(8,128)(2,1)S(1)}, u32[]{:S(2)}, u32[]{:S(2)}) collective-permute-start(bf16[1024,512]{1,0:T(8,128)(2,1)} %constant_dynamic-update-slice_fusion.12.refs_3_), channel_id=1, source_target_pairs={{0,12},{2,14},{4,0},{6,2},{8,4},{10,6},{12,8},{14,10},{16,28},{18,... | collective-permute-start | bytes 3145736 | tf_op jit(solution)/shard_map/ppermute | solution.py:34
  61.3 26.9 %collective-permute-done.11.refs_1_ = bf16[1024,512]{1,0:T(8,128)(2,1)S(1)} collective-permute-done((bf16[1024,512]{1,0:T(8,128)(2,1)}, bf16[1024,512]{1,0:T(8,128)(2,1)S(1)}, u32[]{:S(2)}, u32[]{:S(2)}) %collective-permute-start.11) | collective-permute-done | bytes 1048608 | tf_op jit(solution)/shard_map/ppermute | solution.py:34
  88.2 5.3 %collective-permute-start.14 = (bf16[1024,512]{1,0:T(8,128)(2,1)}, bf16[1024,512]{1,0:T(8,128)(2,1)}, u32[]{:S(2)}, u32[]{:S(2)}) collective-permute-start(bf16[1024,512]{1,0:T(8,128)(2,1)} %constant_dynamic-update-slice_fusion.12.refs_3_), channel_id=1, source_target_pairs={{0,4},{2,6},{4,8},{6,10},{8,12},{10,14},{12,0},{14,2},{16,20},{18,... | collective-permute-start | bytes 3145736 | tf_op jit(solution)/shard_map/ppermute | solution.py:34
  93.9 1.9 collective-permute-start.15
  96.1 27.8 %collective-permute-done.14.refs_5_ = bf16[1024,512]{1,0:T(8,128)(2,1)} collective-permute-done((bf16[1024,512]{1,0:T(8,128)(2,1)}, bf16[1024,512]{1,0:T(8,128)(2,1)}, u32[]{:S(2)}, u32[]{:S(2)}) %collective-permute-start.14) | collective-permute-done | bytes 1048608 | tf_op jit(solution)/shard_map/ppermute | solution.py:34
  123.9 1.8 collective-permute-start.17
  125.7 1.1 slice.107
  127.4 13.5 %first_part.1 = (f32[1024,512]{1,0:T(8,128)}, f32[1024,512]{1,0:T(8,128)}, bf16[1024,1024]{1,0:T(8,128)(2,1)}, bf16[1024,1024]{1,0:T(8,128)(2,1)}) custom-call(s32[2,32]{1,0:T(2,128)S(1)} %pad_add_fusion.order_ref, bf16[512,4096]{1,0:T(8,128)(2,1)} %bitcast.59, bf16[512,4096]{1,0:T(8,128)(2,1)} %collective-permute-done.other_ref, ...), custom_call_target="tpu_custom_call" | custom-call | flops 6442450944 | bytes 23068672 | tf_op jit(solution)/shard_map/first_part/pallas_call | solution.py:101
  141.0 6.8 %last_part.1 = (f32[512,1024]{1,0:T(8,128)S(1)}, bf16[512,1024]{1,0:T(8,128)(2,1)}) custom-call(f32[1024,512]{1,0:T(8,128)} %get-tuple-element.18.key_ref, f32[1024,512]{1,0:T(8,128)} %get-tuple-element.19.value_ref, bf16[1024,1024]{1,0:T(8,128)(2,1)} %get-tuple-element.20.key_tok_ref, bf16[1024,1024]{1,0:T(8,128)(2,1)} %get-tuple-element.21.value_tok_ref, ...), custom_call_target="tpu_custom_call" | custom-call | flops 2147483648 | bytes 13631488 | tf_op jit(solution)/shard_map/last_part/pallas_call | solution.py:148
  147.8 8.3 %all-to-all-start = ((bf16[32,16,1024]{2,1,0:T(8,128)(2,1)}), bf16[32,16,1024]{2,1,0:T(8,128)(2,1)S(1)}, u32[]{:S(2)}, u32[]{:S(2)}) async-start(bf16[32,16,1024]{2,1,0:T(8,128)(2,1)} %bitcast.24), calls=%async_computation | async-start | bytes 2097152 | tf_op jit(solution)/shard_map/all_to_all | solution.py:550
  156.2 1.4 collective-permute-start.23
  157.6 0.8 copy.16.a_ref
  160.1 2.5 %copy-done = bf16[20480,128]{1,0:T(8,128)(2,1)S(1)} copy-done((bf16[20480,128]{1,0:T(8,128)(2,1)S(1)}, bf16[20480,128]{1,0:T(8,128)(2,1)}, u32[]{:S(2)}) %copy-start) | copy-done | bytes 5242904
  162.6 0.8 filter_part.1
  163.4 0.7 copy-done.5
  164.7 8.0 %all-to-all-done.x_ref = bf16[32,16,1024]{2,1,0:T(8,128)(2,1)S(1)} async-done(((bf16[32,16,1024]{2,1,0:T(8,128)(2,1)}), bf16[32,16,1024]{2,1,0:T(8,128)(2,1)S(1)}, u32[]{:S(2)}, u32[]{:S(2)}) %all-to-all-start) | async-done | bytes 1048608 | tf_op jit(solution)/shard_map/all_to_all | solution.py:550
  172.7 0.9 copy-done.2
  173.7 0.9 copy-done.3
  174.6 0.9 copy-done.6
  175.5 0.9 copy-done.8
  176.4 1.6 copy-done.9
  178.0 12.0 %long_conv.1 = bf16[32,16,1024]{2,1,0:T(8,128)(2,1)S(1)} custom-call(bf16[32,16,1024]{2,1,0:T(8,128)(2,1)S(1)} %all-to-all-done.x_ref, bf16[2,512,1024]{2,1,0:T(8,128)(2,1)S(1)} %copy-done.9, bf16[2,1024,512]{2,1,0:T(8,128)(2,1)} %constant.194.clone.inv_hbm, f32[64,1024]{1,0:T(8,128)S(1)} %pad_maximum_fusion.3.tw_hbm, bf16[256,256]{1,0:T(8,128)(2,1)S(1)} %copy-done.3, ...), custom_call_target="tpu_custom_call" | custom-call | flops 8000000000 | bytes 8388608 | tf_op jit(solution)/shard_map/long_conv/pallas_call | solution.py:420
  190.1 1.0 copy-done.1
  191.0 5.1 %all-to-all-start.1 = ((bf16[32,16,1024]{2,1,0:T(8,128)(2,1)}), bf16[32,16,1024]{2,1,0:T(8,128)(2,1)}, u32[]{:S(2)}, u32[]{:S(2)}) async-start(bf16[32,16,1024]{2,1,0:T(8,128)(2,1)} %copy-done.1), calls=%async_computation.1 | async-start | bytes 2097152 | tf_op jit(solution)/shard_map/all_to_all | solution.py:558
  196.2 2.2 copy-done.4
  198.4 8.6 %gate_part.1 = bf16[512,1024]{1,0:T(8,128)(2,1)S(1)} custom-call(bf16[512,4096]{1,0:T(8,128)(2,1)S(1)} %bitcast.60, bf16[512,4096]{1,0:T(8,128)(2,1)} %collective-permute-done.other_ref, bf16[32,640,128]{2,1,0:T(8,128)(2,1)} %bitcast.56), custom_call_target="tpu_custom_call" | custom-call | flops 4294967296 | bytes 13631488 | tf_op jit(solution)/shard_map/gate_part/pallas_call | solution.py:197
  207.1 4.3 %all-to-all-done.1 = bf16[32,16,1024]{2,1,0:T(8,128)(2,1)} async-done(((bf16[32,16,1024]{2,1,0:T(8,128)(2,1)}), bf16[32,16,1024]{2,1,0:T(8,128)(2,1)}, u32[]{:S(2)}, u32[]{:S(2)}) %all-to-all-start.1) | async-done | bytes 1048608 | tf_op jit(solution)/shard_map/all_to_all | solution.py:558
  211.3 1.7 fusion.1
  213.0 1.0 copy-done.10
  214.1 3.6 %collective-permute-start.19 = (bf16[512,256]{1,0:T(8,128)(2,1)S(1)}, bf16[512,256]{1,0:T(8,128)(2,1)S(1)}, u32[]{:S(2)}, u32[]{:S(2)}) collective-permute-start(bf16[512,256]{1,0:T(8,128)(2,1)S(1)} %get-tuple-element.51), channel_id=1, source_target_pairs={{0,2},{2,0},{4,6},{6,4},{8,10},{10,8},{12,14},{14,12},{16,18},{18,... | collective-permute-start | bytes 786440 | tf_op jit(solution)/shard_map/ppermute | solution.py:34
  217.7 1.7 collective-permute-start.21
  219.4 1.0 broadcast_select_fusion.1
  220.5 5.9 %mix_part.1.total_ref = f32[256,4096]{1,0:T(8,128)S(1)} custom-call(bf16[1024,256]{1,0:T(8,128)(2,1)S(1)} %pad_maximum_fusion.here, bf16[1024,4096]{1,0:T(8,128)(2,1)} %w_here.1), custom_call_target="tpu_custom_call" | custom-call | flops 2147483648 | bytes 12582912 | tf_op jit(solution)/shard_map/mix_part/pallas_call | solution.py:254
  226.4 4.9 %collective-permute-done.21.far_h = bf16[512,256]{1,0:T(8,128)(2,1)S(1)} collective-permute-done((bf16[512,256]{1,0:T(8,128)(2,1)S(1)}, bf16[512,256]{1,0:T(8,128)(2,1)S(1)}, u32[]{:S(2)}, u32[]{:S(2)}) %collective-permute-start.21) | collective-permute-done | bytes 262176 | tf_op jit(solution)/shard_map/ppermute | solution.py:576
  231.3 6.8 %mix_more.1 = bf16[256,4096]{1,0:T(8,128)(2,1)} custom-call(f32[256,4096]{1,0:T(8,128)S(1)} %mix_part.1.total_ref, bf16[512,256]{1,0:T(8,128)(2,1)S(1)} %collective-permute-done.20.near_h, bf16[512,256]{1,0:T(8,128)(2,1)S(1)} %collective-permute-done.21.far_h, bf16[512,4096]{1,0:T(8,128)(2,1)} %collective-permute-done.22.w_near, ...), custom_call_target="tpu_custom_call" | custom-call | flops 2147483648 | bytes 12582912 | tf_op jit(solution)/shard_map/mix_more/pallas_call | solution.py:254
  (86 shorter events, 6.9 us)
Async XLA Ops:
  6.5 7.2 %copy-start.11 = (bf16[64,3,1024]{2,0,1:T(8,128)(2,1)S(1)}, bf16[64,3,1024]{2,0,1:T(8,128)(2,1)}, u32[]{:S(2)}) copy-start(bf16[64,3,1024]{2,0,1:T(8,128)(2,1)} %param.11) | copy-start | bytes 1179652
  6.5 153.6 %all-gather.3.cloned.1.call-start = ((), (), s32[]{:S(2)}) async-start(), calls=%async_computation.2 | async-start | bytes 5406720 | tf_op jit(solution)/shard_map/all_gather | solution.py:525
  10.6 2.4 collective-permute-start.1
  13.8 4.2 %collective-permute-start.2 = (bf16[128,512]{1,0:T(8,128)(2,1)S(1)}, bf16[128,512]{1,0:T(8,128)(2,1)S(1)}, u32[]{:S(2)}, u32[]{:S(2)}) collective-permute-start(bf16[128,512]{1,0:T(8,128)(2,1)S(1)} %pad_maximum_fusion.6), channel_id=1, source_target_pairs={{0,2},{2,0},{4,6},{6,4},{8,10},{10,8},{12,14},{14,12},{16,18},{18,... | collective-permute-start | bytes 393224 | tf_op jit(solution)/shard_map/ppermute | solution.py:34
  14.2 7.4 %collective-permute-start.4 = (bf16[128,512]{1,0:T(8,128)(2,1)S(1)}, bf16[128,512]{1,0:T(8,128)(2,1)S(1)}, u32[]{:S(2)}, u32[]{:S(2)}) collective-permute-start(bf16[128,512]{1,0:T(8,128)(2,1)S(1)} %pad_maximum_fusion.6), channel_id=1, source_target_pairs={{0,66},{2,64},{4,70},{6,68},{8,74},{10,72},{12,78},{14,76},{16,82}... | collective-permute-start | bytes 393224 | tf_op jit(solution)/shard_map/ppermute | solution.py:34
  18.7 6.3 %collective-permute-start.3 = (bf16[128,512]{1,0:T(8,128)(2,1)S(1)}, bf16[128,512]{1,0:T(8,128)(2,1)S(1)}, u32[]{:S(2)}, u32[]{:S(2)}) collective-permute-start(bf16[128,512]{1,0:T(8,128)(2,1)S(1)} %pad_maximum_fusion.7), channel_id=1, source_target_pairs={{0,64},{2,66},{4,68},{6,70},{8,72},{10,74},{12,76},{14,78},{16,80}... | collective-permute-start | bytes 393224 | tf_op jit(solution)/shard_map/ppermute | solution.py:34
  26.4 8.2 %collective-permute-start.5 = (bf16[256,512]{1,0:T(8,128)(2,1)S(1)}, bf16[256,512]{1,0:T(8,128)(2,1)S(1)}, u32[]{:S(2)}, u32[]{:S(2)}) collective-permute-start(bf16[256,512]{1,0:T(8,128)(2,1)S(1)} %pad_maximum_fusion.1), channel_id=1, source_target_pairs={{0,12},{2,14},{4,0},{6,2},{8,4},{10,6},{12,8},{14,10},{16,28},{18,... | collective-permute-start | bytes 786440 | tf_op jit(solution)/shard_map/ppermute | solution.py:34
  28.9 9.4 %collective-permute-start.6 = (bf16[256,512]{1,0:T(8,128)(2,1)S(1)}, bf16[256,512]{1,0:T(8,128)(2,1)S(1)}, u32[]{:S(2)}, u32[]{:S(2)}) collective-permute-start(bf16[256,512]{1,0:T(8,128)(2,1)S(1)} %pad_maximum_fusion.1), channel_id=1, source_target_pairs={{0,8},{2,10},{4,12},{6,14},{8,0},{10,2},{12,4},{14,6},{16,24},{18,... | collective-permute-start | bytes 786440 | tf_op jit(solution)/shard_map/ppermute | solution.py:34
  29.4 97.3 %collective-permute-start = (bf16[512,4096]{1,0:T(8,128)(2,1)}, bf16[512,4096]{1,0:T(8,128)(2,1)}, u32[]{:S(2)}, u32[]{:S(2)}) collective-permute-start(bf16[512,4096]{1,0:T(8,128)(2,1)} %bitcast.58), channel_id=1, source_target_pairs={{0,2},{2,0},{4,6},{6,4},{8,10},{10,8},{12,14},{14,12},{16,18},{18,... | collective-permute-start | bytes 12582920 | tf_op jit(solution)/shard_map/ppermute | solution.py:34
  31.2 14.3 %collective-permute-start.7 = (bf16[256,512]{1,0:T(8,128)(2,1)S(1)}, bf16[256,512]{1,0:T(8,128)(2,1)S(1)}, u32[]{:S(2)}, u32[]{:S(2)}) collective-permute-start(bf16[256,512]{1,0:T(8,128)(2,1)S(1)} %pad_maximum_fusion.1), channel_id=1, source_target_pairs={{0,4},{2,6},{4,8},{6,10},{8,12},{10,14},{12,0},{14,2},{16,20},{18,... | collective-permute-start | bytes 786440 | tf_op jit(solution)/shard_map/ppermute | solution.py:34
  31.8 14.4 %collective-permute-start.8 = (bf16[256,512]{1,0:T(8,128)(2,1)S(1)}, bf16[256,512]{1,0:T(8,128)(2,1)S(1)}, u32[]{:S(2)}, u32[]{:S(2)}) collective-permute-start(bf16[256,512]{1,0:T(8,128)(2,1)S(1)} %pad_maximum_fusion.2), channel_id=1, source_target_pairs={{0,48},{2,50},{4,52},{6,54},{8,56},{10,58},{12,60},{14,62},{16,0},... | collective-permute-start | bytes 786440 | tf_op jit(solution)/shard_map/ppermute | solution.py:34
  34.6 12.3 %collective-permute-start.9 = (bf16[256,512]{1,0:T(8,128)(2,1)S(1)}, bf16[256,512]{1,0:T(8,128)(2,1)S(1)}, u32[]{:S(2)}, u32[]{:S(2)}) collective-permute-start(bf16[256,512]{1,0:T(8,128)(2,1)S(1)} %pad_maximum_fusion.2), channel_id=1, source_target_pairs={{0,32},{2,34},{4,36},{6,38},{8,40},{10,42},{12,44},{14,46},{16,48}... | collective-permute-start | bytes 786440 | tf_op jit(solution)/shard_map/ppermute | solution.py:34
  38.3 9.4 %collective-permute-start.10 = (bf16[256,512]{1,0:T(8,128)(2,1)S(1)}, bf16[256,512]{1,0:T(8,128)(2,1)S(1)}, u32[]{:S(2)}, u32[]{:S(2)}) collective-permute-start(bf16[256,512]{1,0:T(8,128)(2,1)S(1)} %pad_maximum_fusion.2), channel_id=1, source_target_pairs={{0,16},{2,18},{4,20},{6,22},{8,24},{10,26},{12,28},{14,30},{16,32}... | collective-permute-start | bytes 786440 | tf_op jit(solution)/shard_map/ppermute | solution.py:34
  48.4 45.2 %copy-start.13 = (s32[32]{0:T(128)S(1)}, s32[32]{0:T(128)}, u32[]{:S(2)}) copy-start(s32[32]{0:T(128)} %constant.192.clone) | copy-start | bytes 388
  48.4 45.2 %copy-start.14 = (s32[32]{0:T(128)S(1)}, s32[32]{0:T(128)}, u32[]{:S(2)}) copy-start(s32[32]{0:T(128)} %constant.191.clone) | copy-start | bytes 388
  48.4 45.2 %copy-start.15 = (s32[32]{0:T(128)S(1)}, s32[32]{0:T(128)}, u32[]{:S(2)}) copy-start(s32[32]{0:T(128)} %constant.190.clone) | copy-start | bytes 388
  53.1 103.1 %collective-permute-start.22 = (bf16[512,4096]{1,0:T(8,128)(2,1)}, bf16[512,4096]{1,0:T(8,128)(2,1)}, u32[]{:S(2)}, u32[]{:S(2)}) collective-permute-start(bf16[512,4096]{1,0:T(8,128)(2,1)} %constant_dynamic-slice_fusion), channel_id=1, source_target_pairs={{0,1},{1,0},{2,67},{3,66},{4,5},{5,4},{6,71},{7,70},{8,9},{9,8},{1... | collective-permute-start | bytes 12582920 | tf_op jit(solution)/shard_map/ppermute | solution.py:545
  55.6 32.7 %collective-permute-start.11 = (bf16[1024,512]{1,0:T(8,128)(2,1)}, bf16[1024,512]{1,0:T(8,128)(2,1)S(1)}, u32[]{:S(2)}, u32[]{:S(2)}) collective-permute-start(bf16[1024,512]{1,0:T(8,128)(2,1)} %constant_dynamic-update-slice_fusion.5.refs_0_), channel_id=1, source_target_pairs={{0,48},{2,50},{4,52},{6,54},{8,56},{10,58},{12,60},{14,62},{16,0},... | collective-permute-start | bytes 3145736 | tf_op jit(solution)/shard_map/ppermute | solution.py:34
  58.3 35.6 %collective-permute-start.12 = (bf16[1024,512]{1,0:T(8,128)(2,1)}, bf16[1024,512]{1,0:T(8,128)(2,1)S(1)}, u32[]{:S(2)}, u32[]{:S(2)}) collective-permute-start(bf16[1024,512]{1,0:T(8,128)(2,1)} %constant_dynamic-update-slice_fusion.5.refs_0_), channel_id=1, source_target_pairs={{0,16},{2,18},{4,20},{6,22},{8,24},{10,26},{12,28},{14,30},{16,32}... | collective-permute-start | bytes 3145736 | tf_op jit(solution)/shard_map/ppermute | solution.py:34
  58.3 37.6 %collective-permute-start.13 = (bf16[1024,512]{1,0:T(8,128)(2,1)}, bf16[1024,512]{1,0:T(8,128)(2,1)S(1)}, u32[]{:S(2)}, u32[]{:S(2)}) collective-permute-start(bf16[1024,512]{1,0:T(8,128)(2,1)} %constant_dynamic-update-slice_fusion.12.refs_3_), channel_id=1, source_target_pairs={{0,12},{2,14},{4,0},{6,2},{8,4},{10,6},{12,8},{14,10},{16,28},{18,... | collective-permute-start | bytes 3145736 | tf_op jit(solution)/shard_map/ppermute | solution.py:34
  88.2 35.6 %collective-permute-start.14 = (bf16[1024,512]{1,0:T(8,128)(2,1)}, bf16[1024,512]{1,0:T(8,128)(2,1)}, u32[]{:S(2)}, u32[]{:S(2)}) collective-permute-start(bf16[1024,512]{1,0:T(8,128)(2,1)} %constant_dynamic-update-slice_fusion.12.refs_3_), channel_id=1, source_target_pairs={{0,4},{2,6},{4,8},{6,10},{8,12},{10,14},{12,0},{14,2},{16,20},{18,... | collective-permute-start | bytes 3145736 | tf_op jit(solution)/shard_map/ppermute | solution.py:34
  93.9 47.0 %collective-permute-start.15 = (bf16[512,512]{1,0:T(8,128)(2,1)S(1)}, bf16[512,512]{1,0:T(8,128)(2,1)S(1)}, u32[]{:S(2)}, u32[]{:S(2)}) collective-permute-start(bf16[512,512]{1,0:T(8,128)(2,1)S(1)} %slice.104), channel_id=1, source_target_pairs={{0,48},{2,50},{4,52},{6,54},{8,56},{10,58},{12,60},{14,62},{16,0},... | collective-permute-start | bytes 1572872 | tf_op jit(solution)/shard_map/ppermute | solution.py:34
  95.9 45.0 %collective-permute-start.16 = (bf16[512,512]{1,0:T(8,128)(2,1)S(1)}, bf16[512,512]{1,0:T(8,128)(2,1)S(1)}, u32[]{:S(2)}, u32[]{:S(2)}) collective-permute-start(bf16[512,512]{1,0:T(8,128)(2,1)S(1)} %slice.105), channel_id=1, source_target_pairs={{0,16},{2,18},{4,20},{6,22},{8,24},{10,26},{12,28},{14,30},{16,32}... | collective-permute-start | bytes 1572872 | tf_op jit(solution)/shard_map/ppermute | solution.py:34
  123.9 17.1 %collective-permute-start.17 = (bf16[512,512]{1,0:T(8,128)(2,1)S(1)}, bf16[512,512]{1,0:T(8,128)(2,1)S(1)}, u32[]{:S(2)}, u32[]{:S(2)}) collective-permute-start(bf16[512,512]{1,0:T(8,128)(2,1)S(1)} %slice.106), channel_id=1, source_target_pairs={{0,12},{2,14},{4,0},{6,2},{8,4},{10,6},{12,8},{14,10},{16,28},{18,... | collective-permute-start | bytes 1572872 | tf_op jit(solution)/shard_map/ppermute | solution.py:34
  126.8 14.2 %collective-permute-start.18 = (bf16[512,512]{1,0:T(8,128)(2,1)S(1)}, bf16[512,512]{1,0:T(8,128)(2,1)S(1)}, u32[]{:S(2)}, u32[]{:S(2)}) collective-permute-start(bf16[512,512]{1,0:T(8,128)(2,1)S(1)} %slice.107), channel_id=1, source_target_pairs={{0,4},{2,6},{4,8},{6,10},{8,12},{10,14},{12,0},{14,2},{16,20},{18,... | collective-permute-start | bytes 1572872 | tf_op jit(solution)/shard_map/ppermute | solution.py:34
  147.8 24.9 %all-to-all-start = ((bf16[32,16,1024]{2,1,0:T(8,128)(2,1)}), bf16[32,16,1024]{2,1,0:T(8,128)(2,1)S(1)}, u32[]{:S(2)}, u32[]{:S(2)}) async-start(bf16[32,16,1024]{2,1,0:T(8,128)(2,1)} %bitcast.24), calls=%async_computation | async-start | bytes 2097152 | tf_op jit(solution)/shard_map/all_to_all | solution.py:550
  156.2 70.2 %collective-permute-start.23 = (bf16[512,4096]{1,0:T(8,128)(2,1)}, bf16[512,4096]{1,0:T(8,128)(2,1)}, u32[]{:S(2)}, u32[]{:S(2)}) collective-permute-start(bf16[512,4096]{1,0:T(8,128)(2,1)} %collective-permute-done.22.w_near), channel_id=1, source_target_pairs={{0,2},{2,0},{4,6},{6,4},{8,10},{10,8},{12,14},{14,12},{16,18},{18,... | collective-permute-start | bytes 12582920 | tf_op jit(solution)/shard_map/ppermute | solution.py:34
  160.1 2.5 %copy-start = (bf16[20480,128]{1,0:T(8,128)(2,1)S(1)}, bf16[20480,128]{1,0:T(8,128)(2,1)}, u32[]{:S(2)}) copy-start(bf16[20480,128]{1,0:T(8,128)(2,1)} %all-gather.3.cloned.1.call-done) | copy-start | bytes 15728644
  163.4 0.7 copy-start.5
  164.1 0.6 copy-start.7
  172.7 0.9 copy-start.2
  173.6 0.9 copy-start.3
  174.6 0.9 copy-start.6
  175.5 0.9 copy-start.8
  176.4 1.6 copy-start.9
  190.0 1.0 copy-start.1
  191.0 5.1 %copy-start.12 = (f32[1024]{0:T(1024)S(1)}, f32[1024]{0:T(1024)}, u32[]{:S(2)}) copy-start(f32[1024]{0:T(1024)} %param.13) | copy-start | bytes 12292
  191.0 20.3 %all-to-all-start.1 = ((bf16[32,16,1024]{2,1,0:T(8,128)(2,1)}), bf16[32,16,1024]{2,1,0:T(8,128)(2,1)}, u32[]{:S(2)}, u32[]{:S(2)}) async-start(bf16[32,16,1024]{2,1,0:T(8,128)(2,1)} %copy-done.1), calls=%async_computation.1 | async-start | bytes 2097152 | tf_op jit(solution)/shard_map/all_to_all | solution.py:558
  196.2 2.2 copy-start.4
  213.0 1.0 copy-start.10
  214.1 5.3 %collective-permute-start.19 = (bf16[512,256]{1,0:T(8,128)(2,1)S(1)}, bf16[512,256]{1,0:T(8,128)(2,1)S(1)}, u32[]{:S(2)}, u32[]{:S(2)}) collective-permute-start(bf16[512,256]{1,0:T(8,128)(2,1)S(1)} %get-tuple-element.51), channel_id=1, source_target_pairs={{0,2},{2,0},{4,6},{6,4},{8,10},{10,8},{12,14},{14,12},{16,18},{18,... | collective-permute-start | bytes 786440 | tf_op jit(solution)/shard_map/ppermute | solution.py:34
  217.7 8.7 %collective-permute-start.20 = (bf16[512,256]{1,0:T(8,128)(2,1)S(1)}, bf16[512,256]{1,0:T(8,128)(2,1)S(1)}, u32[]{:S(2)}, u32[]{:S(2)}) collective-permute-start(bf16[512,256]{1,0:T(8,128)(2,1)S(1)} %get-tuple-element.50), channel_id=1, source_target_pairs={{0,1},{1,0},{2,3},{3,2},{4,5},{5,4},{6,7},{7,6},{8,9},{9,8},{10,11... | collective-permute-start | bytes 786440 | tf_op jit(solution)/shard_map/ppermute | solution.py:571
  217.7 13.7 %collective-permute-start.21 = (bf16[512,256]{1,0:T(8,128)(2,1)S(1)}, bf16[512,256]{1,0:T(8,128)(2,1)S(1)}, u32[]{:S(2)}, u32[]{:S(2)}) collective-permute-start(bf16[512,256]{1,0:T(8,128)(2,1)S(1)} %get-tuple-element.49), channel_id=1, source_target_pairs={{0,3},{1,2},{2,1},{3,0},{4,7},{5,6},{6,5},{7,4},{8,11},{9,10},{10,... | collective-permute-start | bytes 786440 | tf_op jit(solution)/shard_map/ppermute | solution.py:576
Sparse Core Ops, SparseCore 0:
  13.9 108.2 all-gather.2

commit v4 on v3

--- a/solution.py
+++ b/solution.py
@@ -14,6 +14,7 @@
 F32 = jnp.float32
 HIGH = lax.Precision.HIGHEST
 SEQ = 64
+VMEM = 60 * 2**20
 CHIPS = 32
 SAME_CORE = [[2 * p + j for p in range(CHIPS)] for j in range(2)]
 
@@ -117,7 +118,7 @@
         ),
         out_shape=[jax.ShapeDtypeStruct((2 * rows, chan), F32)] * 2
         + [jax.ShapeDtypeStruct((2 * rows, quarter), BF16)] * 2,
-        compiler_params=pltpu.CompilerParams(vmem_limit_bytes=48 * 2**20),
+        compiler_params=pltpu.CompilerParams(vmem_limit_bytes=VMEM),
         cost_estimate=pl.CostEstimate(
             flops=2 * 2 * 2 * rows * 3 * quarter * chan, bytes_accessed=22 * 2**20, transcendentals=0
         ),
@@ -156,7 +157,7 @@
             jax.ShapeDtypeStruct((chan, total), F32),
             jax.ShapeDtypeStruct((chan, total), BF16),
         ],
-        compiler_params=pltpu.CompilerParams(vmem_limit_bytes=48 * 2**20),
+        compiler_params=pltpu.CompilerParams(vmem_limit_bytes=VMEM),
         cost_estimate=pl.CostEstimate(
             flops=2 * 2 * total * quarter * chan, bytes_accessed=13 * 2**20, transcendentals=0
         ),
@@ -204,7 +205,7 @@
         ],
         out_specs=pl.BlockSpec((chan, tile), lambda i: (0, i)),
         out_shape=jax.ShapeDtypeStruct((chan, 2 * rows), BF16),
-        compiler_params=pltpu.CompilerParams(vmem_limit_bytes=48 * 2**20),
+        compiler_params=pltpu.CompilerParams(vmem_limit_bytes=VMEM),
         cost_estimate=pl.CostEstimate(
             flops=2 * 2 * rows * width * chan, bytes_accessed=13 * 2**20, transcendentals=0
         ),
@@ -258,7 +259,7 @@
         out_specs=pl.BlockSpec((rows, tile), lambda i: (0, i)),
         out_shape=jax.ShapeDtypeStruct((rows, width), F32 if total is None else BF16),
         scratch_shapes=[pltpu.VMEM((rows, depth), BF16)],
-        compiler_params=pltpu.CompilerParams(vmem_limit_bytes=48 * 2**20),
+        compiler_params=pltpu.CompilerParams(vmem_limit_bytes=VMEM),
         cost_estimate=pl.CostEstimate(
             flops=2 * rows * depth * width, bytes_accessed=12 * 2**20, transcendentals=0
         ),
@@ -332,7 +333,7 @@
             jax.ShapeDtypeStruct((cols, 2 * rows), F32),
             jax.ShapeDtypeStruct((2 * lanes, 2 * lanes), BF16),
         ],
-        compiler_params=pltpu.CompilerParams(vmem_limit_bytes=32 * 2**20),
+        compiler_params=pltpu.CompilerParams(vmem_limit_bytes=VMEM),
         cost_estimate=pl.CostEstimate(flops=10**9, bytes_accessed=2**20, transcendentals=0),
         name="filter_part",
     )(z.reshape(1), gathered, cs, twist)
@@ -430,7 +431,7 @@
             pltpu.VMEM((2, both // 128, chips * chans, 128), F32),
             pltpu.SemaphoreType.DMA((3,)),
         ],
-        compiler_params=pltpu.CompilerParams(vmem_limit_bytes=48 * 2**20),
+        compiler_params=pltpu.CompilerParams(vmem_limit_bytes=VMEM),
         cost_estimate=pl.CostEstimate(flops=8 * 10**9, bytes_accessed=8 * 2**20, transcendentals=0),
         name="long_conv",
     )(x, fwd, inv, tw, a, ai, m, f)
@@ -523,6 +524,7 @@
         axis=0,
     )
     gathered = lax.all_gather(gate_block, "seq", axis=0, axis_index_groups=SAME_CORE)
+    key_block, value_block, other = lax.optimization_barrier((key_block, value_block, other))
     key_line, value_line, late = lax.optimization_barrier(
         (gather_line(key_block, "dx"), gather_line(value_block, "dy"), core)
     )

time: 246 us -> 219 us (0.89)
  waiting for transfers between devices: 82.8 us -> 57 us
  Pallas kernels: 54.5 us -> 66.3 us
  local copies, waits for them, and re-layouts: 29.2 us -> 18.9 us
  starting transfers between devices: 56.4 us -> 53.2 us
    ppermute x21, waiting for transfers between devices: 65.5 us -> 46.1 us  [send(): return lax.ppermute(value, 'seq', perm)]
    unnamed x40 -> x32, local copies, waits for them, and re-layouts: 19.1 us -> 5.98 us
    all_to_all x1, waiting for transfers between devices: 8 us -> 2.58 us  [per_device(): mine_ch = lax.all_to_all(packed, 'seq', 0, 0, axis_index_groups=SAME_CORE)]
    pallas_call x1, Pallas kernels: 12 us -> 15.9 us  [long_conv(): pl.pallas_call(conv_kernel, in_specs=[vmem, hbm, hbm, hbm, vmem, vmem, vm...]
    all_to_all x1, starting transfers between devices: 8.35 us -> 5.24 us  [per_device(): mine_ch = lax.all_to_all(packed, 'seq', 0, 0, axis_index_groups=SAME_CORE)]
    ppermute x21, starting transfers between devices: 38.7 us -> 35.6 us  [send(): return lax.ppermute(value, 'seq', perm)]
    slice x2, local copies, waits for them, and re-layouts: 0.07 us -> 2.97 us  [gather_lines(): e2a = send(e1[:half], **{axis: -1})]
    pallas_call x2, Pallas kernels: 12.7 us -> 15.4 us  [mix_part(): pl.pallas_call(mix_kernel if total is None else mix_more_kernel, grid=(4,...]
  transfers between devices with their start and end apart: 27 -> 27, of which waited for: 9 -> 10; matrix products, arithmetic and copies ran while one was open for 8% -> 11% of each run, Pallas kernels for 19% -> 27%
where the time goes in v4:
time: 219 us; the launch traced here: 217 us
  Pallas kernels  66.3 us (30%)
  waiting for transfers between devices  57 us (26%)
  starting transfers between devices  53.2 us (24%)
  local copies, waits for them, and re-layouts  18.9 us (9%)
  between operations  13.8 us (6%)
  other arithmetic  8.26 us (4%)
    ppermute x21, waiting for transfers between devices, send(): return lax.ppermute(value, 'seq', perm)  46.1 us
    ppermute x21, starting transfers between devices, send(): return lax.ppermute(value, 'seq', perm)  35.6 us
    pallas_call x1, Pallas kernels, long_conv(): pl.pallas_call(conv_kernel, in_specs=[vmem, hbm, hbm, hbm, vmem, vmem, vm...  15.9 us
    pallas_call x2, Pallas kernels, mix_part(): pl.pallas_call(mix_kernel if total is None else mix_more_kernel, grid=(4,...  15.4 us
    pallas_call x1, Pallas kernels, first_part(): pl.pallas_call(first_kernel, grid_spec=pltpu.PrefetchScalarGridSpec(num_s...  14.6 us
    pallas_call x1, Pallas kernels, gate_part(): pl.pallas_call(gate_kernel, grid=(4,), in_specs=[pl.BlockSpec((tile, widt...  9.98 us
    pallas_call x1, Pallas kernels, last_part(): pl.pallas_call(last_kernel, grid=(4,), in_specs=[pl.BlockSpec((tile, chan...  7.88 us
    all_to_all x1, starting transfers between devices, per_device(): conv = lax.all_to_all(conv, 'seq', 0, 0, axis_index_groups=SAME_CORE)  7.12 us
  transfers between devices with their start and end apart: 27, of which 10 were waited for; matrix products, arithmetic and copies ran while one was open for 11% of the time, Pallas kernels for 27%

profile of v4, /device:TPU:1, one launch (start us, length us, event | category | flops | bytes accessed | tf_op | source)
XLA Modules:
  0.0 217.5 jit_solution(1596031005505552048)
XLA Ops:
  6.5 1.4 collective-permute-start.3
  8.0 0.7 fusion.35
  8.7 0.9 copy.14
  9.7 0.7 fusion.34
  10.5 0.7 fusion.33
  11.2 0.7 fusion.32
  12.1 0.8 dynamic-slice_bitcast_fusion.11
  12.8 2.0 collective-permute-done.4
  14.9 0.7 pad_maximum_fusion.6
  15.7 0.5 collective-permute-start
  16.2 3.7 %collective-permute-start.2 = (bf16[128,512]{1,0:T(8,128)(2,1)S(1)}, bf16[128,512]{1,0:T(8,128)(2,1)S(1)}, u32[]{:S(2)}, u32[]{:S(2)}) collective-permute-start(bf16[128,512]{1,0:T(8,128)(2,1)S(1)} %pad_maximum_fusion.7), channel_id=1, source_target_pairs={{0,66},{2,64},{4,70},{6,68},{8,74},{10,72},{12,78},{14,76},{16,82}... | collective-permute-start | bytes 393224 | tf_op jit(solution)/shard_map/ppermute | solution.py:35
  19.9 1.0 collective-permute-start.1
  21.0 2.6 %collective-permute-done.2 = bf16[128,512]{1,0:T(8,128)(2,1)S(1)} collective-permute-done((bf16[128,512]{1,0:T(8,128)(2,1)S(1)}, bf16[128,512]{1,0:T(8,128)(2,1)S(1)}, u32[]{:S(2)}, u32[]{:S(2)}) %collective-permute-start.2) | collective-permute-done | bytes 131104 | tf_op jit(solution)/shard_map/ppermute | solution.py:35
  23.6 2.6 %collective-permute-done.1 = bf16[128,512]{1,0:T(8,128)(2,1)S(1)} collective-permute-done((bf16[128,512]{1,0:T(8,128)(2,1)S(1)}, bf16[128,512]{1,0:T(8,128)(2,1)S(1)}, u32[]{:S(2)}, u32[]{:S(2)}) %collective-permute-start.1) | collective-permute-done | bytes 131104 | tf_op jit(solution)/shard_map/ppermute | solution.py:35
  26.3 1.3 collective-permute-start.7
  27.6 2.5 %collective-permute-start.6 = (bf16[256,512]{1,0:T(8,128)(2,1)S(1)}, bf16[256,512]{1,0:T(8,128)(2,1)S(1)}, u32[]{:S(2)}, u32[]{:S(2)}) collective-permute-start(bf16[256,512]{1,0:T(8,128)(2,1)S(1)} %get-tuple-element.20), channel_id=1, source_target_pairs={{0,8},{2,10},{4,12},{6,14},{8,0},{10,2},{12,4},{14,6},{16,24},{18,... | collective-permute-start | bytes 786440 | tf_op jit(solution)/shard_map/ppermute | solution.py:35
  30.1 1.2 collective-permute-start.5
  31.2 1.3 collective-permute-start.10
  32.5 2.6 %collective-permute-start.9 = (bf16[256,512]{1,0:T(8,128)(2,1)S(1)}, bf16[256,512]{1,0:T(8,128)(2,1)S(1)}, u32[]{:S(2)}, u32[]{:S(2)}) collective-permute-start(bf16[256,512]{1,0:T(8,128)(2,1)S(1)} %get-tuple-element.21), channel_id=1, source_target_pairs={{0,32},{2,34},{4,36},{6,38},{8,40},{10,42},{12,44},{14,46},{16,48}... | collective-permute-start | bytes 786440 | tf_op jit(solution)/shard_map/ppermute | solution.py:35
  35.1 2.5 %collective-permute-start.8 = (bf16[256,512]{1,0:T(8,128)(2,1)S(1)}, bf16[256,512]{1,0:T(8,128)(2,1)S(1)}, u32[]{:S(2)}, u32[]{:S(2)}) collective-permute-start(bf16[256,512]{1,0:T(8,128)(2,1)S(1)} %get-tuple-element.21), channel_id=1, source_target_pairs={{0,48},{2,50},{4,52},{6,54},{8,56},{10,58},{12,60},{14,62},{16,0},... | collective-permute-start | bytes 786440 | tf_op jit(solution)/shard_map/ppermute | solution.py:35
  37.6 5.0 %collective-permute-done.6 = bf16[256,512]{1,0:T(8,128)(2,1)S(1)} collective-permute-done((bf16[256,512]{1,0:T(8,128)(2,1)S(1)}, bf16[256,512]{1,0:T(8,128)(2,1)S(1)}, u32[]{:S(2)}, u32[]{:S(2)}) %collective-permute-start.6) | collective-permute-done | bytes 262176 | tf_op jit(solution)/shard_map/ppermute | solution.py:35
  42.6 0.2 collective-permute-done.5
  42.9 3.9 %collective-permute-done.9 = bf16[256,512]{1,0:T(8,128)(2,1)S(1)} collective-permute-done((bf16[256,512]{1,0:T(8,128)(2,1)S(1)}, bf16[256,512]{1,0:T(8,128)(2,1)S(1)}, u32[]{:S(2)}, u32[]{:S(2)}) %collective-permute-start.9) | collective-permute-done | bytes 262176 | tf_op jit(solution)/shard_map/ppermute | solution.py:35
  46.9 5.1 %constant_dynamic-slice_fusion = bf16[512,4096]{1,0:T(8,128)(2,1)} fusion(bf16[1024,4096]{1,0:T(8,128)(2,1)} %w_here.1, s32[]{:T(128)S(6)} %select_n.276), kind=kLoop, calls=%fused_computation.107 | loop fusion | bytes 8388612 | tf_op jit(solution)/shard_map/dynamic_slice | solution.py:532
  52.0 3.5 %collective-permute-start.22 = (bf16[512,4096]{1,0:T(8,128)(2,1)}, bf16[512,4096]{1,0:T(8,128)(2,1)}, u32[]{:S(2)}, u32[]{:S(2)}) collective-permute-start(bf16[512,4096]{1,0:T(8,128)(2,1)} %constant_dynamic-slice_fusion), channel_id=1, source_target_pairs={{0,1},{1,0},{2,67},{3,66},{4,5},{5,4},{6,71},{7,70},{8,9},{9,8},{1... | collective-permute-start | bytes 12582920 | tf_op jit(solution)/shard_map/ppermute | solution.py:547
  55.4 2.6 %collective-permute-start.11 = (bf16[1024,512]{1,0:T(8,128)(2,1)S(1)}, bf16[1024,512]{1,0:T(8,128)(2,1)}, u32[]{:S(2)}, u32[]{:S(2)}) collective-permute-start(bf16[1024,512]{1,0:T(8,128)(2,1)S(1)} %pad_maximum_fusion.refs_0_), channel_id=1, source_target_pairs={{0,48},{2,50},{4,52},{6,54},{8,56},{10,58},{12,60},{14,62},{16,0},... | collective-permute-start | bytes 3145736 | tf_op jit(solution)/shard_map/ppermute | solution.py:35
  58.2 1.5 collective-permute-start.14
  59.7 0.6 pad_add_fusion.order_ref
  60.3 0.2 fusion.40
  60.6 29.7 %collective-permute-done.11.refs_1_ = bf16[1024,512]{1,0:T(8,128)(2,1)} collective-permute-done((bf16[1024,512]{1,0:T(8,128)(2,1)S(1)}, bf16[1024,512]{1,0:T(8,128)(2,1)}, u32[]{:S(2)}, u32[]{:S(2)}) %collective-permute-start.11) | collective-permute-done | bytes 1048608 | tf_op jit(solution)/shard_map/ppermute | solution.py:35
  90.2 1.1 slice.104
  91.3 3.2 %collective-permute-start.15 = (bf16[512,512]{1,0:T(8,128)(2,1)S(1)}, bf16[512,512]{1,0:T(8,128)(2,1)S(1)}, u32[]{:S(2)}, u32[]{:S(2)}) collective-permute-start(bf16[512,512]{1,0:T(8,128)(2,1)S(1)} %slice.104), channel_id=1, source_target_pairs={{0,48},{2,50},{4,52},{6,54},{8,56},{10,58},{12,60},{14,62},{16,0},... | collective-permute-start | bytes 1572872 | tf_op jit(solution)/shard_map/ppermute | solution.py:35
  94.5 1.1 slice.105
  95.7 1.9 slice.106
  97.6 1.1 slice.107
  98.7 1.7 collective-permute-start.18
  100.4 14.6 %first_part.1 = (f32[1024,512]{1,0:T(8,128)}, f32[1024,512]{1,0:T(8,128)}, bf16[1024,1024]{1,0:T(8,128)(2,1)}, bf16[1024,1024]{1,0:T(8,128)(2,1)}) custom-call(s32[2,32]{1,0:T(2,128)} %pad_add_fusion.order_ref, bf16[512,4096]{1,0:T(8,128)(2,1)} %bitcast.69, bf16[512,4096]{1,0:T(8,128)(2,1)} %collective-permute-done.3.other_ref, bf16[1024,512]{1,0:T(8,128)(2,1)} %copy-done, ...), custom_call_target="tpu_custom_call" | custom-call | flops 6442450944 | bytes 23068672 | tf_op jit(solution)/shard_map/first_part/pallas_call | solution.py:102
  115.0 0.7 copy-done.3
  115.9 0.2 copy-done.5
  116.1 0.2 copy-done.6
  116.4 7.9 %last_part.1 = (f32[512,1024]{1,0:T(8,128)}, bf16[512,1024]{1,0:T(8,128)(2,1)}) custom-call(f32[1024,512]{1,0:T(8,128)} %get-tuple-element.24.key_ref, f32[1024,512]{1,0:T(8,128)} %get-tuple-element.25.value_ref, bf16[1024,1024]{1,0:T(8,128)(2,1)} %get-tuple-element.26.key_tok_ref, bf16[1024,1024]{1,0:T(8,128)(2,1)} %get-tuple-element.27.value_tok_ref, ...), custom_call_target="tpu_custom_call" | custom-call | flops 2147483648 | bytes 13631488 | tf_op jit(solution)/shard_map/last_part/pallas_call | solution.py:149
  124.2 5.2 %all-to-all-start = ((bf16[32,16,1024]{2,1,0:T(8,128)(2,1)}), bf16[32,16,1024]{2,1,0:T(8,128)(2,1)S(1)}, u32[]{:S(2)}, u32[]{:S(2)}) async-start(bf16[32,16,1024]{2,1,0:T(8,128)(2,1)} %bitcast.58), calls=%async_computation | async-start | bytes 2097152 | tf_op jit(solution)/shard_map/all_to_all | solution.py:552
  129.5 4.5 %collective-permute-start.23 = (bf16[512,4096]{1,0:T(8,128)(2,1)}, bf16[512,4096]{1,0:T(8,128)(2,1)}, u32[]{:S(2)}, u32[]{:S(2)}) collective-permute-start(bf16[512,4096]{1,0:T(8,128)(2,1)} %collective-permute-done.22.w_near), channel_id=1, source_target_pairs={{0,2},{2,0},{4,6},{6,4},{8,10},{10,8},{12,14},{14,12},{16,18},{18,... | collective-permute-start | bytes 12582920 | tf_op jit(solution)/shard_map/ppermute | solution.py:35
  134.0 0.8 copy.16.a_ref
  134.8 0.7 fusion.9.ai_ref
  135.5 0.3 fusion.37
  135.8 0.7 pad_maximum_fusion.11
  136.5 0.6 fusion.15
  137.1 0.7 pad_maximum_fusion.5.tw_hbm
  137.8 2.6 %filter_part.1 = (f32[64,1024]{1,0:T(8,128)}, bf16[256,256]{1,0:T(8,128)(2,1)}) custom-call(s32[1]{0:T(128)} %bitcast.26.z_ref, bf16[32,640,128]{2,1,0:T(8,128)(2,1)} %bitcast.56, f32[2,64,64]{2,1,0:T(8,128)} %get-tuple-element.75.cs_ref, f32[2,64,64]{2,1,0:T(8,128)} %get-tuple-element.76.twist_ref), custom_call_target="tpu_custom_call" | custom-call | flops 1000000000 | bytes 1048576 | tf_op jit(solution)/shard_map/filter_part/pallas_call | solution.py:317
  140.4 2.6 %all-to-all-done.x_ref = bf16[32,16,1024]{2,1,0:T(8,128)(2,1)S(1)} async-done(((bf16[32,16,1024]{2,1,0:T(8,128)(2,1)}), bf16[32,16,1024]{2,1,0:T(8,128)(2,1)S(1)}, u32[]{:S(2)}, u32[]{:S(2)}) %all-to-all-start) | async-done | bytes 1048608 | tf_op jit(solution)/shard_map/all_to_all | solution.py:552
  143.0 1.0 copy-done.2
  143.9 15.9 %long_conv.1 = bf16[32,16,1024]{2,1,0:T(8,128)(2,1)} custom-call(bf16[32,16,1024]{2,1,0:T(8,128)(2,1)} %copy-done.2, bf16[2,512,1024]{2,1,0:T(8,128)(2,1)} %constant.193.clone.fwd_hbm, bf16[2,1024,512]{2,1,0:T(8,128)(2,1)} %constant.194.clone.inv_hbm, f32[64,1024]{1,0:T(8,128)} %pad_maximum_fusion.5.tw_hbm, bf16[256,256]{1,0:T(8,128)(2,1)} %copy.16.a_ref, ...), custom_call_target="tpu_custom_call" | custom-call | flops 8000000000 | bytes 8388608 | tf_op jit(solution)/shard_map/long_conv/pallas_call | solution.py:421
  159.9 7.1 %all-to-all-start.1 = ((bf16[32,16,1024]{2,1,0:T(8,128)(2,1)}), bf16[32,16,1024]{2,1,0:T(8,128)(2,1)S(1)}, u32[]{:S(2)}, u32[]{:S(2)}) async-start(bf16[32,16,1024]{2,1,0:T(8,128)(2,1)} %long_conv.1), calls=%async_computation.1 | async-start | bytes 2097152 | tf_op jit(solution)/shard_map/all_to_all | solution.py:560
  167.1 10.0 %gate_part.1 = bf16[512,1024]{1,0:T(8,128)(2,1)} custom-call(bf16[512,4096]{1,0:T(8,128)(2,1)} %bitcast.70, bf16[512,4096]{1,0:T(8,128)(2,1)} %collective-permute-done.3.other_ref, bf16[32,640,128]{2,1,0:T(8,128)(2,1)} %bitcast.57), custom_call_target="tpu_custom_call" | custom-call | flops 4294967296 | bytes 13631488 | tf_op jit(solution)/shard_map/gate_part/pallas_call | solution.py:198
  177.1 4.8 %all-to-all-done.1 = bf16[32,16,1024]{2,1,0:T(8,128)(2,1)S(1)} async-done(((bf16[32,16,1024]{2,1,0:T(8,128)(2,1)}), bf16[32,16,1024]{2,1,0:T(8,128)(2,1)S(1)}, u32[]{:S(2)}, u32[]{:S(2)}) %all-to-all-start.1) | async-done | bytes 1048608 | tf_op jit(solution)/shard_map/all_to_all | solution.py:560
  181.8 2.3 %fusion.1 = bf16[512,1024]{1,0:T(8,128)(2,1)S(1)} fusion(f32[512,1024]{1,0:T(8,128)} %get-tuple-element.31, bf16[512,1024]{1,0:T(8,128)(2,1)} %gate_part.1, bf16[32,16,1024]{2,1,0:T(8,128)(2,1)S(1)} %all-to-all-done.1, f32[512]{0:T(512)S(1)} %dynamic_slice.34), kind=kLoop, calls=%fused_computation.2 | loop fusion | flops 3145728 | bytes 5244928 | tf_op jit(solution)/shard_map/convert_element_type | solution.py:565
  184.3 4.0 %collective-permute-start.19 = (bf16[512,256]{1,0:T(8,128)(2,1)S(1)}, bf16[512,256]{1,0:T(8,128)(2,1)S(1)}, u32[]{:S(2)}, u32[]{:S(2)}) collective-permute-start(bf16[512,256]{1,0:T(8,128)(2,1)S(1)} %get-tuple-element.43), channel_id=1, source_target_pairs={{0,2},{2,0},{4,6},{6,4},{8,10},{10,8},{12,14},{14,12},{16,18},{18,... | collective-permute-start | bytes 786440 | tf_op jit(solution)/shard_map/ppermute | solution.py:35
  188.2 1.7 collective-permute-start.21
  190.1 0.8 pad_maximum_fusion.2.here
  190.9 7.4 %mix_part.1.total_ref = f32[256,4096]{1,0:T(8,128)} custom-call(bf16[1024,256]{1,0:T(8,128)(2,1)} %pad_maximum_fusion.2.here, bf16[1024,4096]{1,0:T(8,128)(2,1)} %w_here.1), custom_call_target="tpu_custom_call" | custom-call | flops 2147483648 | bytes 12582912 | tf_op jit(solution)/shard_map/mix_part/pallas_call | solution.py:255
  198.3 3.6 %collective-permute-done.21.far_h = bf16[512,256]{1,0:T(8,128)(2,1)S(1)} collective-permute-done((bf16[512,256]{1,0:T(8,128)(2,1)S(1)}, bf16[512,256]{1,0:T(8,128)(2,1)S(1)}, u32[]{:S(2)}, u32[]{:S(2)}) %collective-permute-start.21) | collective-permute-done | bytes 262176 | tf_op jit(solution)/shard_map/ppermute | solution.py:578
  201.9 0.7 copy-done.9
  202.6 8.0 %mix_more.1 = bf16[256,4096]{1,0:T(8,128)(2,1)} custom-call(f32[256,4096]{1,0:T(8,128)} %mix_part.1.total_ref, bf16[512,256]{1,0:T(8,128)(2,1)} %copy-done.8, bf16[512,256]{1,0:T(8,128)(2,1)} %copy-done.9, bf16[512,4096]{1,0:T(8,128)(2,1)} %collective-permute-done.22.w_near, bf16[512,4096]{1,0:T(8,128)(2,1)} %collective-permute-done.23.w_far), custom_call_target="tpu_custom_call" | custom-call | flops 2147483648 | bytes 12582912 | tf_op jit(solution)/shard_map/mix_more/pallas_call | solution.py:255
  (76 shorter events, 1.7 us)
Async XLA Ops:
  6.5 9.1 %copy-start.7 = (bf16[64,3,1024]{2,0,1:T(8,128)(2,1)S(1)}, bf16[64,3,1024]{2,0,1:T(8,128)(2,1)}, u32[]{:S(2)}) copy-start(bf16[64,3,1024]{2,0,1:T(8,128)(2,1)} %param.11) | copy-start | bytes 1179652
  6.5 131.3 %all-gather.3.cloned.1.call-start = ((), (), s32[]{:S(2)}) async-start(), calls=%async_computation.2 | async-start | bytes 5406720 | tf_op jit(solution)/shard_map/all_gather | solution.py:526
  6.5 19.8 %collective-permute-start.3 = (bf16[512,4096]{1,0:T(8,128)(2,1)}, bf16[512,4096]{1,0:T(8,128)(2,1)}, u32[]{:S(2)}, u32[]{:S(2)}) collective-permute-start(bf16[512,4096]{1,0:T(8,128)(2,1)} %bitcast.68), channel_id=1, source_target_pairs={{0,2},{2,0},{4,6},{6,4},{8,10},{10,8},{12,14},{14,12},{16,18},{18,... | collective-permute-start | bytes 12582920 | tf_op jit(solution)/shard_map/ppermute | solution.py:35
  11.9 2.9 %collective-permute-start.4 = (bf16[320,128]{1,0:T(8,128)(2,1)S(1)}, bf16[320,128]{1,0:T(8,128)(2,1)S(1)}, u32[]{:S(2)}, u32[]{:S(2)}) collective-permute-start(bf16[320,128]{1,0:T(8,128)(2,1)S(1)} %constant_dynamic-update-slice_fusion), channel_id=1, source_target_pairs={{0,2},{2,0},{4,6},{6,4},{8,10},{10,8},{12,14},{14,12},{16,18},{18,... | collective-permute-start | bytes 245768 | tf_op jit(solution)/shard_map/ppermute | solution.py:35
  15.7 4.2 %collective-permute-start = (bf16[128,512]{1,0:T(8,128)(2,1)S(1)}, bf16[128,512]{1,0:T(8,128)(2,1)S(1)}, u32[]{:S(2)}, u32[]{:S(2)}) collective-permute-start(bf16[128,512]{1,0:T(8,128)(2,1)S(1)} %pad_maximum_fusion.7), channel_id=1, source_target_pairs={{0,2},{2,0},{4,6},{6,4},{8,10},{10,8},{12,14},{14,12},{16,18},{18,... | collective-permute-start | bytes 393224 | tf_op jit(solution)/shard_map/ppermute | solution.py:35
  16.2 7.4 %collective-permute-start.2 = (bf16[128,512]{1,0:T(8,128)(2,1)S(1)}, bf16[128,512]{1,0:T(8,128)(2,1)S(1)}, u32[]{:S(2)}, u32[]{:S(2)}) collective-permute-start(bf16[128,512]{1,0:T(8,128)(2,1)S(1)} %pad_maximum_fusion.7), channel_id=1, source_target_pairs={{0,66},{2,64},{4,70},{6,68},{8,74},{10,72},{12,78},{14,76},{16,82}... | collective-permute-start | bytes 393224 | tf_op jit(solution)/shard_map/ppermute | solution.py:35
  19.9 6.3 %collective-permute-start.1 = (bf16[128,512]{1,0:T(8,128)(2,1)S(1)}, bf16[128,512]{1,0:T(8,128)(2,1)S(1)}, u32[]{:S(2)}, u32[]{:S(2)}) collective-permute-start(bf16[128,512]{1,0:T(8,128)(2,1)S(1)} %pad_maximum_fusion.8), channel_id=1, source_target_pairs={{0,64},{2,66},{4,68},{6,70},{8,72},{10,74},{12,76},{14,78},{16,80}... | collective-permute-start | bytes 393224 | tf_op jit(solution)/shard_map/ppermute | solution.py:35
  26.3 8.8 %collective-permute-start.7 = (bf16[256,512]{1,0:T(8,128)(2,1)S(1)}, bf16[256,512]{1,0:T(8,128)(2,1)S(1)}, u32[]{:S(2)}, u32[]{:S(2)}) collective-permute-start(bf16[256,512]{1,0:T(8,128)(2,1)S(1)} %get-tuple-element.20), channel_id=1, source_target_pairs={{0,4},{2,6},{4,8},{6,10},{8,12},{10,14},{12,0},{14,2},{16,20},{18,... | collective-permute-start | bytes 786440 | tf_op jit(solution)/shard_map/ppermute | solution.py:35
  27.6 15.0 %collective-permute-start.6 = (bf16[256,512]{1,0:T(8,128)(2,1)S(1)}, bf16[256,512]{1,0:T(8,128)(2,1)S(1)}, u32[]{:S(2)}, u32[]{:S(2)}) collective-permute-start(bf16[256,512]{1,0:T(8,128)(2,1)S(1)} %get-tuple-element.20), channel_id=1, source_target_pairs={{0,8},{2,10},{4,12},{6,14},{8,0},{10,2},{12,4},{14,6},{16,24},{18,... | collective-permute-start | bytes 786440 | tf_op jit(solution)/shard_map/ppermute | solution.py:35
  30.1 12.7 %collective-permute-start.5 = (bf16[256,512]{1,0:T(8,128)(2,1)S(1)}, bf16[256,512]{1,0:T(8,128)(2,1)S(1)}, u32[]{:S(2)}, u32[]{:S(2)}) collective-permute-start(bf16[256,512]{1,0:T(8,128)(2,1)S(1)} %get-tuple-element.20), channel_id=1, source_target_pairs={{0,12},{2,14},{4,0},{6,2},{8,4},{10,6},{12,8},{14,10},{16,28},{18,... | collective-permute-start | bytes 786440 | tf_op jit(solution)/shard_map/ppermute | solution.py:35
  31.2 11.7 %collective-permute-start.10 = (bf16[256,512]{1,0:T(8,128)(2,1)S(1)}, bf16[256,512]{1,0:T(8,128)(2,1)S(1)}, u32[]{:S(2)}, u32[]{:S(2)}) collective-permute-start(bf16[256,512]{1,0:T(8,128)(2,1)S(1)} %get-tuple-element.21), channel_id=1, source_target_pairs={{0,16},{2,18},{4,20},{6,22},{8,24},{10,26},{12,28},{14,30},{16,32}... | collective-permute-start | bytes 786440 | tf_op jit(solution)/shard_map/ppermute | solution.py:35
  32.5 14.3 %collective-permute-start.9 = (bf16[256,512]{1,0:T(8,128)(2,1)S(1)}, bf16[256,512]{1,0:T(8,128)(2,1)S(1)}, u32[]{:S(2)}, u32[]{:S(2)}) collective-permute-start(bf16[256,512]{1,0:T(8,128)(2,1)S(1)} %get-tuple-element.21), channel_id=1, source_target_pairs={{0,32},{2,34},{4,36},{6,38},{8,40},{10,42},{12,44},{14,46},{16,48}... | collective-permute-start | bytes 786440 | tf_op jit(solution)/shard_map/ppermute | solution.py:35
  35.1 11.6 %collective-permute-start.8 = (bf16[256,512]{1,0:T(8,128)(2,1)S(1)}, bf16[256,512]{1,0:T(8,128)(2,1)S(1)}, u32[]{:S(2)}, u32[]{:S(2)}) collective-permute-start(bf16[256,512]{1,0:T(8,128)(2,1)S(1)} %get-tuple-element.21), channel_id=1, source_target_pairs={{0,48},{2,50},{4,52},{6,54},{8,56},{10,58},{12,60},{14,62},{16,0},... | collective-permute-start | bytes 786440 | tf_op jit(solution)/shard_map/ppermute | solution.py:35
  42.9 15.1 %copy-start = (bf16[1024,512]{1,0:T(8,128)(2,1)}, bf16[1024,512]{1,0:T(8,128)(2,1)S(1)}, u32[]{:S(2)}) copy-start(bf16[1024,512]{1,0:T(8,128)(2,1)S(1)} %pad_maximum_fusion.refs_0_) | copy-start | bytes 3145732
  46.9 11.3 %copy-start.1 = (bf16[1024,512]{1,0:T(8,128)(2,1)}, bf16[1024,512]{1,0:T(8,128)(2,1)S(1)}, u32[]{:S(2)}) copy-start(bf16[1024,512]{1,0:T(8,128)(2,1)S(1)} %pad_maximum_fusion.1.refs_3_) | copy-start | bytes 3145732
  46.9 12.8 %copy-start.11 = (s32[32]{0:T(128)S(1)}, s32[32]{0:T(128)}, u32[]{:S(2)}) copy-start(s32[32]{0:T(128)} %constant.192.clone) | copy-start | bytes 388
  46.9 12.8 %copy-start.12 = (s32[32]{0:T(128)S(1)}, s32[32]{0:T(128)}, u32[]{:S(2)}) copy-start(s32[32]{0:T(128)} %constant.191.clone) | copy-start | bytes 388
  46.9 12.7 %copy-start.13 = (s32[32]{0:T(128)S(1)}, s32[32]{0:T(128)}, u32[]{:S(2)}) copy-start(s32[32]{0:T(128)} %constant.190.clone) | copy-start | bytes 388
  52.0 77.5 %collective-permute-start.22 = (bf16[512,4096]{1,0:T(8,128)(2,1)}, bf16[512,4096]{1,0:T(8,128)(2,1)}, u32[]{:S(2)}, u32[]{:S(2)}) collective-permute-start(bf16[512,4096]{1,0:T(8,128)(2,1)} %constant_dynamic-slice_fusion), channel_id=1, source_target_pairs={{0,1},{1,0},{2,67},{3,66},{4,5},{5,4},{6,71},{7,70},{8,9},{9,8},{1... | collective-permute-start | bytes 12582920 | tf_op jit(solution)/shard_map/ppermute | solution.py:547
  55.4 34.8 %collective-permute-start.11 = (bf16[1024,512]{1,0:T(8,128)(2,1)S(1)}, bf16[1024,512]{1,0:T(8,128)(2,1)}, u32[]{:S(2)}, u32[]{:S(2)}) collective-permute-start(bf16[1024,512]{1,0:T(8,128)(2,1)S(1)} %pad_maximum_fusion.refs_0_), channel_id=1, source_target_pairs={{0,48},{2,50},{4,52},{6,54},{8,56},{10,58},{12,60},{14,62},{16,0},... | collective-permute-start | bytes 3145736 | tf_op jit(solution)/shard_map/ppermute | solution.py:35
  58.0 36.5 %collective-permute-start.12 = (bf16[1024,512]{1,0:T(8,128)(2,1)S(1)}, bf16[1024,512]{1,0:T(8,128)(2,1)}, u32[]{:S(2)}, u32[]{:S(2)}) collective-permute-start(bf16[1024,512]{1,0:T(8,128)(2,1)S(1)} %pad_maximum_fusion.refs_0_), channel_id=1, source_target_pairs={{0,16},{2,18},{4,20},{6,22},{8,24},{10,26},{12,28},{14,30},{16,32}... | collective-permute-start | bytes 3145736 | tf_op jit(solution)/shard_map/ppermute | solution.py:35
  58.2 37.5 %collective-permute-start.13 = (bf16[1024,512]{1,0:T(8,128)(2,1)S(1)}, bf16[1024,512]{1,0:T(8,128)(2,1)}, u32[]{:S(2)}, u32[]{:S(2)}) collective-permute-start(bf16[1024,512]{1,0:T(8,128)(2,1)S(1)} %pad_maximum_fusion.1.refs_3_), channel_id=1, source_target_pairs={{0,12},{2,14},{4,0},{6,2},{8,4},{10,6},{12,8},{14,10},{16,28},{18,... | collective-permute-start | bytes 3145736 | tf_op jit(solution)/shard_map/ppermute | solution.py:35
  58.2 39.4 %collective-permute-start.14 = (bf16[1024,512]{1,0:T(8,128)(2,1)S(1)}, bf16[1024,512]{1,0:T(8,128)(2,1)}, u32[]{:S(2)}, u32[]{:S(2)}) collective-permute-start(bf16[1024,512]{1,0:T(8,128)(2,1)S(1)} %pad_maximum_fusion.1.refs_3_), channel_id=1, source_target_pairs={{0,4},{2,6},{4,8},{6,10},{8,12},{10,14},{12,0},{14,2},{16,20},{18,... | collective-permute-start | bytes 3145736 | tf_op jit(solution)/shard_map/ppermute | solution.py:35
  91.3 23.6 %collective-permute-start.15 = (bf16[512,512]{1,0:T(8,128)(2,1)S(1)}, bf16[512,512]{1,0:T(8,128)(2,1)S(1)}, u32[]{:S(2)}, u32[]{:S(2)}) collective-permute-start(bf16[512,512]{1,0:T(8,128)(2,1)S(1)} %slice.104), channel_id=1, source_target_pairs={{0,48},{2,50},{4,52},{6,54},{8,56},{10,58},{12,60},{14,62},{16,0},... | collective-permute-start | bytes 1572872 | tf_op jit(solution)/shard_map/ppermute | solution.py:35
  95.6 19.4 %collective-permute-start.16 = (bf16[512,512]{1,0:T(8,128)(2,1)S(1)}, bf16[512,512]{1,0:T(8,128)(2,1)S(1)}, u32[]{:S(2)}, u32[]{:S(2)}) collective-permute-start(bf16[512,512]{1,0:T(8,128)(2,1)S(1)} %slice.105), channel_id=1, source_target_pairs={{0,16},{2,18},{4,20},{6,22},{8,24},{10,26},{12,28},{14,30},{16,32}... | collective-permute-start | bytes 1572872 | tf_op jit(solution)/shard_map/ppermute | solution.py:35
  97.6 17.4 %collective-permute-start.17 = (bf16[512,512]{1,0:T(8,128)(2,1)}, bf16[512,512]{1,0:T(8,128)(2,1)S(1)}, u32[]{:S(2)}, u32[]{:S(2)}) collective-permute-start(bf16[512,512]{1,0:T(8,128)(2,1)} %slice.106), channel_id=1, source_target_pairs={{0,12},{2,14},{4,0},{6,2},{8,4},{10,6},{12,8},{14,10},{16,28},{18,... | collective-permute-start | bytes 1572872 | tf_op jit(solution)/shard_map/ppermute | solution.py:35
  98.7 16.3 %collective-permute-start.18 = (bf16[512,512]{1,0:T(8,128)(2,1)S(1)}, bf16[512,512]{1,0:T(8,128)(2,1)S(1)}, u32[]{:S(2)}, u32[]{:S(2)}) collective-permute-start(bf16[512,512]{1,0:T(8,128)(2,1)S(1)} %slice.107), channel_id=1, source_target_pairs={{0,4},{2,6},{4,8},{6,10},{8,12},{10,14},{12,0},{14,2},{16,20},{18,... | collective-permute-start | bytes 1572872 | tf_op jit(solution)/shard_map/ppermute | solution.py:35
  114.9 0.8 copy-start.3
  115.0 0.9 copy-start.4
  115.0 1.1 copy-start.5
  115.0 1.4 copy-start.6
  124.2 18.7 %all-to-all-start = ((bf16[32,16,1024]{2,1,0:T(8,128)(2,1)}), bf16[32,16,1024]{2,1,0:T(8,128)(2,1)S(1)}, u32[]{:S(2)}, u32[]{:S(2)}) async-start(bf16[32,16,1024]{2,1,0:T(8,128)(2,1)} %bitcast.58), calls=%async_computation | async-start | bytes 2097152 | tf_op jit(solution)/shard_map/all_to_all | solution.py:552
  129.5 72.4 %collective-permute-start.23 = (bf16[512,4096]{1,0:T(8,128)(2,1)}, bf16[512,4096]{1,0:T(8,128)(2,1)}, u32[]{:S(2)}, u32[]{:S(2)}) collective-permute-start(bf16[512,4096]{1,0:T(8,128)(2,1)} %collective-permute-done.22.w_near), channel_id=1, source_target_pairs={{0,2},{2,0},{4,6},{6,4},{8,10},{10,8},{12,14},{14,12},{16,18},{18,... | collective-permute-start | bytes 12582920 | tf_op jit(solution)/shard_map/ppermute | solution.py:35
  143.0 1.0 copy-start.2
  159.9 7.2 %copy-start.10 = (f32[1024]{0:T(1024)S(1)}, f32[1024]{0:T(1024)}, u32[]{:S(2)}) copy-start(f32[1024]{0:T(1024)} %param.13) | copy-start | bytes 12292
  159.9 22.0 %all-to-all-start.1 = ((bf16[32,16,1024]{2,1,0:T(8,128)(2,1)}), bf16[32,16,1024]{2,1,0:T(8,128)(2,1)S(1)}, u32[]{:S(2)}, u32[]{:S(2)}) async-start(bf16[32,16,1024]{2,1,0:T(8,128)(2,1)} %long_conv.1), calls=%async_computation.1 | async-start | bytes 2097152 | tf_op jit(solution)/shard_map/all_to_all | solution.py:560
  184.3 5.7 %collective-permute-start.19 = (bf16[512,256]{1,0:T(8,128)(2,1)S(1)}, bf16[512,256]{1,0:T(8,128)(2,1)S(1)}, u32[]{:S(2)}, u32[]{:S(2)}) collective-permute-start(bf16[512,256]{1,0:T(8,128)(2,1)S(1)} %get-tuple-element.43), channel_id=1, source_target_pairs={{0,2},{2,0},{4,6},{6,4},{8,10},{10,8},{12,14},{14,12},{16,18},{18,... | collective-permute-start | bytes 786440 | tf_op jit(solution)/shard_map/ppermute | solution.py:35
  188.2 10.1 %collective-permute-start.20 = (bf16[512,256]{1,0:T(8,128)(2,1)S(1)}, bf16[512,256]{1,0:T(8,128)(2,1)S(1)}, u32[]{:S(2)}, u32[]{:S(2)}) collective-permute-start(bf16[512,256]{1,0:T(8,128)(2,1)S(1)} %get-tuple-element.42), channel_id=1, source_target_pairs={{0,1},{1,0},{2,3},{3,2},{4,5},{5,4},{6,7},{7,6},{8,9},{9,8},{10,11... | collective-permute-start | bytes 786440 | tf_op jit(solution)/shard_map/ppermute | solution.py:573
  188.2 13.7 %collective-permute-start.21 = (bf16[512,256]{1,0:T(8,128)(2,1)S(1)}, bf16[512,256]{1,0:T(8,128)(2,1)S(1)}, u32[]{:S(2)}, u32[]{:S(2)}) collective-permute-start(bf16[512,256]{1,0:T(8,128)(2,1)S(1)} %get-tuple-element.41), channel_id=1, source_target_pairs={{0,3},{1,2},{2,1},{3,0},{4,7},{5,6},{6,5},{7,4},{8,11},{9,10},{10,... | collective-permute-start | bytes 786440 | tf_op jit(solution)/shard_map/ppermute | solution.py:578
  198.3 3.6 %copy-start.8 = (bf16[512,256]{1,0:T(8,128)(2,1)}, bf16[512,256]{1,0:T(8,128)(2,1)S(1)}, u32[]{:S(2)}) copy-start(bf16[512,256]{1,0:T(8,128)(2,1)S(1)} %collective-permute-done.20.near_h) | copy-start | bytes 786436
  201.9 0.7 copy-start.9
Sparse Core Ops, SparseCore 0:
  15.8 106.0 all-gather.2

commit v5 on v4

--- a/solution.py
+++ b/solution.py
@@ -33,12 +33,6 @@
         z, y, x, c = coords(s)
         perm.append((s, index_of((z + dz) % 2, (y + dy) % 4, (x + dx) % 4, c ^ dc)))
     return lax.ppermute(value, "seq", perm)
-
-
-def split_np(table):
-    upper = table.astype(np.float32).astype(ml_dtypes.bfloat16)
-    lower = (table - upper.astype(np.float64)).astype(np.float32).astype(ml_dtypes.bfloat16)
-    return upper, lower
 
 
 def split_table(table):
@@ -69,38 +63,59 @@
     return jnp.concatenate(blocks, axis=1)
 
 
-def first_kernel(order_ref, mine_ref, other_ref, *refs):
-    weights, (key_ref, value_ref, key_tok_ref, value_tok_ref) = refs[:6], refs[6:]
+def by_column(run, mine_ref, other_ref):
+    step = pl.program_id(0)
+
+    @pl.when(step < 2)
+    def _():
+        run(mine_ref)
+
+    @pl.when(step >= 2)
+    def _():
+        run(other_ref)
+
+
+def first_kernel(order_ref, mine_ref, other_ref, key_line, value_line, *outs):
+    key_ref, value_ref, key_tok_ref, value_tok_ref = outs
 
     def run(tok_ref):
-        for row, total_ref, last_ref in ((0, key_ref, key_tok_ref), (1, value_ref, value_tok_ref)):
-            line, e1, e3 = weights[3 * row : 3 * row + 3]
-            total = jnp.dot(picked(order_ref, row, 0, tok_ref), line[...], preferred_element_type=F32)
+        for row, line, total_ref, last_ref in (
+            (0, key_line, key_ref, key_tok_ref),
+            (1, value_line, value_ref, value_tok_ref),
+        ):
+            total_ref[...] = jnp.dot(
+                picked(order_ref, row, 0, tok_ref), line[...], preferred_element_type=F32
+            )
+            last_ref[...] = picked(order_ref, row, 2, tok_ref)
+
+    by_column(run, mine_ref, other_ref)
+
+
+def second_kernel(order_ref, mine_ref, other_ref, key_in, value_in, k1, k3, v1, v3, key_ref, value_ref):
+    def run(tok_ref):
+        for row, before, e1, e3, total_ref in (
+            (0, key_in, k1, k3, key_ref),
+            (1, value_in, v1, v3, value_ref),
+        ):
+            total = before[...]
             total += jnp.dot(picked(order_ref, row, 1, tok_ref), e1[...], preferred_element_type=F32)
             total += jnp.dot(picked(order_ref, row, 3, tok_ref), e3[...], preferred_element_type=F32)
             total_ref[...] = total
-            last_ref[...] = picked(order_ref, row, 2, tok_ref)
-
-    step = pl.program_id(0)
-
-    @pl.when(step < 2)
-    def _():
-        run(mine_ref)
-
-    @pl.when(step >= 2)
-    def _():
-        run(other_ref)
-
-
-def first_part(order, mine, other, key_pieces, value_pieces):
+
+    by_column(run, mine_ref, other_ref)
+
+
+def sum_part(kernel, name, order, mine, other, totals, weights, last):
     rows, width = mine.shape
-    chan = key_pieces[0].shape[1]
+    chan = weights[0].shape[1]
     tile = rows // 2
-    weights = [key_pieces[0], key_pieces[1], key_pieces[4]]
-    weights += [value_pieces[0], value_pieces[1], value_pieces[4]]
     quarter = width // 4
+    by_row = [pl.BlockSpec((tile, chan), lambda i, o: (i, 0))] * 2
+    tokens_out = [pl.BlockSpec((tile, quarter), lambda i, o: (i, 0))] * 2
+    shapes = [jax.ShapeDtypeStruct((2 * rows, chan), F32)] * 2
+    token_shapes = [jax.ShapeDtypeStruct((2 * rows, quarter), BF16)] * 2
     return pl.pallas_call(
-        first_kernel,
+        kernel,
         grid_spec=pltpu.PrefetchScalarGridSpec(
             num_scalar_prefetch=1,
             grid=(4,),
@@ -108,22 +123,17 @@
                 pl.BlockSpec((tile, width), lambda i, o: (jnp.minimum(i, 1), 0)),
                 pl.BlockSpec((tile, width), lambda i, o: (jnp.maximum(i - 2, 0), 0)),
             ]
-            + [pl.BlockSpec((quarter, chan), lambda i, o: (0, 0))] * 6,
-            out_specs=[
-                pl.BlockSpec((tile, chan), lambda i, o: (i, 0)),
-                pl.BlockSpec((tile, chan), lambda i, o: (i, 0)),
-                pl.BlockSpec((tile, quarter), lambda i, o: (i, 0)),
-                pl.BlockSpec((tile, quarter), lambda i, o: (i, 0)),
-            ],
+            + by_row[: len(totals)]
+            + [pl.BlockSpec((quarter, chan), lambda i, o: (0, 0))] * len(weights),
+            out_specs=by_row + (tokens_out if last else []),
         ),
-        out_shape=[jax.ShapeDtypeStruct((2 * rows, chan), F32)] * 2
-        + [jax.ShapeDtypeStruct((2 * rows, quarter), BF16)] * 2,
+        out_shape=shapes + (token_shapes if last else []),
         compiler_params=pltpu.CompilerParams(vmem_limit_bytes=VMEM),
         cost_estimate=pl.CostEstimate(
-            flops=2 * 2 * 2 * rows * 3 * quarter * chan, bytes_accessed=22 * 2**20, transcendentals=0
+            flops=2 * 2 * rows * quarter * chan * len(weights), bytes_accessed=18 * 2**20, transcendentals=0
         ),
-        name="first_part",
-    )(order, mine, other, *weights)
+        name=name,
+    )(order, mine, other, *totals, *weights)
 
 
 def last_kernel(key_ref, value_ref, key_tok_ref, value_tok_ref, ka, kb, va, vb, out_ref, send_ref):
@@ -141,11 +151,10 @@
     send_ref[...] = source.astype(BF16)
 
 
-def last_part(first, key_pieces, value_pieces):
-    total, chan = first[0].shape
-    quarter = first[2].shape[1]
+def last_part(totals, tokens, weights):
+    total, chan = totals[0].shape
+    quarter = tokens[0].shape[1]
     tile = total // 4
-    weights = [*key_pieces[2:4], *value_pieces[2:4]]
     return pl.pallas_call(
         last_kernel,
         grid=(4,),
@@ -162,38 +171,23 @@
             flops=2 * 2 * total * quarter * chan, bytes_accessed=13 * 2**20, transcendentals=0
         ),
         name="last_part",
-    )(*first, *weights)
+    )(*totals, *tokens, *weights)
 
 
 def gate_kernel(mine_ref, other_ref, weight_ref, out_ref):
-    step = pl.program_id(0)
-    chips, deep, _ = weight_ref.shape
-    depth = deep // 4
+    chips, deep, chan = weight_ref.shape
 
     def run(tok_ref):
-        for k in range(0, 4, 2):
-            parts = [
-                weight_ref[:, i * depth : (i + 1) * depth, :].reshape(chips * depth, 128)
-                for i in (k, k + 1)
-            ]
-            weight = jnp.concatenate(parts, axis=1)
-            gate = jnp.dot(tok_ref[...], weight, preferred_element_type=F32)
-            out_ref[k * 128 : (k + 2) * 128, :] = gate.T.astype(BF16)
-
-    @pl.when(step < 2)
-    def _():
-        run(mine_ref)
-
-    @pl.when(step >= 2)
-    def _():
-        run(other_ref)
+        weight = weight_ref[...].reshape(chips * deep, chan)
+        gate = jnp.dot(tok_ref[...], weight, preferred_element_type=F32)
+        out_ref[...] = gate.T.astype(BF16)
+
+    by_column(run, mine_ref, other_ref)
 
 
 def gate_part(mine, other, gathered):
     rows, width = mine.shape
-    chips = gathered.shape[0]
-    depth = width // chips
-    chan = 4 * 128
+    chips, _, chan = gathered.shape
     tile = rows // 2
     return pl.pallas_call(
         gate_kernel,
@@ -201,7 +195,7 @@
         in_specs=[
             pl.BlockSpec((tile, width), lambda i: (jnp.minimum(i, 1), 0)),
             pl.BlockSpec((tile, width), lambda i: (jnp.maximum(i - 2, 0), 0)),
-            pl.BlockSpec((chips, 4 * depth, 128), lambda i: (0, 0, 0)),
+            pl.BlockSpec((chips, width // chips, chan), lambda i: (0, 0, 0)),
         ],
         out_specs=pl.BlockSpec((chan, tile), lambda i: (0, i)),
         out_shape=jax.ShapeDtypeStruct((chan, 2 * rows), BF16),
@@ -269,11 +263,16 @@
 
 def filter_kernel(z_ref, x_ref, cs_ref, twist_ref, f_ref, m_ref):
     chips, _, lanes = x_ref.shape
-    x = x_ref[...].reshape(2 * chips, 2, 16, lanes)
+    lanes = lanes // 2
     points = 2 * chips * 16
     rows, cols = points // 2, lanes // 2
-    upper = x[:, 0].reshape(points, lanes)
-    lower = x[:, 1].reshape(points, lanes)
+
+    def part(n):
+        rows_of = slice(16 * n, 16 * (n + 1))
+        cores = [x_ref[:, rows_of, c * lanes : (c + 1) * lanes] for c in range(2)]
+        return jnp.stack(cores, axis=1).reshape(points, lanes)
+
+    upper, lower = part(0), part(1)
     whole = (upper.astype(F32) + lower.astype(F32)).T
     i = lax.broadcasted_iota(jnp.int32, (rows, rows), 0)
     j = lax.broadcasted_iota(jnp.int32, (rows, rows), 1)
@@ -320,7 +319,7 @@
             num_scalar_prefetch=1,
             grid=(1,),
             in_specs=[
-                pl.BlockSpec((chips, 64, lanes), lambda i, z: (0, 8 + z[0], 0)),
+                pl.BlockSpec((chips, 32, 2 * lanes), lambda i, z: (0, 4, z[0])),
                 pl.BlockSpec(cs.shape, lambda i, z: (0, 0, 0)),
                 pl.BlockSpec(twist.shape, lambda i, z: (0, 0, 0)),
             ],
@@ -355,8 +354,7 @@
     copies[0].wait()
     for col in range(2):
         x = x_ref[:, :, col * rows : (col + 1) * rows].reshape(chips * chans, rows)
-        r = jnp.dot(x, fwd_ref[0], preferred_element_type=F32)
-        r += jnp.dot(x, fwd_ref[1], preferred_element_type=F32)
+        r = jnp.dot(x, fwd_ref[...], preferred_element_type=F32)
         r = r.reshape(chips, chans, 2 * rows)
         if col == 0:
             copies[1].wait()
@@ -409,8 +407,7 @@
     copies[2].wait()
     for col in range(2):
         q = jnp.concatenate([q_ref[col, k].astype(BF16) for k in range(2 * blocks)], axis=1)
-        y = jnp.dot(q, inv_ref[0], preferred_element_type=F32)
-        y += jnp.dot(q, inv_ref[1], preferred_element_type=F32)
+        y = jnp.dot(q, inv_ref[...], preferred_element_type=F32)
         y_ref[:, :, col * rows : (col + 1) * rows] = y.astype(BF16).reshape(chips, chans, rows)
 
 
@@ -467,15 +464,6 @@
     return jnp.concatenate([block, d1, d2, d3], axis=0)
 
 
-def gather_lines(line, axis):
-    e1 = send(line, **{axis: -1})
-    e3 = send(line, **{axis: 1})
-    half = line.shape[0] // 2
-    e2a = send(e1[:half], **{axis: -1})
-    e2b = send(e3[half:], **{axis: 1})
-    return line, e1, e2a, e2b, e3
-
-
 def per_device(tokens, in_weight, filter_spectrum, skip_bias, out_weight):
     rows, _, width = tokens.shape
     cols = SEQ
@@ -487,21 +475,20 @@
     depth = in_weight.shape[0]
 
     mine = tokens.reshape(rows, width)
-    filt = jnp.transpose(filter_spectrum, (3, 1, 0, 2)).reshape(4, 1, -1, 2 * cols)
-    filt = jnp.concatenate(split_table(filt), axis=1).reshape(4, -1, 2 * cols)
+    filt = jnp.transpose(filter_spectrum, (3, 1, 0, 2)).reshape(4, -1, 2 * cols)
+    filt = jnp.concatenate(split_table(filt), axis=1)
 
     def half_for(c):
         w = lax.dynamic_slice_in_dim(in_weight, c * chan, chan, 2)
         f = lax.dynamic_slice_in_dim(filt, 2 * c, 2, 0)
-        g = jnp.concatenate([w[:, 0, i * 128 : (i + 1) * 128] for i in range(chan // 128)], axis=0)
-        return jnp.concatenate([w[:, 1], w[:, 2]], axis=0), g.reshape(-1, depth, 128), f
-
-    keep, keep_g, keep_f = half_for(core)
-    give, give_g, give_f = half_for(1 - core)
-    near_g = send(jnp.concatenate([give_g.reshape(-1, 128), give_f.reshape(-1, 128)], axis=0), dc=1)
+        return jnp.transpose(w, (1, 0, 2)).reshape(3 * depth, chan), jnp.concatenate([f[0], f[1]], axis=1)
+
+    keep, keep_f = half_for(core)
+    give, give_f = half_for(1 - core)
+    far_near = send(give[depth:], dz=1, dc=1)
+    far = send(keep[depth:], dz=1)
     near = send(give, dc=1)
-    far = send(keep, dz=1)
-    far_near = send(give, dz=1, dc=1)
+    near_f = send(give_f, dc=1)
     other = send(mine, dc=1)
 
     def ordered(own, partner, axis=0):
@@ -509,35 +496,49 @@
             [jnp.where(core == 0, own, partner), jnp.where(core == 0, partner, own)], axis=axis
         )
 
-    key_block = jnp.concatenate(
-        [ordered(keep[:depth], near[:depth]), ordered(far[:depth], far_near[:depth])], axis=0
-    )
-    value_block = jnp.concatenate(
-        [ordered(keep[depth:], near[depth:]), ordered(far[depth:], far_near[depth:])], axis=0
-    )
-    cut = 4 * depth
+    def block_of(n):
+        own, away = slice(n * depth, (n + 1) * depth), slice((n - 1) * depth, n * depth)
+        return jnp.concatenate([ordered(keep[own], near[own]), ordered(far[away], far_near[away])], axis=0)
+
+    key_block, value_block = block_of(1), block_of(2)
+    f_lanes = 2 * cols
     gate_block = jnp.concatenate(
         [
-            ordered(keep_g, near_g[:cut].reshape(keep_g.shape), 1).reshape(-1, 128),
-            ordered(keep_f, near_g[cut:].reshape(keep_f.shape), 1).reshape(-1, 128),
+            ordered(keep[:depth], near[:depth]),
+            jnp.concatenate(
+                [
+                    ordered(keep_f[:, :f_lanes], near_f[:, :f_lanes], 1),
+                    ordered(keep_f[:, f_lanes:], near_f[:, f_lanes:], 1),
+                ],
+                axis=1,
+            ),
         ],
         axis=0,
     )
     gathered = lax.all_gather(gate_block, "seq", axis=0, axis_index_groups=SAME_CORE)
     key_block, value_block, other = lax.optimization_barrier((key_block, value_block, other))
-    key_line, value_line, late = lax.optimization_barrier(
-        (gather_line(key_block, "dx"), gather_line(value_block, "dy"), core)
+    half_ow = out_weight.shape[0] // 2
+    ow_part = lax.dynamic_slice_in_dim(out_weight, core * half_ow, half_ow, 0)
+    key_line, value_line, ow_part = lax.optimization_barrier(
+        (gather_line(key_block, "dx"), gather_line(value_block, "dy"), ow_part)
     )
-    half_ow = out_weight.shape[0] // 2
-    ow_part = lax.dynamic_slice_in_dim(out_weight, late * half_ow, half_ow, 0)
-    key_pieces = gather_lines(key_line, "dy")
-    value_pieces = gather_lines(value_line, "dx")
 
     order = np.arange(32)
     p_, q_, dz = order // 8, (order // 2) % 4, order % 2
     key_order = ((z ^ dz) * 4 + (y + p_) % 4) * 4 + (x + q_) % 4
     value_order = ((z ^ dz) * 4 + (y + q_) % 4) * 4 + (x + p_) % 4
-    first = first_part(jnp.stack([key_order, value_order]), mine, other, key_pieces, value_pieces)
+    order = jnp.stack([key_order, value_order])
+    first = sum_part(first_kernel, "first_part", order, mine, other, [], [key_line, value_line], True)
+    near_lines = [send(key_line, dy=-1), send(key_line, dy=1), send(value_line, dx=-1), send(value_line, dx=1)]
+    near_lines, first = lax.optimization_barrier((near_lines, first))
+    half = key_line.shape[0] // 2
+    last_lines = [
+        send(near_lines[0][:half], dy=-1),
+        send(near_lines[1][half:], dy=1),
+        send(near_lines[2][:half], dx=-1),
+        send(near_lines[3][half:], dx=1),
+    ]
+    totals = sum_part(second_kernel, "second_part", order, mine, other, first[:2], near_lines, False)
 
     perm = []
     for t in range(SEQ):
@@ -547,15 +548,15 @@
     ow_same = lax.ppermute(ow_part, ("seq", "ch"), perm)
     ow_cross = send(ow_same, dc=1)
 
-    source, packed = last_part(first, key_pieces, value_pieces)
+    source, packed = last_part(totals, first[2:], last_lines)
     packed = packed.reshape(CHIPS, chan // CHIPS, 2 * rows)
     mine_ch = lax.all_to_all(packed, "seq", 0, 0, axis_index_groups=SAME_CORE)
 
     tw, a, ai, cs, twist = column_tables(core, rows, cols, padded)
     f, m = filter_part(z, gathered, cs, twist)
     forward, inverse = row_tables(rows, padded)
-    fwd = jnp.asarray(np.stack(split_np(forward)))
-    inv = jnp.asarray(np.stack(split_np(inverse)))
+    fwd = jnp.asarray(forward.astype(np.float32).astype(ml_dtypes.bfloat16))
+    inv = jnp.asarray(inverse.astype(np.float32).astype(ml_dtypes.bfloat16))
     conv = long_conv(mine_ch, fwd, inv, tw, a, ai, m, f)
     conv = lax.all_to_all(conv, "seq", 0, 0, axis_index_groups=SAME_CORE)
     conv = conv.reshape(chan, 2 * rows).astype(F32)

time: 219 us -> 210 us (0.959)
  starting transfers between devices: 53.2 us -> 38.2 us
  waiting for transfers between devices: 57 us -> 62.2 us
  Pallas kernels: 66.3 us -> 71 us
  local copies, waits for them, and re-layouts: 18.9 us -> 15.9 us
    ppermute x21, starting transfers between devices: 35.6 us -> 25.4 us  [send(): return lax.ppermute(value, 'seq', perm)]
    pallas_call x1 -> x2, Pallas kernels: 14.6 us -> 21.9 us  [sum_part(): pl.pallas_call(kernel, grid_spec=pltpu.PrefetchScalarGridSpec(num_scalar_...]
    all_to_all x1, waiting for transfers between devices: 2.58 us -> 9.22 us  [per_device(): mine_ch = lax.all_to_all(packed, 'seq', 0, 0, axis_index_groups=SAME_CORE)]
    unnamed x32 -> x28, local copies, waits for them, and re-layouts: 5.98 us -> 2.57 us
    all_to_all x1, starting transfers between devices: 7.12 us -> 4.46 us  [per_device(): conv = lax.all_to_all(conv, 'seq', 0, 0, axis_index_groups=SAME_CORE)]
    pallas_call x1, Pallas kernels: 15.9 us -> 13.4 us  [long_conv(): pl.pallas_call(conv_kernel, in_specs=[vmem, hbm, hbm, hbm, vmem, vmem, vm...]
    slice x5 -> x6, local copies, waits for them, and re-layouts: 5.12 us -> 5.68 us  [the longest x1 1.88 us: per_device(): near_lines[2][:half]]
    dynamic_slice x2 -> x1, local copies, waits for them, and re-layouts: 5.05 us -> 4.67 us  [per_device(): ow_part = lax.dynamic_slice_in_dim(out_weight, core * half_ow, half_ow, 0)]
  transfers between devices with their start and end apart: 27 -> 27, of which waited for: 10 -> 12; matrix products, arithmetic and copies ran while one was open for 11% -> 10% of each run, Pallas kernels for 27% -> 30%
where the time goes in v5:
time: 210 us; the launch traced here: 209 us
  Pallas kernels  71 us (34%)
  waiting for transfers between devices  62.2 us (30%)
  starting transfers between devices  38.2 us (18%)
  local copies, waits for them, and re-layouts  15.9 us (8%)
  between operations  13.7 us (7%)
  other arithmetic  8.13 us (4%)
    ppermute x21, waiting for transfers between devices, send(): return lax.ppermute(value, 'seq', perm)  43.9 us
    ppermute x21, starting transfers between devices, send(): return lax.ppermute(value, 'seq', perm)  25.4 us
    pallas_call x2, Pallas kernels, sum_part(): pl.pallas_call(kernel, grid_spec=pltpu.PrefetchScalarGridSpec(num_scalar_...  21.9 us
    pallas_call x2, Pallas kernels, mix_part(): pl.pallas_call(mix_kernel if total is None else mix_more_kernel, grid=(4,...  15.4 us
    pallas_call x1, Pallas kernels, long_conv(): pl.pallas_call(conv_kernel, in_specs=[vmem, hbm, hbm, hbm, vmem, vmem, vm...  13.4 us
    pallas_call x1, Pallas kernels, gate_part(): pl.pallas_call(gate_kernel, grid=(4,), in_specs=[pl.BlockSpec((tile, widt...  9.92 us
    all_to_all x1, waiting for transfers between devices, per_device(): mine_ch = lax.all_to_all(packed, 'seq', 0, 0, axis_index_groups=SAME_CORE)  9.22 us
    pallas_call x1, Pallas kernels, last_part(): pl.pallas_call(last_kernel, grid=(4,), in_specs=[pl.BlockSpec((tile, chan...  7.79 us
  transfers between devices with their start and end apart: 27, of which 12 were waited for; matrix products, arithmetic and copies ran while one was open for 10% of the time, Pallas kernels for 30%

profile of v5, /device:TPU:1, one launch (start us, length us, event | category | flops | bytes accessed | tf_op | source)
XLA Modules:
  0.0 209.2 jit_solution(10872390751832310189)
XLA Ops:
  6.5 0.9 copy.11
  7.6 1.5 collective-permute-start.4
  9.1 1.0 dynamic-slice_bitcast_fusion
  10.1 0.1 collective-permute-start
  10.3 0.5 collective-permute-start.3
  10.7 0.9 collective-permute-done
  11.7 0.7 maximum_maximum_fusion
  12.4 3.8 %collective-permute-start.1 = (bf16[128,512]{1,0:T(8,128)(2,1)S(1)}, bf16[128,512]{1,0:T(8,128)(2,1)S(1)}, u32[]{:S(2)}, u32[]{:S(2)}) collective-permute-start(bf16[128,512]{1,0:T(8,128)(2,1)S(1)} %bitcast.65), channel_id=1, source_target_pairs={{0,64},{2,66},{4,68},{6,70},{8,72},{10,74},{12,76},{14,78},{16,80}... | collective-permute-start | bytes 393224 | tf_op jit(solution)/shard_map/ppermute | solution.py:35
  16.2 0.1 collective-permute-start.2
  16.3 3.6 %collective-permute-done.1 = bf16[128,512]{1,0:T(8,128)(2,1)S(1)} collective-permute-done((bf16[128,512]{1,0:T(8,128)(2,1)S(1)}, bf16[128,512]{1,0:T(8,128)(2,1)S(1)}, u32[]{:S(2)}, u32[]{:S(2)}) %collective-permute-start.1) | collective-permute-done | bytes 131104 | tf_op jit(solution)/shard_map/ppermute | solution.py:35
  19.9 3.4 %collective-permute-done.2 = bf16[128,512]{1,0:T(8,128)(2,1)S(1)} collective-permute-done((bf16[128,512]{1,0:T(8,128)(2,1)S(1)}, bf16[128,512]{1,0:T(8,128)(2,1)S(1)}, u32[]{:S(2)}, u32[]{:S(2)}) %collective-permute-start.2) | collective-permute-done | bytes 131104 | tf_op jit(solution)/shard_map/ppermute | solution.py:35
  23.4 1.4 collective-permute-start.10
  24.8 1.5 collective-permute-start.8
  26.3 1.6 collective-permute-start.9
  27.9 2.5 %collective-permute-start.5 = (bf16[256,512]{1,0:T(8,128)(2,1)S(1)}, bf16[256,512]{1,0:T(8,128)(2,1)S(1)}, u32[]{:S(2)}, u32[]{:S(2)}) collective-permute-start(bf16[256,512]{1,0:T(8,128)(2,1)S(1)} %get-tuple-element.30), channel_id=1, source_target_pairs={{0,12},{2,14},{4,0},{6,2},{8,4},{10,6},{12,8},{14,10},{16,28},{18,... | collective-permute-start | bytes 786440 | tf_op jit(solution)/shard_map/ppermute | solution.py:35
  30.4 0.5 collective-permute-start.6
  30.9 2.0 collective-permute-done.10
  32.9 1.3 collective-permute-start.7
  34.2 4.7 %constant_dynamic-slice_fusion.3 = bf16[512,4096]{1,0:T(8,128)(2,1)} fusion(bf16[1024,4096]{1,0:T(8,128)(2,1)} %w_here.1, s32[]{:T(128)S(6)} %select_n.230), kind=kLoop, calls=%fused_computation.104 | loop fusion | bytes 8388612 | tf_op jit(solution)/shard_map/dynamic_slice | solution.py:521
  38.9 1.8 collective-permute-done.9
  40.8 5.8 %collective-permute-done.7 = bf16[256,512]{1,0:T(8,128)(2,1)S(1)} collective-permute-done((bf16[256,512]{1,0:T(8,128)(2,1)S(1)}, bf16[256,512]{1,0:T(8,128)(2,1)S(1)}, u32[]{:S(2)}, u32[]{:S(2)}) %collective-permute-start.7) | collective-permute-done | bytes 262176 | tf_op jit(solution)/shard_map/ppermute | solution.py:35
  46.7 2.7 %collective-permute-start.22 = (bf16[512,4096]{1,0:T(8,128)(2,1)}, bf16[512,4096]{1,0:T(8,128)(2,1)}, u32[]{:S(2)}, u32[]{:S(2)}) collective-permute-start(bf16[512,4096]{1,0:T(8,128)(2,1)} %constant_dynamic-slice_fusion.3), channel_id=1, source_target_pairs={{0,1},{1,0},{2,67},{3,66},{4,5},{5,4},{6,71},{7,70},{8,9},{9,8},{1... | collective-permute-start | bytes 12582920 | tf_op jit(solution)/shard_map/ppermute | solution.py:548
  49.4 0.5 collective-permute-start.11
  49.9 1.0 collective-permute-start.12
  50.8 1.5 collective-permute-start.14
  52.4 0.6 pad_add_fusion.order_ref
  52.9 10.3 %first_part.1 = (f32[1024,512]{1,0:T(8,128)}, f32[1024,512]{1,0:T(8,128)}, bf16[1024,1024]{1,0:T(8,128)(2,1)}, bf16[1024,1024]{1,0:T(8,128)(2,1)}) custom-call(s32[2,32]{1,0:T(2,128)} %pad_add_fusion.order_ref, bf16[512,4096]{1,0:T(8,128)(2,1)} %bitcast.57, bf16[512,4096]{1,0:T(8,128)(2,1)} %collective-permute-done.3.other_ref, bf16[1024,512]{1,0:T(8,128)(2,1)} %copy-done.1, ...), custom_call_target="tpu_custom_call" | custom-call | flops 2147483648 | bytes 18874368 | tf_op jit(solution)/shard_map/first_part/pallas_call | solution.py:117
  63.2 21.5 %collective-permute-done.11.k1 = bf16[1024,512]{1,0:T(8,128)(2,1)S(1)} collective-permute-done((bf16[1024,512]{1,0:T(8,128)(2,1)S(1)}, bf16[1024,512]{1,0:T(8,128)(2,1)S(1)}, u32[]{:S(2)}, u32[]{:S(2)}) %collective-permute-start.11) | collective-permute-done | bytes 1048608 | tf_op jit(solution)/shard_map/ppermute | solution.py:35
  84.7 1.4 collective-permute-done.12.k3
  86.3 1.9 slice.105
  88.1 1.4 collective-permute-start.16
  89.6 1.9 slice.106
  91.5 1.9 slice.107
  93.3 1.5 collective-permute-start.18
  94.8 0.2 fusion.38
  95.1 11.7 %second_part.1 = (f32[1024,512]{1,0:T(8,128)}, f32[1024,512]{1,0:T(8,128)}) custom-call(s32[2,32]{1,0:T(2,128)} %pad_add_fusion.order_ref, bf16[512,4096]{1,0:T(8,128)(2,1)} %bitcast.58, bf16[512,4096]{1,0:T(8,128)(2,1)} %collective-permute-done.3.other_ref, f32[1024,512]{1,0:T(8,128)} %get-tuple-element.38.key_in, f32[1024,512]{1,0:T(8,128)} %get-tuple-element.39.value_in, ...), custom_call_target="tpu_custom_call" | custom-call | flops 4294967296 | bytes 18874368 | tf_op jit(solution)/shard_map/second_part/pallas_call | solution.py:117
  106.8 3.4 %collective-permute-done.18.vb = bf16[512,512]{1,0:T(8,128)(2,1)S(1)} collective-permute-done((bf16[512,512]{1,0:T(8,128)(2,1)}, bf16[512,512]{1,0:T(8,128)(2,1)S(1)}, u32[]{:S(2)}, u32[]{:S(2)}) %collective-permute-start.18) | collective-permute-done | bytes 524320 | tf_op jit(solution)/shard_map/ppermute | solution.py:35
  110.2 0.8 copy-done.7
  111.1 7.8 %last_part.1 = (f32[512,1024]{1,0:T(8,128)}, bf16[512,1024]{1,0:T(8,128)(2,1)}) custom-call(f32[1024,512]{1,0:T(8,128)} %get-tuple-element.44.key_ref, f32[1024,512]{1,0:T(8,128)} %get-tuple-element.45.value_ref, bf16[1024,1024]{1,0:T(8,128)(2,1)} %get-tuple-element.46.key_tok_ref, bf16[1024,1024]{1,0:T(8,128)(2,1)} %get-tuple-element.47.value_tok_ref, ...), custom_call_target="tpu_custom_call" | custom-call | flops 2147483648 | bytes 13631488 | tf_op jit(solution)/shard_map/last_part/pallas_call | solution.py:158
  118.9 3.9 %all-to-all-start = ((bf16[32,16,1024]{2,1,0:T(8,128)(2,1)}), bf16[32,16,1024]{2,1,0:T(8,128)(2,1)S(1)}, u32[]{:S(2)}, u32[]{:S(2)}) async-start(bf16[32,16,1024]{2,1,0:T(8,128)(2,1)} %bitcast.62), calls=%async_computation | async-start | bytes 2097152 | tf_op jit(solution)/shard_map/all_to_all | solution.py:553
  122.8 1.2 collective-permute-start.23
  124.1 0.8 copy.12.a_ref
  124.9 0.7 fusion.9.ai_ref
  125.6 0.3 fusion.35
  125.9 0.7 pad_maximum_fusion.6
  126.5 0.6 fusion.15
  127.1 0.7 pad_maximum_fusion.5.tw_hbm
  127.8 2.5 %filter_part.1 = (f32[64,1024]{1,0:T(8,128)}, bf16[256,256]{1,0:T(8,128)(2,1)}) custom-call(s32[1]{0:T(128)} %bitcast.19.z_ref, bf16[32,160,512]{2,1,0:T(8,128)(2,1)} %bitcast.60, f32[2,64,64]{2,1,0:T(8,128)} %get-tuple-element.93.cs_ref, f32[2,64,64]{2,1,0:T(8,128)} %get-tuple-element.94.twist_ref), custom_call_target="tpu_custom_call" | custom-call | flops 1000000000 | bytes 1048576 | tf_op jit(solution)/shard_map/filter_part/pallas_call | solution.py:316
  130.4 9.2 %all-to-all-done.x_ref = bf16[32,16,1024]{2,1,0:T(8,128)(2,1)S(1)} async-done(((bf16[32,16,1024]{2,1,0:T(8,128)(2,1)}), bf16[32,16,1024]{2,1,0:T(8,128)(2,1)S(1)}, u32[]{:S(2)}, u32[]{:S(2)}) %all-to-all-start) | async-done | bytes 1048608 | tf_op jit(solution)/shard_map/all_to_all | solution.py:553
  139.6 1.0 copy-done.3
  140.6 13.4 %long_conv.1 = bf16[32,16,1024]{2,1,0:T(8,128)(2,1)} custom-call(bf16[32,16,1024]{2,1,0:T(8,128)(2,1)} %copy-done.3, bf16[512,1024]{1,0:T(8,128)(2,1)} %constant.193.clone.fwd_hbm, bf16[1024,512]{1,0:T(8,128)(2,1)} %constant.194.clone.inv_hbm, f32[64,1024]{1,0:T(8,128)} %pad_maximum_fusion.5.tw_hbm, bf16[256,256]{1,0:T(8,128)(2,1)} %copy.12.a_ref, ...), custom_call_target="tpu_custom_call" | custom-call | flops 8000000000 | bytes 8388608 | tf_op jit(solution)/shard_map/long_conv/pallas_call | solution.py:418
  154.0 4.5 %all-to-all-start.1 = ((bf16[32,16,1024]{2,1,0:T(8,128)(2,1)}), bf16[32,16,1024]{2,1,0:T(8,128)(2,1)S(1)}, u32[]{:S(2)}, u32[]{:S(2)}) async-start(bf16[32,16,1024]{2,1,0:T(8,128)(2,1)} %long_conv.1), calls=%async_computation.1 | async-start | bytes 2097152 | tf_op jit(solution)/shard_map/all_to_all | solution.py:561
  158.6 9.9 %gate_part.1 = bf16[512,1024]{1,0:T(8,128)(2,1)} custom-call(bf16[512,4096]{1,0:T(8,128)(2,1)} %bitcast.59, bf16[512,4096]{1,0:T(8,128)(2,1)} %collective-permute-done.3.other_ref, bf16[32,160,512]{2,1,0:T(8,128)(2,1)} %bitcast.61), custom_call_target="tpu_custom_call" | custom-call | flops 4294967296 | bytes 13631488 | tf_op jit(solution)/shard_map/gate_part/pallas_call | solution.py:192
  168.5 5.5 %all-to-all-done.1 = bf16[32,16,1024]{2,1,0:T(8,128)(2,1)S(1)} async-done(((bf16[32,16,1024]{2,1,0:T(8,128)(2,1)}), bf16[32,16,1024]{2,1,0:T(8,128)(2,1)S(1)}, u32[]{:S(2)}, u32[]{:S(2)}) %all-to-all-start.1) | async-done | bytes 1048608 | tf_op jit(solution)/shard_map/all_to_all | solution.py:561
  173.9 2.3 %fusion.1 = bf16[512,1024]{1,0:T(8,128)(2,1)S(1)} fusion(f32[512,1024]{1,0:T(8,128)} %get-tuple-element.51, bf16[512,1024]{1,0:T(8,128)(2,1)} %gate_part.1, bf16[32,16,1024]{2,1,0:T(8,128)(2,1)S(1)} %all-to-all-done.1, f32[512]{0:T(512)S(1)} %dynamic_slice.35), kind=kLoop, calls=%fused_computation.2 | loop fusion | flops 3145728 | bytes 5244928 | tf_op jit(solution)/shard_map/convert_element_type | solution.py:566
  176.2 0.1 constant_dynamic-slice_fusion
  176.4 3.5 %collective-permute-start.19 = (bf16[512,256]{1,0:T(8,128)(2,1)S(1)}, bf16[512,256]{1,0:T(8,128)(2,1)S(1)}, u32[]{:S(2)}, u32[]{:S(2)}) collective-permute-start(bf16[512,256]{1,0:T(8,128)(2,1)S(1)} %get-tuple-element.59), channel_id=1, source_target_pairs={{0,2},{2,0},{4,6},{6,4},{8,10},{10,8},{12,14},{14,12},{16,18},{18,... | collective-permute-start | bytes 786440 | tf_op jit(solution)/shard_map/ppermute | solution.py:35
  179.9 1.7 collective-permute-start.21
  181.6 0.1 broadcast_select_fusion.1
  181.8 0.8 pad_maximum_fusion.2.here
  182.6 7.4 %mix_part.1.total_ref = f32[256,4096]{1,0:T(8,128)} custom-call(bf16[1024,256]{1,0:T(8,128)(2,1)} %pad_maximum_fusion.2.here, bf16[1024,4096]{1,0:T(8,128)(2,1)} %w_here.1), custom_call_target="tpu_custom_call" | custom-call | flops 2147483648 | bytes 12582912 | tf_op jit(solution)/shard_map/mix_part/pallas_call | solution.py:249
  190.0 3.6 %collective-permute-done.21.far_h = bf16[512,256]{1,0:T(8,128)(2,1)S(1)} collective-permute-done((bf16[512,256]{1,0:T(8,128)(2,1)S(1)}, bf16[512,256]{1,0:T(8,128)(2,1)S(1)}, u32[]{:S(2)}, u32[]{:S(2)}) %collective-permute-start.21) | collective-permute-done | bytes 262176 | tf_op jit(solution)/shard_map/ppermute | solution.py:579
  193.6 0.7 copy-done.9
  194.3 8.0 %mix_more.1 = bf16[256,4096]{1,0:T(8,128)(2,1)} custom-call(f32[256,4096]{1,0:T(8,128)} %mix_part.1.total_ref, bf16[512,256]{1,0:T(8,128)(2,1)} %copy-done.8, bf16[512,256]{1,0:T(8,128)(2,1)} %copy-done.9, bf16[512,4096]{1,0:T(8,128)(2,1)} %collective-permute-done.22.w_near, bf16[512,4096]{1,0:T(8,128)(2,1)} %collective-permute-done.23.w_far), custom_call_target="tpu_custom_call" | custom-call | flops 2147483648 | bytes 12582912 | tf_op jit(solution)/shard_map/mix_more/pallas_call | solution.py:249
  (66 shorter events, 0.9 us)
Async XLA Ops:
  6.5 121.3 %all-gather.3.cloned.1.call-start = ((), (), s32[]{:S(2)}) async-start(), calls=%async_computation.2 | async-start | bytes 5406720 | tf_op jit(solution)/shard_map/all_gather | solution.py:518
  7.6 3.1 %collective-permute-start.4 = (bf16[32,256]{1,0:T(8,128)(2,1)S(1)}, bf16[32,256]{1,0:T(8,128)(2,1)S(1)}, u32[]{:S(2)}, u32[]{:S(2)}) collective-permute-start(bf16[32,256]{1,0:T(8,128)(2,1)S(1)} %pad_maximum_fusion.8), channel_id=1, source_target_pairs={{0,2},{2,0},{4,6},{6,4},{8,10},{10,8},{12,14},{14,12},{16,18},{18,... | collective-permute-start | bytes 49160 | tf_op jit(solution)/shard_map/ppermute | solution.py:35
  10.1 1.5 collective-permute-start
  10.3 13.2 %collective-permute-start.3 = (bf16[512,4096]{1,0:T(8,128)(2,1)}, bf16[512,4096]{1,0:T(8,128)(2,1)}, u32[]{:S(2)}, u32[]{:S(2)}) collective-permute-start(bf16[512,4096]{1,0:T(8,128)(2,1)} %bitcast.56), channel_id=1, source_target_pairs={{0,2},{2,0},{4,6},{6,4},{8,10},{10,8},{12,14},{14,12},{16,18},{18,... | collective-permute-start | bytes 12582920 | tf_op jit(solution)/shard_map/ppermute | solution.py:35
  12.4 7.5 %collective-permute-start.1 = (bf16[128,512]{1,0:T(8,128)(2,1)S(1)}, bf16[128,512]{1,0:T(8,128)(2,1)S(1)}, u32[]{:S(2)}, u32[]{:S(2)}) collective-permute-start(bf16[128,512]{1,0:T(8,128)(2,1)S(1)} %bitcast.65), channel_id=1, source_target_pairs={{0,64},{2,66},{4,68},{6,70},{8,72},{10,74},{12,76},{14,78},{16,80}... | collective-permute-start | bytes 393224 | tf_op jit(solution)/shard_map/ppermute | solution.py:35
  16.2 7.2 %collective-permute-start.2 = (bf16[128,512]{1,0:T(8,128)(2,1)S(1)}, bf16[128,512]{1,0:T(8,128)(2,1)S(1)}, u32[]{:S(2)}, u32[]{:S(2)}) collective-permute-start(bf16[128,512]{1,0:T(8,128)(2,1)S(1)} %bitcast.66), channel_id=1, source_target_pairs={{0,66},{2,64},{4,70},{6,68},{8,74},{10,72},{12,78},{14,76},{16,82}... | collective-permute-start | bytes 393224 | tf_op jit(solution)/shard_map/ppermute | solution.py:35
  23.4 9.5 %collective-permute-start.10 = (bf16[256,512]{1,0:T(8,128)(2,1)S(1)}, bf16[256,512]{1,0:T(8,128)(2,1)S(1)}, u32[]{:S(2)}, u32[]{:S(2)}) collective-permute-start(bf16[256,512]{1,0:T(8,128)(2,1)S(1)} %get-tuple-element.31), channel_id=1, source_target_pairs={{0,16},{2,18},{4,20},{6,22},{8,24},{10,26},{12,28},{14,30},{16,32}... | collective-permute-start | bytes 786440 | tf_op jit(solution)/shard_map/ppermute | solution.py:35
  24.8 14.1 %collective-permute-start.8 = (bf16[256,512]{1,0:T(8,128)(2,1)S(1)}, bf16[256,512]{1,0:T(8,128)(2,1)S(1)}, u32[]{:S(2)}, u32[]{:S(2)}) collective-permute-start(bf16[256,512]{1,0:T(8,128)(2,1)S(1)} %get-tuple-element.31), channel_id=1, source_target_pairs={{0,48},{2,50},{4,52},{6,54},{8,56},{10,58},{12,60},{14,62},{16,0},... | collective-permute-start | bytes 786440 | tf_op jit(solution)/shard_map/ppermute | solution.py:35
  26.3 14.4 %collective-permute-start.9 = (bf16[256,512]{1,0:T(8,128)(2,1)S(1)}, bf16[256,512]{1,0:T(8,128)(2,1)S(1)}, u32[]{:S(2)}, u32[]{:S(2)}) collective-permute-start(bf16[256,512]{1,0:T(8,128)(2,1)S(1)} %get-tuple-element.31), channel_id=1, source_target_pairs={{0,32},{2,34},{4,36},{6,38},{8,40},{10,42},{12,44},{14,46},{16,48}... | collective-permute-start | bytes 786440 | tf_op jit(solution)/shard_map/ppermute | solution.py:35
  27.9 12.9 %collective-permute-start.5 = (bf16[256,512]{1,0:T(8,128)(2,1)S(1)}, bf16[256,512]{1,0:T(8,128)(2,1)S(1)}, u32[]{:S(2)}, u32[]{:S(2)}) collective-permute-start(bf16[256,512]{1,0:T(8,128)(2,1)S(1)} %get-tuple-element.30), channel_id=1, source_target_pairs={{0,12},{2,14},{4,0},{6,2},{8,4},{10,6},{12,8},{14,10},{16,28},{18,... | collective-permute-start | bytes 786440 | tf_op jit(solution)/shard_map/ppermute | solution.py:35
  30.4 10.4 %collective-permute-start.6 = (bf16[256,512]{1,0:T(8,128)(2,1)S(1)}, bf16[256,512]{1,0:T(8,128)(2,1)S(1)}, u32[]{:S(2)}, u32[]{:S(2)}) collective-permute-start(bf16[256,512]{1,0:T(8,128)(2,1)S(1)} %get-tuple-element.30), channel_id=1, source_target_pairs={{0,8},{2,10},{4,12},{6,14},{8,0},{10,2},{12,4},{14,6},{16,24},{18,... | collective-permute-start | bytes 786440 | tf_op jit(solution)/shard_map/ppermute | solution.py:35
  32.9 13.7 %collective-permute-start.7 = (bf16[256,512]{1,0:T(8,128)(2,1)S(1)}, bf16[256,512]{1,0:T(8,128)(2,1)S(1)}, u32[]{:S(2)}, u32[]{:S(2)}) collective-permute-start(bf16[256,512]{1,0:T(8,128)(2,1)S(1)} %get-tuple-element.30), channel_id=1, source_target_pairs={{0,4},{2,6},{4,8},{6,10},{8,12},{10,14},{12,0},{14,2},{16,20},{18,... | collective-permute-start | bytes 786440 | tf_op jit(solution)/shard_map/ppermute | solution.py:35
  38.9 13.4 %copy-start.11 = (s32[32]{0:T(128)S(1)}, s32[32]{0:T(128)}, u32[]{:S(2)}) copy-start(s32[32]{0:T(128)} %constant.190.clone) | copy-start | bytes 388
  38.9 13.4 %copy-start.12 = (s32[32]{0:T(128)S(1)}, s32[32]{0:T(128)}, u32[]{:S(2)}) copy-start(s32[32]{0:T(128)} %constant.191.clone) | copy-start | bytes 388
  38.9 13.4 %copy-start.13 = (s32[32]{0:T(128)S(1)}, s32[32]{0:T(128)}, u32[]{:S(2)}) copy-start(s32[32]{0:T(128)} %constant.192.clone) | copy-start | bytes 388
  40.8 12.2 %copy-start = (bf16[1024,512]{1,0:T(8,128)(2,1)}, bf16[1024,512]{1,0:T(8,128)(2,1)S(1)}, u32[]{:S(2)}) copy-start(bf16[1024,512]{1,0:T(8,128)(2,1)S(1)} %pad_maximum_fusion.1.value_line) | copy-start | bytes 3145732
  46.7 6.2 %copy-start.1 = (bf16[1024,512]{1,0:T(8,128)(2,1)}, bf16[1024,512]{1,0:T(8,128)(2,1)S(1)}, u32[]{:S(2)}) copy-start(bf16[1024,512]{1,0:T(8,128)(2,1)S(1)} %pad_maximum_fusion.key_line) | copy-start | bytes 3145732
  46.7 76.1 %collective-permute-start.22 = (bf16[512,4096]{1,0:T(8,128)(2,1)}, bf16[512,4096]{1,0:T(8,128)(2,1)}, u32[]{:S(2)}, u32[]{:S(2)}) collective-permute-start(bf16[512,4096]{1,0:T(8,128)(2,1)} %constant_dynamic-slice_fusion.3), channel_id=1, source_target_pairs={{0,1},{1,0},{2,67},{3,66},{4,5},{5,4},{6,71},{7,70},{8,9},{9,8},{1... | collective-permute-start | bytes 12582920 | tf_op jit(solution)/shard_map/ppermute | solution.py:548
  49.4 35.3 %collective-permute-start.11 = (bf16[1024,512]{1,0:T(8,128)(2,1)S(1)}, bf16[1024,512]{1,0:T(8,128)(2,1)S(1)}, u32[]{:S(2)}, u32[]{:S(2)}) collective-permute-start(bf16[1024,512]{1,0:T(8,128)(2,1)S(1)} %pad_maximum_fusion.key_line), channel_id=1, source_target_pairs={{0,48},{2,50},{4,52},{6,54},{8,56},{10,58},{12,60},{14,62},{16,0},... | collective-permute-start | bytes 3145736 | tf_op jit(solution)/shard_map/ppermute | solution.py:35
  49.9 36.3 %collective-permute-start.12 = (bf16[1024,512]{1,0:T(8,128)(2,1)S(1)}, bf16[1024,512]{1,0:T(8,128)(2,1)}, u32[]{:S(2)}, u32[]{:S(2)}) collective-permute-start(bf16[1024,512]{1,0:T(8,128)(2,1)S(1)} %pad_maximum_fusion.key_line), channel_id=1, source_target_pairs={{0,16},{2,18},{4,20},{6,22},{8,24},{10,26},{12,28},{14,30},{16,32}... | collective-permute-start | bytes 3145736 | tf_op jit(solution)/shard_map/ppermute | solution.py:35
  50.8 35.3 %collective-permute-start.13 = (bf16[1024,512]{1,0:T(8,128)(2,1)S(1)}, bf16[1024,512]{1,0:T(8,128)(2,1)}, u32[]{:S(2)}, u32[]{:S(2)}) collective-permute-start(bf16[1024,512]{1,0:T(8,128)(2,1)S(1)} %pad_maximum_fusion.1.value_line), channel_id=1, source_target_pairs={{0,12},{2,14},{4,0},{6,2},{8,4},{10,6},{12,8},{14,10},{16,28},{18,... | collective-permute-start | bytes 3145736 | tf_op jit(solution)/shard_map/ppermute | solution.py:35
  50.8 35.3 %collective-permute-start.14 = (bf16[1024,512]{1,0:T(8,128)(2,1)S(1)}, bf16[1024,512]{1,0:T(8,128)(2,1)}, u32[]{:S(2)}, u32[]{:S(2)}) collective-permute-start(bf16[1024,512]{1,0:T(8,128)(2,1)S(1)} %pad_maximum_fusion.1.value_line), channel_id=1, source_target_pairs={{0,4},{2,6},{4,8},{6,10},{8,12},{10,14},{12,0},{14,2},{16,20},{18,... | collective-permute-start | bytes 3145736 | tf_op jit(solution)/shard_map/ppermute | solution.py:35
  84.7 8.6 %copy-start.2 = (bf16[1024,512]{1,0:T(8,128)(2,1)}, bf16[1024,512]{1,0:T(8,128)(2,1)S(1)}, u32[]{:S(2)}) copy-start(bf16[1024,512]{1,0:T(8,128)(2,1)S(1)} %collective-permute-done.11.k1) | copy-start | bytes 3145732
  86.2 20.6 %collective-permute-start.15 = (bf16[512,512]{1,0:T(8,128)(2,1)S(1)}, bf16[512,512]{1,0:T(8,128)(2,1)S(1)}, u32[]{:S(2)}, u32[]{:S(2)}) collective-permute-start(bf16[512,512]{1,0:T(8,128)(2,1)S(1)} %slice.104), channel_id=1, source_target_pairs={{0,48},{2,50},{4,52},{6,54},{8,56},{10,58},{12,60},{14,62},{16,0},... | collective-permute-start | bytes 1572872 | tf_op jit(solution)/shard_map/ppermute | solution.py:35
  88.1 18.7 %collective-permute-start.16 = (bf16[512,512]{1,0:T(8,128)(2,1)}, bf16[512,512]{1,0:T(8,128)(2,1)S(1)}, u32[]{:S(2)}, u32[]{:S(2)}) collective-permute-start(bf16[512,512]{1,0:T(8,128)(2,1)} %slice.105), channel_id=1, source_target_pairs={{0,16},{2,18},{4,20},{6,22},{8,24},{10,26},{12,28},{14,30},{16,32}... | collective-permute-start | bytes 1572872 | tf_op jit(solution)/shard_map/ppermute | solution.py:35
  91.4 15.4 %collective-permute-start.17 = (bf16[512,512]{1,0:T(8,128)(2,1)}, bf16[512,512]{1,0:T(8,128)(2,1)S(1)}, u32[]{:S(2)}, u32[]{:S(2)}) collective-permute-start(bf16[512,512]{1,0:T(8,128)(2,1)} %slice.106), channel_id=1, source_target_pairs={{0,12},{2,14},{4,0},{6,2},{8,4},{10,6},{12,8},{14,10},{16,28},{18,... | collective-permute-start | bytes 1572872 | tf_op jit(solution)/shard_map/ppermute | solution.py:35
  93.3 16.9 %collective-permute-start.18 = (bf16[512,512]{1,0:T(8,128)(2,1)}, bf16[512,512]{1,0:T(8,128)(2,1)S(1)}, u32[]{:S(2)}, u32[]{:S(2)}) collective-permute-start(bf16[512,512]{1,0:T(8,128)(2,1)} %slice.107), channel_id=1, source_target_pairs={{0,4},{2,6},{4,8},{6,10},{8,12},{10,14},{12,0},{14,2},{16,20},{18,... | collective-permute-start | bytes 1572872 | tf_op jit(solution)/shard_map/ppermute | solution.py:35
  106.8 3.4 %copy-start.4 = (bf16[512,512]{1,0:T(8,128)(2,1)}, bf16[512,512]{1,0:T(8,128)(2,1)S(1)}, u32[]{:S(2)}) copy-start(bf16[512,512]{1,0:T(8,128)(2,1)S(1)} %collective-permute-done.15.ka) | copy-start | bytes 1572868
  106.8 3.4 %copy-start.5 = (bf16[512,512]{1,0:T(8,128)(2,1)}, bf16[512,512]{1,0:T(8,128)(2,1)S(1)}, u32[]{:S(2)}) copy-start(bf16[512,512]{1,0:T(8,128)(2,1)S(1)} %collective-permute-done.16.kb) | copy-start | bytes 1572868
  106.8 3.4 %copy-start.6 = (bf16[512,512]{1,0:T(8,128)(2,1)}, bf16[512,512]{1,0:T(8,128)(2,1)S(1)}, u32[]{:S(2)}) copy-start(bf16[512,512]{1,0:T(8,128)(2,1)S(1)} %collective-permute-done.17.va) | copy-start | bytes 1572868
  110.2 0.8 copy-start.7
  118.9 20.7 %all-to-all-start = ((bf16[32,16,1024]{2,1,0:T(8,128)(2,1)}), bf16[32,16,1024]{2,1,0:T(8,128)(2,1)S(1)}, u32[]{:S(2)}, u32[]{:S(2)}) async-start(bf16[32,16,1024]{2,1,0:T(8,128)(2,1)} %bitcast.62), calls=%async_computation | async-start | bytes 2097152 | tf_op jit(solution)/shard_map/all_to_all | solution.py:553
  122.8 70.8 %collective-permute-start.23 = (bf16[512,4096]{1,0:T(8,128)(2,1)}, bf16[512,4096]{1,0:T(8,128)(2,1)}, u32[]{:S(2)}, u32[]{:S(2)}) collective-permute-start(bf16[512,4096]{1,0:T(8,128)(2,1)} %collective-permute-done.22.w_near), channel_id=1, source_target_pairs={{0,2},{2,0},{4,6},{6,4},{8,10},{10,8},{12,14},{14,12},{16,18},{18,... | collective-permute-start | bytes 12582920 | tf_op jit(solution)/shard_map/ppermute | solution.py:35
  139.6 1.0 copy-start.3
  154.0 4.5 %copy-start.10 = (f32[1024]{0:T(1024)S(1)}, f32[1024]{0:T(1024)}, u32[]{:S(2)}) copy-start(f32[1024]{0:T(1024)} %param.13) | copy-start | bytes 12292
  154.0 19.9 %all-to-all-start.1 = ((bf16[32,16,1024]{2,1,0:T(8,128)(2,1)}), bf16[32,16,1024]{2,1,0:T(8,128)(2,1)S(1)}, u32[]{:S(2)}, u32[]{:S(2)}) async-start(bf16[32,16,1024]{2,1,0:T(8,128)(2,1)} %long_conv.1), calls=%async_computation.1 | async-start | bytes 2097152 | tf_op jit(solution)/shard_map/all_to_all | solution.py:561
  176.4 5.3 %collective-permute-start.19 = (bf16[512,256]{1,0:T(8,128)(2,1)S(1)}, bf16[512,256]{1,0:T(8,128)(2,1)S(1)}, u32[]{:S(2)}, u32[]{:S(2)}) collective-permute-start(bf16[512,256]{1,0:T(8,128)(2,1)S(1)} %get-tuple-element.59), channel_id=1, source_target_pairs={{0,2},{2,0},{4,6},{6,4},{8,10},{10,8},{12,14},{14,12},{16,18},{18,... | collective-permute-start | bytes 786440 | tf_op jit(solution)/shard_map/ppermute | solution.py:35
  179.9 10.1 %collective-permute-start.20 = (bf16[512,256]{1,0:T(8,128)(2,1)S(1)}, bf16[512,256]{1,0:T(8,128)(2,1)S(1)}, u32[]{:S(2)}, u32[]{:S(2)}) collective-permute-start(bf16[512,256]{1,0:T(8,128)(2,1)S(1)} %get-tuple-element.58), channel_id=1, source_target_pairs={{0,1},{1,0},{2,3},{3,2},{4,5},{5,4},{6,7},{7,6},{8,9},{9,8},{10,11... | collective-permute-start | bytes 786440 | tf_op jit(solution)/shard_map/ppermute | solution.py:574
  179.9 13.7 %collective-permute-start.21 = (bf16[512,256]{1,0:T(8,128)(2,1)S(1)}, bf16[512,256]{1,0:T(8,128)(2,1)S(1)}, u32[]{:S(2)}, u32[]{:S(2)}) collective-permute-start(bf16[512,256]{1,0:T(8,128)(2,1)S(1)} %get-tuple-element.57), channel_id=1, source_target_pairs={{0,3},{1,2},{2,1},{3,0},{4,7},{5,6},{6,5},{7,4},{8,11},{9,10},{10,... | collective-permute-start | bytes 786440 | tf_op jit(solution)/shard_map/ppermute | solution.py:579
  190.0 3.6 %copy-start.8 = (bf16[512,256]{1,0:T(8,128)(2,1)}, bf16[512,256]{1,0:T(8,128)(2,1)S(1)}, u32[]{:S(2)}) copy-start(bf16[512,256]{1,0:T(8,128)(2,1)S(1)} %collective-permute-done.20.near_h) | copy-start | bytes 786436
  193.6 0.7 copy-start.9
Sparse Core Ops, SparseCore 0:
  12.5 105.2 all-gather.2

commit v6 on v5

--- a/solution.py
+++ b/solution.py
@@ -136,7 +136,34 @@
     )(order, mine, other, *totals, *weights)
 
 
-def last_kernel(key_ref, value_ref, key_tok_ref, value_tok_ref, ka, kb, va, vb, out_ref, send_ref):
+def cut_kernel(k1, k3, v1, v3, o1, o2, o3, o4, sems):
+    half = o1.shape[0]
+    copies = [
+        pltpu.make_async_copy(src.at[pl.ds(start, half)], dst, sems.at[i])
+        for i, (src, start, dst) in enumerate(((k1, 0, o1), (k3, half, o2), (v1, 0, o3), (v3, half, o4)))
+    ]
+    for copy in copies:
+        copy.start()
+    for copy in copies:
+        copy.wait()
+
+
+def cut_halves(lines):
+    hbm = pl.BlockSpec(memory_space=pl.ANY)
+    rows, width = lines[0].shape
+    return pl.pallas_call(
+        cut_kernel,
+        in_specs=[hbm] * 4,
+        out_specs=[hbm] * 4,
+        out_shape=[jax.ShapeDtypeStruct((rows // 2, width), BF16)] * 4,
+        scratch_shapes=[pltpu.SemaphoreType.DMA((4,))],
+        compiler_params=pltpu.CompilerParams(vmem_limit_bytes=VMEM),
+        cost_estimate=pl.CostEstimate(flops=0, bytes_accessed=4 * rows * width * 2, transcendentals=0),
+        name="cut_halves",
+    )(*lines)
+
+
+def last_kernel(key_ref, value_ref, key_tok_ref, value_tok_ref, ka, kb, va, vb, send_ref):
     half = ka.shape[0]
 
     def finish(total_ref, tok_ref, wa, wb):
@@ -146,9 +173,7 @@
         return total.astype(BF16).astype(F32)
 
     source = finish(key_ref, key_tok_ref, ka, kb) * finish(value_ref, value_tok_ref, va, vb)
-    source = source.T
-    out_ref[...] = source
-    send_ref[...] = source.astype(BF16)
+    send_ref[...] = source.T.astype(BF16)
 
 
 def last_part(totals, tokens, weights):
@@ -161,11 +186,8 @@
         in_specs=[pl.BlockSpec((tile, chan), lambda i: (i, 0))] * 2
         + [pl.BlockSpec((tile, quarter), lambda i: (i, 0))] * 2
         + [pl.BlockSpec((quarter // 2, chan), lambda i: (0, 0))] * 4,
-        out_specs=[pl.BlockSpec((chan, tile), lambda i: (0, i))] * 2,
-        out_shape=[
-            jax.ShapeDtypeStruct((chan, total), F32),
-            jax.ShapeDtypeStruct((chan, total), BF16),
-        ],
+        out_specs=pl.BlockSpec((chan, tile), lambda i: (0, i)),
+        out_shape=jax.ShapeDtypeStruct((chan, total), BF16),
         compiler_params=pltpu.CompilerParams(vmem_limit_bytes=VMEM),
         cost_estimate=pl.CostEstimate(
             flops=2 * 2 * total * quarter * chan, bytes_accessed=13 * 2**20, transcendentals=0
@@ -531,12 +553,12 @@
     first = sum_part(first_kernel, "first_part", order, mine, other, [], [key_line, value_line], True)
     near_lines = [send(key_line, dy=-1), send(key_line, dy=1), send(value_line, dx=-1), send(value_line, dx=1)]
     near_lines, first = lax.optimization_barrier((near_lines, first))
-    half = key_line.shape[0] // 2
+    halves = cut_halves(near_lines)
     last_lines = [
-        send(near_lines[0][:half], dy=-1),
-        send(near_lines[1][half:], dy=1),
-        send(near_lines[2][:half], dx=-1),
-        send(near_lines[3][half:], dx=1),
+        send(halves[0], dy=-1),
+        send(halves[1], dy=1),
+        send(halves[2], dx=-1),
+        send(halves[3], dx=1),
     ]
     totals = sum_part(second_kernel, "second_part", order, mine, other, first[:2], near_lines, False)
 
@@ -548,8 +570,8 @@
     ow_same = lax.ppermute(ow_part, ("seq", "ch"), perm)
     ow_cross = send(ow_same, dc=1)
 
-    source, packed = last_part(totals, first[2:], last_lines)
-    packed = packed.reshape(CHIPS, chan // CHIPS, 2 * rows)
+    source = last_part(totals, first[2:], last_lines)
+    packed = source.reshape(CHIPS, chan // CHIPS, 2 * rows)
     mine_ch = lax.all_to_all(packed, "seq", 0, 0, axis_index_groups=SAME_CORE)
 
     tw, a, ai, cs, twist = column_tables(core, rows, cols, padded)
@@ -563,7 +585,7 @@
 
     gate = gate_part(mine, other, gathered).astype(F32)
     skip = lax.dynamic_slice_in_dim(skip_bias, core * chan, chan, 0)[:, None]
-    gated = (gate * (conv + skip * source)).astype(BF16)
+    gated = (gate * (conv + skip * source.astype(F32))).astype(BF16)
 
     kept = rows // 2
     own_here = lax.dynamic_slice(gated, (0, h * kept), (chan, kept))

time: 210 us -> 269 us (1.28)
  Pallas kernels: 71 us -> 135 us
  waiting for transfers between devices: 62.2 us -> 55.2 us
  starting transfers between devices: 38.2 us -> 42.8 us
  local copies, waits for them, and re-layouts: 15.9 us -> 12 us
    pallas_call x0 -> x1, Pallas kernels: none -> 64.7 us  [cut_halves(): pl.pallas_call(cut_kernel, in_specs=[hbm] * 4, out_specs=[hbm] * 4, out_s...]
    ppermute x21, waiting for transfers between devices: 43.9 us -> 34.2 us  [send(): return lax.ppermute(value, 'seq', perm)]
    slice x4 -> x0, local copies, waits for them, and re-layouts: 5.66 us -> none  [the longest x1 1.88 us: per_device(): near_lines[2][:half]]
    ppermute x21, starting transfers between devices: 25.4 us -> 28.9 us  [send(): return lax.ppermute(value, 'seq', perm)]
  transfers between devices with their start and end apart: 27 -> 27, of which waited for: 12 -> 11; matrix products, arithmetic and copies ran while one was open for 10% -> 6% of each run, Pallas kernels for 30% -> 47%
where the time goes in v6:
time: 269 us
  Pallas kernels  135 us (50%)
  waiting for transfers between devices  55.2 us (21%)
  starting transfers between devices  42.8 us (16%)
  between operations  13.7 us (5%)
  local copies, waits for them, and re-layouts  12 us (4%)
  other arithmetic  9.59 us (4%)
    pallas_call x1, Pallas kernels, cut_halves(): pl.pallas_call(cut_kernel, in_specs=[hbm] * 4, out_specs=[hbm] * 4, out_s...  64.7 us
    ppermute x21, waiting for transfers between devices, send(): return lax.ppermute(value, 'seq', perm)  34.2 us
    ppermute x21, starting transfers between devices, send(): return lax.ppermute(value, 'seq', perm)  28.9 us
    pallas_call x2, Pallas kernels, sum_part(): pl.pallas_call(kernel, grid_spec=pltpu.PrefetchScalarGridSpec(num_scalar_...  21.9 us
    pallas_call x2, Pallas kernels, mix_part(): pl.pallas_call(mix_kernel if total is None else mix_more_kernel, grid=(4,...  15.5 us
    pallas_call x1, Pallas kernels, long_conv(): pl.pallas_call(conv_kernel, in_specs=[vmem, hbm, hbm, hbm, vmem, vmem, vm...  13.4 us
    all_to_all x1, waiting for transfers between devices, per_device(): mine_ch = lax.all_to_all(packed, 'seq', 0, 0, axis_index_groups=SAME_CORE)  11.3 us
    pallas_call x1, Pallas kernels, gate_part(): pl.pallas_call(gate_kernel, grid=(4,), in_specs=[pl.BlockSpec((tile, widt...  10 us
  transfers between devices with their start and end apart: 27, of which 11 were waited for; matrix products, arithmetic and copies ran while one was open for 6% of the time, Pallas kernels for 47%

profile of v6, /device:TPU:1, one launch (start us, length us, event | category | flops | bytes accessed | tf_op | source)
XLA Modules:
  0.0 268.5 jit_solution(9162698264521309069)
XLA Ops:
  6.5 0.9 copy.11
  7.6 1.5 collective-permute-start.4
  9.1 1.0 dynamic-slice_bitcast_fusion
  10.3 0.5 collective-permute-start.3
  10.7 0.9 collective-permute-done
  11.7 0.7 maximum_maximum_fusion
  12.4 3.8 %collective-permute-start.2 = (bf16[128,512]{1,0:T(8,128)(2,1)S(1)}, bf16[128,512]{1,0:T(8,128)(2,1)S(1)}, u32[]{:S(2)}, u32[]{:S(2)}) collective-permute-start(bf16[128,512]{1,0:T(8,128)(2,1)S(1)} %bitcast.65), channel_id=1, source_target_pairs={{0,66},{2,64},{4,70},{6,68},{8,74},{10,72},{12,78},{14,76},{16,82}... | collective-permute-start | bytes 393224 | tf_op jit(solution)/shard_map/ppermute | solution.py:35
  16.3 3.6 %collective-permute-done.2 = bf16[128,512]{1,0:T(8,128)(2,1)S(1)} collective-permute-done((bf16[128,512]{1,0:T(8,128)(2,1)S(1)}, bf16[128,512]{1,0:T(8,128)(2,1)S(1)}, u32[]{:S(2)}, u32[]{:S(2)}) %collective-permute-start.2) | collective-permute-done | bytes 131104 | tf_op jit(solution)/shard_map/ppermute | solution.py:35
  19.9 2.6 collective-permute-done.1
  22.6 1.3 collective-permute-start.7
  23.9 2.5 collective-permute-start.6
  26.4 1.2 collective-permute-start.5
  27.5 1.3 collective-permute-start.10
  28.8 2.6 collective-permute-start.9
  31.4 2.4 collective-permute-start.8
  33.9 4.7 %constant_dynamic-slice_fusion.3 = bf16[512,4096]{1,0:T(8,128)(2,1)} fusion(bf16[1024,4096]{1,0:T(8,128)(2,1)} %w_here.1, s32[]{:T(128)S(6)} %select_n.230), kind=kLoop, calls=%fused_computation.104 | loop fusion | bytes 8388612 | tf_op jit(solution)/shard_map/dynamic_slice | solution.py:543
  38.5 0.2 collective-permute-done.6
  38.7 0.4 collective-permute-done.5
  39.1 1.1 pad_maximum_fusion.key_line
  40.2 2.7 %collective-permute-done.9 = bf16[256,512]{1,0:T(8,128)(2,1)S(1)} collective-permute-done((bf16[256,512]{1,0:T(8,128)(2,1)S(1)}, bf16[256,512]{1,0:T(8,128)(2,1)S(1)}, u32[]{:S(2)}, u32[]{:S(2)}) %collective-permute-start.9) | collective-permute-done | bytes 262176 | tf_op jit(solution)/shard_map/ppermute | solution.py:35
  42.9 1.1 pad_maximum_fusion.1.value_line
  44.0 3.7 %collective-permute-start.22 = (bf16[512,4096]{1,0:T(8,128)(2,1)}, bf16[512,4096]{1,0:T(8,128)(2,1)}, u32[]{:S(2)}, u32[]{:S(2)}) collective-permute-start(bf16[512,4096]{1,0:T(8,128)(2,1)} %constant_dynamic-slice_fusion.3), channel_id=1, source_target_pairs={{0,1},{1,0},{2,67},{3,66},{4,5},{5,4},{6,71},{7,70},{8,9},{9,8},{1... | collective-permute-start | bytes 12582920 | tf_op jit(solution)/shard_map/ppermute | solution.py:570
  47.7 2.5 collective-permute-start.11
  50.2 0.4 collective-permute-start.12
  50.5 1.5 collective-permute-start.14
  52.1 0.6 pad_add_fusion.order_ref
  52.6 10.3 %first_part.1 = (f32[1024,512]{1,0:T(8,128)}, f32[1024,512]{1,0:T(8,128)}, bf16[1024,1024]{1,0:T(8,128)(2,1)}, bf16[1024,1024]{1,0:T(8,128)(2,1)}) custom-call(s32[2,32]{1,0:T(2,128)} %pad_add_fusion.order_ref, bf16[512,4096]{1,0:T(8,128)(2,1)} %bitcast.57, bf16[512,4096]{1,0:T(8,128)(2,1)} %collective-permute-done.3.other_ref, ...), custom_call_target="tpu_custom_call" | custom-call | flops 2147483648 | bytes 18874368 | tf_op jit(solution)/shard_map/first_part/pallas_call | solution.py:117
  62.9 21.0 %collective-permute-done.11.k1 = bf16[1024,512]{1,0:T(8,128)(2,1)S(1)} collective-permute-done((bf16[1024,512]{1,0:T(8,128)(2,1)}, bf16[1024,512]{1,0:T(8,128)(2,1)S(1)}, u32[]{:S(2)}, u32[]{:S(2)}) %collective-permute-start.11) | collective-permute-done | bytes 1048608 | tf_op jit(solution)/shard_map/ppermute | solution.py:35
  84.0 2.7 %collective-permute-done.12.k3 = bf16[1024,512]{1,0:T(8,128)(2,1)S(1)} collective-permute-done((bf16[1024,512]{1,0:T(8,128)(2,1)}, bf16[1024,512]{1,0:T(8,128)(2,1)S(1)}, u32[]{:S(2)}, u32[]{:S(2)}) %collective-permute-start.12) | collective-permute-done | bytes 1048608 | tf_op jit(solution)/shard_map/ppermute | solution.py:35
  86.7 1.0 copy-done.2
  87.7 0.3 copy-done.3
  88.0 64.7 %cut_halves.1 = (bf16[512,512]{1,0:T(8,128)(2,1)}, bf16[512,512]{1,0:T(8,128)(2,1)}, bf16[512,512]{1,0:T(8,128)(2,1)}, bf16[512,512]{1,0:T(8,128)(2,1)}) custom-call(bf16[1024,512]{1,0:T(8,128)(2,1)} %copy-done.1, bf16[1024,512]{1,0:T(8,128)(2,1)} %copy-done.2, bf16[1024,512]{1,0:T(8,128)(2,1)} %copy-done.3, bf16[1024,512]{1,0:T(8,128)(2,1)} %collective-permute-done.14.v3), custom_call_target="tpu_custom_call" | custom-call | bytes 4194304 | tf_op jit(solution)/shard_map/cut_halves/pallas_call | solution.py:154
  152.7 0.4 collective-permute-start.15
  153.0 1.2 collective-permute-start.16
  154.2 1.5 collective-permute-start.18
  155.7 0.2 fusion.38
  156.0 11.7 %second_part.1 = (f32[1024,512]{1,0:T(8,128)}, f32[1024,512]{1,0:T(8,128)}) custom-call(s32[2,32]{1,0:T(2,128)} %pad_add_fusion.order_ref, bf16[512,4096]{1,0:T(8,128)(2,1)} %bitcast.58, bf16[512,4096]{1,0:T(8,128)(2,1)} %collective-permute-done.3.other_ref, f32[1024,512]{1,0:T(8,128)} %get-tuple-element.40.key_in, f32[1024,512]{1,0:T(8,128)} %get-tuple-element.41.value_in, ...), custom_call_target="tpu_custom_call" | custom-call | flops 4294967296 | bytes 18874368 | tf_op jit(solution)/shard_map/second_part/pallas_call | solution.py:117
  167.7 1.6 collective-permute-start.23
  169.4 0.8 copy-done.5
  170.3 0.2 copy-done.7
  170.6 7.2 %last_part.1 = bf16[512,1024]{1,0:T(8,128)(2,1)} custom-call(f32[1024,512]{1,0:T(8,128)} %get-tuple-element.46.key_ref, f32[1024,512]{1,0:T(8,128)} %get-tuple-element.47.value_ref, bf16[1024,1024]{1,0:T(8,128)(2,1)} %get-tuple-element.48.key_tok_ref, bf16[1024,1024]{1,0:T(8,128)(2,1)} %get-tuple-element.49.value_tok_ref, bf16[512,512]{1,0:T(8,128)(2,1)} %copy-done.5, ...), custom_call_target="tpu_custom_call" | custom-call | flops 2147483648 | bytes 13631488 | tf_op jit(solution)/shard_map/last_part/pallas_call | solution.py:183
  177.8 4.0 %all-to-all-start = ((bf16[32,16,1024]{2,1,0:T(8,128)(2,1)}), bf16[32,16,1024]{2,1,0:T(8,128)(2,1)S(1)}, u32[]{:S(2)}, u32[]{:S(2)}) async-start(bf16[32,16,1024]{2,1,0:T(8,128)(2,1)} %bitcast.60), calls=%async_computation | async-start | bytes 2097152 | tf_op jit(solution)/shard_map/all_to_all | solution.py:575
  181.9 0.8 copy.12.a_ref
  182.7 0.7 fusion.9.ai_ref
  183.4 0.3 fusion.35
  183.7 0.7 pad_maximum_fusion.6
  184.4 0.6 fusion.15
  185.0 0.7 pad_maximum_fusion.5.tw_hbm
  185.7 2.5 filter_part.1
  188.2 11.3 %all-to-all-done.x_ref = bf16[32,16,1024]{2,1,0:T(8,128)(2,1)S(1)} async-done(((bf16[32,16,1024]{2,1,0:T(8,128)(2,1)}), bf16[32,16,1024]{2,1,0:T(8,128)(2,1)S(1)}, u32[]{:S(2)}, u32[]{:S(2)}) %all-to-all-start) | async-done | bytes 1048608 | tf_op jit(solution)/shard_map/all_to_all | solution.py:575
  199.5 1.0 copy-done.4
  200.5 13.4 %long_conv.1 = bf16[32,16,1024]{2,1,0:T(8,128)(2,1)} custom-call(bf16[32,16,1024]{2,1,0:T(8,128)(2,1)} %copy-done.4, bf16[512,1024]{1,0:T(8,128)(2,1)} %constant.193.clone.fwd_hbm, bf16[1024,512]{1,0:T(8,128)(2,1)} %constant.194.clone.inv_hbm, f32[64,1024]{1,0:T(8,128)} %pad_maximum_fusion.5.tw_hbm, bf16[256,256]{1,0:T(8,128)(2,1)} %copy.12.a_ref, ...), custom_call_target="tpu_custom_call" | custom-call | flops 8000000000 | bytes 8388608 | tf_op jit(solution)/shard_map/long_conv/pallas_call | solution.py:440
  213.9 4.4 %all-to-all-start.1 = ((bf16[32,16,1024]{2,1,0:T(8,128)(2,1)}), bf16[32,16,1024]{2,1,0:T(8,128)(2,1)S(1)}, u32[]{:S(2)}, u32[]{:S(2)}) async-start(bf16[32,16,1024]{2,1,0:T(8,128)(2,1)} %long_conv.1), calls=%async_computation.1 | async-start | bytes 2097152 | tf_op jit(solution)/shard_map/all_to_all | solution.py:583
  218.5 10.0 %gate_part.1 = bf16[512,1024]{1,0:T(8,128)(2,1)} custom-call(bf16[512,4096]{1,0:T(8,128)(2,1)} %bitcast.59, bf16[512,4096]{1,0:T(8,128)(2,1)} %collective-permute-done.3.other_ref, bf16[32,160,512]{2,1,0:T(8,128)(2,1)} %bitcast.62), custom_call_target="tpu_custom_call" | custom-call | flops 4294967296 | bytes 13631488 | tf_op jit(solution)/shard_map/gate_part/pallas_call | solution.py:214
  228.5 6.1 %all-to-all-done.1 = bf16[32,16,1024]{2,1,0:T(8,128)(2,1)S(1)} async-done(((bf16[32,16,1024]{2,1,0:T(8,128)(2,1)}), bf16[32,16,1024]{2,1,0:T(8,128)(2,1)S(1)}, u32[]{:S(2)}, u32[]{:S(2)}) %all-to-all-start.1) | async-done | bytes 1048608 | tf_op jit(solution)/shard_map/all_to_all | solution.py:583
  234.6 1.7 fusion.1
  236.4 2.8 %collective-permute-start.19 = (bf16[512,256]{1,0:T(8,128)(2,1)S(1)}, bf16[512,256]{1,0:T(8,128)(2,1)S(1)}, u32[]{:S(2)}, u32[]{:S(2)}) collective-permute-start(bf16[512,256]{1,0:T(8,128)(2,1)S(1)} %get-tuple-element.63), channel_id=1, source_target_pairs={{0,2},{2,0},{4,6},{6,4},{8,10},{10,8},{12,14},{14,12},{16,18},{18,... | collective-permute-start | bytes 786440 | tf_op jit(solution)/shard_map/ppermute | solution.py:35
  239.2 0.5 collective-permute-start.20
  239.8 1.2 collective-permute-start.21
  241.1 0.8 pad_maximum_fusion.2.here
  241.9 7.5 %mix_part.1.total_ref = f32[256,4096]{1,0:T(8,128)} custom-call(bf16[1024,256]{1,0:T(8,128)(2,1)} %pad_maximum_fusion.2.here, bf16[1024,4096]{1,0:T(8,128)(2,1)} %w_here.1), custom_call_target="tpu_custom_call" | custom-call | flops 2147483648 | bytes 12582912 | tf_op jit(solution)/shard_map/mix_part/pallas_call | solution.py:271
  249.4 3.5 %collective-permute-done.21.far_h = bf16[512,256]{1,0:T(8,128)(2,1)S(1)} collective-permute-done((bf16[512,256]{1,0:T(8,128)(2,1)S(1)}, bf16[512,256]{1,0:T(8,128)(2,1)S(1)}, u32[]{:S(2)}, u32[]{:S(2)}) %collective-permute-start.21) | collective-permute-done | bytes 262176 | tf_op jit(solution)/shard_map/ppermute | solution.py:601
  252.9 0.7 copy-done.10
  253.6 8.0 %mix_more.1 = bf16[256,4096]{1,0:T(8,128)(2,1)} custom-call(f32[256,4096]{1,0:T(8,128)} %mix_part.1.total_ref, bf16[512,256]{1,0:T(8,128)(2,1)} %copy-done.9, bf16[512,256]{1,0:T(8,128)(2,1)} %copy-done.10, bf16[512,4096]{1,0:T(8,128)(2,1)} %collective-permute-done.22.w_near, bf16[512,4096]{1,0:T(8,128)(2,1)} %collective-permute-done.23.w_far), custom_call_target="tpu_custom_call" | custom-call | flops 2147483648 | bytes 12582912 | tf_op jit(solution)/shard_map/mix_more/pallas_call | solution.py:271
  (65 shorter events, 1.4 us)
Async XLA Ops:
  6.5 179.2 %all-gather.3.cloned.1.call-start = ((), (), s32[]{:S(2)}) async-start(), calls=%async_computation.2 | async-start | bytes 5406720 | tf_op jit(solution)/shard_map/all_gather | solution.py:540
  7.6 3.1 %collective-permute-start.4 = (bf16[32,256]{1,0:T(8,128)(2,1)S(1)}, bf16[32,256]{1,0:T(8,128)(2,1)S(1)}, u32[]{:S(2)}, u32[]{:S(2)}) collective-permute-start(bf16[32,256]{1,0:T(8,128)(2,1)S(1)} %pad_maximum_fusion.8), channel_id=1, source_target_pairs={{0,2},{2,0},{4,6},{6,4},{8,10},{10,8},{12,14},{14,12},{16,18},{18,... | collective-permute-start | bytes 49160 | tf_op jit(solution)/shard_map/ppermute | solution.py:35
  10.1 1.5 collective-permute-start
  10.3 12.4 %collective-permute-start.3 = (bf16[512,4096]{1,0:T(8,128)(2,1)}, bf16[512,4096]{1,0:T(8,128)(2,1)}, u32[]{:S(2)}, u32[]{:S(2)}) collective-permute-start(bf16[512,4096]{1,0:T(8,128)(2,1)} %bitcast.56), channel_id=1, source_target_pairs={{0,2},{2,0},{4,6},{6,4},{8,10},{10,8},{12,14},{14,12},{16,18},{18,... | collective-permute-start | bytes 12582920 | tf_op jit(solution)/shard_map/ppermute | solution.py:35
  12.4 7.5 %collective-permute-start.2 = (bf16[128,512]{1,0:T(8,128)(2,1)S(1)}, bf16[128,512]{1,0:T(8,128)(2,1)S(1)}, u32[]{:S(2)}, u32[]{:S(2)}) collective-permute-start(bf16[128,512]{1,0:T(8,128)(2,1)S(1)} %bitcast.65), channel_id=1, source_target_pairs={{0,66},{2,64},{4,70},{6,68},{8,74},{10,72},{12,78},{14,76},{16,82}... | collective-permute-start | bytes 393224 | tf_op jit(solution)/shard_map/ppermute | solution.py:35
  16.2 6.3 %collective-permute-start.1 = (bf16[128,512]{1,0:T(8,128)(2,1)S(1)}, bf16[128,512]{1,0:T(8,128)(2,1)S(1)}, u32[]{:S(2)}, u32[]{:S(2)}) collective-permute-start(bf16[128,512]{1,0:T(8,128)(2,1)S(1)} %bitcast.66), channel_id=1, source_target_pairs={{0,64},{2,66},{4,68},{6,70},{8,72},{10,74},{12,76},{14,78},{16,80}... | collective-permute-start | bytes 393224 | tf_op jit(solution)/shard_map/ppermute | solution.py:35
  22.6 8.8 %collective-permute-start.7 = (bf16[256,512]{1,0:T(8,128)(2,1)S(1)}, bf16[256,512]{1,0:T(8,128)(2,1)S(1)}, u32[]{:S(2)}, u32[]{:S(2)}) collective-permute-start(bf16[256,512]{1,0:T(8,128)(2,1)S(1)} %get-tuple-element.32), channel_id=1, source_target_pairs={{0,4},{2,6},{4,8},{6,10},{8,12},{10,14},{12,0},{14,2},{16,20},{18,... | collective-permute-start | bytes 786440 | tf_op jit(solution)/shard_map/ppermute | solution.py:35
  23.9 14.8 %collective-permute-start.6 = (bf16[256,512]{1,0:T(8,128)(2,1)S(1)}, bf16[256,512]{1,0:T(8,128)(2,1)S(1)}, u32[]{:S(2)}, u32[]{:S(2)}) collective-permute-start(bf16[256,512]{1,0:T(8,128)(2,1)S(1)} %get-tuple-element.32), channel_id=1, source_target_pairs={{0,8},{2,10},{4,12},{6,14},{8,0},{10,2},{12,4},{14,6},{16,24},{18,... | collective-permute-start | bytes 786440 | tf_op jit(solution)/shard_map/ppermute | solution.py:35
  26.4 12.8 %collective-permute-start.5 = (bf16[256,512]{1,0:T(8,128)(2,1)S(1)}, bf16[256,512]{1,0:T(8,128)(2,1)S(1)}, u32[]{:S(2)}, u32[]{:S(2)}) collective-permute-start(bf16[256,512]{1,0:T(8,128)(2,1)S(1)} %get-tuple-element.32), channel_id=1, source_target_pairs={{0,12},{2,14},{4,0},{6,2},{8,4},{10,6},{12,8},{14,10},{16,28},{18,... | collective-permute-start | bytes 786440 | tf_op jit(solution)/shard_map/ppermute | solution.py:35
  27.5 12.7 %collective-permute-start.10 = (bf16[256,512]{1,0:T(8,128)(2,1)S(1)}, bf16[256,512]{1,0:T(8,128)(2,1)S(1)}, u32[]{:S(2)}, u32[]{:S(2)}) collective-permute-start(bf16[256,512]{1,0:T(8,128)(2,1)S(1)} %get-tuple-element.33), channel_id=1, source_target_pairs={{0,16},{2,18},{4,20},{6,22},{8,24},{10,26},{12,28},{14,30},{16,32}... | collective-permute-start | bytes 786440 | tf_op jit(solution)/shard_map/ppermute | solution.py:35
  28.8 14.1 %collective-permute-start.9 = (bf16[256,512]{1,0:T(8,128)(2,1)S(1)}, bf16[256,512]{1,0:T(8,128)(2,1)S(1)}, u32[]{:S(2)}, u32[]{:S(2)}) collective-permute-start(bf16[256,512]{1,0:T(8,128)(2,1)S(1)} %get-tuple-element.33), channel_id=1, source_target_pairs={{0,32},{2,34},{4,36},{6,38},{8,40},{10,42},{12,44},{14,46},{16,48}... | collective-permute-start | bytes 786440 | tf_op jit(solution)/shard_map/ppermute | solution.py:35
  31.4 11.5 %collective-permute-start.8 = (bf16[256,512]{1,0:T(8,128)(2,1)S(1)}, bf16[256,512]{1,0:T(8,128)(2,1)S(1)}, u32[]{:S(2)}, u32[]{:S(2)}) collective-permute-start(bf16[256,512]{1,0:T(8,128)(2,1)S(1)} %get-tuple-element.33), channel_id=1, source_target_pairs={{0,48},{2,50},{4,52},{6,54},{8,56},{10,58},{12,60},{14,62},{16,0},... | collective-permute-start | bytes 786440 | tf_op jit(solution)/shard_map/ppermute | solution.py:35
  38.5 13.5 %copy-start.12 = (s32[32]{0:T(128)S(1)}, s32[32]{0:T(128)}, u32[]{:S(2)}) copy-start(s32[32]{0:T(128)} %constant.192.clone) | copy-start | bytes 388
  38.5 13.5 %copy-start.13 = (s32[32]{0:T(128)S(1)}, s32[32]{0:T(128)}, u32[]{:S(2)}) copy-start(s32[32]{0:T(128)} %constant.191.clone) | copy-start | bytes 388
  38.5 13.5 %copy-start.14 = (s32[32]{0:T(128)S(1)}, s32[32]{0:T(128)}, u32[]{:S(2)}) copy-start(s32[32]{0:T(128)} %constant.190.clone) | copy-start | bytes 388
  44.0 123.7 %collective-permute-start.22 = (bf16[512,4096]{1,0:T(8,128)(2,1)}, bf16[512,4096]{1,0:T(8,128)(2,1)}, u32[]{:S(2)}, u32[]{:S(2)}) collective-permute-start(bf16[512,4096]{1,0:T(8,128)(2,1)} %constant_dynamic-slice_fusion.3), channel_id=1, source_target_pairs={{0,1},{1,0},{2,67},{3,66},{4,5},{5,4},{6,71},{7,70},{8,9},{9,8},{1... | collective-permute-start | bytes 12582920 | tf_op jit(solution)/shard_map/ppermute | solution.py:570
  47.7 36.3 %collective-permute-start.11 = (bf16[1024,512]{1,0:T(8,128)(2,1)}, bf16[1024,512]{1,0:T(8,128)(2,1)S(1)}, u32[]{:S(2)}, u32[]{:S(2)}) collective-permute-start(bf16[1024,512]{1,0:T(8,128)(2,1)} %pad_maximum_fusion.key_line), channel_id=1, source_target_pairs={{0,48},{2,50},{4,52},{6,54},{8,56},{10,58},{12,60},{14,62},{16,0},... | collective-permute-start | bytes 3145736 | tf_op jit(solution)/shard_map/ppermute | solution.py:35
  50.2 36.5 %collective-permute-start.12 = (bf16[1024,512]{1,0:T(8,128)(2,1)}, bf16[1024,512]{1,0:T(8,128)(2,1)S(1)}, u32[]{:S(2)}, u32[]{:S(2)}) collective-permute-start(bf16[1024,512]{1,0:T(8,128)(2,1)} %pad_maximum_fusion.key_line), channel_id=1, source_target_pairs={{0,16},{2,18},{4,20},{6,22},{8,24},{10,26},{12,28},{14,30},{16,32}... | collective-permute-start | bytes 3145736 | tf_op jit(solution)/shard_map/ppermute | solution.py:35
  50.5 36.1 %collective-permute-start.13 = (bf16[1024,512]{1,0:T(8,128)(2,1)}, bf16[1024,512]{1,0:T(8,128)(2,1)S(1)}, u32[]{:S(2)}, u32[]{:S(2)}) collective-permute-start(bf16[1024,512]{1,0:T(8,128)(2,1)} %pad_maximum_fusion.1.value_line), channel_id=1, source_target_pairs={{0,12},{2,14},{4,0},{6,2},{8,4},{10,6},{12,8},{14,10},{16,28},{18,... | collective-permute-start | bytes 3145736 | tf_op jit(solution)/shard_map/ppermute | solution.py:35
  50.5 36.1 %collective-permute-start.14 = (bf16[1024,512]{1,0:T(8,128)(2,1)}, bf16[1024,512]{1,0:T(8,128)(2,1)}, u32[]{:S(2)}, u32[]{:S(2)}) collective-permute-start(bf16[1024,512]{1,0:T(8,128)(2,1)} %pad_maximum_fusion.1.value_line), channel_id=1, source_target_pairs={{0,4},{2,6},{4,8},{6,10},{8,12},{10,14},{12,0},{14,2},{16,20},{18,... | collective-permute-start | bytes 3145736 | tf_op jit(solution)/shard_map/ppermute | solution.py:35
  83.9 2.7 %copy-start.1 = (bf16[1024,512]{1,0:T(8,128)(2,1)}, bf16[1024,512]{1,0:T(8,128)(2,1)S(1)}, u32[]{:S(2)}) copy-start(bf16[1024,512]{1,0:T(8,128)(2,1)S(1)} %collective-permute-done.11.k1) | copy-start | bytes 3145732
  86.7 1.0 copy-start.2
  86.7 1.3 copy-start.3
  152.7 16.6 %collective-permute-start.15 = (bf16[512,512]{1,0:T(8,128)(2,1)}, bf16[512,512]{1,0:T(8,128)(2,1)S(1)}, u32[]{:S(2)}, u32[]{:S(2)}) collective-permute-start(bf16[512,512]{1,0:T(8,128)(2,1)} %get-tuple-element.50), channel_id=1, source_target_pairs={{0,48},{2,50},{4,52},{6,54},{8,56},{10,58},{12,60},{14,62},{16,0},... | collective-permute-start | bytes 1572872 | tf_op jit(solution)/shard_map/ppermute | solution.py:35
  153.0 16.3 %collective-permute-start.16 = (bf16[512,512]{1,0:T(8,128)(2,1)}, bf16[512,512]{1,0:T(8,128)(2,1)S(1)}, u32[]{:S(2)}, u32[]{:S(2)}) collective-permute-start(bf16[512,512]{1,0:T(8,128)(2,1)} %get-tuple-element.51), channel_id=1, source_target_pairs={{0,16},{2,18},{4,20},{6,22},{8,24},{10,26},{12,28},{14,30},{16,32}... | collective-permute-start | bytes 1572872 | tf_op jit(solution)/shard_map/ppermute | solution.py:35
  154.2 15.1 %collective-permute-start.17 = (bf16[512,512]{1,0:T(8,128)(2,1)}, bf16[512,512]{1,0:T(8,128)(2,1)S(1)}, u32[]{:S(2)}, u32[]{:S(2)}) collective-permute-start(bf16[512,512]{1,0:T(8,128)(2,1)} %get-tuple-element.52), channel_id=1, source_target_pairs={{0,12},{2,14},{4,0},{6,2},{8,4},{10,6},{12,8},{14,10},{16,28},{18,... | collective-permute-start | bytes 1572872 | tf_op jit(solution)/shard_map/ppermute | solution.py:35
  154.2 15.1 %collective-permute-start.18 = (bf16[512,512]{1,0:T(8,128)(2,1)}, bf16[512,512]{1,0:T(8,128)(2,1)S(1)}, u32[]{:S(2)}, u32[]{:S(2)}) collective-permute-start(bf16[512,512]{1,0:T(8,128)(2,1)} %get-tuple-element.53), channel_id=1, source_target_pairs={{0,4},{2,6},{4,8},{6,10},{8,12},{10,14},{12,0},{14,2},{16,20},{18,... | collective-permute-start | bytes 1572872 | tf_op jit(solution)/shard_map/ppermute | solution.py:35
  167.7 85.3 %collective-permute-start.23 = (bf16[512,4096]{1,0:T(8,128)(2,1)}, bf16[512,4096]{1,0:T(8,128)(2,1)}, u32[]{:S(2)}, u32[]{:S(2)}) collective-permute-start(bf16[512,4096]{1,0:T(8,128)(2,1)} %collective-permute-done.22.w_near), channel_id=1, source_target_pairs={{0,2},{2,0},{4,6},{6,4},{8,10},{10,8},{12,14},{14,12},{16,18},{18,... | collective-permute-start | bytes 12582920 | tf_op jit(solution)/shard_map/ppermute | solution.py:35
  169.3 0.8 copy-start.5
  169.3 1.0 copy-start.6
  169.3 1.1 copy-start.7
  169.3 1.3 copy-start.8
  177.8 21.7 %all-to-all-start = ((bf16[32,16,1024]{2,1,0:T(8,128)(2,1)}), bf16[32,16,1024]{2,1,0:T(8,128)(2,1)S(1)}, u32[]{:S(2)}, u32[]{:S(2)}) async-start(bf16[32,16,1024]{2,1,0:T(8,128)(2,1)} %bitcast.60), calls=%async_computation | async-start | bytes 2097152 | tf_op jit(solution)/shard_map/all_to_all | solution.py:575
  199.5 1.0 copy-start.4
  213.9 4.5 %copy-start.11 = (f32[1024]{0:T(1024)S(1)}, f32[1024]{0:T(1024)}, u32[]{:S(2)}) copy-start(f32[1024]{0:T(1024)} %param.13) | copy-start | bytes 12292
  213.9 20.6 %all-to-all-start.1 = ((bf16[32,16,1024]{2,1,0:T(8,128)(2,1)}), bf16[32,16,1024]{2,1,0:T(8,128)(2,1)S(1)}, u32[]{:S(2)}, u32[]{:S(2)}) async-start(bf16[32,16,1024]{2,1,0:T(8,128)(2,1)} %long_conv.1), calls=%async_computation.1 | async-start | bytes 2097152 | tf_op jit(solution)/shard_map/all_to_all | solution.py:583
  218.5 16.1 %copy-start = (bf16[512,1024]{1,0:T(8,128)(2,1)S(1)}, bf16[512,1024]{1,0:T(8,128)(2,1)}, u32[]{:S(2)}) copy-start(bf16[512,1024]{1,0:T(8,128)(2,1)} %last_part.1) | copy-start | bytes 3145732
  236.4 4.5 %collective-permute-start.19 = (bf16[512,256]{1,0:T(8,128)(2,1)S(1)}, bf16[512,256]{1,0:T(8,128)(2,1)S(1)}, u32[]{:S(2)}, u32[]{:S(2)}) collective-permute-start(bf16[512,256]{1,0:T(8,128)(2,1)S(1)} %get-tuple-element.63), channel_id=1, source_target_pairs={{0,2},{2,0},{4,6},{6,4},{8,10},{10,8},{12,14},{14,12},{16,18},{18,... | collective-permute-start | bytes 786440 | tf_op jit(solution)/shard_map/ppermute | solution.py:35
  239.2 10.2 %collective-permute-start.20 = (bf16[512,256]{1,0:T(8,128)(2,1)S(1)}, bf16[512,256]{1,0:T(8,128)(2,1)S(1)}, u32[]{:S(2)}, u32[]{:S(2)}) collective-permute-start(bf16[512,256]{1,0:T(8,128)(2,1)S(1)} %get-tuple-element.62), channel_id=1, source_target_pairs={{0,1},{1,0},{2,3},{3,2},{4,5},{5,4},{6,7},{7,6},{8,9},{9,8},{10,11... | collective-permute-start | bytes 786440 | tf_op jit(solution)/shard_map/ppermute | solution.py:596
  239.8 13.1 %collective-permute-start.21 = (bf16[512,256]{1,0:T(8,128)(2,1)S(1)}, bf16[512,256]{1,0:T(8,128)(2,1)S(1)}, u32[]{:S(2)}, u32[]{:S(2)}) collective-permute-start(bf16[512,256]{1,0:T(8,128)(2,1)S(1)} %get-tuple-element.61), channel_id=1, source_target_pairs={{0,3},{1,2},{2,1},{3,0},{4,7},{5,6},{6,5},{7,4},{8,11},{9,10},{10,... | collective-permute-start | bytes 786440 | tf_op jit(solution)/shard_map/ppermute | solution.py:601
  249.4 3.5 %copy-start.9 = (bf16[512,256]{1,0:T(8,128)(2,1)}, bf16[512,256]{1,0:T(8,128)(2,1)S(1)}, u32[]{:S(2)}) copy-start(bf16[512,256]{1,0:T(8,128)(2,1)S(1)} %collective-permute-done.20.near_h) | copy-start | bytes 786436
  252.9 0.7 copy-start.10
Sparse Core Ops, SparseCore 0:
  12.5 105.7 all-gather.2

commit v7 on v6

--- a/solution.py
+++ b/solution.py
@@ -136,27 +136,22 @@
     )(order, mine, other, *totals, *weights)
 
 
-def cut_kernel(k1, k3, v1, v3, o1, o2, o3, o4, sems):
-    half = o1.shape[0]
-    copies = [
-        pltpu.make_async_copy(src.at[pl.ds(start, half)], dst, sems.at[i])
-        for i, (src, start, dst) in enumerate(((k1, 0, o1), (k3, half, o2), (v1, 0, o3), (v3, half, o4)))
-    ]
-    for copy in copies:
-        copy.start()
-    for copy in copies:
-        copy.wait()
+def cut_kernel(*refs):
+    for src, dst in zip(refs[:4], refs[4:], strict=True):
+        dst[...] = src[...]
 
 
 def cut_halves(lines):
-    hbm = pl.BlockSpec(memory_space=pl.ANY)
     rows, width = lines[0].shape
+    tile = rows // 4
+    upper = pl.BlockSpec((tile, width), lambda i: (i, 0))
+    lower = pl.BlockSpec((tile, width), lambda i: (i + 2, 0))
     return pl.pallas_call(
         cut_kernel,
-        in_specs=[hbm] * 4,
-        out_specs=[hbm] * 4,
+        grid=(2,),
+        in_specs=[upper, lower, upper, lower],
+        out_specs=[upper] * 4,
         out_shape=[jax.ShapeDtypeStruct((rows // 2, width), BF16)] * 4,
-        scratch_shapes=[pltpu.SemaphoreType.DMA((4,))],
         compiler_params=pltpu.CompilerParams(vmem_limit_bytes=VMEM),
         cost_estimate=pl.CostEstimate(flops=0, bytes_accessed=4 * rows * width * 2, transcendentals=0),
         name="cut_halves",

time: 269 us -> 222 us (0.83)
  Pallas kernels: 135 us -> 73.4 us
  waiting for transfers between devices: 55.2 us -> 67.3 us
    pallas_call x1, Pallas kernels: 64.7 us -> 2.6 us  [cut_halves(): pl.pallas_call(cut_kernel, grid=(2,), in_specs=[upper, lower, upper, lowe...]
    ppermute x1, waiting for transfers between devices: 0.01 us -> 12.2 us  [per_device(): ow_same = lax.ppermute(ow_part, ('seq', 'ch'), perm)]
    all_to_all x1, starting transfers between devices: 3.98 us -> 6.77 us  [per_device(): mine_ch = lax.all_to_all(packed, 'seq', 0, 0, axis_index_groups=SAME_CORE)]
  transfers between devices with their start and end apart: 27 -> 27, of which waited for: 11 -> 12; matrix products, arithmetic and copies ran while one was open for 6% -> 7% of each run, Pallas kernels for 47% -> 30%
where the time goes in v7:
time: 222 us; the launch traced here: 221 us
  Pallas kernels  73.4 us (33%)
  waiting for transfers between devices  67.3 us (30%)
  starting transfers between devices  45 us (20%)
  between operations  13.7 us (6%)
  local copies, waits for them, and re-layouts  12 us (5%)
  other arithmetic  9.59 us (4%)
    ppermute x21, waiting for transfers between devices, send(): return lax.ppermute(value, 'seq', perm)  34.2 us
    ppermute x21, starting transfers between devices, send(): return lax.ppermute(value, 'seq', perm)  28.4 us
    pallas_call x2, Pallas kernels, sum_part(): pl.pallas_call(kernel, grid_spec=pltpu.PrefetchScalarGridSpec(num_scalar_...  22.1 us
    pallas_call x2, Pallas kernels, mix_part(): pl.pallas_call(mix_kernel if total is None else mix_more_kernel, grid=(4,...  15.5 us
    pallas_call x1, Pallas kernels, long_conv(): pl.pallas_call(conv_kernel, in_specs=[vmem, hbm, hbm, hbm, vmem, vmem, vm...  13.4 us
    ppermute x1, waiting for transfers between devices, per_device(): ow_same = lax.ppermute(ow_part, ('seq', 'ch'), perm)  12.2 us
    all_to_all x1, waiting for transfers between devices, per_device(): mine_ch = lax.all_to_all(packed, 'seq', 0, 0, axis_index_groups=SAME_CORE)  11.3 us
    pallas_call x1, Pallas kernels, gate_part(): pl.pallas_call(gate_kernel, grid=(4,), in_specs=[pl.BlockSpec((tile, widt...  10 us
  transfers between devices with their start and end apart: 27, of which 12 were waited for; matrix products, arithmetic and copies ran while one was open for 7% of the time, Pallas kernels for 30%

profile of v7, /device:TPU:1, one launch (start us, length us, event | category | flops | bytes accessed | tf_op | source)
XLA Modules:
  0.0 221.0 jit_solution(16492103354954895192)
XLA Ops:
  6.5 0.9 copy.11
  7.6 1.5 collective-permute-start.4
  9.1 1.0 dynamic-slice_bitcast_fusion
  10.3 0.5 collective-permute-start.3
  10.7 0.9 collective-permute-done
  11.7 0.7 maximum_maximum_fusion
  12.4 3.8 %collective-permute-start.2 = (bf16[128,512]{1,0:T(8,128)(2,1)S(1)}, bf16[128,512]{1,0:T(8,128)(2,1)S(1)}, u32[]{:S(2)}, u32[]{:S(2)}) collective-permute-start(bf16[128,512]{1,0:T(8,128)(2,1)S(1)} %bitcast.65), channel_id=1, source_target_pairs={{0,66},{2,64},{4,70},{6,68},{8,74},{10,72},{12,78},{14,76},{16,82}... | collective-permute-start | bytes 393224 | tf_op jit(solution)/shard_map/ppermute | solution.py:35
  16.3 3.6 %collective-permute-done.2 = bf16[128,512]{1,0:T(8,128)(2,1)S(1)} collective-permute-done((bf16[128,512]{1,0:T(8,128)(2,1)S(1)}, bf16[128,512]{1,0:T(8,128)(2,1)S(1)}, u32[]{:S(2)}, u32[]{:S(2)}) %collective-permute-start.2) | collective-permute-done | bytes 131104 | tf_op jit(solution)/shard_map/ppermute | solution.py:35
  19.9 2.6 %collective-permute-done.1 = bf16[128,512]{1,0:T(8,128)(2,1)S(1)} collective-permute-done((bf16[128,512]{1,0:T(8,128)(2,1)S(1)}, bf16[128,512]{1,0:T(8,128)(2,1)S(1)}, u32[]{:S(2)}, u32[]{:S(2)}) %collective-permute-start.1) | collective-permute-done | bytes 131104 | tf_op jit(solution)/shard_map/ppermute | solution.py:35
  22.6 1.3 collective-permute-start.7
  23.9 2.5 %collective-permute-start.6 = (bf16[256,512]{1,0:T(8,128)(2,1)S(1)}, bf16[256,512]{1,0:T(8,128)(2,1)S(1)}, u32[]{:S(2)}, u32[]{:S(2)}) collective-permute-start(bf16[256,512]{1,0:T(8,128)(2,1)S(1)} %get-tuple-element.32), channel_id=1, source_target_pairs={{0,8},{2,10},{4,12},{6,14},{8,0},{10,2},{12,4},{14,6},{16,24},{18,... | collective-permute-start | bytes 786440 | tf_op jit(solution)/shard_map/ppermute | solution.py:35
  26.4 1.2 collective-permute-start.5
  27.5 1.3 collective-permute-start.10
  28.8 2.6 %collective-permute-start.9 = (bf16[256,512]{1,0:T(8,128)(2,1)S(1)}, bf16[256,512]{1,0:T(8,128)(2,1)S(1)}, u32[]{:S(2)}, u32[]{:S(2)}) collective-permute-start(bf16[256,512]{1,0:T(8,128)(2,1)S(1)} %get-tuple-element.33), channel_id=1, source_target_pairs={{0,32},{2,34},{4,36},{6,38},{8,40},{10,42},{12,44},{14,46},{16,48}... | collective-permute-start | bytes 786440 | tf_op jit(solution)/shard_map/ppermute | solution.py:35
  31.4 2.4 %collective-permute-start.8 = (bf16[256,512]{1,0:T(8,128)(2,1)S(1)}, bf16[256,512]{1,0:T(8,128)(2,1)S(1)}, u32[]{:S(2)}, u32[]{:S(2)}) collective-permute-start(bf16[256,512]{1,0:T(8,128)(2,1)S(1)} %get-tuple-element.33), channel_id=1, source_target_pairs={{0,48},{2,50},{4,52},{6,54},{8,56},{10,58},{12,60},{14,62},{16,0},... | collective-permute-start | bytes 786440 | tf_op jit(solution)/shard_map/ppermute | solution.py:35
  33.9 4.7 %constant_dynamic-slice_fusion.3 = bf16[512,4096]{1,0:T(8,128)(2,1)} fusion(bf16[1024,4096]{1,0:T(8,128)(2,1)} %w_here.1, s32[]{:T(128)S(6)} %select_n.230), kind=kLoop, calls=%fused_computation.104 | loop fusion | bytes 8388612 | tf_op jit(solution)/shard_map/dynamic_slice | solution.py:538
  38.7 0.4 collective-permute-done.5
  39.1 1.1 pad_maximum_fusion.key_line
  40.2 2.7 %collective-permute-done.9 = bf16[256,512]{1,0:T(8,128)(2,1)S(1)} collective-permute-done((bf16[256,512]{1,0:T(8,128)(2,1)S(1)}, bf16[256,512]{1,0:T(8,128)(2,1)S(1)}, u32[]{:S(2)}, u32[]{:S(2)}) %collective-permute-start.9) | collective-permute-done | bytes 262176 | tf_op jit(solution)/shard_map/ppermute | solution.py:35
  42.9 1.1 pad_maximum_fusion.1.value_line
  44.0 3.7 %collective-permute-start.22 = (bf16[512,4096]{1,0:T(8,128)(2,1)}, bf16[512,4096]{1,0:T(8,128)(2,1)}, u32[]{:S(2)}, u32[]{:S(2)}) collective-permute-start(bf16[512,4096]{1,0:T(8,128)(2,1)} %constant_dynamic-slice_fusion.3), channel_id=1, source_target_pairs={{0,1},{1,0},{2,67},{3,66},{4,5},{5,4},{6,71},{7,70},{8,9},{9,8},{1... | collective-permute-start | bytes 12582920 | tf_op jit(solution)/shard_map/ppermute | solution.py:565
  47.7 2.5 %collective-permute-start.11 = (bf16[1024,512]{1,0:T(8,128)(2,1)}, bf16[1024,512]{1,0:T(8,128)(2,1)S(1)}, u32[]{:S(2)}, u32[]{:S(2)}) collective-permute-start(bf16[1024,512]{1,0:T(8,128)(2,1)} %pad_maximum_fusion.key_line), channel_id=1, source_target_pairs={{0,48},{2,50},{4,52},{6,54},{8,56},{10,58},{12,60},{14,62},{16,0},... | collective-permute-start | bytes 3145736 | tf_op jit(solution)/shard_map/ppermute | solution.py:35
  50.2 0.4 collective-permute-start.12
  50.5 1.5 collective-permute-start.14
  52.1 0.6 pad_add_fusion.order_ref
  52.6 10.3 %first_part.1 = (f32[1024,512]{1,0:T(8,128)}, f32[1024,512]{1,0:T(8,128)}, bf16[1024,1024]{1,0:T(8,128)(2,1)}, bf16[1024,1024]{1,0:T(8,128)(2,1)}) custom-call(s32[2,32]{1,0:T(2,128)} %pad_add_fusion.order_ref, bf16[512,4096]{1,0:T(8,128)(2,1)} %bitcast.57, bf16[512,4096]{1,0:T(8,128)(2,1)} %collective-permute-done.3.other_ref, ...), custom_call_target="tpu_custom_call" | custom-call | flops 2147483648 | bytes 18874368 | tf_op jit(solution)/shard_map/first_part/pallas_call | solution.py:117
  62.9 21.0 %collective-permute-done.11.k1.refs_0_ = bf16[1024,512]{1,0:T(8,128)(2,1)S(1)} collective-permute-done((bf16[1024,512]{1,0:T(8,128)(2,1)}, bf16[1024,512]{1,0:T(8,128)(2,1)S(1)}, u32[]{:S(2)}, u32[]{:S(2)}) %collective-permute-start.11) | collective-permute-done | bytes 1048608 | tf_op jit(solution)/shard_map/ppermute | solution.py:35
  84.0 2.7 %collective-permute-done.12.k3.refs_1_ = bf16[1024,512]{1,0:T(8,128)(2,1)S(1)} collective-permute-done((bf16[1024,512]{1,0:T(8,128)(2,1)}, bf16[1024,512]{1,0:T(8,128)(2,1)S(1)}, u32[]{:S(2)}, u32[]{:S(2)}) %collective-permute-start.12) | collective-permute-done | bytes 1048608 | tf_op jit(solution)/shard_map/ppermute | solution.py:35
  86.7 1.0 copy-done.2
  87.7 0.3 copy-done.3
  88.0 2.6 %cut_halves.1 = (bf16[512,512]{1,0:T(8,128)(2,1)}, bf16[512,512]{1,0:T(8,128)(2,1)}, bf16[512,512]{1,0:T(8,128)(2,1)}, bf16[512,512]{1,0:T(8,128)(2,1)}) custom-call(bf16[1024,512]{1,0:T(8,128)(2,1)} %copy-done.1, bf16[1024,512]{1,0:T(8,128)(2,1)} %copy-done.2, bf16[1024,512]{1,0:T(8,128)(2,1)} %copy-done.3, bf16[1024,512]{1,0:T(8,128)(2,1)} %collective-permute-done.14.v3.refs_3_), custom_call_target="tpu_custom_call" | custom-call | bytes 4194304 | tf_op jit(solution)/shard_map/cut_halves/pallas_call | solution.py:149
  90.6 0.3 collective-permute-start.15
  90.9 1.2 collective-permute-start.16
  92.1 1.5 collective-permute-start.18
  93.5 0.2 fusion.38
  93.8 11.8 %second_part.1 = (f32[1024,512]{1,0:T(8,128)}, f32[1024,512]{1,0:T(8,128)}) custom-call(s32[2,32]{1,0:T(2,128)} %pad_add_fusion.order_ref, bf16[512,4096]{1,0:T(8,128)(2,1)} %bitcast.58, bf16[512,4096]{1,0:T(8,128)(2,1)} %collective-permute-done.3.other_ref, f32[1024,512]{1,0:T(8,128)} %get-tuple-element.40.key_in, f32[1024,512]{1,0:T(8,128)} %get-tuple-element.41.value_in, ...), custom_call_target="tpu_custom_call" | custom-call | flops 4294967296 | bytes 18874368 | tf_op jit(solution)/shard_map/second_part/pallas_call | solution.py:117
  105.7 12.2 %collective-permute-done.22.w_near = bf16[512,4096]{1,0:T(8,128)(2,1)} collective-permute-done((bf16[512,4096]{1,0:T(8,128)(2,1)}, bf16[512,4096]{1,0:T(8,128)(2,1)}, u32[]{:S(2)}, u32[]{:S(2)}) %collective-permute-start.22) | collective-permute-done | bytes 4194336 | tf_op jit(solution)/shard_map/ppermute | solution.py:565
  117.8 1.2 collective-permute-start.23
  119.0 0.8 copy-done.5
  120.0 0.2 copy-done.7
  120.3 7.2 %last_part.1 = bf16[512,1024]{1,0:T(8,128)(2,1)} custom-call(f32[1024,512]{1,0:T(8,128)} %get-tuple-element.46.key_ref, f32[1024,512]{1,0:T(8,128)} %get-tuple-element.47.value_ref, bf16[1024,1024]{1,0:T(8,128)(2,1)} %get-tuple-element.48.key_tok_ref, bf16[1024,1024]{1,0:T(8,128)(2,1)} %get-tuple-element.49.value_tok_ref, bf16[512,512]{1,0:T(8,128)(2,1)} %copy-done.5, ...), custom_call_target="tpu_custom_call" | custom-call | flops 2147483648 | bytes 13631488 | tf_op jit(solution)/shard_map/last_part/pallas_call | solution.py:178
  127.5 6.8 %all-to-all-start = ((bf16[32,16,1024]{2,1,0:T(8,128)(2,1)}), bf16[32,16,1024]{2,1,0:T(8,128)(2,1)S(1)}, u32[]{:S(2)}, u32[]{:S(2)}) async-start(bf16[32,16,1024]{2,1,0:T(8,128)(2,1)} %bitcast.60), calls=%async_computation | async-start | bytes 2097152 | tf_op jit(solution)/shard_map/all_to_all | solution.py:570
  134.3 0.8 copy.12.a_ref
  135.2 0.7 fusion.9.ai_ref
  135.9 0.3 fusion.35
  136.2 0.7 pad_maximum_fusion.6
  136.9 0.6 fusion.15
  137.5 0.7 pad_maximum_fusion.5.tw_hbm
  138.2 2.5 %filter_part.1 = (f32[64,1024]{1,0:T(8,128)}, bf16[256,256]{1,0:T(8,128)(2,1)}) custom-call(s32[1]{0:T(128)} %bitcast.19.z_ref, bf16[32,160,512]{2,1,0:T(8,128)(2,1)} %bitcast.61, f32[2,64,64]{2,1,0:T(8,128)} %get-tuple-element.97.cs_ref, f32[2,64,64]{2,1,0:T(8,128)} %get-tuple-element.98.twist_ref), custom_call_target="tpu_custom_call" | custom-call | flops 1000000000 | bytes 1048576 | tf_op jit(solution)/shard_map/filter_part/pallas_call | solution.py:333
  140.7 11.3 %all-to-all-done.x_ref = bf16[32,16,1024]{2,1,0:T(8,128)(2,1)S(1)} async-done(((bf16[32,16,1024]{2,1,0:T(8,128)(2,1)}), bf16[32,16,1024]{2,1,0:T(8,128)(2,1)S(1)}, u32[]{:S(2)}, u32[]{:S(2)}) %all-to-all-start) | async-done | bytes 1048608 | tf_op jit(solution)/shard_map/all_to_all | solution.py:570
  152.0 1.0 copy-done.4
  153.0 13.4 %long_conv.1 = bf16[32,16,1024]{2,1,0:T(8,128)(2,1)} custom-call(bf16[32,16,1024]{2,1,0:T(8,128)(2,1)} %copy-done.4, bf16[512,1024]{1,0:T(8,128)(2,1)} %constant.193.clone.fwd_hbm, bf16[1024,512]{1,0:T(8,128)(2,1)} %constant.194.clone.inv_hbm, f32[64,1024]{1,0:T(8,128)} %pad_maximum_fusion.5.tw_hbm, bf16[256,256]{1,0:T(8,128)(2,1)} %copy.12.a_ref, ...), custom_call_target="tpu_custom_call" | custom-call | flops 8000000000 | bytes 8388608 | tf_op jit(solution)/shard_map/long_conv/pallas_call | solution.py:435
  166.4 4.4 %all-to-all-start.1 = ((bf16[32,16,1024]{2,1,0:T(8,128)(2,1)}), bf16[32,16,1024]{2,1,0:T(8,128)(2,1)S(1)}, u32[]{:S(2)}, u32[]{:S(2)}) async-start(bf16[32,16,1024]{2,1,0:T(8,128)(2,1)} %long_conv.1), calls=%async_computation.1 | async-start | bytes 2097152 | tf_op jit(solution)/shard_map/all_to_all | solution.py:578
  170.9 10.0 %gate_part.1 = bf16[512,1024]{1,0:T(8,128)(2,1)} custom-call(bf16[512,4096]{1,0:T(8,128)(2,1)} %bitcast.59, bf16[512,4096]{1,0:T(8,128)(2,1)} %collective-permute-done.3.other_ref, bf16[32,160,512]{2,1,0:T(8,128)(2,1)} %bitcast.62), custom_call_target="tpu_custom_call" | custom-call | flops 4294967296 | bytes 13631488 | tf_op jit(solution)/shard_map/gate_part/pallas_call | solution.py:209
  180.9 6.1 %all-to-all-done.1 = bf16[32,16,1024]{2,1,0:T(8,128)(2,1)S(1)} async-done(((bf16[32,16,1024]{2,1,0:T(8,128)(2,1)}), bf16[32,16,1024]{2,1,0:T(8,128)(2,1)S(1)}, u32[]{:S(2)}, u32[]{:S(2)}) %all-to-all-start.1) | async-done | bytes 1048608 | tf_op jit(solution)/shard_map/all_to_all | solution.py:578
  187.1 1.7 fusion.1
  188.9 2.8 %collective-permute-start.19 = (bf16[512,256]{1,0:T(8,128)(2,1)S(1)}, bf16[512,256]{1,0:T(8,128)(2,1)S(1)}, u32[]{:S(2)}, u32[]{:S(2)}) collective-permute-start(bf16[512,256]{1,0:T(8,128)(2,1)S(1)} %get-tuple-element.63), channel_id=1, source_target_pairs={{0,2},{2,0},{4,6},{6,4},{8,10},{10,8},{12,14},{14,12},{16,18},{18,... | collective-permute-start | bytes 786440 | tf_op jit(solution)/shard_map/ppermute | solution.py:35
  191.7 0.7 collective-permute-start.20
  192.5 1.0 collective-permute-start.21
  193.6 0.8 pad_maximum_fusion.2.here
  194.4 7.5 %mix_part.1.total_ref = f32[256,4096]{1,0:T(8,128)} custom-call(bf16[1024,256]{1,0:T(8,128)(2,1)} %pad_maximum_fusion.2.here, bf16[1024,4096]{1,0:T(8,128)(2,1)} %w_here.1), custom_call_target="tpu_custom_call" | custom-call | flops 2147483648 | bytes 12582912 | tf_op jit(solution)/shard_map/mix_part/pallas_call | solution.py:266
  201.9 3.5 %collective-permute-done.21.far_h = bf16[512,256]{1,0:T(8,128)(2,1)S(1)} collective-permute-done((bf16[512,256]{1,0:T(8,128)(2,1)S(1)}, bf16[512,256]{1,0:T(8,128)(2,1)S(1)}, u32[]{:S(2)}, u32[]{:S(2)}) %collective-permute-start.21) | collective-permute-done | bytes 262176 | tf_op jit(solution)/shard_map/ppermute | solution.py:596
  205.4 0.7 copy-done.10
  206.1 8.0 %mix_more.1 = bf16[256,4096]{1,0:T(8,128)(2,1)} custom-call(f32[256,4096]{1,0:T(8,128)} %mix_part.1.total_ref, bf16[512,256]{1,0:T(8,128)(2,1)} %copy-done.9, bf16[512,256]{1,0:T(8,128)(2,1)} %copy-done.10, bf16[512,4096]{1,0:T(8,128)(2,1)} %collective-permute-done.22.w_near, bf16[512,4096]{1,0:T(8,128)(2,1)} %collective-permute-done.23.w_far), custom_call_target="tpu_custom_call" | custom-call | flops 2147483648 | bytes 12582912 | tf_op jit(solution)/shard_map/mix_more/pallas_call | solution.py:266
  (65 shorter events, 1.6 us)
Async XLA Ops:
  6.5 131.6 %all-gather.3.cloned.1.call-start = ((), (), s32[]{:S(2)}) async-start(), calls=%async_computation.2 | async-start | bytes 5406720 | tf_op jit(solution)/shard_map/all_gather | solution.py:535
  7.6 3.1 %collective-permute-start.4 = (bf16[32,256]{1,0:T(8,128)(2,1)S(1)}, bf16[32,256]{1,0:T(8,128)(2,1)S(1)}, u32[]{:S(2)}, u32[]{:S(2)}) collective-permute-start(bf16[32,256]{1,0:T(8,128)(2,1)S(1)} %pad_maximum_fusion.8), channel_id=1, source_target_pairs={{0,2},{2,0},{4,6},{6,4},{8,10},{10,8},{12,14},{14,12},{16,18},{18,... | collective-permute-start | bytes 49160 | tf_op jit(solution)/shard_map/ppermute | solution.py:35
  10.1 1.5 collective-permute-start
  10.3 12.4 %collective-permute-start.3 = (bf16[512,4096]{1,0:T(8,128)(2,1)}, bf16[512,4096]{1,0:T(8,128)(2,1)}, u32[]{:S(2)}, u32[]{:S(2)}) collective-permute-start(bf16[512,4096]{1,0:T(8,128)(2,1)} %bitcast.56), channel_id=1, source_target_pairs={{0,2},{2,0},{4,6},{6,4},{8,10},{10,8},{12,14},{14,12},{16,18},{18,... | collective-permute-start | bytes 12582920 | tf_op jit(solution)/shard_map/ppermute | solution.py:35
  12.4 7.5 %collective-permute-start.2 = (bf16[128,512]{1,0:T(8,128)(2,1)S(1)}, bf16[128,512]{1,0:T(8,128)(2,1)S(1)}, u32[]{:S(2)}, u32[]{:S(2)}) collective-permute-start(bf16[128,512]{1,0:T(8,128)(2,1)S(1)} %bitcast.65), channel_id=1, source_target_pairs={{0,66},{2,64},{4,70},{6,68},{8,74},{10,72},{12,78},{14,76},{16,82}... | collective-permute-start | bytes 393224 | tf_op jit(solution)/shard_map/ppermute | solution.py:35
  16.2 6.3 %collective-permute-start.1 = (bf16[128,512]{1,0:T(8,128)(2,1)S(1)}, bf16[128,512]{1,0:T(8,128)(2,1)S(1)}, u32[]{:S(2)}, u32[]{:S(2)}) collective-permute-start(bf16[128,512]{1,0:T(8,128)(2,1)S(1)} %bitcast.66), channel_id=1, source_target_pairs={{0,64},{2,66},{4,68},{6,70},{8,72},{10,74},{12,76},{14,78},{16,80}... | collective-permute-start | bytes 393224 | tf_op jit(solution)/shard_map/ppermute | solution.py:35
  22.6 8.8 %collective-permute-start.7 = (bf16[256,512]{1,0:T(8,128)(2,1)S(1)}, bf16[256,512]{1,0:T(8,128)(2,1)S(1)}, u32[]{:S(2)}, u32[]{:S(2)}) collective-permute-start(bf16[256,512]{1,0:T(8,128)(2,1)S(1)} %get-tuple-element.32), channel_id=1, source_target_pairs={{0,4},{2,6},{4,8},{6,10},{8,12},{10,14},{12,0},{14,2},{16,20},{18,... | collective-permute-start | bytes 786440 | tf_op jit(solution)/shard_map/ppermute | solution.py:35
  23.9 14.8 %collective-permute-start.6 = (bf16[256,512]{1,0:T(8,128)(2,1)S(1)}, bf16[256,512]{1,0:T(8,128)(2,1)S(1)}, u32[]{:S(2)}, u32[]{:S(2)}) collective-permute-start(bf16[256,512]{1,0:T(8,128)(2,1)S(1)} %get-tuple-element.32), channel_id=1, source_target_pairs={{0,8},{2,10},{4,12},{6,14},{8,0},{10,2},{12,4},{14,6},{16,24},{18,... | collective-permute-start | bytes 786440 | tf_op jit(solution)/shard_map/ppermute | solution.py:35
  26.4 12.8 %collective-permute-start.5 = (bf16[256,512]{1,0:T(8,128)(2,1)S(1)}, bf16[256,512]{1,0:T(8,128)(2,1)S(1)}, u32[]{:S(2)}, u32[]{:S(2)}) collective-permute-start(bf16[256,512]{1,0:T(8,128)(2,1)S(1)} %get-tuple-element.32), channel_id=1, source_target_pairs={{0,12},{2,14},{4,0},{6,2},{8,4},{10,6},{12,8},{14,10},{16,28},{18,... | collective-permute-start | bytes 786440 | tf_op jit(solution)/shard_map/ppermute | solution.py:35
  27.5 12.7 %collective-permute-start.10 = (bf16[256,512]{1,0:T(8,128)(2,1)S(1)}, bf16[256,512]{1,0:T(8,128)(2,1)S(1)}, u32[]{:S(2)}, u32[]{:S(2)}) collective-permute-start(bf16[256,512]{1,0:T(8,128)(2,1)S(1)} %get-tuple-element.33), channel_id=1, source_target_pairs={{0,16},{2,18},{4,20},{6,22},{8,24},{10,26},{12,28},{14,30},{16,32}... | collective-permute-start | bytes 786440 | tf_op jit(solution)/shard_map/ppermute | solution.py:35
  28.8 14.1 %collective-permute-start.9 = (bf16[256,512]{1,0:T(8,128)(2,1)S(1)}, bf16[256,512]{1,0:T(8,128)(2,1)S(1)}, u32[]{:S(2)}, u32[]{:S(2)}) collective-permute-start(bf16[256,512]{1,0:T(8,128)(2,1)S(1)} %get-tuple-element.33), channel_id=1, source_target_pairs={{0,32},{2,34},{4,36},{6,38},{8,40},{10,42},{12,44},{14,46},{16,48}... | collective-permute-start | bytes 786440 | tf_op jit(solution)/shard_map/ppermute | solution.py:35
  31.4 11.5 %collective-permute-start.8 = (bf16[256,512]{1,0:T(8,128)(2,1)S(1)}, bf16[256,512]{1,0:T(8,128)(2,1)S(1)}, u32[]{:S(2)}, u32[]{:S(2)}) collective-permute-start(bf16[256,512]{1,0:T(8,128)(2,1)S(1)} %get-tuple-element.33), channel_id=1, source_target_pairs={{0,48},{2,50},{4,52},{6,54},{8,56},{10,58},{12,60},{14,62},{16,0},... | collective-permute-start | bytes 786440 | tf_op jit(solution)/shard_map/ppermute | solution.py:35
  38.5 13.5 %copy-start.12 = (s32[32]{0:T(128)S(1)}, s32[32]{0:T(128)}, u32[]{:S(2)}) copy-start(s32[32]{0:T(128)} %constant.192.clone) | copy-start | bytes 388
  38.5 13.5 %copy-start.13 = (s32[32]{0:T(128)S(1)}, s32[32]{0:T(128)}, u32[]{:S(2)}) copy-start(s32[32]{0:T(128)} %constant.191.clone) | copy-start | bytes 388
  38.5 13.5 %copy-start.14 = (s32[32]{0:T(128)S(1)}, s32[32]{0:T(128)}, u32[]{:S(2)}) copy-start(s32[32]{0:T(128)} %constant.190.clone) | copy-start | bytes 388
  44.0 73.8 %collective-permute-start.22 = (bf16[512,4096]{1,0:T(8,128)(2,1)}, bf16[512,4096]{1,0:T(8,128)(2,1)}, u32[]{:S(2)}, u32[]{:S(2)}) collective-permute-start(bf16[512,4096]{1,0:T(8,128)(2,1)} %constant_dynamic-slice_fusion.3), channel_id=1, source_target_pairs={{0,1},{1,0},{2,67},{3,66},{4,5},{5,4},{6,71},{7,70},{8,9},{9,8},{1... | collective-permute-start | bytes 12582920 | tf_op jit(solution)/shard_map/ppermute | solution.py:565
  47.7 36.3 %collective-permute-start.11 = (bf16[1024,512]{1,0:T(8,128)(2,1)}, bf16[1024,512]{1,0:T(8,128)(2,1)S(1)}, u32[]{:S(2)}, u32[]{:S(2)}) collective-permute-start(bf16[1024,512]{1,0:T(8,128)(2,1)} %pad_maximum_fusion.key_line), channel_id=1, source_target_pairs={{0,48},{2,50},{4,52},{6,54},{8,56},{10,58},{12,60},{14,62},{16,0},... | collective-permute-start | bytes 3145736 | tf_op jit(solution)/shard_map/ppermute | solution.py:35
  50.2 36.5 %collective-permute-start.12 = (bf16[1024,512]{1,0:T(8,128)(2,1)}, bf16[1024,512]{1,0:T(8,128)(2,1)S(1)}, u32[]{:S(2)}, u32[]{:S(2)}) collective-permute-start(bf16[1024,512]{1,0:T(8,128)(2,1)} %pad_maximum_fusion.key_line), channel_id=1, source_target_pairs={{0,16},{2,18},{4,20},{6,22},{8,24},{10,26},{12,28},{14,30},{16,32}... | collective-permute-start | bytes 3145736 | tf_op jit(solution)/shard_map/ppermute | solution.py:35
  50.5 36.1 %collective-permute-start.13 = (bf16[1024,512]{1,0:T(8,128)(2,1)}, bf16[1024,512]{1,0:T(8,128)(2,1)S(1)}, u32[]{:S(2)}, u32[]{:S(2)}) collective-permute-start(bf16[1024,512]{1,0:T(8,128)(2,1)} %pad_maximum_fusion.1.value_line), channel_id=1, source_target_pairs={{0,12},{2,14},{4,0},{6,2},{8,4},{10,6},{12,8},{14,10},{16,28},{18,... | collective-permute-start | bytes 3145736 | tf_op jit(solution)/shard_map/ppermute | solution.py:35
  50.5 36.1 %collective-permute-start.14 = (bf16[1024,512]{1,0:T(8,128)(2,1)}, bf16[1024,512]{1,0:T(8,128)(2,1)}, u32[]{:S(2)}, u32[]{:S(2)}) collective-permute-start(bf16[1024,512]{1,0:T(8,128)(2,1)} %pad_maximum_fusion.1.value_line), channel_id=1, source_target_pairs={{0,4},{2,6},{4,8},{6,10},{8,12},{10,14},{12,0},{14,2},{16,20},{18,... | collective-permute-start | bytes 3145736 | tf_op jit(solution)/shard_map/ppermute | solution.py:35
  83.9 2.7 %copy-start.1 = (bf16[1024,512]{1,0:T(8,128)(2,1)}, bf16[1024,512]{1,0:T(8,128)(2,1)S(1)}, u32[]{:S(2)}) copy-start(bf16[1024,512]{1,0:T(8,128)(2,1)S(1)} %collective-permute-done.11.k1.refs_0_) | copy-start | bytes 3145732
  86.7 1.0 copy-start.2
  86.7 1.3 copy-start.3
  90.6 28.4 %collective-permute-start.15 = (bf16[512,512]{1,0:T(8,128)(2,1)}, bf16[512,512]{1,0:T(8,128)(2,1)S(1)}, u32[]{:S(2)}, u32[]{:S(2)}) collective-permute-start(bf16[512,512]{1,0:T(8,128)(2,1)} %get-tuple-element.50), channel_id=1, source_target_pairs={{0,48},{2,50},{4,52},{6,54},{8,56},{10,58},{12,60},{14,62},{16,0},... | collective-permute-start | bytes 1572872 | tf_op jit(solution)/shard_map/ppermute | solution.py:35
  90.9 28.1 %collective-permute-start.16 = (bf16[512,512]{1,0:T(8,128)(2,1)}, bf16[512,512]{1,0:T(8,128)(2,1)S(1)}, u32[]{:S(2)}, u32[]{:S(2)}) collective-permute-start(bf16[512,512]{1,0:T(8,128)(2,1)} %get-tuple-element.51), channel_id=1, source_target_pairs={{0,16},{2,18},{4,20},{6,22},{8,24},{10,26},{12,28},{14,30},{16,32}... | collective-permute-start | bytes 1572872 | tf_op jit(solution)/shard_map/ppermute | solution.py:35
  92.1 26.9 %collective-permute-start.17 = (bf16[512,512]{1,0:T(8,128)(2,1)}, bf16[512,512]{1,0:T(8,128)(2,1)S(1)}, u32[]{:S(2)}, u32[]{:S(2)}) collective-permute-start(bf16[512,512]{1,0:T(8,128)(2,1)} %get-tuple-element.52), channel_id=1, source_target_pairs={{0,12},{2,14},{4,0},{6,2},{8,4},{10,6},{12,8},{14,10},{16,28},{18,... | collective-permute-start | bytes 1572872 | tf_op jit(solution)/shard_map/ppermute | solution.py:35
  92.1 27.0 %collective-permute-start.18 = (bf16[512,512]{1,0:T(8,128)(2,1)}, bf16[512,512]{1,0:T(8,128)(2,1)S(1)}, u32[]{:S(2)}, u32[]{:S(2)}) collective-permute-start(bf16[512,512]{1,0:T(8,128)(2,1)} %get-tuple-element.53), channel_id=1, source_target_pairs={{0,4},{2,6},{4,8},{6,10},{8,12},{10,14},{12,0},{14,2},{16,20},{18,... | collective-permute-start | bytes 1572872 | tf_op jit(solution)/shard_map/ppermute | solution.py:35
  117.8 87.6 %collective-permute-start.23 = (bf16[512,4096]{1,0:T(8,128)(2,1)}, bf16[512,4096]{1,0:T(8,128)(2,1)}, u32[]{:S(2)}, u32[]{:S(2)}) collective-permute-start(bf16[512,4096]{1,0:T(8,128)(2,1)} %collective-permute-done.22.w_near), channel_id=1, source_target_pairs={{0,2},{2,0},{4,6},{6,4},{8,10},{10,8},{12,14},{14,12},{16,18},{18,... | collective-permute-start | bytes 12582920 | tf_op jit(solution)/shard_map/ppermute | solution.py:35
  119.0 0.8 copy-start.5
  119.0 1.0 copy-start.6
  119.0 1.1 copy-start.7
  119.0 1.3 copy-start.8
  127.5 24.5 %all-to-all-start = ((bf16[32,16,1024]{2,1,0:T(8,128)(2,1)}), bf16[32,16,1024]{2,1,0:T(8,128)(2,1)S(1)}, u32[]{:S(2)}, u32[]{:S(2)}) async-start(bf16[32,16,1024]{2,1,0:T(8,128)(2,1)} %bitcast.60), calls=%async_computation | async-start | bytes 2097152 | tf_op jit(solution)/shard_map/all_to_all | solution.py:570
  152.0 1.0 copy-start.4
  166.4 4.4 %copy-start.11 = (f32[1024]{0:T(1024)S(1)}, f32[1024]{0:T(1024)}, u32[]{:S(2)}) copy-start(f32[1024]{0:T(1024)} %param.13) | copy-start | bytes 12292
  166.4 20.6 %all-to-all-start.1 = ((bf16[32,16,1024]{2,1,0:T(8,128)(2,1)}), bf16[32,16,1024]{2,1,0:T(8,128)(2,1)S(1)}, u32[]{:S(2)}, u32[]{:S(2)}) async-start(bf16[32,16,1024]{2,1,0:T(8,128)(2,1)} %long_conv.1), calls=%async_computation.1 | async-start | bytes 2097152 | tf_op jit(solution)/shard_map/all_to_all | solution.py:578
  170.9 16.1 %copy-start = (bf16[512,1024]{1,0:T(8,128)(2,1)S(1)}, bf16[512,1024]{1,0:T(8,128)(2,1)}, u32[]{:S(2)}) copy-start(bf16[512,1024]{1,0:T(8,128)(2,1)} %last_part.1) | copy-start | bytes 3145732
  188.9 4.5 %collective-permute-start.19 = (bf16[512,256]{1,0:T(8,128)(2,1)S(1)}, bf16[512,256]{1,0:T(8,128)(2,1)S(1)}, u32[]{:S(2)}, u32[]{:S(2)}) collective-permute-start(bf16[512,256]{1,0:T(8,128)(2,1)S(1)} %get-tuple-element.63), channel_id=1, source_target_pairs={{0,2},{2,0},{4,6},{6,4},{8,10},{10,8},{12,14},{14,12},{16,18},{18,... | collective-permute-start | bytes 786440 | tf_op jit(solution)/shard_map/ppermute | solution.py:35
  191.7 10.2 %collective-permute-start.20 = (bf16[512,256]{1,0:T(8,128)(2,1)S(1)}, bf16[512,256]{1,0:T(8,128)(2,1)S(1)}, u32[]{:S(2)}, u32[]{:S(2)}) collective-permute-start(bf16[512,256]{1,0:T(8,128)(2,1)S(1)} %get-tuple-element.62), channel_id=1, source_target_pairs={{0,1},{1,0},{2,3},{3,2},{4,5},{5,4},{6,7},{7,6},{8,9},{9,8},{10,11... | collective-permute-start | bytes 786440 | tf_op jit(solution)/shard_map/ppermute | solution.py:591
  192.5 12.9 %collective-permute-start.21 = (bf16[512,256]{1,0:T(8,128)(2,1)S(1)}, bf16[512,256]{1,0:T(8,128)(2,1)S(1)}, u32[]{:S(2)}, u32[]{:S(2)}) collective-permute-start(bf16[512,256]{1,0:T(8,128)(2,1)S(1)} %get-tuple-element.61), channel_id=1, source_target_pairs={{0,3},{1,2},{2,1},{3,0},{4,7},{5,6},{6,5},{7,4},{8,11},{9,10},{10,... | collective-permute-start | bytes 786440 | tf_op jit(solution)/shard_map/ppermute | solution.py:596
  201.9 3.5 %copy-start.9 = (bf16[512,256]{1,0:T(8,128)(2,1)}, bf16[512,256]{1,0:T(8,128)(2,1)S(1)}, u32[]{:S(2)}) copy-start(bf16[512,256]{1,0:T(8,128)(2,1)S(1)} %collective-permute-done.20.near_h) | copy-start | bytes 786436
  205.4 0.7 copy-start.10
Sparse Core Ops, SparseCore 0:
  12.5 105.7 all-gather.2

commit v8 on v7

--- a/solution.py
+++ b/solution.py
@@ -563,11 +563,12 @@
         for th in range(2):
             perm.append((t * 2 + th, index_of(tz ^ tc, ty, tx, tc) * 2 + 1 - th))
     ow_same = lax.ppermute(ow_part, ("seq", "ch"), perm)
-    ow_cross = send(ow_same, dc=1)
 
     source = last_part(totals, first[2:], last_lines)
     packed = source.reshape(CHIPS, chan // CHIPS, 2 * rows)
     mine_ch = lax.all_to_all(packed, "seq", 0, 0, axis_index_groups=SAME_CORE)
+    mine_ch, ow_same = lax.optimization_barrier((mine_ch, ow_same))
+    ow_cross = send(ow_same, dc=1)
 
     tw, a, ai, cs, twist = column_tables(core, rows, cols, padded)
     f, m = filter_part(z, gathered, cs, twist)

time: 222 us -> 215 us (0.968)
  waiting for transfers between devices: 67.3 us -> 64 us
    ppermute x1, waiting for transfers between devices: 12.2 us -> 0.01 us  [per_device(): ow_same = lax.ppermute(ow_part, ('seq', 'ch'), perm)]
    all_to_all x1, waiting for transfers between devices: 11.3 us -> 16 us  [per_device(): mine_ch = lax.all_to_all(packed, 'seq', 0, 0, axis_index_groups=SAME_CORE)]
    all_to_all x1, starting transfers between devices: 6.77 us -> 3.93 us  [per_device(): mine_ch = lax.all_to_all(packed, 'seq', 0, 0, axis_index_groups=SAME_CORE)]
    ppermute x21, waiting for transfers between devices: 34.2 us -> 37 us  [send(): return lax.ppermute(value, 'seq', perm)]
  transfers between devices with their start and end apart: 27 -> 27, of which waited for: 12 -> 15; matrix products, arithmetic and copies ran while one was open for 7% -> 8% of each run, Pallas kernels for 30% -> 31%
where the time goes in v8:
time: 215 us; the launch traced here: 214 us
  Pallas kernels  73.6 us (34%)
  waiting for transfers between devices  64 us (30%)
  starting transfers between devices  42.9 us (20%)
  between operations  13.6 us (6%)
  local copies, waits for them, and re-layouts  10.6 us (5%)
  other arithmetic  9.58 us (4%)
    ppermute x21, waiting for transfers between devices, send(): return lax.ppermute(value, 'seq', perm)  37 us
    ppermute x21, starting transfers between devices, send(): return lax.ppermute(value, 'seq', perm)  29.1 us
    pallas_call x2, Pallas kernels, sum_part(): pl.pallas_call(kernel, grid_spec=pltpu.PrefetchScalarGridSpec(num_scalar_...  22 us
    all_to_all x1, waiting for transfers between devices, per_device(): mine_ch = lax.all_to_all(packed, 'seq', 0, 0, axis_index_groups=SAME_CORE)  16 us
    pallas_call x2, Pallas kernels, mix_part(): pl.pallas_call(mix_kernel if total is None else mix_more_kernel, grid=(4,...  15.5 us
    pallas_call x1, Pallas kernels, long_conv(): pl.pallas_call(conv_kernel, in_specs=[vmem, hbm, hbm, hbm, vmem, vmem, vm...  13.4 us
    pallas_call x1, Pallas kernels, gate_part(): pl.pallas_call(gate_kernel, grid=(4,), in_specs=[pl.BlockSpec((tile, widt...  10 us
    pallas_call x1, Pallas kernels, last_part(): pl.pallas_call(last_kernel, grid=(4,), in_specs=[pl.BlockSpec((tile, chan...  7.54 us
  transfers between devices with their start and end apart: 27, of which 15 were waited for; matrix products, arithmetic and copies ran while one was open for 8% of the time, Pallas kernels for 31%

profile of v8, /device:TPU:1, one launch (start us, length us, event | category | flops | bytes accessed | tf_op | source)
XLA Modules:
  0.0 214.2 jit_solution(6707027864389316678)
XLA Ops:
  6.5 0.9 copy.11
  7.6 1.5 collective-permute-start.4
  9.1 1.0 dynamic-slice_bitcast_fusion
  10.3 0.5 collective-permute-start.3
  10.7 0.9 collective-permute-done
  11.7 0.7 maximum_maximum_fusion
  12.4 3.8 %collective-permute-start.2 = (bf16[128,512]{1,0:T(8,128)(2,1)S(1)}, bf16[128,512]{1,0:T(8,128)(2,1)S(1)}, u32[]{:S(2)}, u32[]{:S(2)}) collective-permute-start(bf16[128,512]{1,0:T(8,128)(2,1)S(1)} %bitcast.65), channel_id=1, source_target_pairs={{0,66},{2,64},{4,70},{6,68},{8,74},{10,72},{12,78},{14,76},{16,82}... | collective-permute-start | bytes 393224 | tf_op jit(solution)/shard_map/ppermute | solution.py:35
  16.3 3.6 %collective-permute-done.2 = bf16[128,512]{1,0:T(8,128)(2,1)S(1)} collective-permute-done((bf16[128,512]{1,0:T(8,128)(2,1)S(1)}, bf16[128,512]{1,0:T(8,128)(2,1)S(1)}, u32[]{:S(2)}, u32[]{:S(2)}) %collective-permute-start.2) | collective-permute-done | bytes 131104 | tf_op jit(solution)/shard_map/ppermute | solution.py:35
  19.9 2.6 %collective-permute-done.1 = bf16[128,512]{1,0:T(8,128)(2,1)S(1)} collective-permute-done((bf16[128,512]{1,0:T(8,128)(2,1)S(1)}, bf16[128,512]{1,0:T(8,128)(2,1)S(1)}, u32[]{:S(2)}, u32[]{:S(2)}) %collective-permute-start.1) | collective-permute-done | bytes 131104 | tf_op jit(solution)/shard_map/ppermute | solution.py:35
  22.6 1.3 collective-permute-start.7
  23.9 2.5 %collective-permute-start.6 = (bf16[256,512]{1,0:T(8,128)(2,1)S(1)}, bf16[256,512]{1,0:T(8,128)(2,1)S(1)}, u32[]{:S(2)}, u32[]{:S(2)}) collective-permute-start(bf16[256,512]{1,0:T(8,128)(2,1)S(1)} %get-tuple-element.34), channel_id=1, source_target_pairs={{0,8},{2,10},{4,12},{6,14},{8,0},{10,2},{12,4},{14,6},{16,24},{18,... | collective-permute-start | bytes 786440 | tf_op jit(solution)/shard_map/ppermute | solution.py:35
  26.4 1.2 collective-permute-start.5
  27.5 1.3 collective-permute-start.10
  28.8 2.6 %collective-permute-start.9 = (bf16[256,512]{1,0:T(8,128)(2,1)S(1)}, bf16[256,512]{1,0:T(8,128)(2,1)S(1)}, u32[]{:S(2)}, u32[]{:S(2)}) collective-permute-start(bf16[256,512]{1,0:T(8,128)(2,1)S(1)} %get-tuple-element.35), channel_id=1, source_target_pairs={{0,32},{2,34},{4,36},{6,38},{8,40},{10,42},{12,44},{14,46},{16,48}... | collective-permute-start | bytes 786440 | tf_op jit(solution)/shard_map/ppermute | solution.py:35
  31.4 2.4 %collective-permute-start.8 = (bf16[256,512]{1,0:T(8,128)(2,1)S(1)}, bf16[256,512]{1,0:T(8,128)(2,1)S(1)}, u32[]{:S(2)}, u32[]{:S(2)}) collective-permute-start(bf16[256,512]{1,0:T(8,128)(2,1)S(1)} %get-tuple-element.35), channel_id=1, source_target_pairs={{0,48},{2,50},{4,52},{6,54},{8,56},{10,58},{12,60},{14,62},{16,0},... | collective-permute-start | bytes 786440 | tf_op jit(solution)/shard_map/ppermute | solution.py:35
  33.9 4.7 %constant_dynamic-slice_fusion.3 = bf16[512,4096]{1,0:T(8,128)(2,1)} fusion(bf16[1024,4096]{1,0:T(8,128)(2,1)} %w_here.1, s32[]{:T(128)S(6)} %select_n.230), kind=kLoop, calls=%fused_computation.104 | loop fusion | bytes 8388612 | tf_op jit(solution)/shard_map/dynamic_slice | solution.py:538
  38.5 0.2 collective-permute-done.6
  38.7 0.4 collective-permute-done.5
  39.1 1.1 pad_maximum_fusion.key_line
  40.2 2.7 %collective-permute-done.9 = bf16[256,512]{1,0:T(8,128)(2,1)S(1)} collective-permute-done((bf16[256,512]{1,0:T(8,128)(2,1)S(1)}, bf16[256,512]{1,0:T(8,128)(2,1)S(1)}, u32[]{:S(2)}, u32[]{:S(2)}) %collective-permute-start.9) | collective-permute-done | bytes 262176 | tf_op jit(solution)/shard_map/ppermute | solution.py:35
  42.9 1.1 pad_maximum_fusion.1.value_line
  44.0 3.7 %collective-permute-start.19 = (bf16[512,4096]{1,0:T(8,128)(2,1)}, bf16[512,4096]{1,0:T(8,128)(2,1)}, u32[]{:S(2)}, u32[]{:S(2)}) collective-permute-start(bf16[512,4096]{1,0:T(8,128)(2,1)} %constant_dynamic-slice_fusion.3), channel_id=1, source_target_pairs={{0,1},{1,0},{2,67},{3,66},{4,5},{5,4},{6,71},{7,70},{8,9},{9,8},{1... | collective-permute-start | bytes 12582920 | tf_op jit(solution)/shard_map/ppermute | solution.py:565
  47.7 2.5 %collective-permute-start.11 = (bf16[1024,512]{1,0:T(8,128)(2,1)}, bf16[1024,512]{1,0:T(8,128)(2,1)S(1)}, u32[]{:S(2)}, u32[]{:S(2)}) collective-permute-start(bf16[1024,512]{1,0:T(8,128)(2,1)} %pad_maximum_fusion.key_line), channel_id=1, source_target_pairs={{0,48},{2,50},{4,52},{6,54},{8,56},{10,58},{12,60},{14,62},{16,0},... | collective-permute-start | bytes 3145736 | tf_op jit(solution)/shard_map/ppermute | solution.py:35
  50.2 0.4 collective-permute-start.12
  50.5 1.5 collective-permute-start.14
  52.0 0.6 pad_add_fusion.order_ref
  52.6 10.3 %first_part.1 = (f32[1024,512]{1,0:T(8,128)}, f32[1024,512]{1,0:T(8,128)}, bf16[1024,1024]{1,0:T(8,128)(2,1)}, bf16[1024,1024]{1,0:T(8,128)(2,1)}) custom-call(s32[2,32]{1,0:T(2,128)} %pad_add_fusion.order_ref, bf16[512,4096]{1,0:T(8,128)(2,1)} %bitcast.57, bf16[512,4096]{1,0:T(8,128)(2,1)} %collective-permute-done.3.other_ref, ...), custom_call_target="tpu_custom_call" | custom-call | flops 2147483648 | bytes 18874368 | tf_op jit(solution)/shard_map/first_part/pallas_call | solution.py:117
  62.9 21.1 %collective-permute-done.11.k1.refs_0_ = bf16[1024,512]{1,0:T(8,128)(2,1)S(1)} collective-permute-done((bf16[1024,512]{1,0:T(8,128)(2,1)}, bf16[1024,512]{1,0:T(8,128)(2,1)S(1)}, u32[]{:S(2)}, u32[]{:S(2)}) %collective-permute-start.11) | collective-permute-done | bytes 1048608 | tf_op jit(solution)/shard_map/ppermute | solution.py:35
  84.0 2.7 %collective-permute-done.12.k3.refs_1_ = bf16[1024,512]{1,0:T(8,128)(2,1)S(1)} collective-permute-done((bf16[1024,512]{1,0:T(8,128)(2,1)}, bf16[1024,512]{1,0:T(8,128)(2,1)S(1)}, u32[]{:S(2)}, u32[]{:S(2)}) %collective-permute-start.12) | collective-permute-done | bytes 1048608 | tf_op jit(solution)/shard_map/ppermute | solution.py:35
  86.7 1.0 copy-done.2
  87.7 0.3 copy-done.3
  88.0 2.6 %cut_halves.1 = (bf16[512,512]{1,0:T(8,128)(2,1)}, bf16[512,512]{1,0:T(8,128)(2,1)}, bf16[512,512]{1,0:T(8,128)(2,1)}, bf16[512,512]{1,0:T(8,128)(2,1)}) custom-call(bf16[1024,512]{1,0:T(8,128)(2,1)} %copy-done.1, bf16[1024,512]{1,0:T(8,128)(2,1)} %copy-done.2, bf16[1024,512]{1,0:T(8,128)(2,1)} %copy-done.3, bf16[1024,512]{1,0:T(8,128)(2,1)} %collective-permute-done.14.v3.refs_3_), custom_call_target="tpu_custom_call" | custom-call | bytes 4194304 | tf_op jit(solution)/shard_map/cut_halves/pallas_call | solution.py:149
  90.6 0.3 collective-permute-start.15
  90.9 1.2 collective-permute-start.16
  92.1 1.5 collective-permute-start.18
  93.5 11.8 %second_part.1 = (f32[1024,512]{1,0:T(8,128)}, f32[1024,512]{1,0:T(8,128)}) custom-call(s32[2,32]{1,0:T(2,128)} %pad_add_fusion.order_ref, bf16[512,4096]{1,0:T(8,128)(2,1)} %bitcast.58, bf16[512,4096]{1,0:T(8,128)(2,1)} %collective-permute-done.3.other_ref, f32[1024,512]{1,0:T(8,128)} %get-tuple-element.42.key_in, f32[1024,512]{1,0:T(8,128)} %get-tuple-element.43.value_in, ...), custom_call_target="tpu_custom_call" | custom-call | flops 4294967296 | bytes 18874368 | tf_op jit(solution)/shard_map/second_part/pallas_call | solution.py:117
  105.3 0.7 collective-permute-done.15.ka
  106.0 1.1 collective-permute-done.16.kb
  107.3 0.8 collective-permute-done.18.vb
  108.2 0.8 copy-done.8
  108.9 7.5 %last_part.1 = bf16[512,1024]{1,0:T(8,128)(2,1)} custom-call(f32[1024,512]{1,0:T(8,128)} %get-tuple-element.48.key_ref, f32[1024,512]{1,0:T(8,128)} %get-tuple-element.49.value_ref, bf16[1024,1024]{1,0:T(8,128)(2,1)} %get-tuple-element.50.key_tok_ref, bf16[1024,1024]{1,0:T(8,128)(2,1)} %get-tuple-element.51.value_tok_ref, bf16[512,512]{1,0:T(8,128)(2,1)} %copy-done.5, ...), custom_call_target="tpu_custom_call" | custom-call | flops 2147483648 | bytes 13631488 | tf_op jit(solution)/shard_map/last_part/pallas_call | solution.py:178
  116.5 3.9 %all-to-all-start = ((bf16[32,16,1024]{2,1,0:T(8,128)(2,1)}), bf16[32,16,1024]{2,1,0:T(8,128)(2,1)S(1)}, u32[]{:S(2)}, u32[]{:S(2)}) async-start(bf16[32,16,1024]{2,1,0:T(8,128)(2,1)} %bitcast.60), calls=%async_computation | async-start | bytes 2097152 | tf_op jit(solution)/shard_map/all_to_all | solution.py:569
  120.4 0.2 fusion.38
  120.6 16.0 %all-to-all-done.x_ref = bf16[32,16,1024]{2,1,0:T(8,128)(2,1)S(1)} async-done(((bf16[32,16,1024]{2,1,0:T(8,128)(2,1)}), bf16[32,16,1024]{2,1,0:T(8,128)(2,1)S(1)}, u32[]{:S(2)}, u32[]{:S(2)}) %all-to-all-start) | async-done | bytes 1048608 | tf_op jit(solution)/shard_map/all_to_all | solution.py:569
  136.6 2.7 %collective-permute-start.23 = (bf16[512,4096]{1,0:T(8,128)(2,1)}, bf16[512,4096]{1,0:T(8,128)(2,1)}, u32[]{:S(2)}, u32[]{:S(2)}) collective-permute-start(bf16[512,4096]{1,0:T(8,128)(2,1)} %collective-permute-done.19.w_near), channel_id=1, source_target_pairs={{0,2},{2,0},{4,6},{6,4},{8,10},{10,8},{12,14},{14,12},{16,18},{18,... | collective-permute-start | bytes 12582920 | tf_op jit(solution)/shard_map/ppermute | solution.py:35
  139.5 0.8 copy.12.a_ref
  140.3 0.7 fusion.9.ai_ref
  141.0 0.3 fusion.35
  141.3 0.7 pad_maximum_fusion.6
  142.0 0.6 fusion.15
  142.6 0.7 pad_maximum_fusion.5.tw_hbm
  143.3 2.5 %filter_part.1 = (f32[64,1024]{1,0:T(8,128)}, bf16[256,256]{1,0:T(8,128)(2,1)}) custom-call(s32[1]{0:T(128)} %bitcast.19.z_ref, bf16[32,160,512]{2,1,0:T(8,128)(2,1)} %bitcast.61, f32[2,64,64]{2,1,0:T(8,128)} %get-tuple-element.101.cs_ref, f32[2,64,64]{2,1,0:T(8,128)} %get-tuple-element.102.twist_ref), custom_call_target="tpu_custom_call" | custom-call | flops 1000000000 | bytes 1048576 | tf_op jit(solution)/shard_map/filter_part/pallas_call | solution.py:333
  145.8 13.4 %long_conv.1 = bf16[32,16,1024]{2,1,0:T(8,128)(2,1)} custom-call(bf16[32,16,1024]{2,1,0:T(8,128)(2,1)} %copy-done.4, bf16[512,1024]{1,0:T(8,128)(2,1)} %constant.193.clone.fwd_hbm, bf16[1024,512]{1,0:T(8,128)(2,1)} %constant.194.clone.inv_hbm, f32[64,1024]{1,0:T(8,128)} %pad_maximum_fusion.5.tw_hbm, bf16[256,256]{1,0:T(8,128)(2,1)} %copy.12.a_ref, ...), custom_call_target="tpu_custom_call" | custom-call | flops 8000000000 | bytes 8388608 | tf_op jit(solution)/shard_map/long_conv/pallas_call | solution.py:435
  159.2 4.4 %all-to-all-start.1 = ((bf16[32,16,1024]{2,1,0:T(8,128)(2,1)}), bf16[32,16,1024]{2,1,0:T(8,128)(2,1)S(1)}, u32[]{:S(2)}, u32[]{:S(2)}) async-start(bf16[32,16,1024]{2,1,0:T(8,128)(2,1)} %long_conv.1), calls=%async_computation.1 | async-start | bytes 2097152 | tf_op jit(solution)/shard_map/all_to_all | solution.py:579
  163.7 10.0 %gate_part.1 = bf16[512,1024]{1,0:T(8,128)(2,1)} custom-call(bf16[512,4096]{1,0:T(8,128)(2,1)} %bitcast.59, bf16[512,4096]{1,0:T(8,128)(2,1)} %collective-permute-done.3.other_ref, bf16[32,160,512]{2,1,0:T(8,128)(2,1)} %bitcast.62), custom_call_target="tpu_custom_call" | custom-call | flops 4294967296 | bytes 13631488 | tf_op jit(solution)/shard_map/gate_part/pallas_call | solution.py:209
  173.7 7.4 %all-to-all-done.1 = bf16[32,16,1024]{2,1,0:T(8,128)(2,1)S(1)} async-done(((bf16[32,16,1024]{2,1,0:T(8,128)(2,1)}), bf16[32,16,1024]{2,1,0:T(8,128)(2,1)S(1)}, u32[]{:S(2)}, u32[]{:S(2)}) %all-to-all-start.1) | async-done | bytes 1048608 | tf_op jit(solution)/shard_map/all_to_all | solution.py:579
  181.1 1.7 fusion.1
  183.0 1.9 collective-permute-start.20
  184.9 1.7 collective-permute-start.22
  186.8 0.8 pad_maximum_fusion.2.here
  187.6 7.5 %mix_part.1.total_ref = f32[256,4096]{1,0:T(8,128)} custom-call(bf16[1024,256]{1,0:T(8,128)(2,1)} %pad_maximum_fusion.2.here, bf16[1024,4096]{1,0:T(8,128)(2,1)} %w_here.1), custom_call_target="tpu_custom_call" | custom-call | flops 2147483648 | bytes 12582912 | tf_op jit(solution)/shard_map/mix_part/pallas_call | solution.py:266
  195.1 3.5 %collective-permute-done.22.far_h = bf16[512,256]{1,0:T(8,128)(2,1)S(1)} collective-permute-done((bf16[512,256]{1,0:T(8,128)(2,1)S(1)}, bf16[512,256]{1,0:T(8,128)(2,1)S(1)}, u32[]{:S(2)}, u32[]{:S(2)}) %collective-permute-start.22) | collective-permute-done | bytes 262176 | tf_op jit(solution)/shard_map/ppermute | solution.py:597
  198.6 0.7 copy-done.10
  199.3 8.0 %mix_more.1 = bf16[256,4096]{1,0:T(8,128)(2,1)} custom-call(f32[256,4096]{1,0:T(8,128)} %mix_part.1.total_ref, bf16[512,256]{1,0:T(8,128)(2,1)} %copy-done.9, bf16[512,256]{1,0:T(8,128)(2,1)} %copy-done.10, bf16[512,4096]{1,0:T(8,128)(2,1)} %collective-permute-done.19.w_near, bf16[512,4096]{1,0:T(8,128)(2,1)} %collective-permute-done.23.w_far), custom_call_target="tpu_custom_call" | custom-call | flops 2147483648 | bytes 12582912 | tf_op jit(solution)/shard_map/mix_more/pallas_call | solution.py:266
  (65 shorter events, 1.2 us)
Async XLA Ops:
  6.5 136.7 %all-gather.3.cloned.1.call-start = ((), (), s32[]{:S(2)}) async-start(), calls=%async_computation.2 | async-start | bytes 5406720 | tf_op jit(solution)/shard_map/all_gather | solution.py:535
  7.6 3.1 %collective-permute-start.4 = (bf16[32,256]{1,0:T(8,128)(2,1)S(1)}, bf16[32,256]{1,0:T(8,128)(2,1)S(1)}, u32[]{:S(2)}, u32[]{:S(2)}) collective-permute-start(bf16[32,256]{1,0:T(8,128)(2,1)S(1)} %pad_maximum_fusion.8), channel_id=1, source_target_pairs={{0,2},{2,0},{4,6},{6,4},{8,10},{10,8},{12,14},{14,12},{16,18},{18,... | collective-permute-start | bytes 49160 | tf_op jit(solution)/shard_map/ppermute | solution.py:35
  10.1 1.5 collective-permute-start
  10.3 12.4 %collective-permute-start.3 = (bf16[512,4096]{1,0:T(8,128)(2,1)}, bf16[512,4096]{1,0:T(8,128)(2,1)}, u32[]{:S(2)}, u32[]{:S(2)}) collective-permute-start(bf16[512,4096]{1,0:T(8,128)(2,1)} %bitcast.56), channel_id=1, source_target_pairs={{0,2},{2,0},{4,6},{6,4},{8,10},{10,8},{12,14},{14,12},{16,18},{18,... | collective-permute-start | bytes 12582920 | tf_op jit(solution)/shard_map/ppermute | solution.py:35
  12.4 7.5 %collective-permute-start.2 = (bf16[128,512]{1,0:T(8,128)(2,1)S(1)}, bf16[128,512]{1,0:T(8,128)(2,1)S(1)}, u32[]{:S(2)}, u32[]{:S(2)}) collective-permute-start(bf16[128,512]{1,0:T(8,128)(2,1)S(1)} %bitcast.65), channel_id=1, source_target_pairs={{0,66},{2,64},{4,70},{6,68},{8,74},{10,72},{12,78},{14,76},{16,82}... | collective-permute-start | bytes 393224 | tf_op jit(solution)/shard_map/ppermute | solution.py:35
  16.2 6.3 %collective-permute-start.1 = (bf16[128,512]{1,0:T(8,128)(2,1)S(1)}, bf16[128,512]{1,0:T(8,128)(2,1)S(1)}, u32[]{:S(2)}, u32[]{:S(2)}) collective-permute-start(bf16[128,512]{1,0:T(8,128)(2,1)S(1)} %bitcast.66), channel_id=1, source_target_pairs={{0,64},{2,66},{4,68},{6,70},{8,72},{10,74},{12,76},{14,78},{16,80}... | collective-permute-start | bytes 393224 | tf_op jit(solution)/shard_map/ppermute | solution.py:35
  22.6 8.8 %collective-permute-start.7 = (bf16[256,512]{1,0:T(8,128)(2,1)S(1)}, bf16[256,512]{1,0:T(8,128)(2,1)S(1)}, u32[]{:S(2)}, u32[]{:S(2)}) collective-permute-start(bf16[256,512]{1,0:T(8,128)(2,1)S(1)} %get-tuple-element.34), channel_id=1, source_target_pairs={{0,4},{2,6},{4,8},{6,10},{8,12},{10,14},{12,0},{14,2},{16,20},{18,... | collective-permute-start | bytes 786440 | tf_op jit(solution)/shard_map/ppermute | solution.py:35
  23.9 14.8 %collective-permute-start.6 = (bf16[256,512]{1,0:T(8,128)(2,1)S(1)}, bf16[256,512]{1,0:T(8,128)(2,1)S(1)}, u32[]{:S(2)}, u32[]{:S(2)}) collective-permute-start(bf16[256,512]{1,0:T(8,128)(2,1)S(1)} %get-tuple-element.34), channel_id=1, source_target_pairs={{0,8},{2,10},{4,12},{6,14},{8,0},{10,2},{12,4},{14,6},{16,24},{18,... | collective-permute-start | bytes 786440 | tf_op jit(solution)/shard_map/ppermute | solution.py:35
  26.4 12.8 %collective-permute-start.5 = (bf16[256,512]{1,0:T(8,128)(2,1)S(1)}, bf16[256,512]{1,0:T(8,128)(2,1)S(1)}, u32[]{:S(2)}, u32[]{:S(2)}) collective-permute-start(bf16[256,512]{1,0:T(8,128)(2,1)S(1)} %get-tuple-element.34), channel_id=1, source_target_pairs={{0,12},{2,14},{4,0},{6,2},{8,4},{10,6},{12,8},{14,10},{16,28},{18,... | collective-permute-start | bytes 786440 | tf_op jit(solution)/shard_map/ppermute | solution.py:35
  27.5 12.7 %collective-permute-start.10 = (bf16[256,512]{1,0:T(8,128)(2,1)S(1)}, bf16[256,512]{1,0:T(8,128)(2,1)S(1)}, u32[]{:S(2)}, u32[]{:S(2)}) collective-permute-start(bf16[256,512]{1,0:T(8,128)(2,1)S(1)} %get-tuple-element.35), channel_id=1, source_target_pairs={{0,16},{2,18},{4,20},{6,22},{8,24},{10,26},{12,28},{14,30},{16,32}... | collective-permute-start | bytes 786440 | tf_op jit(solution)/shard_map/ppermute | solution.py:35
  28.8 14.1 %collective-permute-start.9 = (bf16[256,512]{1,0:T(8,128)(2,1)S(1)}, bf16[256,512]{1,0:T(8,128)(2,1)S(1)}, u32[]{:S(2)}, u32[]{:S(2)}) collective-permute-start(bf16[256,512]{1,0:T(8,128)(2,1)S(1)} %get-tuple-element.35), channel_id=1, source_target_pairs={{0,32},{2,34},{4,36},{6,38},{8,40},{10,42},{12,44},{14,46},{16,48}... | collective-permute-start | bytes 786440 | tf_op jit(solution)/shard_map/ppermute | solution.py:35
  31.4 11.5 %collective-permute-start.8 = (bf16[256,512]{1,0:T(8,128)(2,1)S(1)}, bf16[256,512]{1,0:T(8,128)(2,1)S(1)}, u32[]{:S(2)}, u32[]{:S(2)}) collective-permute-start(bf16[256,512]{1,0:T(8,128)(2,1)S(1)} %get-tuple-element.35), channel_id=1, source_target_pairs={{0,48},{2,50},{4,52},{6,54},{8,56},{10,58},{12,60},{14,62},{16,0},... | collective-permute-start | bytes 786440 | tf_op jit(solution)/shard_map/ppermute | solution.py:35
  38.5 13.5 %copy-start.12 = (s32[32]{0:T(128)S(1)}, s32[32]{0:T(128)}, u32[]{:S(2)}) copy-start(s32[32]{0:T(128)} %constant.192.clone) | copy-start | bytes 388
  38.5 13.5 %copy-start.13 = (s32[32]{0:T(128)S(1)}, s32[32]{0:T(128)}, u32[]{:S(2)}) copy-start(s32[32]{0:T(128)} %constant.191.clone) | copy-start | bytes 388
  38.5 13.5 %copy-start.14 = (s32[32]{0:T(128)S(1)}, s32[32]{0:T(128)}, u32[]{:S(2)}) copy-start(s32[32]{0:T(128)} %constant.190.clone) | copy-start | bytes 388
  44.0 92.7 %collective-permute-start.19 = (bf16[512,4096]{1,0:T(8,128)(2,1)}, bf16[512,4096]{1,0:T(8,128)(2,1)}, u32[]{:S(2)}, u32[]{:S(2)}) collective-permute-start(bf16[512,4096]{1,0:T(8,128)(2,1)} %constant_dynamic-slice_fusion.3), channel_id=1, source_target_pairs={{0,1},{1,0},{2,67},{3,66},{4,5},{5,4},{6,71},{7,70},{8,9},{9,8},{1... | collective-permute-start | bytes 12582920 | tf_op jit(solution)/shard_map/ppermute | solution.py:565
  47.7 36.3 %collective-permute-start.11 = (bf16[1024,512]{1,0:T(8,128)(2,1)}, bf16[1024,512]{1,0:T(8,128)(2,1)S(1)}, u32[]{:S(2)}, u32[]{:S(2)}) collective-permute-start(bf16[1024,512]{1,0:T(8,128)(2,1)} %pad_maximum_fusion.key_line), channel_id=1, source_target_pairs={{0,48},{2,50},{4,52},{6,54},{8,56},{10,58},{12,60},{14,62},{16,0},... | collective-permute-start | bytes 3145736 | tf_op jit(solution)/shard_map/ppermute | solution.py:35
  50.2 36.5 %collective-permute-start.12 = (bf16[1024,512]{1,0:T(8,128)(2,1)}, bf16[1024,512]{1,0:T(8,128)(2,1)S(1)}, u32[]{:S(2)}, u32[]{:S(2)}) collective-permute-start(bf16[1024,512]{1,0:T(8,128)(2,1)} %pad_maximum_fusion.key_line), channel_id=1, source_target_pairs={{0,16},{2,18},{4,20},{6,22},{8,24},{10,26},{12,28},{14,30},{16,32}... | collective-permute-start | bytes 3145736 | tf_op jit(solution)/shard_map/ppermute | solution.py:35
  50.5 36.1 %collective-permute-start.13 = (bf16[1024,512]{1,0:T(8,128)(2,1)}, bf16[1024,512]{1,0:T(8,128)(2,1)S(1)}, u32[]{:S(2)}, u32[]{:S(2)}) collective-permute-start(bf16[1024,512]{1,0:T(8,128)(2,1)} %pad_maximum_fusion.1.value_line), channel_id=1, source_target_pairs={{0,12},{2,14},{4,0},{6,2},{8,4},{10,6},{12,8},{14,10},{16,28},{18,... | collective-permute-start | bytes 3145736 | tf_op jit(solution)/shard_map/ppermute | solution.py:35
  50.5 36.1 %collective-permute-start.14 = (bf16[1024,512]{1,0:T(8,128)(2,1)}, bf16[1024,512]{1,0:T(8,128)(2,1)}, u32[]{:S(2)}, u32[]{:S(2)}) collective-permute-start(bf16[1024,512]{1,0:T(8,128)(2,1)} %pad_maximum_fusion.1.value_line), channel_id=1, source_target_pairs={{0,4},{2,6},{4,8},{6,10},{8,12},{10,14},{12,0},{14,2},{16,20},{18,... | collective-permute-start | bytes 3145736 | tf_op jit(solution)/shard_map/ppermute | solution.py:35
  83.9 2.7 %copy-start.1 = (bf16[1024,512]{1,0:T(8,128)(2,1)}, bf16[1024,512]{1,0:T(8,128)(2,1)S(1)}, u32[]{:S(2)}) copy-start(bf16[1024,512]{1,0:T(8,128)(2,1)S(1)} %collective-permute-done.11.k1.refs_0_) | copy-start | bytes 3145732
  86.7 1.0 copy-start.2
  86.7 1.3 copy-start.3
  90.6 15.4 %collective-permute-start.15 = (bf16[512,512]{1,0:T(8,128)(2,1)}, bf16[512,512]{1,0:T(8,128)(2,1)S(1)}, u32[]{:S(2)}, u32[]{:S(2)}) collective-permute-start(bf16[512,512]{1,0:T(8,128)(2,1)} %get-tuple-element.52), channel_id=1, source_target_pairs={{0,48},{2,50},{4,52},{6,54},{8,56},{10,58},{12,60},{14,62},{16,0},... | collective-permute-start | bytes 1572872 | tf_op jit(solution)/shard_map/ppermute | solution.py:35
  90.9 16.3 %collective-permute-start.16 = (bf16[512,512]{1,0:T(8,128)(2,1)}, bf16[512,512]{1,0:T(8,128)(2,1)S(1)}, u32[]{:S(2)}, u32[]{:S(2)}) collective-permute-start(bf16[512,512]{1,0:T(8,128)(2,1)} %get-tuple-element.53), channel_id=1, source_target_pairs={{0,16},{2,18},{4,20},{6,22},{8,24},{10,26},{12,28},{14,30},{16,32}... | collective-permute-start | bytes 1572872 | tf_op jit(solution)/shard_map/ppermute | solution.py:35
  92.1 15.2 %collective-permute-start.17 = (bf16[512,512]{1,0:T(8,128)(2,1)}, bf16[512,512]{1,0:T(8,128)(2,1)S(1)}, u32[]{:S(2)}, u32[]{:S(2)}) collective-permute-start(bf16[512,512]{1,0:T(8,128)(2,1)} %get-tuple-element.54), channel_id=1, source_target_pairs={{0,12},{2,14},{4,0},{6,2},{8,4},{10,6},{12,8},{14,10},{16,28},{18,... | collective-permute-start | bytes 1572872 | tf_op jit(solution)/shard_map/ppermute | solution.py:35
  92.1 16.1 %collective-permute-start.18 = (bf16[512,512]{1,0:T(8,128)(2,1)}, bf16[512,512]{1,0:T(8,128)(2,1)S(1)}, u32[]{:S(2)}, u32[]{:S(2)}) collective-permute-start(bf16[512,512]{1,0:T(8,128)(2,1)} %get-tuple-element.55), channel_id=1, source_target_pairs={{0,4},{2,6},{4,8},{6,10},{8,12},{10,14},{12,0},{14,2},{16,20},{18,... | collective-permute-start | bytes 1572872 | tf_op jit(solution)/shard_map/ppermute | solution.py:35
  106.0 2.1 copy-start.5
  107.2 1.0 copy-start.6
  107.3 0.9 copy-start.7
  108.1 0.8 copy-start.8
  116.5 20.2 %all-to-all-start = ((bf16[32,16,1024]{2,1,0:T(8,128)(2,1)}), bf16[32,16,1024]{2,1,0:T(8,128)(2,1)S(1)}, u32[]{:S(2)}, u32[]{:S(2)}) async-start(bf16[32,16,1024]{2,1,0:T(8,128)(2,1)} %bitcast.60), calls=%async_computation | async-start | bytes 2097152 | tf_op jit(solution)/shard_map/all_to_all | solution.py:569
  136.6 9.2 %copy-start.4 = (bf16[32,16,1024]{2,1,0:T(8,128)(2,1)}, bf16[32,16,1024]{2,1,0:T(8,128)(2,1)S(1)}, u32[]{:S(2)}) copy-start(bf16[32,16,1024]{2,1,0:T(8,128)(2,1)S(1)} %all-to-all-done.x_ref) | copy-start | bytes 3145732
  136.6 62.0 %collective-permute-start.23 = (bf16[512,4096]{1,0:T(8,128)(2,1)}, bf16[512,4096]{1,0:T(8,128)(2,1)}, u32[]{:S(2)}, u32[]{:S(2)}) collective-permute-start(bf16[512,4096]{1,0:T(8,128)(2,1)} %collective-permute-done.19.w_near), channel_id=1, source_target_pairs={{0,2},{2,0},{4,6},{6,4},{8,10},{10,8},{12,14},{14,12},{16,18},{18,... | collective-permute-start | bytes 12582920 | tf_op jit(solution)/shard_map/ppermute | solution.py:35
  159.2 4.4 %copy-start.11 = (f32[1024]{0:T(1024)S(1)}, f32[1024]{0:T(1024)}, u32[]{:S(2)}) copy-start(f32[1024]{0:T(1024)} %param.13) | copy-start | bytes 12292
  159.2 21.9 %all-to-all-start.1 = ((bf16[32,16,1024]{2,1,0:T(8,128)(2,1)}), bf16[32,16,1024]{2,1,0:T(8,128)(2,1)S(1)}, u32[]{:S(2)}, u32[]{:S(2)}) async-start(bf16[32,16,1024]{2,1,0:T(8,128)(2,1)} %long_conv.1), calls=%async_computation.1 | async-start | bytes 2097152 | tf_op jit(solution)/shard_map/all_to_all | solution.py:579
  163.7 17.4 %copy-start = (bf16[512,1024]{1,0:T(8,128)(2,1)S(1)}, bf16[512,1024]{1,0:T(8,128)(2,1)}, u32[]{:S(2)}) copy-start(bf16[512,1024]{1,0:T(8,128)(2,1)} %last_part.1) | copy-start | bytes 3145732
  183.0 3.6 %collective-permute-start.20 = (bf16[512,256]{1,0:T(8,128)(2,1)S(1)}, bf16[512,256]{1,0:T(8,128)(2,1)S(1)}, u32[]{:S(2)}, u32[]{:S(2)}) collective-permute-start(bf16[512,256]{1,0:T(8,128)(2,1)S(1)} %get-tuple-element.67), channel_id=1, source_target_pairs={{0,2},{2,0},{4,6},{6,4},{8,10},{10,8},{12,14},{14,12},{16,18},{18,... | collective-permute-start | bytes 786440 | tf_op jit(solution)/shard_map/ppermute | solution.py:35
  184.9 10.2 %collective-permute-start.21 = (bf16[512,256]{1,0:T(8,128)(2,1)S(1)}, bf16[512,256]{1,0:T(8,128)(2,1)S(1)}, u32[]{:S(2)}, u32[]{:S(2)}) collective-permute-start(bf16[512,256]{1,0:T(8,128)(2,1)S(1)} %get-tuple-element.66), channel_id=1, source_target_pairs={{0,1},{1,0},{2,3},{3,2},{4,5},{5,4},{6,7},{7,6},{8,9},{9,8},{10,11... | collective-permute-start | bytes 786440 | tf_op jit(solution)/shard_map/ppermute | solution.py:592
  184.9 13.7 %collective-permute-start.22 = (bf16[512,256]{1,0:T(8,128)(2,1)S(1)}, bf16[512,256]{1,0:T(8,128)(2,1)S(1)}, u32[]{:S(2)}, u32[]{:S(2)}) collective-permute-start(bf16[512,256]{1,0:T(8,128)(2,1)S(1)} %get-tuple-element.65), channel_id=1, source_target_pairs={{0,3},{1,2},{2,1},{3,0},{4,7},{5,6},{6,5},{7,4},{8,11},{9,10},{10,... | collective-permute-start | bytes 786440 | tf_op jit(solution)/shard_map/ppermute | solution.py:597
  195.1 3.5 %copy-start.9 = (bf16[512,256]{1,0:T(8,128)(2,1)}, bf16[512,256]{1,0:T(8,128)(2,1)S(1)}, u32[]{:S(2)}) copy-start(bf16[512,256]{1,0:T(8,128)(2,1)S(1)} %collective-permute-done.21.near_h) | copy-start | bytes 786436
  198.6 0.7 copy-start.10
Sparse Core Ops, SparseCore 0:
  12.5 105.7 all-gather.2

commit v9 on v7

--- a/solution.py
+++ b/solution.py
@@ -547,7 +547,8 @@
     order = jnp.stack([key_order, value_order])
     first = sum_part(first_kernel, "first_part", order, mine, other, [], [key_line, value_line], True)
     near_lines = [send(key_line, dy=-1), send(key_line, dy=1), send(value_line, dx=-1), send(value_line, dx=1)]
-    near_lines, first = lax.optimization_barrier((near_lines, first))
+    tables = column_tables(core, rows, cols, padded)
+    near_lines, first, tables = lax.optimization_barrier((near_lines, first, tables))
     halves = cut_halves(near_lines)
     last_lines = [
         send(halves[0], dy=-1),
@@ -563,18 +564,19 @@
         for th in range(2):
             perm.append((t * 2 + th, index_of(tz ^ tc, ty, tx, tc) * 2 + 1 - th))
     ow_same = lax.ppermute(ow_part, ("seq", "ch"), perm)
-    ow_cross = send(ow_same, dc=1)
 
     source = last_part(totals, first[2:], last_lines)
     packed = source.reshape(CHIPS, chan // CHIPS, 2 * rows)
     mine_ch = lax.all_to_all(packed, "seq", 0, 0, axis_index_groups=SAME_CORE)
 
-    tw, a, ai, cs, twist = column_tables(core, rows, cols, padded)
+    tw, a, ai, cs, twist = tables
     f, m = filter_part(z, gathered, cs, twist)
     forward, inverse = row_tables(rows, padded)
     fwd = jnp.asarray(forward.astype(np.float32).astype(ml_dtypes.bfloat16))
     inv = jnp.asarray(inverse.astype(np.float32).astype(ml_dtypes.bfloat16))
     conv = long_conv(mine_ch, fwd, inv, tw, a, ai, m, f)
+    conv, ow_same = lax.optimization_barrier((conv, ow_same))
+    ow_cross = send(ow_same, dc=1)
     conv = lax.all_to_all(conv, "seq", 0, 0, axis_index_groups=SAME_CORE)
     conv = conv.reshape(chan, 2 * rows).astype(F32)
 

time: 222 us -> 211 us (0.950)
  waiting for transfers between devices: 67.3 us -> 57.1 us
    ppermute x1, waiting for transfers between devices: 12.2 us -> 0.01 us  [per_device(): ow_same = lax.ppermute(ow_part, ('seq', 'ch'), perm)]
  transfers between devices with their start and end apart: 27 -> 27, of which waited for: 12 -> 11; matrix products, arithmetic and copies ran while one was open for 7% -> 7% of each run, Pallas kernels for 30% -> 31%
where the time goes in v9:
time: 211 us; the launch traced here: 210 us
  Pallas kernels  73.7 us (35%)
  waiting for transfers between devices  57.1 us (27%)
  starting transfers between devices  44.2 us (21%)
  between operations  13.8 us (7%)
  local copies, waits for them, and re-layouts  11.8 us (6%)
  other arithmetic  9.63 us (5%)
    ppermute x21, waiting for transfers between devices, send(): return lax.ppermute(value, 'seq', perm)  33.9 us
    ppermute x21, starting transfers between devices, send(): return lax.ppermute(value, 'seq', perm)  30.1 us
    pallas_call x2, Pallas kernels, sum_part(): pl.pallas_call(kernel, grid_spec=pltpu.PrefetchScalarGridSpec(num_scalar_...  22.1 us
    pallas_call x2, Pallas kernels, mix_part(): pl.pallas_call(mix_kernel if total is None else mix_more_kernel, grid=(4,...  15.5 us
    pallas_call x1, Pallas kernels, long_conv(): pl.pallas_call(conv_kernel, in_specs=[vmem, hbm, hbm, hbm, vmem, vmem, vm...  13.4 us
    all_to_all x1, waiting for transfers between devices, per_device(): mine_ch = lax.all_to_all(packed, 'seq', 0, 0, axis_index_groups=SAME_CORE)  12.1 us
    pallas_call x1, Pallas kernels, gate_part(): pl.pallas_call(gate_kernel, grid=(4,), in_specs=[pl.BlockSpec((tile, widt...  10 us
    all_to_all x1, waiting for transfers between devices, per_device(): conv = lax.all_to_all(conv, 'seq', 0, 0, axis_index_groups=SAME_CORE)  7.56 us
  transfers between devices with their start and end apart: 27, of which 11 were waited for; matrix products, arithmetic and copies ran while one was open for 7% of the time, Pallas kernels for 31%

profile of v9, /device:TPU:1, one launch (start us, length us, event | category | flops | bytes accessed | tf_op | source)
XLA Modules:
  0.0 210.3 jit_solution(12580666560211865240)
XLA Ops:
  6.5 0.9 copy.11
  7.6 1.5 collective-permute-start.4
  9.1 1.0 dynamic-slice_bitcast_fusion
  10.3 1.4 collective-permute-done
  11.7 0.7 maximum_maximum_fusion
  12.4 0.2 collective-permute-start.3
  12.7 4.0 %collective-permute-start.2 = (bf16[128,512]{1,0:T(8,128)(2,1)S(1)}, bf16[128,512]{1,0:T(8,128)(2,1)S(1)}, u32[]{:S(2)}, u32[]{:S(2)}) collective-permute-start(bf16[128,512]{1,0:T(8,128)(2,1)S(1)} %bitcast.65), channel_id=1, source_target_pairs={{0,66},{2,64},{4,70},{6,68},{8,74},{10,72},{12,78},{14,76},{16,82}... | collective-permute-start | bytes 393224 | tf_op jit(solution)/shard_map/ppermute | solution.py:35
  16.8 3.4 %collective-permute-done.2 = bf16[128,512]{1,0:T(8,128)(2,1)S(1)} collective-permute-done((bf16[128,512]{1,0:T(8,128)(2,1)S(1)}, bf16[128,512]{1,0:T(8,128)(2,1)S(1)}, u32[]{:S(2)}, u32[]{:S(2)}) %collective-permute-start.2) | collective-permute-done | bytes 131104 | tf_op jit(solution)/shard_map/ppermute | solution.py:35
  20.2 3.0 %collective-permute-done.1 = bf16[128,512]{1,0:T(8,128)(2,1)S(1)} collective-permute-done((bf16[128,512]{1,0:T(8,128)(2,1)S(1)}, bf16[128,512]{1,0:T(8,128)(2,1)S(1)}, u32[]{:S(2)}, u32[]{:S(2)}) %collective-permute-start.1) | collective-permute-done | bytes 131104 | tf_op jit(solution)/shard_map/ppermute | solution.py:35
  23.3 1.3 collective-permute-start.7
  24.6 2.5 %collective-permute-start.6 = (bf16[256,512]{1,0:T(8,128)(2,1)S(1)}, bf16[256,512]{1,0:T(8,128)(2,1)S(1)}, u32[]{:S(2)}, u32[]{:S(2)}) collective-permute-start(bf16[256,512]{1,0:T(8,128)(2,1)S(1)} %get-tuple-element.39), channel_id=1, source_target_pairs={{0,8},{2,10},{4,12},{6,14},{8,0},{10,2},{12,4},{14,6},{16,24},{18,... | collective-permute-start | bytes 786440 | tf_op jit(solution)/shard_map/ppermute | solution.py:35
  27.0 1.2 collective-permute-start.5
  28.2 1.3 collective-permute-start.10
  29.5 2.6 %collective-permute-start.9 = (bf16[256,512]{1,0:T(8,128)(2,1)S(1)}, bf16[256,512]{1,0:T(8,128)(2,1)S(1)}, u32[]{:S(2)}, u32[]{:S(2)}) collective-permute-start(bf16[256,512]{1,0:T(8,128)(2,1)S(1)} %get-tuple-element.40), channel_id=1, source_target_pairs={{0,32},{2,34},{4,36},{6,38},{8,40},{10,42},{12,44},{14,46},{16,48}... | collective-permute-start | bytes 786440 | tf_op jit(solution)/shard_map/ppermute | solution.py:35
  32.1 2.7 %collective-permute-start.8 = (bf16[256,512]{1,0:T(8,128)(2,1)S(1)}, bf16[256,512]{1,0:T(8,128)(2,1)S(1)}, u32[]{:S(2)}, u32[]{:S(2)}) collective-permute-start(bf16[256,512]{1,0:T(8,128)(2,1)S(1)} %get-tuple-element.40), channel_id=1, source_target_pairs={{0,48},{2,50},{4,52},{6,54},{8,56},{10,58},{12,60},{14,62},{16,0},... | collective-permute-start | bytes 786440 | tf_op jit(solution)/shard_map/ppermute | solution.py:35
  34.9 4.7 %constant_dynamic-slice_fusion.3 = bf16[512,4096]{1,0:T(8,128)(2,1)} fusion(bf16[1024,4096]{1,0:T(8,128)(2,1)} %w_here.1, s32[]{:T(128)S(6)} %select_n.230), kind=kLoop, calls=%fused_computation.104 | loop fusion | bytes 8388612 | tf_op jit(solution)/shard_map/dynamic_slice | solution.py:538
  39.5 0.3 collective-permute-done.6
  39.8 1.1 pad_maximum_fusion.key_line
  40.9 3.1 %collective-permute-done.9 = bf16[256,512]{1,0:T(8,128)(2,1)S(1)} collective-permute-done((bf16[256,512]{1,0:T(8,128)(2,1)S(1)}, bf16[256,512]{1,0:T(8,128)(2,1)S(1)}, u32[]{:S(2)}, u32[]{:S(2)}) %collective-permute-start.9) | collective-permute-done | bytes 262176 | tf_op jit(solution)/shard_map/ppermute | solution.py:35
  44.0 1.1 pad_maximum_fusion.1.value_line
  45.0 3.3 %collective-permute-start.19 = (bf16[512,4096]{1,0:T(8,128)(2,1)}, bf16[512,4096]{1,0:T(8,128)(2,1)}, u32[]{:S(2)}, u32[]{:S(2)}) collective-permute-start(bf16[512,4096]{1,0:T(8,128)(2,1)} %constant_dynamic-slice_fusion.3), channel_id=1, source_target_pairs={{0,1},{1,0},{2,67},{3,66},{4,5},{5,4},{6,71},{7,70},{8,9},{9,8},{1... | collective-permute-start | bytes 12582920 | tf_op jit(solution)/shard_map/ppermute | solution.py:566
  48.3 0.2 fusion.38
  48.8 2.3 %collective-permute-start.11 = (bf16[1024,512]{1,0:T(8,128)(2,1)}, bf16[1024,512]{1,0:T(8,128)(2,1)S(1)}, u32[]{:S(2)}, u32[]{:S(2)}) collective-permute-start(bf16[1024,512]{1,0:T(8,128)(2,1)} %pad_maximum_fusion.key_line), channel_id=1, source_target_pairs={{0,48},{2,50},{4,52},{6,54},{8,56},{10,58},{12,60},{14,62},{16,0},... | collective-permute-start | bytes 3145736 | tf_op jit(solution)/shard_map/ppermute | solution.py:35
  51.1 0.4 collective-permute-start.12
  51.6 1.4 collective-permute-start.14
  53.0 0.6 pad_add_fusion.order_ref
  53.6 0.7 fusion.9.ai_ref
  54.3 0.3 fusion.35
  54.6 0.7 pad_maximum_fusion.6
  55.3 0.6 fusion.15
  55.9 0.7 pad_maximum_fusion.5.tw_hbm
  56.6 10.4 %first_part.1 = (f32[1024,512]{1,0:T(8,128)}, f32[1024,512]{1,0:T(8,128)}, bf16[1024,1024]{1,0:T(8,128)(2,1)}, bf16[1024,1024]{1,0:T(8,128)(2,1)}) custom-call(s32[2,32]{1,0:T(2,128)} %pad_add_fusion.order_ref, bf16[512,4096]{1,0:T(8,128)(2,1)} %bitcast.57, bf16[512,4096]{1,0:T(8,128)(2,1)} %collective-permute-done.3.other_ref, ...), custom_call_target="tpu_custom_call" | custom-call | flops 2147483648 | bytes 18874368 | tf_op jit(solution)/shard_map/first_part/pallas_call | solution.py:117
  67.0 18.5 %collective-permute-done.11.k1.refs_0_ = bf16[1024,512]{1,0:T(8,128)(2,1)S(1)} collective-permute-done((bf16[1024,512]{1,0:T(8,128)(2,1)}, bf16[1024,512]{1,0:T(8,128)(2,1)S(1)}, u32[]{:S(2)}, u32[]{:S(2)}) %collective-permute-start.11) | collective-permute-done | bytes 1048608 | tf_op jit(solution)/shard_map/ppermute | solution.py:35
  85.4 1.7 collective-permute-done.12.k3.refs_1_
  87.1 1.0 copy-done.2
  88.1 0.3 copy-done.3
  88.4 2.6 %cut_halves.1 = (bf16[512,512]{1,0:T(8,128)(2,1)}, bf16[512,512]{1,0:T(8,128)(2,1)}, bf16[512,512]{1,0:T(8,128)(2,1)}, bf16[512,512]{1,0:T(8,128)(2,1)}) custom-call(bf16[1024,512]{1,0:T(8,128)(2,1)} %copy-done.1, bf16[1024,512]{1,0:T(8,128)(2,1)} %copy-done.2, bf16[1024,512]{1,0:T(8,128)(2,1)} %copy-done.3, bf16[1024,512]{1,0:T(8,128)(2,1)} %collective-permute-done.14.v3.refs_3_), custom_call_target="tpu_custom_call" | custom-call | bytes 4194304 | tf_op jit(solution)/shard_map/cut_halves/pallas_call | solution.py:149
  91.0 0.7 collective-permute-start.15
  91.7 0.8 collective-permute-start.16
  92.5 1.5 collective-permute-start.18
  94.0 11.7 %second_part.1 = (f32[1024,512]{1,0:T(8,128)}, f32[1024,512]{1,0:T(8,128)}) custom-call(s32[2,32]{1,0:T(2,128)} %pad_add_fusion.order_ref, bf16[512,4096]{1,0:T(8,128)(2,1)} %bitcast.58, bf16[512,4096]{1,0:T(8,128)(2,1)} %collective-permute-done.3.other_ref, f32[1024,512]{1,0:T(8,128)} %get-tuple-element.47.key_in, f32[1024,512]{1,0:T(8,128)} %get-tuple-element.48.value_in, ...), custom_call_target="tpu_custom_call" | custom-call | flops 4294967296 | bytes 18874368 | tf_op jit(solution)/shard_map/second_part/pallas_call | solution.py:117
  105.7 2.6 %collective-permute-done.16.kb = bf16[512,512]{1,0:T(8,128)(2,1)S(1)} collective-permute-done((bf16[512,512]{1,0:T(8,128)(2,1)}, bf16[512,512]{1,0:T(8,128)(2,1)S(1)}, u32[]{:S(2)}, u32[]{:S(2)}) %collective-permute-start.16) | collective-permute-done | bytes 524320 | tf_op jit(solution)/shard_map/ppermute | solution.py:35
  108.4 0.8 copy-done.6
  109.1 0.2 copy-done.7
  109.3 0.2 copy-done.8
  109.5 7.6 %last_part.1 = bf16[512,1024]{1,0:T(8,128)(2,1)} custom-call(f32[1024,512]{1,0:T(8,128)} %get-tuple-element.53.key_ref, f32[1024,512]{1,0:T(8,128)} %get-tuple-element.54.value_ref, bf16[1024,1024]{1,0:T(8,128)(2,1)} %get-tuple-element.55.key_tok_ref, bf16[1024,1024]{1,0:T(8,128)(2,1)} %get-tuple-element.56.value_tok_ref, bf16[512,512]{1,0:T(8,128)(2,1)} %copy-done.5, ...), custom_call_target="tpu_custom_call" | custom-call | flops 2147483648 | bytes 13631488 | tf_op jit(solution)/shard_map/last_part/pallas_call | solution.py:178
  117.0 4.7 %all-to-all-start = ((bf16[32,16,1024]{2,1,0:T(8,128)(2,1)}), bf16[32,16,1024]{2,1,0:T(8,128)(2,1)S(1)}, u32[]{:S(2)}, u32[]{:S(2)}) async-start(bf16[32,16,1024]{2,1,0:T(8,128)(2,1)} %bitcast.60), calls=%async_computation | async-start | bytes 2097152 | tf_op jit(solution)/shard_map/all_to_all | solution.py:570
  121.7 0.8 copy.12.a_ref
  122.5 2.5 %filter_part.1 = (f32[64,1024]{1,0:T(8,128)}, bf16[256,256]{1,0:T(8,128)(2,1)}) custom-call(s32[1]{0:T(128)} %bitcast.19.z_ref, bf16[32,160,512]{2,1,0:T(8,128)(2,1)} %bitcast.61, f32[2,64,64]{2,1,0:T(8,128)} %get-tuple-element.64.cs_ref, f32[2,64,64]{2,1,0:T(8,128)} %get-tuple-element.65.twist_ref), custom_call_target="tpu_custom_call" | custom-call | flops 1000000000 | bytes 1048576 | tf_op jit(solution)/shard_map/filter_part/pallas_call | solution.py:333
  125.0 12.1 %all-to-all-done.x_ref = bf16[32,16,1024]{2,1,0:T(8,128)(2,1)S(1)} async-done(((bf16[32,16,1024]{2,1,0:T(8,128)(2,1)}), bf16[32,16,1024]{2,1,0:T(8,128)(2,1)S(1)}, u32[]{:S(2)}, u32[]{:S(2)}) %all-to-all-start) | async-done | bytes 1048608 | tf_op jit(solution)/shard_map/all_to_all | solution.py:570
  137.1 1.0 copy-done.4
  138.1 13.4 %long_conv.1 = bf16[32,16,1024]{2,1,0:T(8,128)(2,1)} custom-call(bf16[32,16,1024]{2,1,0:T(8,128)(2,1)} %copy-done.4, bf16[512,1024]{1,0:T(8,128)(2,1)} %constant.193.clone.fwd_hbm, bf16[1024,512]{1,0:T(8,128)(2,1)} %constant.194.clone.inv_hbm, f32[64,1024]{1,0:T(8,128)} %pad_maximum_fusion.5.tw_hbm, bf16[256,256]{1,0:T(8,128)(2,1)} %copy.12.a_ref, ...), custom_call_target="tpu_custom_call" | custom-call | flops 8000000000 | bytes 8388608 | tf_op jit(solution)/shard_map/long_conv/pallas_call | solution.py:435
  151.5 3.6 %collective-permute-start.23 = (bf16[512,4096]{1,0:T(8,128)(2,1)}, bf16[512,4096]{1,0:T(8,128)(2,1)}, u32[]{:S(2)}, u32[]{:S(2)}) collective-permute-start(bf16[512,4096]{1,0:T(8,128)(2,1)} %collective-permute-done.19.w_near), channel_id=1, source_target_pairs={{0,2},{2,0},{4,6},{6,4},{8,10},{10,8},{12,14},{14,12},{16,18},{18,... | collective-permute-start | bytes 12582920 | tf_op jit(solution)/shard_map/ppermute | solution.py:35
  155.1 4.4 %all-to-all-start.1 = ((bf16[32,16,1024]{2,1,0:T(8,128)(2,1)}), bf16[32,16,1024]{2,1,0:T(8,128)(2,1)S(1)}, u32[]{:S(2)}, u32[]{:S(2)}) async-start(bf16[32,16,1024]{2,1,0:T(8,128)(2,1)} %long_conv.1), calls=%async_computation.1 | async-start | bytes 2097152 | tf_op jit(solution)/shard_map/all_to_all | solution.py:580
  159.7 10.0 %gate_part.1 = bf16[512,1024]{1,0:T(8,128)(2,1)} custom-call(bf16[512,4096]{1,0:T(8,128)(2,1)} %bitcast.59, bf16[512,4096]{1,0:T(8,128)(2,1)} %collective-permute-done.3.other_ref, bf16[32,160,512]{2,1,0:T(8,128)(2,1)} %bitcast.62), custom_call_target="tpu_custom_call" | custom-call | flops 4294967296 | bytes 13631488 | tf_op jit(solution)/shard_map/gate_part/pallas_call | solution.py:209
  169.7 7.6 %all-to-all-done.1 = bf16[32,16,1024]{2,1,0:T(8,128)(2,1)S(1)} async-done(((bf16[32,16,1024]{2,1,0:T(8,128)(2,1)}), bf16[32,16,1024]{2,1,0:T(8,128)(2,1)S(1)}, u32[]{:S(2)}, u32[]{:S(2)}) %all-to-all-start.1) | async-done | bytes 1048608 | tf_op jit(solution)/shard_map/all_to_all | solution.py:580
  177.2 1.7 fusion.1
  179.1 1.9 collective-permute-start.20
  181.0 1.7 collective-permute-start.22
  182.8 0.8 pad_maximum_fusion.2.here
  183.7 7.5 %mix_part.1.total_ref = f32[256,4096]{1,0:T(8,128)} custom-call(bf16[1024,256]{1,0:T(8,128)(2,1)} %pad_maximum_fusion.2.here, bf16[1024,4096]{1,0:T(8,128)(2,1)} %w_here.1), custom_call_target="tpu_custom_call" | custom-call | flops 2147483648 | bytes 12582912 | tf_op jit(solution)/shard_map/mix_part/pallas_call | solution.py:266
  191.2 3.5 %collective-permute-done.22.far_h = bf16[512,256]{1,0:T(8,128)(2,1)S(1)} collective-permute-done((bf16[512,256]{1,0:T(8,128)(2,1)S(1)}, bf16[512,256]{1,0:T(8,128)(2,1)S(1)}, u32[]{:S(2)}, u32[]{:S(2)}) %collective-permute-start.22) | collective-permute-done | bytes 262176 | tf_op jit(solution)/shard_map/ppermute | solution.py:598
  194.7 0.7 copy-done.10
  195.4 8.0 %mix_more.1 = bf16[256,4096]{1,0:T(8,128)(2,1)} custom-call(f32[256,4096]{1,0:T(8,128)} %mix_part.1.total_ref, bf16[512,256]{1,0:T(8,128)(2,1)} %copy-done.9, bf16[512,256]{1,0:T(8,128)(2,1)} %copy-done.10, bf16[512,4096]{1,0:T(8,128)(2,1)} %collective-permute-done.19.w_near, bf16[512,4096]{1,0:T(8,128)(2,1)} %collective-permute-done.23.w_far), custom_call_target="tpu_custom_call" | custom-call | flops 2147483648 | bytes 12582912 | tf_op jit(solution)/shard_map/mix_more/pallas_call | solution.py:266
  (65 shorter events, 1.1 us)
Async XLA Ops:
  6.5 115.9 %all-gather.3.cloned.1.call-start = ((), (), s32[]{:S(2)}) async-start(), calls=%async_computation.2 | async-start | bytes 5406720 | tf_op jit(solution)/shard_map/all_gather | solution.py:535
  7.6 2.7 %collective-permute-start.4 = (bf16[32,256]{1,0:T(8,128)(2,1)S(1)}, bf16[32,256]{1,0:T(8,128)(2,1)S(1)}, u32[]{:S(2)}, u32[]{:S(2)}) collective-permute-start(bf16[32,256]{1,0:T(8,128)(2,1)S(1)} %pad_maximum_fusion.8), channel_id=1, source_target_pairs={{0,2},{2,0},{4,6},{6,4},{8,10},{10,8},{12,14},{14,12},{16,18},{18,... | collective-permute-start | bytes 49160 | tf_op jit(solution)/shard_map/ppermute | solution.py:35
  10.1 1.5 collective-permute-start
  12.4 10.9 %collective-permute-start.3 = (bf16[512,4096]{1,0:T(8,128)(2,1)}, bf16[512,4096]{1,0:T(8,128)(2,1)}, u32[]{:S(2)}, u32[]{:S(2)}) collective-permute-start(bf16[512,4096]{1,0:T(8,128)(2,1)} %bitcast.56), channel_id=1, source_target_pairs={{0,2},{2,0},{4,6},{6,4},{8,10},{10,8},{12,14},{14,12},{16,18},{18,... | collective-permute-start | bytes 12582920 | tf_op jit(solution)/shard_map/ppermute | solution.py:35
  12.7 7.5 %collective-permute-start.2 = (bf16[128,512]{1,0:T(8,128)(2,1)S(1)}, bf16[128,512]{1,0:T(8,128)(2,1)S(1)}, u32[]{:S(2)}, u32[]{:S(2)}) collective-permute-start(bf16[128,512]{1,0:T(8,128)(2,1)S(1)} %bitcast.65), channel_id=1, source_target_pairs={{0,66},{2,64},{4,70},{6,68},{8,74},{10,72},{12,78},{14,76},{16,82}... | collective-permute-start | bytes 393224 | tf_op jit(solution)/shard_map/ppermute | solution.py:35
  16.7 6.5 %collective-permute-start.1 = (bf16[128,512]{1,0:T(8,128)(2,1)S(1)}, bf16[128,512]{1,0:T(8,128)(2,1)S(1)}, u32[]{:S(2)}, u32[]{:S(2)}) collective-permute-start(bf16[128,512]{1,0:T(8,128)(2,1)S(1)} %bitcast.66), channel_id=1, source_target_pairs={{0,64},{2,66},{4,68},{6,70},{8,72},{10,74},{12,76},{14,78},{16,80}... | collective-permute-start | bytes 393224 | tf_op jit(solution)/shard_map/ppermute | solution.py:35
  23.3 8.8 %collective-permute-start.7 = (bf16[256,512]{1,0:T(8,128)(2,1)S(1)}, bf16[256,512]{1,0:T(8,128)(2,1)S(1)}, u32[]{:S(2)}, u32[]{:S(2)}) collective-permute-start(bf16[256,512]{1,0:T(8,128)(2,1)S(1)} %get-tuple-element.39), channel_id=1, source_target_pairs={{0,4},{2,6},{4,8},{6,10},{8,12},{10,14},{12,0},{14,2},{16,20},{18,... | collective-permute-start | bytes 786440 | tf_op jit(solution)/shard_map/ppermute | solution.py:35
  24.6 15.2 %collective-permute-start.6 = (bf16[256,512]{1,0:T(8,128)(2,1)S(1)}, bf16[256,512]{1,0:T(8,128)(2,1)S(1)}, u32[]{:S(2)}, u32[]{:S(2)}) collective-permute-start(bf16[256,512]{1,0:T(8,128)(2,1)S(1)} %get-tuple-element.39), channel_id=1, source_target_pairs={{0,8},{2,10},{4,12},{6,14},{8,0},{10,2},{12,4},{14,6},{16,24},{18,... | collective-permute-start | bytes 786440 | tf_op jit(solution)/shard_map/ppermute | solution.py:35
  27.0 12.8 %collective-permute-start.5 = (bf16[256,512]{1,0:T(8,128)(2,1)S(1)}, bf16[256,512]{1,0:T(8,128)(2,1)S(1)}, u32[]{:S(2)}, u32[]{:S(2)}) collective-permute-start(bf16[256,512]{1,0:T(8,128)(2,1)S(1)} %get-tuple-element.39), channel_id=1, source_target_pairs={{0,12},{2,14},{4,0},{6,2},{8,4},{10,6},{12,8},{14,10},{16,28},{18,... | collective-permute-start | bytes 786440 | tf_op jit(solution)/shard_map/ppermute | solution.py:35
  28.2 12.7 %collective-permute-start.10 = (bf16[256,512]{1,0:T(8,128)(2,1)S(1)}, bf16[256,512]{1,0:T(8,128)(2,1)S(1)}, u32[]{:S(2)}, u32[]{:S(2)}) collective-permute-start(bf16[256,512]{1,0:T(8,128)(2,1)S(1)} %get-tuple-element.40), channel_id=1, source_target_pairs={{0,16},{2,18},{4,20},{6,22},{8,24},{10,26},{12,28},{14,30},{16,32}... | collective-permute-start | bytes 786440 | tf_op jit(solution)/shard_map/ppermute | solution.py:35
  29.5 14.5 %collective-permute-start.9 = (bf16[256,512]{1,0:T(8,128)(2,1)S(1)}, bf16[256,512]{1,0:T(8,128)(2,1)S(1)}, u32[]{:S(2)}, u32[]{:S(2)}) collective-permute-start(bf16[256,512]{1,0:T(8,128)(2,1)S(1)} %get-tuple-element.40), channel_id=1, source_target_pairs={{0,32},{2,34},{4,36},{6,38},{8,40},{10,42},{12,44},{14,46},{16,48}... | collective-permute-start | bytes 786440 | tf_op jit(solution)/shard_map/ppermute | solution.py:35
  32.1 11.8 %collective-permute-start.8 = (bf16[256,512]{1,0:T(8,128)(2,1)S(1)}, bf16[256,512]{1,0:T(8,128)(2,1)S(1)}, u32[]{:S(2)}, u32[]{:S(2)}) collective-permute-start(bf16[256,512]{1,0:T(8,128)(2,1)S(1)} %get-tuple-element.40), channel_id=1, source_target_pairs={{0,48},{2,50},{4,52},{6,54},{8,56},{10,58},{12,60},{14,62},{16,0},... | collective-permute-start | bytes 786440 | tf_op jit(solution)/shard_map/ppermute | solution.py:35
  39.5 9.2 %copy-start.12 = (s32[32]{0:T(128)S(1)}, s32[32]{0:T(128)}, u32[]{:S(2)}) copy-start(s32[32]{0:T(128)} %constant.192.clone) | copy-start | bytes 388
  39.5 9.3 %copy-start.13 = (s32[32]{0:T(128)S(1)}, s32[32]{0:T(128)}, u32[]{:S(2)}) copy-start(s32[32]{0:T(128)} %constant.191.clone) | copy-start | bytes 388
  39.5 9.3 %copy-start.14 = (s32[32]{0:T(128)S(1)}, s32[32]{0:T(128)}, u32[]{:S(2)}) copy-start(s32[32]{0:T(128)} %constant.190.clone) | copy-start | bytes 388
  45.0 106.5 %collective-permute-start.19 = (bf16[512,4096]{1,0:T(8,128)(2,1)}, bf16[512,4096]{1,0:T(8,128)(2,1)}, u32[]{:S(2)}, u32[]{:S(2)}) collective-permute-start(bf16[512,4096]{1,0:T(8,128)(2,1)} %constant_dynamic-slice_fusion.3), channel_id=1, source_target_pairs={{0,1},{1,0},{2,67},{3,66},{4,5},{5,4},{6,71},{7,70},{8,9},{9,8},{1... | collective-permute-start | bytes 12582920 | tf_op jit(solution)/shard_map/ppermute | solution.py:566
  48.8 36.6 %collective-permute-start.11 = (bf16[1024,512]{1,0:T(8,128)(2,1)}, bf16[1024,512]{1,0:T(8,128)(2,1)S(1)}, u32[]{:S(2)}, u32[]{:S(2)}) collective-permute-start(bf16[1024,512]{1,0:T(8,128)(2,1)} %pad_maximum_fusion.key_line), channel_id=1, source_target_pairs={{0,48},{2,50},{4,52},{6,54},{8,56},{10,58},{12,60},{14,62},{16,0},... | collective-permute-start | bytes 3145736 | tf_op jit(solution)/shard_map/ppermute | solution.py:35
  51.1 36.0 %collective-permute-start.12 = (bf16[1024,512]{1,0:T(8,128)(2,1)}, bf16[1024,512]{1,0:T(8,128)(2,1)S(1)}, u32[]{:S(2)}, u32[]{:S(2)}) collective-permute-start(bf16[1024,512]{1,0:T(8,128)(2,1)} %pad_maximum_fusion.key_line), channel_id=1, source_target_pairs={{0,16},{2,18},{4,20},{6,22},{8,24},{10,26},{12,28},{14,30},{16,32}... | collective-permute-start | bytes 3145736 | tf_op jit(solution)/shard_map/ppermute | solution.py:35
  51.5 35.5 %collective-permute-start.13 = (bf16[1024,512]{1,0:T(8,128)(2,1)}, bf16[1024,512]{1,0:T(8,128)(2,1)S(1)}, u32[]{:S(2)}, u32[]{:S(2)}) collective-permute-start(bf16[1024,512]{1,0:T(8,128)(2,1)} %pad_maximum_fusion.1.value_line), channel_id=1, source_target_pairs={{0,12},{2,14},{4,0},{6,2},{8,4},{10,6},{12,8},{14,10},{16,28},{18,... | collective-permute-start | bytes 3145736 | tf_op jit(solution)/shard_map/ppermute | solution.py:35
  51.6 35.5 %collective-permute-start.14 = (bf16[1024,512]{1,0:T(8,128)(2,1)}, bf16[1024,512]{1,0:T(8,128)(2,1)}, u32[]{:S(2)}, u32[]{:S(2)}) collective-permute-start(bf16[1024,512]{1,0:T(8,128)(2,1)} %pad_maximum_fusion.1.value_line), channel_id=1, source_target_pairs={{0,4},{2,6},{4,8},{6,10},{8,12},{10,14},{12,0},{14,2},{16,20},{18,... | collective-permute-start | bytes 3145736 | tf_op jit(solution)/shard_map/ppermute | solution.py:35
  85.4 1.7 copy-start.1
  87.1 1.0 copy-start.2
  87.1 1.3 copy-start.3
  91.0 14.7 %collective-permute-start.15 = (bf16[512,512]{1,0:T(8,128)(2,1)}, bf16[512,512]{1,0:T(8,128)(2,1)S(1)}, u32[]{:S(2)}, u32[]{:S(2)}) collective-permute-start(bf16[512,512]{1,0:T(8,128)(2,1)} %get-tuple-element.57), channel_id=1, source_target_pairs={{0,48},{2,50},{4,52},{6,54},{8,56},{10,58},{12,60},{14,62},{16,0},... | collective-permute-start | bytes 1572872 | tf_op jit(solution)/shard_map/ppermute | solution.py:35
  91.7 16.6 %collective-permute-start.16 = (bf16[512,512]{1,0:T(8,128)(2,1)}, bf16[512,512]{1,0:T(8,128)(2,1)S(1)}, u32[]{:S(2)}, u32[]{:S(2)}) collective-permute-start(bf16[512,512]{1,0:T(8,128)(2,1)} %get-tuple-element.58), channel_id=1, source_target_pairs={{0,16},{2,18},{4,20},{6,22},{8,24},{10,26},{12,28},{14,30},{16,32}... | collective-permute-start | bytes 1572872 | tf_op jit(solution)/shard_map/ppermute | solution.py:35
  92.5 15.8 %collective-permute-start.17 = (bf16[512,512]{1,0:T(8,128)(2,1)}, bf16[512,512]{1,0:T(8,128)(2,1)S(1)}, u32[]{:S(2)}, u32[]{:S(2)}) collective-permute-start(bf16[512,512]{1,0:T(8,128)(2,1)} %get-tuple-element.59), channel_id=1, source_target_pairs={{0,12},{2,14},{4,0},{6,2},{8,4},{10,6},{12,8},{14,10},{16,28},{18,... | collective-permute-start | bytes 1572872 | tf_op jit(solution)/shard_map/ppermute | solution.py:35
  92.5 15.8 %collective-permute-start.18 = (bf16[512,512]{1,0:T(8,128)(2,1)}, bf16[512,512]{1,0:T(8,128)(2,1)S(1)}, u32[]{:S(2)}, u32[]{:S(2)}) collective-permute-start(bf16[512,512]{1,0:T(8,128)(2,1)} %get-tuple-element.60), channel_id=1, source_target_pairs={{0,4},{2,6},{4,8},{6,10},{8,12},{10,14},{12,0},{14,2},{16,20},{18,... | collective-permute-start | bytes 1572872 | tf_op jit(solution)/shard_map/ppermute | solution.py:35
  105.7 2.7 %copy-start.5 = (bf16[512,512]{1,0:T(8,128)(2,1)}, bf16[512,512]{1,0:T(8,128)(2,1)S(1)}, u32[]{:S(2)}) copy-start(bf16[512,512]{1,0:T(8,128)(2,1)S(1)} %collective-permute-done.15.ka) | copy-start | bytes 1572868
  108.3 0.8 copy-start.6
  108.3 1.0 copy-start.7
  108.3 1.1 copy-start.8
  117.0 20.1 %all-to-all-start = ((bf16[32,16,1024]{2,1,0:T(8,128)(2,1)}), bf16[32,16,1024]{2,1,0:T(8,128)(2,1)S(1)}, u32[]{:S(2)}, u32[]{:S(2)}) async-start(bf16[32,16,1024]{2,1,0:T(8,128)(2,1)} %bitcast.60), calls=%async_computation | async-start | bytes 2097152 | tf_op jit(solution)/shard_map/all_to_all | solution.py:570
  137.1 1.0 copy-start.4
  151.5 8.1 %copy-start.11 = (f32[1024]{0:T(1024)S(1)}, f32[1024]{0:T(1024)}, u32[]{:S(2)}) copy-start(f32[1024]{0:T(1024)} %param.13) | copy-start | bytes 12292
  151.5 43.1 %collective-permute-start.23 = (bf16[512,4096]{1,0:T(8,128)(2,1)}, bf16[512,4096]{1,0:T(8,128)(2,1)}, u32[]{:S(2)}, u32[]{:S(2)}) collective-permute-start(bf16[512,4096]{1,0:T(8,128)(2,1)} %collective-permute-done.19.w_near), channel_id=1, source_target_pairs={{0,2},{2,0},{4,6},{6,4},{8,10},{10,8},{12,14},{14,12},{16,18},{18,... | collective-permute-start | bytes 12582920 | tf_op jit(solution)/shard_map/ppermute | solution.py:35
  155.1 22.1 %all-to-all-start.1 = ((bf16[32,16,1024]{2,1,0:T(8,128)(2,1)}), bf16[32,16,1024]{2,1,0:T(8,128)(2,1)S(1)}, u32[]{:S(2)}, u32[]{:S(2)}) async-start(bf16[32,16,1024]{2,1,0:T(8,128)(2,1)} %long_conv.1), calls=%async_computation.1 | async-start | bytes 2097152 | tf_op jit(solution)/shard_map/all_to_all | solution.py:580
  159.7 17.6 %copy-start = (bf16[512,1024]{1,0:T(8,128)(2,1)S(1)}, bf16[512,1024]{1,0:T(8,128)(2,1)}, u32[]{:S(2)}) copy-start(bf16[512,1024]{1,0:T(8,128)(2,1)} %last_part.1) | copy-start | bytes 3145732
  179.1 3.6 %collective-permute-start.20 = (bf16[512,256]{1,0:T(8,128)(2,1)S(1)}, bf16[512,256]{1,0:T(8,128)(2,1)S(1)}, u32[]{:S(2)}, u32[]{:S(2)}) collective-permute-start(bf16[512,256]{1,0:T(8,128)(2,1)S(1)} %get-tuple-element.77), channel_id=1, source_target_pairs={{0,2},{2,0},{4,6},{6,4},{8,10},{10,8},{12,14},{14,12},{16,18},{18,... | collective-permute-start | bytes 786440 | tf_op jit(solution)/shard_map/ppermute | solution.py:35
  181.0 10.2 %collective-permute-start.21 = (bf16[512,256]{1,0:T(8,128)(2,1)S(1)}, bf16[512,256]{1,0:T(8,128)(2,1)S(1)}, u32[]{:S(2)}, u32[]{:S(2)}) collective-permute-start(bf16[512,256]{1,0:T(8,128)(2,1)S(1)} %get-tuple-element.76), channel_id=1, source_target_pairs={{0,1},{1,0},{2,3},{3,2},{4,5},{5,4},{6,7},{7,6},{8,9},{9,8},{10,11... | collective-permute-start | bytes 786440 | tf_op jit(solution)/shard_map/ppermute | solution.py:593
  181.0 13.7 %collective-permute-start.22 = (bf16[512,256]{1,0:T(8,128)(2,1)S(1)}, bf16[512,256]{1,0:T(8,128)(2,1)S(1)}, u32[]{:S(2)}, u32[]{:S(2)}) collective-permute-start(bf16[512,256]{1,0:T(8,128)(2,1)S(1)} %get-tuple-element.75), channel_id=1, source_target_pairs={{0,3},{1,2},{2,1},{3,0},{4,7},{5,6},{6,5},{7,4},{8,11},{9,10},{10,... | collective-permute-start | bytes 786440 | tf_op jit(solution)/shard_map/ppermute | solution.py:598
  191.2 3.5 %copy-start.9 = (bf16[512,256]{1,0:T(8,128)(2,1)}, bf16[512,256]{1,0:T(8,128)(2,1)S(1)}, u32[]{:S(2)}) copy-start(bf16[512,256]{1,0:T(8,128)(2,1)S(1)} %collective-permute-done.21.near_h) | copy-start | bytes 786436
  194.6 0.7 copy-start.10
Sparse Core Ops, SparseCore 0:
  12.5 106.3 all-gather.2

commit v10 on v9

--- a/solution.py
+++ b/solution.py
@@ -63,6 +63,11 @@
     return jnp.concatenate(blocks, axis=1)
 
 
+def stacked(ref, parts):
+    stride = ref.shape[0] // parts
+    return jnp.concatenate([ref[stride * i : stride * i + stride - 16] for i in range(parts)], axis=0)
+
+
 def by_column(run, mine_ref, other_ref):
     step = pl.program_id(0)
 
@@ -84,7 +89,7 @@
             (1, value_line, value_ref, value_tok_ref),
         ):
             total_ref[...] = jnp.dot(
-                picked(order_ref, row, 0, tok_ref), line[...], preferred_element_type=F32
+                picked(order_ref, row, 0, tok_ref), stacked(line, 4), preferred_element_type=F32
             )
             last_ref[...] = picked(order_ref, row, 2, tok_ref)
 
@@ -98,8 +103,8 @@
             (1, value_in, v1, v3, value_ref),
         ):
             total = before[...]
-            total += jnp.dot(picked(order_ref, row, 1, tok_ref), e1[...], preferred_element_type=F32)
-            total += jnp.dot(picked(order_ref, row, 3, tok_ref), e3[...], preferred_element_type=F32)
+            total += jnp.dot(picked(order_ref, row, 1, tok_ref), stacked(e1, 4), preferred_element_type=F32)
+            total += jnp.dot(picked(order_ref, row, 3, tok_ref), stacked(e3, 4), preferred_element_type=F32)
             total_ref[...] = total
 
     by_column(run, mine_ref, other_ref)
@@ -124,7 +129,7 @@
                 pl.BlockSpec((tile, width), lambda i, o: (jnp.maximum(i - 2, 0), 0)),
             ]
             + by_row[: len(totals)]
-            + [pl.BlockSpec((quarter, chan), lambda i, o: (0, 0))] * len(weights),
+            + [pl.BlockSpec(weights[0].shape, lambda i, o: (0, 0))] * len(weights),
             out_specs=by_row + (tokens_out if last else []),
         ),
         out_shape=shapes + (token_shapes if last else []),
@@ -158,70 +163,42 @@
     )(*lines)
 
 
-def last_kernel(key_ref, value_ref, key_tok_ref, value_tok_ref, ka, kb, va, vb, send_ref):
-    half = ka.shape[0]
+def last_kernel(key_ref, value_ref, key_tok_ref, value_tok_ref, ka, kb, va, vb, source_ref, gate_ref):
+    half = key_tok_ref.shape[1] // 2
+    chan = source_ref.shape[0]
 
     def finish(total_ref, tok_ref, wa, wb):
         total = total_ref[...]
-        total += jnp.dot(tok_ref[:, :half], wa[...], preferred_element_type=F32)
-        total += jnp.dot(tok_ref[:, half:], wb[...], preferred_element_type=F32)
+        total += jnp.dot(tok_ref[:, :half], stacked(wa, 2), preferred_element_type=F32)
+        total += jnp.dot(tok_ref[:, half:], stacked(wb, 2), preferred_element_type=F32)
         return total.astype(BF16).astype(F32)
 
-    source = finish(key_ref, key_tok_ref, ka, kb) * finish(value_ref, value_tok_ref, va, vb)
-    send_ref[...] = source.T.astype(BF16)
+    key = finish(key_ref, key_tok_ref, ka, kb)
+    value = finish(value_ref, value_tok_ref, va, vb)
+    source_ref[...] = (key[:, :chan] * value[:, :chan]).T.astype(BF16)
+    gate_ref[: chan // 2, :] = key[:, chan:].T.astype(BF16)
+    gate_ref[chan // 2 :, :] = value[:, chan:].T.astype(BF16)
 
 
 def last_part(totals, tokens, weights):
-    total, chan = totals[0].shape
+    total, wide = totals[0].shape
     quarter = tokens[0].shape[1]
     tile = total // 4
+    chan = wide * 2 // 3
     return pl.pallas_call(
         last_kernel,
         grid=(4,),
-        in_specs=[pl.BlockSpec((tile, chan), lambda i: (i, 0))] * 2
+        in_specs=[pl.BlockSpec((tile, wide), lambda i: (i, 0))] * 2
         + [pl.BlockSpec((tile, quarter), lambda i: (i, 0))] * 2
-        + [pl.BlockSpec((quarter // 2, chan), lambda i: (0, 0))] * 4,
-        out_specs=pl.BlockSpec((chan, tile), lambda i: (0, i)),
-        out_shape=jax.ShapeDtypeStruct((chan, total), BF16),
+        + [pl.BlockSpec(weights[0].shape, lambda i: (0, 0))] * 4,
+        out_specs=[pl.BlockSpec((chan, tile), lambda i: (0, i))] * 2,
+        out_shape=[jax.ShapeDtypeStruct((chan, total), BF16)] * 2,
         compiler_params=pltpu.CompilerParams(vmem_limit_bytes=VMEM),
         cost_estimate=pl.CostEstimate(
-            flops=2 * 2 * total * quarter * chan, bytes_accessed=13 * 2**20, transcendentals=0
+            flops=2 * 2 * total * quarter * wide, bytes_accessed=16 * 2**20, transcendentals=0
         ),
         name="last_part",
     )(*totals, *tokens, *weights)
-
-
-def gate_kernel(mine_ref, other_ref, weight_ref, out_ref):
-    chips, deep, chan = weight_ref.shape
-
-    def run(tok_ref):
-        weight = weight_ref[...].reshape(chips * deep, chan)
-        gate = jnp.dot(tok_ref[...], weight, preferred_element_type=F32)
-        out_ref[...] = gate.T.astype(BF16)
-
-    by_column(run, mine_ref, other_ref)
-
-
-def gate_part(mine, other, gathered):
-    rows, width = mine.shape
-    chips, _, chan = gathered.shape
-    tile = rows // 2
-    return pl.pallas_call(
-        gate_kernel,
-        grid=(4,),
-        in_specs=[
-            pl.BlockSpec((tile, width), lambda i: (jnp.minimum(i, 1), 0)),
-            pl.BlockSpec((tile, width), lambda i: (jnp.maximum(i - 2, 0), 0)),
-            pl.BlockSpec((chips, width // chips, chan), lambda i: (0, 0, 0)),
-        ],
-        out_specs=pl.BlockSpec((chan, tile), lambda i: (0, i)),
-        out_shape=jax.ShapeDtypeStruct((chan, 2 * rows), BF16),
-        compiler_params=pltpu.CompilerParams(vmem_limit_bytes=VMEM),
-        cost_estimate=pl.CostEstimate(
-            flops=2 * 2 * rows * width * chan, bytes_accessed=13 * 2**20, transcendentals=0
-        ),
-        name="gate_part",
-    )(mine, other, gathered)
 
 
 def turn(ref):
@@ -278,18 +255,19 @@
     )(*totals, *parts, *weights)
 
 
-def filter_kernel(z_ref, x_ref, cs_ref, twist_ref, f_ref, m_ref):
-    chips, _, lanes = x_ref.shape
-    lanes = lanes // 2
-    points = 2 * chips * 16
+def filter_kernel(order_ref, *refs):
+    pieces, (cs_ref, twist_ref, f_ref, m_ref, natural_ref) = refs[:32], refs[32:]
+    points, lanes = natural_ref.shape[1:]
     rows, cols = points // 2, lanes // 2
-
-    def part(n):
-        rows_of = slice(16 * n, 16 * (n + 1))
-        cores = [x_ref[:, rows_of, c * lanes : (c + 1) * lanes] for c in range(2)]
-        return jnp.stack(cores, axis=1).reshape(points, lanes)
-
-    upper, lower = part(0), part(1)
+    for row in range(2):
+        for n in range(16):
+            for dz in range(2):
+                chip = order_ref[row, 2 * n + dz]
+                for c in range(2):
+                    start = pl.multiple_of(chip * 32 + 16 * c, 16)
+                    spot = (2 * dz + c) * lanes
+                    natural_ref[row, pl.ds(start, 16), :] = pieces[16 * row + n][:, spot : spot + lanes]
+    upper, lower = natural_ref[0], natural_ref[1]
     whole = (upper.astype(F32) + lower.astype(F32)).T
     i = lax.broadcasted_iota(jnp.int32, (rows, rows), 0)
     j = lax.broadcasted_iota(jnp.int32, (rows, rows), 1)
@@ -325,25 +303,34 @@
             m_ref[spot, spot] = g.astype(BF16)
 
 
-def filter_part(z, gathered, cs, twist):
-    chips = gathered.shape[0]
+def filter_part(order, key_lines, value_lines, cs, twist):
     cols = cs.shape[1]
-    rows = chips * 16
     lanes = 2 * cols
+    points = 16 * SEQ
+    rows = points // 2
+    specs, operands = [], []
+    for lines in (key_lines, value_lines):
+        for line, parts in zip(lines, (4, 4, 2, 2, 4), strict=True):
+            stride = line.shape[0] // parts // 16
+            for i in range(parts):
+                at = stride * (i + 1) - 1
+                specs.append(pl.BlockSpec((16, 4 * lanes), lambda i, o, at=at: (at, 0)))
+                operands.append(line)
     return pl.pallas_call(
         filter_kernel,
         grid_spec=pltpu.PrefetchScalarGridSpec(
             num_scalar_prefetch=1,
             grid=(1,),
-            in_specs=[
-                pl.BlockSpec((chips, 32, 2 * lanes), lambda i, z: (0, 4, z[0])),
-                pl.BlockSpec(cs.shape, lambda i, z: (0, 0, 0)),
-                pl.BlockSpec(twist.shape, lambda i, z: (0, 0, 0)),
+            in_specs=specs
+            + [
+                pl.BlockSpec(cs.shape, lambda i, o: (0, 0, 0)),
+                pl.BlockSpec(twist.shape, lambda i, o: (0, 0, 0)),
             ],
             out_specs=[
-                pl.BlockSpec((cols, 2 * rows), lambda i, z: (0, 0)),
-                pl.BlockSpec((2 * lanes, 2 * lanes), lambda i, z: (0, 0)),
+                pl.BlockSpec((cols, 2 * rows), lambda i, o: (0, 0)),
+                pl.BlockSpec((2 * lanes, 2 * lanes), lambda i, o: (0, 0)),
             ],
+            scratch_shapes=[pltpu.VMEM((2, points, lanes), BF16)],
         ),
         out_shape=[
             jax.ShapeDtypeStruct((cols, 2 * rows), F32),
@@ -352,7 +339,7 @@
         compiler_params=pltpu.CompilerParams(vmem_limit_bytes=VMEM),
         cost_estimate=pl.CostEstimate(flops=10**9, bytes_accessed=2**20, transcendentals=0),
         name="filter_part",
-    )(z.reshape(1), gathered, cs, twist)
+    )(order, *operands, cs, twist)
 
 
 def conv_kernel(
@@ -497,15 +484,17 @@
 
     def half_for(c):
         w = lax.dynamic_slice_in_dim(in_weight, c * chan, chan, 2)
-        f = lax.dynamic_slice_in_dim(filt, 2 * c, 2, 0)
-        return jnp.transpose(w, (1, 0, 2)).reshape(3 * depth, chan), jnp.concatenate([f[0], f[1]], axis=1)
-
-    keep, keep_f = half_for(core)
-    give, give_f = half_for(1 - core)
-    far_near = send(give[depth:], dz=1, dc=1)
-    far = send(keep[depth:], dz=1)
-    near = send(give, dc=1)
-    near_f = send(give_f, dc=1)
+        return jnp.transpose(w, (1, 0, 2)).reshape(3 * depth, chan)
+
+    def load(w, c, z_to):
+        f = lax.dynamic_index_in_dim(filt, 2 * c + z_to, 0, keepdims=False)
+        return jnp.concatenate([w, jnp.pad(f, ((0, 0), (0, chan - 2 * cols)))], axis=0)
+
+    keep, give = half_for(core), half_for(1 - core)
+    far = send(load(keep, core, 1 - z), dz=1)
+    far_near = send(load(give, 1 - core, 1 - z), dz=1, dc=1)
+    near = send(load(give, 1 - core, z), dc=1)
+    keep = load(keep, core, z)
     other = send(mine, dc=1)
 
     def ordered(own, partner, axis=0):
@@ -514,26 +503,29 @@
         )
 
     def block_of(n):
-        own, away = slice(n * depth, (n + 1) * depth), slice((n - 1) * depth, n * depth)
-        return jnp.concatenate([ordered(keep[own], near[own]), ordered(far[away], far_near[away])], axis=0)
-
-    key_block, value_block = block_of(1), block_of(2)
-    f_lanes = 2 * cols
-    gate_block = jnp.concatenate(
-        [
-            ordered(keep[:depth], near[:depth]),
-            jnp.concatenate(
-                [
-                    ordered(keep_f[:, :f_lanes], near_f[:, :f_lanes], 1),
-                    ordered(keep_f[:, f_lanes:], near_f[:, f_lanes:], 1),
-                ],
-                axis=1,
-            ),
-        ],
-        axis=0,
-    )
-    gathered = lax.all_gather(gate_block, "seq", axis=0, axis_index_groups=SAME_CORE)
-    key_block, value_block, other = lax.optimization_barrier((key_block, value_block, other))
+        part = slice(n * depth, (n + 1) * depth)
+        w = jnp.concatenate([ordered(keep[part], near[part]), ordered(far[part], far_near[part])], axis=0)
+        part, lanes = slice(0, depth), slice((n - 1) * chan // 2, n * chan // 2)
+        g = jnp.concatenate(
+            [
+                ordered(keep[part, lanes], near[part, lanes]),
+                ordered(far[part, lanes], far_near[part, lanes]),
+            ],
+            axis=0,
+        )
+        part, lanes = slice(3 * depth + 16 * (n - 1), 3 * depth + 16 * n), slice(0, 2 * cols)
+        f = jnp.concatenate(
+            [
+                ordered(keep[part, lanes], near[part, lanes], 1),
+                ordered(far[part, lanes], far_near[part, lanes], 1),
+            ],
+            axis=1,
+        )
+        return jnp.concatenate(
+            [jnp.concatenate([w, f], axis=0), jnp.pad(g, ((0, 16), (0, 0)))], axis=1
+        )
+
+    key_block, value_block, other = lax.optimization_barrier((block_of(1), block_of(2), other))
     half_ow = out_weight.shape[0] // 2
     ow_part = lax.dynamic_slice_in_dim(out_weight, core * half_ow, half_ow, 0)
     key_line, value_line, ow_part = lax.optimization_barrier(
@@ -565,22 +557,29 @@
             perm.append((t * 2 + th, index_of(tz ^ tc, ty, tx, tc) * 2 + 1 - th))
     ow_same = lax.ppermute(ow_part, ("seq", "ch"), perm)
 
-    source = last_part(totals, first[2:], last_lines)
+    source, gate = last_part(totals, first[2:], last_lines)
     packed = source.reshape(CHIPS, chan // CHIPS, 2 * rows)
     mine_ch = lax.all_to_all(packed, "seq", 0, 0, axis_index_groups=SAME_CORE)
 
     tw, a, ai, cs, twist = tables
-    f, m = filter_part(z, gathered, cs, twist)
+    k1_, k3_, v1_, v3_ = near_lines
+    f, m = filter_part(
+        order,
+        [key_line, k1_, last_lines[0], last_lines[1], k3_],
+        [value_line, v1_, last_lines[2], last_lines[3], v3_],
+        cs,
+        twist,
+    )
     forward, inverse = row_tables(rows, padded)
     fwd = jnp.asarray(forward.astype(np.float32).astype(ml_dtypes.bfloat16))
     inv = jnp.asarray(inverse.astype(np.float32).astype(ml_dtypes.bfloat16))
     conv = long_conv(mine_ch, fwd, inv, tw, a, ai, m, f)
+    conv = lax.all_to_all(conv, "seq", 0, 0, axis_index_groups=SAME_CORE)
     conv, ow_same = lax.optimization_barrier((conv, ow_same))
     ow_cross = send(ow_same, dc=1)
-    conv = lax.all_to_all(conv, "seq", 0, 0, axis_index_groups=SAME_CORE)
     conv = conv.reshape(chan, 2 * rows).astype(F32)
 
-    gate = gate_part(mine, other, gathered).astype(F32)
+    gate = gate.astype(F32)
     skip = lax.dynamic_slice_in_dim(skip_bias, core * chan, chan, 0)[:, None]
     gated = (gate * (conv + skip * source.astype(F32))).astype(BF16)
 

time: 211 us -> 211 us (level)
  waiting for transfers between devices: 57.1 us -> 73.3 us
  between operations: 13.8 us -> 0.31 us
  Pallas kernels: 73.7 us -> 71.1 us
    ppermute x21 -> x20, waiting for transfers between devices: 33.9 us -> 50.3 us  [send(): return lax.ppermute(value, 'seq', perm)]
    pallas_call x2 -> x1, Pallas kernels: 17.5 us -> 9.09 us  [last_part(): pl.pallas_call(last_kernel, grid=(4,), in_specs=[pl.BlockSpec((tile, wide...]
    all_to_all x1, waiting for transfers between devices: 7.56 us -> 12.9 us  [per_device(): conv = lax.all_to_all(conv, 'seq', 0, 0, axis_index_groups=SAME_CORE)]
    pallas_call x2, Pallas kernels: 22.1 us -> 26.5 us  [sum_part(): pl.pallas_call(kernel, grid_spec=pltpu.PrefetchScalarGridSpec(num_scalar_...]
    ppermute x1, waiting for transfers between devices: 3.49 us -> 0.24 us  [per_device(): from_hc = lax.ppermute(oth_there, ('seq', 'ch'), perm2)]
    all_to_all x1, waiting for transfers between devices: 12.1 us -> 9.76 us  [per_device(): mine_ch = lax.all_to_all(packed, 'seq', 0, 0, axis_index_groups=SAME_CORE)]
    ppermute x21 -> x20, starting transfers between devices: 30.1 us -> 29.7 us  [send(): return lax.ppermute(value, 'seq', perm)]
  transfers between devices with their start and end apart: 27 -> 25, of which waited for: 11 -> 15; matrix products, arithmetic and copies ran while one was open for 7% -> 8% of each run, Pallas kernels for 31% -> 30%
where the time goes in v10:
time: 211 us
  waiting for transfers between devices  73.3 us (35%)
  Pallas kernels  71.1 us (34%)
  starting transfers between devices  44.8 us (21%)
  local copies, waits for them, and re-layouts  11.4 us (5%)
  other arithmetic  9.63 us (5%)
    ppermute x20, waiting for transfers between devices, send(): return lax.ppermute(value, 'seq', perm)  50.3 us
    ppermute x20, starting transfers between devices, send(): return lax.ppermute(value, 'seq', perm)  29.7 us
    pallas_call x2, Pallas kernels, sum_part(): pl.pallas_call(kernel, grid_spec=pltpu.PrefetchScalarGridSpec(num_scalar_...  26.5 us
    pallas_call x2, Pallas kernels, mix_part(): pl.pallas_call(mix_kernel if total is None else mix_more_kernel, grid=(4,...  15.4 us
    pallas_call x1, Pallas kernels, long_conv(): pl.pallas_call(conv_kernel, in_specs=[vmem, hbm, hbm, hbm, vmem, vmem, vm...  13.5 us
    all_to_all x1, waiting for transfers between devices, per_device(): conv = lax.all_to_all(conv, 'seq', 0, 0, axis_index_groups=SAME_CORE)  12.9 us
    all_to_all x1, waiting for transfers between devices, per_device(): mine_ch = lax.all_to_all(packed, 'seq', 0, 0, axis_index_groups=SAME_CORE)  9.76 us
    pallas_call x1, Pallas kernels, last_part(): pl.pallas_call(last_kernel, grid=(4,), in_specs=[pl.BlockSpec((tile, wide...  9.09 us
  transfers between devices with their start and end apart: 25, of which 15 were waited for; matrix products, arithmetic and copies ran while one was open for 8% of the time, Pallas kernels for 30%

profile of v10, /device:TPU:1, one launch (start us, length us, event | category | flops | bytes accessed | tf_op | source)
XLA Modules:
  0.0 210.6 jit_solution(9015497055769616581)
XLA Ops:
  0.0 1.4 collective-permute-start.3
  1.4 0.9 copy.11
  2.5 1.1 constant_dynamic-slice_fusion.5
  3.6 3.6 %collective-permute-start.2 = (bf16[224,512]{1,0:T(8,128)(2,1)S(1)}, bf16[224,512]{1,0:T(8,128)(2,1)S(1)}, u32[]{:S(2)}, u32[]{:S(2)}) collective-permute-start(bf16[224,512]{1,0:T(8,128)(2,1)S(1)} %get-tuple-element.107), channel_id=1, source_target_pairs={{0,66},{2,64},{4,70},{6,68},{8,74},{10,72},{12,78},{14,76},{16,82}... | collective-permute-start | bytes 688136 | tf_op jit(solution)/shard_map/ppermute | solution.py:35
  7.4 0.5 collective-permute-start
  7.9 5.5 %collective-permute-done.2 = bf16[224,512]{1,0:T(8,128)(2,1)S(1)} collective-permute-done((bf16[224,512]{1,0:T(8,128)(2,1)S(1)}, bf16[224,512]{1,0:T(8,128)(2,1)S(1)}, u32[]{:S(2)}, u32[]{:S(2)}) %collective-permute-start.2) | collective-permute-done | bytes 229408 | tf_op jit(solution)/shard_map/ppermute | solution.py:35
  13.4 4.8 %collective-permute-done.1 = bf16[224,512]{1,0:T(8,128)(2,1)S(1)} collective-permute-done((bf16[224,512]{1,0:T(8,128)(2,1)S(1)}, bf16[224,512]{1,0:T(8,128)(2,1)S(1)}, u32[]{:S(2)}, u32[]{:S(2)}) %collective-permute-start.1) | collective-permute-done | bytes 229408 | tf_op jit(solution)/shard_map/ppermute | solution.py:35
  18.6 1.3 collective-permute-start.6
  19.9 4.7 %constant_dynamic-slice_fusion.3 = bf16[512,4096]{1,0:T(8,128)(2,1)} fusion(bf16[1024,4096]{1,0:T(8,128)(2,1)} %w_here.1, s32[]{:T(128)S(6)} %select_n.290), kind=kLoop, calls=%fused_computation.141 | loop fusion | bytes 8388612 | tf_op jit(solution)/shard_map/dynamic_slice | solution.py:530
  24.6 2.5 %collective-permute-start.5 = (bf16[272,768]{1,0:T(8,128)(2,1)S(1)}, bf16[272,768]{1,0:T(8,128)(2,1)S(1)}, u32[]{:S(2)}, u32[]{:S(2)}) collective-permute-start(bf16[272,768]{1,0:T(8,128)(2,1)S(1)} %pad_maximum_fusion.3), channel_id=1, source_target_pairs={{0,8},{2,10},{4,12},{6,14},{8,0},{10,2},{12,4},{14,6},{16,24},{18,... | collective-permute-start | bytes 1253384 | tf_op jit(solution)/shard_map/ppermute | solution.py:35
  27.0 1.2 collective-permute-start.4
  28.2 1.4 collective-permute-start.9
  29.6 2.6 %collective-permute-start.8 = (bf16[272,768]{1,0:T(8,128)(2,1)S(1)}, bf16[272,768]{1,0:T(8,128)(2,1)S(1)}, u32[]{:S(2)}, u32[]{:S(2)}) collective-permute-start(bf16[272,768]{1,0:T(8,128)(2,1)S(1)} %pad_maximum_fusion.4), channel_id=1, source_target_pairs={{0,32},{2,34},{4,36},{6,38},{8,40},{10,42},{12,44},{14,46},{16,48}... | collective-permute-start | bytes 1253384 | tf_op jit(solution)/shard_map/ppermute | solution.py:35
  32.2 1.1 collective-permute-start.7
  33.3 0.6 pad_add_fusion.order_ref
  33.9 6.6 %collective-permute-done.5 = bf16[272,768]{1,0:T(8,128)(2,1)S(1)} collective-permute-done((bf16[272,768]{1,0:T(8,128)(2,1)S(1)}, bf16[272,768]{1,0:T(8,128)(2,1)S(1)}, u32[]{:S(2)}, u32[]{:S(2)}) %collective-permute-start.5) | collective-permute-done | bytes 417824 | tf_op jit(solution)/shard_map/ppermute | solution.py:35
  40.5 4.2 %collective-permute-done.4 = bf16[272,768]{1,0:T(8,128)(2,1)S(1)} collective-permute-done((bf16[272,768]{1,0:T(8,128)(2,1)S(1)}, bf16[272,768]{1,0:T(8,128)(2,1)S(1)}, u32[]{:S(2)}, u32[]{:S(2)}) %collective-permute-start.4) | collective-permute-done | bytes 417824 | tf_op jit(solution)/shard_map/ppermute | solution.py:35
  44.7 1.3 pad_maximum_fusion.key_line.refs_0_.refs_1_.refs_2_.refs_3_
  46.0 3.4 %collective-permute-done.8 = bf16[272,768]{1,0:T(8,128)(2,1)S(1)} collective-permute-done((bf16[272,768]{1,0:T(8,128)(2,1)S(1)}, bf16[272,768]{1,0:T(8,128)(2,1)S(1)}, u32[]{:S(2)}, u32[]{:S(2)}) %collective-permute-start.8) | collective-permute-done | bytes 417824 | tf_op jit(solution)/shard_map/ppermute | solution.py:35
  49.4 0.3 collective-permute-done.7
  49.7 1.3 pad_maximum_fusion.1.value_line.refs_16_.refs_17_.refs_18_.refs_19_
  51.0 3.4 %collective-permute-start.10 = (bf16[1088,768]{1,0:T(8,128)(2,1)}, bf16[1088,768]{1,0:T(8,128)(2,1)S(1)}, u32[]{:S(2)}, u32[]{:S(2)}) collective-permute-start(bf16[1088,768]{1,0:T(8,128)(2,1)} %pad_maximum_fusion.key_line.refs_0_.refs_1_.refs_2_.refs_3_), channel_id=1, source_target_pairs={{0,48},{2,50},{4,52},{6,54},{8,56},{10,58},{12,60},{14,62},{16,0},... | collective-permute-start | bytes 5013512 | tf_op jit(solution)/shard_map/ppermute | solution.py:35
  54.5 1.4 collective-permute-start.13
  56.3 0.7 fusion.29.ai_ref
  57.0 0.3 fusion.53
  57.3 0.7 pad_maximum_fusion.6
  58.0 0.6 fusion.35
  58.6 0.7 pad_maximum_fusion.5.tw_hbm
  59.3 2.6 %collective-permute-start.18 = (bf16[512,4096]{1,0:T(8,128)(2,1)}, bf16[512,4096]{1,0:T(8,128)(2,1)}, u32[]{:S(2)}, u32[]{:S(2)}) collective-permute-start(bf16[512,4096]{1,0:T(8,128)(2,1)} %constant_dynamic-slice_fusion.3), channel_id=1, source_target_pairs={{0,1},{1,0},{2,67},{3,66},{4,5},{5,4},{6,71},{7,70},{8,9},{9,8},{1... | collective-permute-start | bytes 12582920 | tf_op jit(solution)/shard_map/ppermute | solution.py:558
  61.8 11.8 %first_part.1 = (f32[1024,768]{1,0:T(8,128)}, f32[1024,768]{1,0:T(8,128)}, bf16[1024,1024]{1,0:T(8,128)(2,1)}, bf16[1024,1024]{1,0:T(8,128)(2,1)}) custom-call(s32[2,32]{1,0:T(2,128)} %pad_add_fusion.order_ref, bf16[512,4096]{1,0:T(8,128)(2,1)} %bitcast.57, bf16[512,4096]{1,0:T(8,128)(2,1)} %collective-permute-done.3.other_ref, ...), custom_call_target="tpu_custom_call" | custom-call | flops 3221225472 | bytes 18874368 | tf_op jit(solution)/shard_map/first_part/pallas_call | solution.py:122
  73.6 16.5 %collective-permute-done.10.k1.refs_0_.refs_4_.refs_5_.refs_6_.refs_7_ = bf16[1088,768]{1,0:T(8,128)(2,1)S(1)} collective-permute-done((bf16[1088,768]{1,0:T(8,128)(2,1)}, bf16[1088,768]{1,0:T(8,128)(2,1)S(1)}, u32[]{:S(2)}, u32[]{:S(2)}) %collective-permute-start.10) | collective-permute-done | bytes 1671200 | tf_op jit(solution)/shard_map/ppermute | solution.py:35
  90.1 3.1 %collective-permute-done.11.k3.refs_1_.refs_12_.refs_13_.refs_14_.refs_15_ = bf16[1088,768]{1,0:T(8,128)(2,1)S(1)} collective-permute-done((bf16[1088,768]{1,0:T(8,128)(2,1)}, bf16[1088,768]{1,0:T(8,128)(2,1)S(1)}, u32[]{:S(2)}, u32[]{:S(2)}) %collective-permute-start.11) | collective-permute-done | bytes 1671200 | tf_op jit(solution)/shard_map/ppermute | solution.py:35
  93.2 1.2 copy-done.1
  94.4 3.2 %cut_halves.1 = (bf16[544,768]{1,0:T(8,128)(2,1)}, bf16[544,768]{1,0:T(8,128)(2,1)}, bf16[544,768]{1,0:T(8,128)(2,1)}, bf16[544,768]{1,0:T(8,128)(2,1)}) custom-call(bf16[1088,768]{1,0:T(8,128)(2,1)} %copy-done, bf16[1088,768]{1,0:T(8,128)(2,1)} %copy-done.1, bf16[1088,768]{1,0:T(8,128)(2,1)} %collective-permute-done.12.v1.refs_2_.refs_20_.refs_21_.refs_22_.refs_23_, ...), custom_call_target="tpu_custom_call" | custom-call | bytes 6684672 | tf_op jit(solution)/shard_map/cut_halves/pallas_call | solution.py:154
  97.6 0.9 collective-permute-start.14
  98.6 0.5 collective-permute-start.15
  99.1 1.4 collective-permute-start.17
  100.6 14.7 %second_part.1 = (f32[1024,768]{1,0:T(8,128)}, f32[1024,768]{1,0:T(8,128)}) custom-call(s32[2,32]{1,0:T(2,128)} %pad_add_fusion.order_ref, bf16[512,4096]{1,0:T(8,128)(2,1)} %bitcast.58, bf16[512,4096]{1,0:T(8,128)(2,1)} %collective-permute-done.3.other_ref, f32[1024,768]{1,0:T(8,128)} %get-tuple-element.49.key_in, f32[1024,768]{1,0:T(8,128)} %get-tuple-element.50.value_in, ...), custom_call_target="tpu_custom_call" | custom-call | flops 6442450944 | bytes 18874368 | tf_op jit(solution)/shard_map/second_part/pallas_call | solution.py:122
  115.3 1.1 collective-permute-done.14.ka.refs_8_.refs_9_
  116.4 1.1 collective-permute-done.15.kb.refs_10_.refs_11_
  117.5 0.7 collective-permute-done.17.vb.refs_26_.refs_27_
  118.2 0.2 copy-done.3
  118.5 0.3 copy-done.4
  118.8 0.4 copy-done.5
  119.1 9.1 %last_part.1 = (bf16[512,1024]{1,0:T(8,128)(2,1)}, bf16[512,1024]{1,0:T(8,128)(2,1)}) custom-call(f32[1024,768]{1,0:T(8,128)} %get-tuple-element.55.key_ref, f32[1024,768]{1,0:T(8,128)} %get-tuple-element.56.value_ref, bf16[1024,1024]{1,0:T(8,128)(2,1)} %get-tuple-element.57.key_tok_ref, bf16[1024,1024]{1,0:T(8,128)(2,1)} %get-tuple-element.58.value_tok_ref, ...), custom_call_target="tpu_custom_call" | custom-call | flops 3221225472 | bytes 16777216 | tf_op jit(solution)/shard_map/last_part/pallas_call | solution.py:188
  128.2 6.0 %all-to-all-start = ((bf16[32,16,1024]{2,1,0:T(8,128)(2,1)}), bf16[32,16,1024]{2,1,0:T(8,128)(2,1)S(1)}, u32[]{:S(2)}, u32[]{:S(2)}) async-start(bf16[32,16,1024]{2,1,0:T(8,128)(2,1)} %bitcast.49), calls=%async_computation | async-start | bytes 2097152 | tf_op jit(solution)/shard_map/all_to_all | solution.py:562
  134.3 0.8 copy.12.a_ref
  135.0 3.4 %filter_part.1 = (f32[64,1024]{1,0:T(8,128)}, bf16[256,256]{1,0:T(8,128)(2,1)}) custom-call(s32[2,32]{1,0:T(2,128)} %pad_add_fusion.order_ref, bf16[1088,768]{1,0:T(8,128)(2,1)} %pad_maximum_fusion.key_line.refs_0_.refs_1_.refs_2_.refs_3_, bf16[1088,768]{1,0:T(8,128)(2,1)} %pad_maximum_fusion.key_line.refs_0_.refs_1_.refs_2_.refs_3_, ...), custom_call_target="tpu_custom_call" | custom-call | flops 1000000000 | bytes 1048576 | tf_op jit(solution)/shard_map/filter_part/pallas_call | solution.py:319
  138.4 9.8 %all-to-all-done.x_ref = bf16[32,16,1024]{2,1,0:T(8,128)(2,1)S(1)} async-done(((bf16[32,16,1024]{2,1,0:T(8,128)(2,1)}), bf16[32,16,1024]{2,1,0:T(8,128)(2,1)S(1)}, u32[]{:S(2)}, u32[]{:S(2)}) %all-to-all-start) | async-done | bytes 1048608 | tf_op jit(solution)/shard_map/all_to_all | solution.py:562
  148.2 1.0 copy-done.7
  149.2 13.5 %long_conv.1 = bf16[32,16,1024]{2,1,0:T(8,128)(2,1)} custom-call(bf16[32,16,1024]{2,1,0:T(8,128)(2,1)} %copy-done.7, bf16[512,1024]{1,0:T(8,128)(2,1)} %constant.204.clone.fwd_hbm, bf16[1024,512]{1,0:T(8,128)(2,1)} %constant.205.clone.inv_hbm, f32[64,1024]{1,0:T(8,128)} %pad_maximum_fusion.5.tw_hbm, bf16[256,256]{1,0:T(8,128)(2,1)} %copy.12.a_ref, ...), custom_call_target="tpu_custom_call" | custom-call | flops 8000000000 | bytes 8388608 | tf_op jit(solution)/shard_map/long_conv/pallas_call | solution.py:422
  162.7 4.4 %all-to-all-start.1 = ((bf16[32,16,1024]{2,1,0:T(8,128)(2,1)}), bf16[32,16,1024]{2,1,0:T(8,128)(2,1)S(1)}, u32[]{:S(2)}, u32[]{:S(2)}) async-start(bf16[32,16,1024]{2,1,0:T(8,128)(2,1)} %long_conv.1), calls=%async_computation.1 | async-start | bytes 2097152 | tf_op jit(solution)/shard_map/all_to_all | solution.py:577
  167.1 12.9 %all-to-all-done.1 = bf16[32,16,1024]{2,1,0:T(8,128)(2,1)S(1)} async-done(((bf16[32,16,1024]{2,1,0:T(8,128)(2,1)}), bf16[32,16,1024]{2,1,0:T(8,128)(2,1)S(1)}, u32[]{:S(2)}, u32[]{:S(2)}) %all-to-all-start.1) | async-done | bytes 1048608 | tf_op jit(solution)/shard_map/all_to_all | solution.py:577
  180.0 6.1 %collective-permute-start.22 = (bf16[512,4096]{1,0:T(8,128)(2,1)}, bf16[512,4096]{1,0:T(8,128)(2,1)}, u32[]{:S(2)}, u32[]{:S(2)}) collective-permute-start(bf16[512,4096]{1,0:T(8,128)(2,1)} %collective-permute-done.18.w_near), channel_id=1, source_target_pairs={{0,2},{2,0},{4,6},{6,4},{8,10},{10,8},{12,14},{14,12},{16,18},{18,... | collective-permute-start | bytes 12582920 | tf_op jit(solution)/shard_map/ppermute | solution.py:35
  186.2 1.7 fusion.1
  188.2 0.8 collective-permute-start.20
  189.0 1.3 collective-permute-start.21
  190.3 3.0 %collective-permute-done.19 = bf16[512,256]{1,0:T(8,128)(2,1)S(1)} collective-permute-done((bf16[512,256]{1,0:T(8,128)(2,1)S(1)}, bf16[512,256]{1,0:T(8,128)(2,1)S(1)}, u32[]{:S(2)}, u32[]{:S(2)}) %collective-permute-start.19) | collective-permute-done | bytes 262176 | tf_op jit(solution)/shard_map/ppermute | solution.py:35
  193.4 0.8 pad_maximum_fusion.2.here
  194.3 7.4 %mix_part.1.total_ref = f32[256,4096]{1,0:T(8,128)} custom-call(bf16[1024,256]{1,0:T(8,128)(2,1)} %pad_maximum_fusion.2.here, bf16[1024,4096]{1,0:T(8,128)(2,1)} %w_here.1), custom_call_target="tpu_custom_call" | custom-call | flops 2147483648 | bytes 12582912 | tf_op jit(solution)/shard_map/mix_part/pallas_call | solution.py:243
  201.7 0.2 collective-permute-done.21.far_h
  201.9 0.5 copy-done.8
  202.4 0.2 copy-done.9
  202.6 8.0 %mix_more.1 = bf16[256,4096]{1,0:T(8,128)(2,1)} custom-call(f32[256,4096]{1,0:T(8,128)} %mix_part.1.total_ref, bf16[512,256]{1,0:T(8,128)(2,1)} %copy-done.8, bf16[512,256]{1,0:T(8,128)(2,1)} %copy-done.9, bf16[512,4096]{1,0:T(8,128)(2,1)} %collective-permute-done.18.w_near, bf16[512,4096]{1,0:T(8,128)(2,1)} %collective-permute-done.22.w_far), custom_call_target="tpu_custom_call" | custom-call | flops 2147483648 | bytes 12582912 | tf_op jit(solution)/shard_map/mix_more/pallas_call | solution.py:243
  (63 shorter events, 1.6 us)
Async XLA Ops:
  0.0 18.6 %collective-permute-start.3 = (bf16[512,4096]{1,0:T(8,128)(2,1)}, bf16[512,4096]{1,0:T(8,128)(2,1)}, u32[]{:S(2)}, u32[]{:S(2)}) collective-permute-start(bf16[512,4096]{1,0:T(8,128)(2,1)} %bitcast.56), channel_id=1, source_target_pairs={{0,2},{2,0},{4,6},{6,4},{8,10},{10,8},{12,14},{14,12},{16,18},{18,... | collective-permute-start | bytes 12582920 | tf_op jit(solution)/shard_map/ppermute | solution.py:35
  3.6 9.8 %collective-permute-start.2 = (bf16[224,512]{1,0:T(8,128)(2,1)S(1)}, bf16[224,512]{1,0:T(8,128)(2,1)S(1)}, u32[]{:S(2)}, u32[]{:S(2)}) collective-permute-start(bf16[224,512]{1,0:T(8,128)(2,1)S(1)} %get-tuple-element.107), channel_id=1, source_target_pairs={{0,66},{2,64},{4,70},{6,68},{8,74},{10,72},{12,78},{14,76},{16,82}... | collective-permute-start | bytes 688136 | tf_op jit(solution)/shard_map/ppermute | solution.py:35
  7.2 11.0 %collective-permute-start.1 = (bf16[224,512]{1,0:T(8,128)(2,1)S(1)}, bf16[224,512]{1,0:T(8,128)(2,1)S(1)}, u32[]{:S(2)}, u32[]{:S(2)}) collective-permute-start(bf16[224,512]{1,0:T(8,128)(2,1)S(1)} %fusion.18), channel_id=1, source_target_pairs={{0,64},{2,66},{4,68},{6,70},{8,72},{10,74},{12,76},{14,78},{16,80}... | collective-permute-start | bytes 688136 | tf_op jit(solution)/shard_map/ppermute | solution.py:35
  7.4 10.8 %collective-permute-start = (bf16[224,512]{1,0:T(8,128)(2,1)S(1)}, bf16[224,512]{1,0:T(8,128)(2,1)S(1)}, u32[]{:S(2)}, u32[]{:S(2)}) collective-permute-start(bf16[224,512]{1,0:T(8,128)(2,1)S(1)} %get-tuple-element.106), channel_id=1, source_target_pairs={{0,2},{2,0},{4,6},{6,4},{8,10},{10,8},{12,14},{14,12},{16,18},{18,... | collective-permute-start | bytes 688136 | tf_op jit(solution)/shard_map/ppermute | solution.py:35
  18.6 9.6 %copy-start.11 = (s32[32]{0:T(128)S(1)}, s32[32]{0:T(128)}, u32[]{:S(2)}) copy-start(s32[32]{0:T(128)} %constant.203.clone) | copy-start | bytes 388
  18.6 9.6 %copy-start.12 = (s32[32]{0:T(128)S(1)}, s32[32]{0:T(128)}, u32[]{:S(2)}) copy-start(s32[32]{0:T(128)} %constant.202.clone) | copy-start | bytes 388
  18.6 9.6 %copy-start.13 = (s32[32]{0:T(128)S(1)}, s32[32]{0:T(128)}, u32[]{:S(2)}) copy-start(s32[32]{0:T(128)} %constant.201.clone) | copy-start | bytes 388
  18.6 13.6 %collective-permute-start.6 = (bf16[272,768]{1,0:T(8,128)(2,1)S(1)}, bf16[272,768]{1,0:T(8,128)(2,1)S(1)}, u32[]{:S(2)}, u32[]{:S(2)}) collective-permute-start(bf16[272,768]{1,0:T(8,128)(2,1)S(1)} %pad_maximum_fusion.3), channel_id=1, source_target_pairs={{0,4},{2,6},{4,8},{6,10},{8,12},{10,14},{12,0},{14,2},{16,20},{18,... | collective-permute-start | bytes 1253384 | tf_op jit(solution)/shard_map/ppermute | solution.py:35
  24.6 15.9 %collective-permute-start.5 = (bf16[272,768]{1,0:T(8,128)(2,1)S(1)}, bf16[272,768]{1,0:T(8,128)(2,1)S(1)}, u32[]{:S(2)}, u32[]{:S(2)}) collective-permute-start(bf16[272,768]{1,0:T(8,128)(2,1)S(1)} %pad_maximum_fusion.3), channel_id=1, source_target_pairs={{0,8},{2,10},{4,12},{6,14},{8,0},{10,2},{12,4},{14,6},{16,24},{18,... | collective-permute-start | bytes 1253384 | tf_op jit(solution)/shard_map/ppermute | solution.py:35
  27.0 17.6 %collective-permute-start.4 = (bf16[272,768]{1,0:T(8,128)(2,1)S(1)}, bf16[272,768]{1,0:T(8,128)(2,1)S(1)}, u32[]{:S(2)}, u32[]{:S(2)}) collective-permute-start(bf16[272,768]{1,0:T(8,128)(2,1)S(1)} %pad_maximum_fusion.3), channel_id=1, source_target_pairs={{0,12},{2,14},{4,0},{6,2},{8,4},{10,6},{12,8},{14,10},{16,28},{18,... | collective-permute-start | bytes 1253384 | tf_op jit(solution)/shard_map/ppermute | solution.py:35
  28.2 17.8 %collective-permute-start.9 = (bf16[272,768]{1,0:T(8,128)(2,1)S(1)}, bf16[272,768]{1,0:T(8,128)(2,1)S(1)}, u32[]{:S(2)}, u32[]{:S(2)}) collective-permute-start(bf16[272,768]{1,0:T(8,128)(2,1)S(1)} %pad_maximum_fusion.4), channel_id=1, source_target_pairs={{0,16},{2,18},{4,20},{6,22},{8,24},{10,26},{12,28},{14,30},{16,32}... | collective-permute-start | bytes 1253384 | tf_op jit(solution)/shard_map/ppermute | solution.py:35
  29.6 19.8 %collective-permute-start.8 = (bf16[272,768]{1,0:T(8,128)(2,1)S(1)}, bf16[272,768]{1,0:T(8,128)(2,1)S(1)}, u32[]{:S(2)}, u32[]{:S(2)}) collective-permute-start(bf16[272,768]{1,0:T(8,128)(2,1)S(1)} %pad_maximum_fusion.4), channel_id=1, source_target_pairs={{0,32},{2,34},{4,36},{6,38},{8,40},{10,42},{12,44},{14,46},{16,48}... | collective-permute-start | bytes 1253384 | tf_op jit(solution)/shard_map/ppermute | solution.py:35
  32.2 17.5 %collective-permute-start.7 = (bf16[272,768]{1,0:T(8,128)(2,1)S(1)}, bf16[272,768]{1,0:T(8,128)(2,1)S(1)}, u32[]{:S(2)}, u32[]{:S(2)}) collective-permute-start(bf16[272,768]{1,0:T(8,128)(2,1)S(1)} %pad_maximum_fusion.4), channel_id=1, source_target_pairs={{0,48},{2,50},{4,52},{6,54},{8,56},{10,58},{12,60},{14,62},{16,0},... | collective-permute-start | bytes 1253384 | tf_op jit(solution)/shard_map/ppermute | solution.py:35
  51.0 39.1 %collective-permute-start.10 = (bf16[1088,768]{1,0:T(8,128)(2,1)}, bf16[1088,768]{1,0:T(8,128)(2,1)S(1)}, u32[]{:S(2)}, u32[]{:S(2)}) collective-permute-start(bf16[1088,768]{1,0:T(8,128)(2,1)} %pad_maximum_fusion.key_line.refs_0_.refs_1_.refs_2_.refs_3_), channel_id=1, source_target_pairs={{0,48},{2,50},{4,52},{6,54},{8,56},{10,58},{12,60},{14,62},{16,0},... | collective-permute-start | bytes 5013512 | tf_op jit(solution)/shard_map/ppermute | solution.py:35
  54.4 38.8 %collective-permute-start.11 = (bf16[1088,768]{1,0:T(8,128)(2,1)}, bf16[1088,768]{1,0:T(8,128)(2,1)S(1)}, u32[]{:S(2)}, u32[]{:S(2)}) collective-permute-start(bf16[1088,768]{1,0:T(8,128)(2,1)} %pad_maximum_fusion.key_line.refs_0_.refs_1_.refs_2_.refs_3_), channel_id=1, source_target_pairs={{0,16},{2,18},{4,20},{6,22},{8,24},{10,26},{12,28},{14,30},{16,32}... | collective-permute-start | bytes 5013512 | tf_op jit(solution)/shard_map/ppermute | solution.py:35
  54.5 38.8 %collective-permute-start.12 = (bf16[1088,768]{1,0:T(8,128)(2,1)}, bf16[1088,768]{1,0:T(8,128)(2,1)}, u32[]{:S(2)}, u32[]{:S(2)}) collective-permute-start(bf16[1088,768]{1,0:T(8,128)(2,1)} %pad_maximum_fusion.1.value_line.refs_16_.refs_17_.refs_18_.refs_19_), channel_id=1, source_target_pairs={{0,12},{2,14},{4,0},{6,2},{8,4},{10,6},{12,8},{14,10},{16,28},{18,... | collective-permute-start | bytes 5013512 | tf_op jit(solution)/shard_map/ppermute | solution.py:35
  54.5 38.8 %collective-permute-start.13 = (bf16[1088,768]{1,0:T(8,128)(2,1)}, bf16[1088,768]{1,0:T(8,128)(2,1)}, u32[]{:S(2)}, u32[]{:S(2)}) collective-permute-start(bf16[1088,768]{1,0:T(8,128)(2,1)} %pad_maximum_fusion.1.value_line.refs_16_.refs_17_.refs_18_.refs_19_), channel_id=1, source_target_pairs={{0,4},{2,6},{4,8},{6,10},{8,12},{10,14},{12,0},{14,2},{16,20},{18,... | collective-permute-start | bytes 5013512 | tf_op jit(solution)/shard_map/ppermute | solution.py:35
  59.3 107.8 %collective-permute-start.18 = (bf16[512,4096]{1,0:T(8,128)(2,1)}, bf16[512,4096]{1,0:T(8,128)(2,1)}, u32[]{:S(2)}, u32[]{:S(2)}) collective-permute-start(bf16[512,4096]{1,0:T(8,128)(2,1)} %constant_dynamic-slice_fusion.3), channel_id=1, source_target_pairs={{0,1},{1,0},{2,67},{3,66},{4,5},{5,4},{6,71},{7,70},{8,9},{9,8},{1... | collective-permute-start | bytes 12582920 | tf_op jit(solution)/shard_map/ppermute | solution.py:558
  90.1 3.1 %copy-start = (bf16[1088,768]{1,0:T(8,128)(2,1)}, bf16[1088,768]{1,0:T(8,128)(2,1)S(1)}, u32[]{:S(2)}) copy-start(bf16[1088,768]{1,0:T(8,128)(2,1)S(1)} %collective-permute-done.10.k1.refs_0_.refs_4_.refs_5_.refs_6_.refs_7_) | copy-start | bytes 5013508
  93.2 1.2 copy-start.1
  97.6 18.7 %collective-permute-start.14 = (bf16[544,768]{1,0:T(8,128)(2,1)}, bf16[544,768]{1,0:T(8,128)(2,1)S(1)}, u32[]{:S(2)}, u32[]{:S(2)}) collective-permute-start(bf16[544,768]{1,0:T(8,128)(2,1)} %get-tuple-element.59), channel_id=1, source_target_pairs={{0,48},{2,50},{4,52},{6,54},{8,56},{10,58},{12,60},{14,62},{16,0},... | collective-permute-start | bytes 2506760 | tf_op jit(solution)/shard_map/ppermute | solution.py:35
  98.6 19.0 %collective-permute-start.15 = (bf16[544,768]{1,0:T(8,128)(2,1)}, bf16[544,768]{1,0:T(8,128)(2,1)S(1)}, u32[]{:S(2)}, u32[]{:S(2)}) collective-permute-start(bf16[544,768]{1,0:T(8,128)(2,1)} %get-tuple-element.60), channel_id=1, source_target_pairs={{0,16},{2,18},{4,20},{6,22},{8,24},{10,26},{12,28},{14,30},{16,32}... | collective-permute-start | bytes 2506760 | tf_op jit(solution)/shard_map/ppermute | solution.py:35
  99.1 18.4 %collective-permute-start.16 = (bf16[544,768]{1,0:T(8,128)(2,1)}, bf16[544,768]{1,0:T(8,128)(2,1)S(1)}, u32[]{:S(2)}, u32[]{:S(2)}) collective-permute-start(bf16[544,768]{1,0:T(8,128)(2,1)} %get-tuple-element.61), channel_id=1, source_target_pairs={{0,12},{2,14},{4,0},{6,2},{8,4},{10,6},{12,8},{14,10},{16,28},{18,... | collective-permute-start | bytes 2506760 | tf_op jit(solution)/shard_map/ppermute | solution.py:35
  99.1 19.1 %collective-permute-start.17 = (bf16[544,768]{1,0:T(8,128)(2,1)}, bf16[544,768]{1,0:T(8,128)(2,1)S(1)}, u32[]{:S(2)}, u32[]{:S(2)}) collective-permute-start(bf16[544,768]{1,0:T(8,128)(2,1)} %get-tuple-element.62), channel_id=1, source_target_pairs={{0,4},{2,6},{4,8},{6,10},{8,12},{10,14},{12,0},{14,2},{16,20},{18,... | collective-permute-start | bytes 2506760 | tf_op jit(solution)/shard_map/ppermute | solution.py:35
  116.4 1.9 copy-start.2
  117.5 0.9 copy-start.3
  117.5 1.2 copy-start.4
  118.2 0.9 copy-start.5
  128.2 20.0 %all-to-all-start = ((bf16[32,16,1024]{2,1,0:T(8,128)(2,1)}), bf16[32,16,1024]{2,1,0:T(8,128)(2,1)S(1)}, u32[]{:S(2)}, u32[]{:S(2)}) async-start(bf16[32,16,1024]{2,1,0:T(8,128)(2,1)} %bitcast.49), calls=%async_computation | async-start | bytes 2097152 | tf_op jit(solution)/shard_map/all_to_all | solution.py:562
  148.2 1.0 copy-start.7
  149.2 37.0 %copy-start.10 = (f32[1024]{0:T(1024)S(1)}, f32[1024]{0:T(1024)}, u32[]{:S(2)}) copy-start(f32[1024]{0:T(1024)} %param.13) | copy-start | bytes 12292
  149.2 37.1 %copy-start.6 = (bf16[512,1024]{1,0:T(8,128)(2,1)S(1)}, bf16[512,1024]{1,0:T(8,128)(2,1)}, u32[]{:S(2)}) copy-start(bf16[512,1024]{1,0:T(8,128)(2,1)} %get-tuple-element.64) | copy-start | bytes 3145732
  162.7 17.4 %all-to-all-start.1 = ((bf16[32,16,1024]{2,1,0:T(8,128)(2,1)}), bf16[32,16,1024]{2,1,0:T(8,128)(2,1)S(1)}, u32[]{:S(2)}, u32[]{:S(2)}) async-start(bf16[32,16,1024]{2,1,0:T(8,128)(2,1)} %long_conv.1), calls=%async_computation.1 | async-start | bytes 2097152 | tf_op jit(solution)/shard_map/all_to_all | solution.py:577
  180.0 21.9 %collective-permute-start.22 = (bf16[512,4096]{1,0:T(8,128)(2,1)}, bf16[512,4096]{1,0:T(8,128)(2,1)}, u32[]{:S(2)}, u32[]{:S(2)}) collective-permute-start(bf16[512,4096]{1,0:T(8,128)(2,1)} %collective-permute-done.18.w_near), channel_id=1, source_target_pairs={{0,2},{2,0},{4,6},{6,4},{8,10},{10,8},{12,14},{14,12},{16,18},{18,... | collective-permute-start | bytes 12582920 | tf_op jit(solution)/shard_map/ppermute | solution.py:35
  188.1 5.2 %collective-permute-start.19 = (bf16[512,256]{1,0:T(8,128)(2,1)S(1)}, bf16[512,256]{1,0:T(8,128)(2,1)S(1)}, u32[]{:S(2)}, u32[]{:S(2)}) collective-permute-start(bf16[512,256]{1,0:T(8,128)(2,1)S(1)} %get-tuple-element.81), channel_id=1, source_target_pairs={{0,2},{2,0},{4,6},{6,4},{8,10},{10,8},{12,14},{14,12},{16,18},{18,... | collective-permute-start | bytes 786440 | tf_op jit(solution)/shard_map/ppermute | solution.py:35
  188.2 13.5 %collective-permute-start.20 = (bf16[512,256]{1,0:T(8,128)(2,1)S(1)}, bf16[512,256]{1,0:T(8,128)(2,1)S(1)}, u32[]{:S(2)}, u32[]{:S(2)}) collective-permute-start(bf16[512,256]{1,0:T(8,128)(2,1)S(1)} %get-tuple-element.80), channel_id=1, source_target_pairs={{0,1},{1,0},{2,3},{3,2},{4,5},{5,4},{6,7},{7,6},{8,9},{9,8},{10,11... | collective-permute-start | bytes 786440 | tf_op jit(solution)/shard_map/ppermute | solution.py:592
  189.0 12.9 %collective-permute-start.21 = (bf16[512,256]{1,0:T(8,128)(2,1)S(1)}, bf16[512,256]{1,0:T(8,128)(2,1)S(1)}, u32[]{:S(2)}, u32[]{:S(2)}) collective-permute-start(bf16[512,256]{1,0:T(8,128)(2,1)S(1)} %get-tuple-element.79), channel_id=1, source_target_pairs={{0,3},{1,2},{2,1},{3,0},{4,7},{5,6},{6,5},{7,4},{8,11},{9,10},{10,... | collective-permute-start | bytes 786440 | tf_op jit(solution)/shard_map/ppermute | solution.py:597
  201.7 0.7 copy-start.8
  201.9 0.7 copy-start.9

commit v11 on v10

--- a/solution.py
+++ b/solution.py
@@ -525,9 +525,11 @@
             [jnp.concatenate([w, f], axis=0), jnp.pad(g, ((0, 16), (0, 0)))], axis=1
         )
 
-    key_block, value_block, other = lax.optimization_barrier((block_of(1), block_of(2), other))
     half_ow = out_weight.shape[0] // 2
     ow_part = lax.dynamic_slice_in_dim(out_weight, core * half_ow, half_ow, 0)
+    key_block, value_block, other, ow_part = lax.optimization_barrier(
+        (block_of(1), block_of(2), other, ow_part)
+    )
     key_line, value_line, ow_part = lax.optimization_barrier(
         (gather_line(key_block, "dx"), gather_line(value_block, "dy"), ow_part)
     )
@@ -573,10 +575,10 @@
     forward, inverse = row_tables(rows, padded)
     fwd = jnp.asarray(forward.astype(np.float32).astype(ml_dtypes.bfloat16))
     inv = jnp.asarray(inverse.astype(np.float32).astype(ml_dtypes.bfloat16))
+    mine_ch, ow_same, f, m = lax.optimization_barrier((mine_ch, ow_same, f, m))
+    ow_cross = send(ow_same, dc=1)
     conv = long_conv(mine_ch, fwd, inv, tw, a, ai, m, f)
     conv = lax.all_to_all(conv, "seq", 0, 0, axis_index_groups=SAME_CORE)
-    conv, ow_same = lax.optimization_barrier((conv, ow_same))
-    ow_cross = send(ow_same, dc=1)
     conv = conv.reshape(chan, 2 * rows).astype(F32)
 
     gate = gate.astype(F32)

time: 211 us -> 213 us (level)
  waiting for transfers between devices: 73.3 us -> 78.1 us
    ppermute x20, waiting for transfers between devices: 50.3 us -> 45.5 us  [send(): return lax.ppermute(value, 'seq', perm)]
    all_to_all x1, waiting for transfers between devices: 12.9 us -> 17.3 us  [per_device(): conv = lax.all_to_all(conv, 'seq', 0, 0, axis_index_groups=SAME_CORE)]
    ppermute x1, waiting for transfers between devices: 0.24 us -> 3.57 us  [per_device(): from_hc = lax.ppermute(oth_there, ('seq', 'ch'), perm2)]
    unnamed x28, local copies, waits for them, and re-layouts: 3.78 us -> 1.64 us
where the time goes in v11:
time: 213 us
  waiting for transfers between devices  78.1 us (37%)
  Pallas kernels  71.2 us (33%)
  starting transfers between devices  44.1 us (21%)
  other arithmetic  9.63 us (5%)
  local copies, waits for them, and re-layouts  9.31 us (4%)
    ppermute x20, waiting for transfers between devices, send(): return lax.ppermute(value, 'seq', perm)  45.5 us
    ppermute x20, starting transfers between devices, send(): return lax.ppermute(value, 'seq', perm)  31.6 us
    pallas_call x2, Pallas kernels, sum_part(): pl.pallas_call(kernel, grid_spec=pltpu.PrefetchScalarGridSpec(num_scalar_...  26.6 us
    all_to_all x1, waiting for transfers between devices, per_device(): conv = lax.all_to_all(conv, 'seq', 0, 0, axis_index_groups=SAME_CORE)  17.3 us
    pallas_call x2, Pallas kernels, mix_part(): pl.pallas_call(mix_kernel if total is None else mix_more_kernel, grid=(4,...  15.4 us
    pallas_call x1, Pallas kernels, long_conv(): pl.pallas_call(conv_kernel, in_specs=[vmem, hbm, hbm, hbm, vmem, vmem, vm...  13.5 us
    all_to_all x1, waiting for transfers between devices, per_device(): mine_ch = lax.all_to_all(packed, 'seq', 0, 0, axis_index_groups=SAME_CORE)  11.6 us
    pallas_call x1, Pallas kernels, last_part(): pl.pallas_call(last_kernel, grid=(4,), in_specs=[pl.BlockSpec((tile, wide...  9.09 us
  transfers between devices with their start and end apart: 25, of which 15 were waited for; matrix products, arithmetic and copies ran while one was open for 8% of the time, Pallas kernels for 30%

profile of v11, /device:TPU:1, one launch (start us, length us, event | category | flops | bytes accessed | tf_op | source)
XLA Modules:
  0.0 212.6 jit_solution(15993109960571982067)
XLA Ops:
  0.0 1.4 collective-permute-start.3
  1.4 0.9 copy.11
  2.5 1.1 constant_dynamic-slice_fusion.5
  3.5 3.6 %collective-permute-start.2 = (bf16[224,512]{1,0:T(8,128)(2,1)S(1)}, bf16[224,512]{1,0:T(8,128)(2,1)S(1)}, u32[]{:S(2)}, u32[]{:S(2)}) collective-permute-start(bf16[224,512]{1,0:T(8,128)(2,1)S(1)} %get-tuple-element.113), channel_id=1, source_target_pairs={{0,66},{2,64},{4,70},{6,68},{8,74},{10,72},{12,78},{14,76},{16,82}... | collective-permute-start | bytes 688136 | tf_op jit(solution)/shard_map/ppermute | solution.py:35
  7.2 0.2 collective-permute-start.1
  7.4 0.5 collective-permute-start
  7.9 4.7 %constant_dynamic-slice_fusion.3 = bf16[512,4096]{1,0:T(8,128)(2,1)} fusion(bf16[1024,4096]{1,0:T(8,128)(2,1)} %w_here.1, s32[]{:T(128)S(6)} %select_n.290), kind=kLoop, calls=%fused_computation.141 | loop fusion | bytes 8388612 | tf_op jit(solution)/shard_map/dynamic_slice | solution.py:529
  12.6 0.8 collective-permute-done.2
  13.4 4.8 %collective-permute-done.1 = bf16[224,512]{1,0:T(8,128)(2,1)S(1)} collective-permute-done((bf16[224,512]{1,0:T(8,128)(2,1)S(1)}, bf16[224,512]{1,0:T(8,128)(2,1)S(1)}, u32[]{:S(2)}, u32[]{:S(2)}) %collective-permute-start.1) | collective-permute-done | bytes 229408 | tf_op jit(solution)/shard_map/ppermute | solution.py:35
  18.6 1.3 collective-permute-start.6
  19.9 2.5 %collective-permute-start.5 = (bf16[272,768]{1,0:T(8,128)(2,1)S(1)}, bf16[272,768]{1,0:T(8,128)(2,1)S(1)}, u32[]{:S(2)}, u32[]{:S(2)}) collective-permute-start(bf16[272,768]{1,0:T(8,128)(2,1)S(1)} %pad_maximum_fusion.3), channel_id=1, source_target_pairs={{0,8},{2,10},{4,12},{6,14},{8,0},{10,2},{12,4},{14,6},{16,24},{18,... | collective-permute-start | bytes 1253384 | tf_op jit(solution)/shard_map/ppermute | solution.py:35
  22.4 1.2 collective-permute-start.4
  23.5 1.3 collective-permute-start.9
  24.8 2.6 %collective-permute-start.8 = (bf16[272,768]{1,0:T(8,128)(2,1)S(1)}, bf16[272,768]{1,0:T(8,128)(2,1)S(1)}, u32[]{:S(2)}, u32[]{:S(2)}) collective-permute-start(bf16[272,768]{1,0:T(8,128)(2,1)S(1)} %pad_maximum_fusion.4), channel_id=1, source_target_pairs={{0,32},{2,34},{4,36},{6,38},{8,40},{10,42},{12,44},{14,46},{16,48}... | collective-permute-start | bytes 1253384 | tf_op jit(solution)/shard_map/ppermute | solution.py:35
  27.4 3.1 %collective-permute-done.6 = bf16[272,768]{1,0:T(8,128)(2,1)S(1)} collective-permute-done((bf16[272,768]{1,0:T(8,128)(2,1)S(1)}, bf16[272,768]{1,0:T(8,128)(2,1)S(1)}, u32[]{:S(2)}, u32[]{:S(2)}) %collective-permute-start.6) | collective-permute-done | bytes 417824 | tf_op jit(solution)/shard_map/ppermute | solution.py:35
  30.5 2.7 %collective-permute-start.7 = (bf16[272,768]{1,0:T(8,128)(2,1)S(1)}, bf16[272,768]{1,0:T(8,128)(2,1)S(1)}, u32[]{:S(2)}, u32[]{:S(2)}) collective-permute-start(bf16[272,768]{1,0:T(8,128)(2,1)S(1)} %pad_maximum_fusion.4), channel_id=1, source_target_pairs={{0,48},{2,50},{4,52},{6,54},{8,56},{10,58},{12,60},{14,62},{16,0},... | collective-permute-start | bytes 1253384 | tf_op jit(solution)/shard_map/ppermute | solution.py:35
  33.3 7.2 %collective-permute-done.5 = bf16[272,768]{1,0:T(8,128)(2,1)S(1)} collective-permute-done((bf16[272,768]{1,0:T(8,128)(2,1)S(1)}, bf16[272,768]{1,0:T(8,128)(2,1)S(1)}, u32[]{:S(2)}, u32[]{:S(2)}) %collective-permute-start.5) | collective-permute-done | bytes 417824 | tf_op jit(solution)/shard_map/ppermute | solution.py:35
  40.5 1.3 pad_maximum_fusion.key_line.refs_0_.refs_1_.refs_2_.refs_3_
  41.8 2.8 %collective-permute-done.8 = bf16[272,768]{1,0:T(8,128)(2,1)S(1)} collective-permute-done((bf16[272,768]{1,0:T(8,128)(2,1)S(1)}, bf16[272,768]{1,0:T(8,128)(2,1)S(1)}, u32[]{:S(2)}, u32[]{:S(2)}) %collective-permute-start.8) | collective-permute-done | bytes 417824 | tf_op jit(solution)/shard_map/ppermute | solution.py:35
  44.6 1.3 pad_maximum_fusion.1.value_line.refs_16_.refs_17_.refs_18_.refs_19_
  45.9 2.1 collective-permute-start.18
  48.1 0.6 pad_add_fusion.order_ref
  48.7 2.7 %collective-permute-start.10 = (bf16[1088,768]{1,0:T(8,128)(2,1)}, bf16[1088,768]{1,0:T(8,128)(2,1)S(1)}, u32[]{:S(2)}, u32[]{:S(2)}) collective-permute-start(bf16[1088,768]{1,0:T(8,128)(2,1)} %pad_maximum_fusion.key_line.refs_0_.refs_1_.refs_2_.refs_3_), channel_id=1, source_target_pairs={{0,48},{2,50},{4,52},{6,54},{8,56},{10,58},{12,60},{14,62},{16,0},... | collective-permute-start | bytes 5013512 | tf_op jit(solution)/shard_map/ppermute | solution.py:35
  51.4 1.1 collective-permute-start.11
  52.5 1.5 collective-permute-start.13
  54.0 0.2 fusion.56
  54.4 0.7 fusion.29.ai_ref
  55.0 0.3 fusion.53
  55.4 0.7 pad_maximum_fusion.6
  56.0 0.6 fusion.35
  56.6 0.7 pad_maximum_fusion.5.tw_hbm
  57.3 11.9 %first_part.1 = (f32[1024,768]{1,0:T(8,128)}, f32[1024,768]{1,0:T(8,128)}, bf16[1024,1024]{1,0:T(8,128)(2,1)}, bf16[1024,1024]{1,0:T(8,128)(2,1)}) custom-call(s32[2,32]{1,0:T(2,128)} %pad_add_fusion.order_ref, bf16[512,4096]{1,0:T(8,128)(2,1)} %bitcast.57, bf16[512,4096]{1,0:T(8,128)(2,1)} %collective-permute-done.3.other_ref, ...), custom_call_target="tpu_custom_call" | custom-call | flops 3221225472 | bytes 18874368 | tf_op jit(solution)/shard_map/first_part/pallas_call | solution.py:122
  69.2 19.8 %collective-permute-done.10.k1.refs_0_.refs_4_.refs_5_.refs_6_.refs_7_ = bf16[1088,768]{1,0:T(8,128)(2,1)S(1)} collective-permute-done((bf16[1088,768]{1,0:T(8,128)(2,1)}, bf16[1088,768]{1,0:T(8,128)(2,1)S(1)}, u32[]{:S(2)}, u32[]{:S(2)}) %collective-permute-start.10) | collective-permute-done | bytes 1671200 | tf_op jit(solution)/shard_map/ppermute | solution.py:35
  88.9 1.7 collective-permute-done.11.k3.refs_1_.refs_12_.refs_13_.refs_14_.refs_15_
  90.6 0.4 collective-permute-done.12.v1.refs_2_.refs_20_.refs_21_.refs_22_.refs_23_
  91.0 1.2 collective-permute-done.13.v3.refs_3_.refs_28_.refs_29_.refs_30_.refs_31_
  92.2 3.2 %cut_halves.1 = (bf16[544,768]{1,0:T(8,128)(2,1)}, bf16[544,768]{1,0:T(8,128)(2,1)}, bf16[544,768]{1,0:T(8,128)(2,1)}, bf16[544,768]{1,0:T(8,128)(2,1)}) custom-call(bf16[1088,768]{1,0:T(8,128)(2,1)} %copy-done, bf16[1088,768]{1,0:T(8,128)(2,1)} %copy-done.1, bf16[1088,768]{1,0:T(8,128)(2,1)} %collective-permute-done.12.v1.refs_2_.refs_20_.refs_21_.refs_22_.refs_23_, ...), custom_call_target="tpu_custom_call" | custom-call | bytes 6684672 | tf_op jit(solution)/shard_map/cut_halves/pallas_call | solution.py:154
  95.5 1.3 collective-permute-start.14
  96.7 0.5 collective-permute-start.15
  97.3 1.4 collective-permute-start.17
  98.7 14.7 %second_part.1 = (f32[1024,768]{1,0:T(8,128)}, f32[1024,768]{1,0:T(8,128)}) custom-call(s32[2,32]{1,0:T(2,128)} %pad_add_fusion.order_ref, bf16[512,4096]{1,0:T(8,128)(2,1)} %bitcast.58, bf16[512,4096]{1,0:T(8,128)(2,1)} %collective-permute-done.3.other_ref, f32[1024,768]{1,0:T(8,128)} %get-tuple-element.53.key_in, f32[1024,768]{1,0:T(8,128)} %get-tuple-element.54.value_in, ...), custom_call_target="tpu_custom_call" | custom-call | flops 6442450944 | bytes 18874368 | tf_op jit(solution)/shard_map/second_part/pallas_call | solution.py:122
  113.4 2.2 %collective-permute-done.14.ka.refs_8_.refs_9_ = bf16[544,768]{1,0:T(8,128)(2,1)S(1)} collective-permute-done((bf16[544,768]{1,0:T(8,128)(2,1)}, bf16[544,768]{1,0:T(8,128)(2,1)S(1)}, u32[]{:S(2)}, u32[]{:S(2)}) %collective-permute-start.14) | collective-permute-done | bytes 835616 | tf_op jit(solution)/shard_map/ppermute | solution.py:35
  115.6 0.8 collective-permute-done.15.kb.refs_10_.refs_11_
  116.4 0.8 collective-permute-done.17.vb.refs_26_.refs_27_
  117.1 0.1 copy-done.3
  117.3 0.3 copy-done.4
  117.6 0.5 copy-done.5
  118.1 9.1 %last_part.1 = (bf16[512,1024]{1,0:T(8,128)(2,1)}, bf16[512,1024]{1,0:T(8,128)(2,1)}) custom-call(f32[1024,768]{1,0:T(8,128)} %get-tuple-element.59.key_ref, f32[1024,768]{1,0:T(8,128)} %get-tuple-element.60.value_ref, bf16[1024,1024]{1,0:T(8,128)(2,1)} %get-tuple-element.61.key_tok_ref, bf16[1024,1024]{1,0:T(8,128)(2,1)} %get-tuple-element.62.value_tok_ref, ...), custom_call_target="tpu_custom_call" | custom-call | flops 3221225472 | bytes 16777216 | tf_op jit(solution)/shard_map/last_part/pallas_call | solution.py:188
  127.1 4.2 %all-to-all-start = ((bf16[32,16,1024]{2,1,0:T(8,128)(2,1)}), bf16[32,16,1024]{2,1,0:T(8,128)(2,1)S(1)}, u32[]{:S(2)}, u32[]{:S(2)}) async-start(bf16[32,16,1024]{2,1,0:T(8,128)(2,1)} %bitcast.49), calls=%async_computation | async-start | bytes 2097152 | tf_op jit(solution)/shard_map/all_to_all | solution.py:564
  131.3 3.5 %filter_part.1 = (f32[64,1024]{1,0:T(8,128)}, bf16[256,256]{1,0:T(8,128)(2,1)}) custom-call(s32[2,32]{1,0:T(2,128)} %pad_add_fusion.order_ref, bf16[1088,768]{1,0:T(8,128)(2,1)} %pad_maximum_fusion.key_line.refs_0_.refs_1_.refs_2_.refs_3_, bf16[1088,768]{1,0:T(8,128)(2,1)} %pad_maximum_fusion.key_line.refs_0_.refs_1_.refs_2_.refs_3_, ...), custom_call_target="tpu_custom_call" | custom-call | flops 1000000000 | bytes 1048576 | tf_op jit(solution)/shard_map/filter_part/pallas_call | solution.py:319
  134.8 11.6 %all-to-all-done.x_ref = bf16[32,16,1024]{2,1,0:T(8,128)(2,1)S(1)} async-done(((bf16[32,16,1024]{2,1,0:T(8,128)(2,1)}), bf16[32,16,1024]{2,1,0:T(8,128)(2,1)S(1)}, u32[]{:S(2)}, u32[]{:S(2)}) %all-to-all-start) | async-done | bytes 1048608 | tf_op jit(solution)/shard_map/all_to_all | solution.py:564
  146.5 3.8 %collective-permute-start.22 = (bf16[512,4096]{1,0:T(8,128)(2,1)}, bf16[512,4096]{1,0:T(8,128)(2,1)}, u32[]{:S(2)}, u32[]{:S(2)}) collective-permute-start(bf16[512,4096]{1,0:T(8,128)(2,1)} %collective-permute-done.18.w_near), channel_id=1, source_target_pairs={{0,2},{2,0},{4,6},{6,4},{8,10},{10,8},{12,14},{14,12},{16,18},{18,... | collective-permute-start | bytes 12582920 | tf_op jit(solution)/shard_map/ppermute | solution.py:35
  150.3 0.7 copy.12.a_ref
  151.0 13.5 %long_conv.1 = bf16[32,16,1024]{2,1,0:T(8,128)(2,1)} custom-call(bf16[32,16,1024]{2,1,0:T(8,128)(2,1)} %copy-done.7, bf16[512,1024]{1,0:T(8,128)(2,1)} %constant.204.clone.fwd_hbm, bf16[1024,512]{1,0:T(8,128)(2,1)} %constant.205.clone.inv_hbm, f32[64,1024]{1,0:T(8,128)} %pad_maximum_fusion.5.tw_hbm, bf16[256,256]{1,0:T(8,128)(2,1)} %copy.12.a_ref, ...), custom_call_target="tpu_custom_call" | custom-call | flops 8000000000 | bytes 8388608 | tf_op jit(solution)/shard_map/long_conv/pallas_call | solution.py:422
  164.5 4.4 %all-to-all-start.1 = ((bf16[32,16,1024]{2,1,0:T(8,128)(2,1)}), bf16[32,16,1024]{2,1,0:T(8,128)(2,1)S(1)}, u32[]{:S(2)}, u32[]{:S(2)}) async-start(bf16[32,16,1024]{2,1,0:T(8,128)(2,1)} %long_conv.1), calls=%async_computation.1 | async-start | bytes 2097152 | tf_op jit(solution)/shard_map/all_to_all | solution.py:581
  169.0 17.3 %all-to-all-done.1 = bf16[32,16,1024]{2,1,0:T(8,128)(2,1)S(1)} async-done(((bf16[32,16,1024]{2,1,0:T(8,128)(2,1)}), bf16[32,16,1024]{2,1,0:T(8,128)(2,1)S(1)}, u32[]{:S(2)}, u32[]{:S(2)}) %all-to-all-start.1) | async-done | bytes 1048608 | tf_op jit(solution)/shard_map/all_to_all | solution.py:581
  186.4 1.7 fusion.1
  188.2 2.0 collective-permute-start.19
  190.3 1.7 collective-permute-start.21
  192.1 0.8 pad_maximum_fusion.2.here
  192.9 7.4 %mix_part.1.total_ref = f32[256,4096]{1,0:T(8,128)} custom-call(bf16[1024,256]{1,0:T(8,128)(2,1)} %pad_maximum_fusion.2.here, bf16[1024,4096]{1,0:T(8,128)(2,1)} %w_here.1), custom_call_target="tpu_custom_call" | custom-call | flops 2147483648 | bytes 12582912 | tf_op jit(solution)/shard_map/mix_part/pallas_call | solution.py:243
  200.3 3.6 %collective-permute-done.21.far_h = bf16[512,256]{1,0:T(8,128)(2,1)S(1)} collective-permute-done((bf16[512,256]{1,0:T(8,128)(2,1)S(1)}, bf16[512,256]{1,0:T(8,128)(2,1)S(1)}, u32[]{:S(2)}, u32[]{:S(2)}) %collective-permute-start.21) | collective-permute-done | bytes 262176 | tf_op jit(solution)/shard_map/ppermute | solution.py:599
  203.9 0.7 copy-done.9
  204.6 8.0 %mix_more.1 = bf16[256,4096]{1,0:T(8,128)(2,1)} custom-call(f32[256,4096]{1,0:T(8,128)} %mix_part.1.total_ref, bf16[512,256]{1,0:T(8,128)(2,1)} %copy-done.8, bf16[512,256]{1,0:T(8,128)(2,1)} %copy-done.9, bf16[512,4096]{1,0:T(8,128)(2,1)} %collective-permute-done.18.w_near, bf16[512,4096]{1,0:T(8,128)(2,1)} %collective-permute-done.22.w_far), custom_call_target="tpu_custom_call" | custom-call | flops 2147483648 | bytes 12582912 | tf_op jit(solution)/shard_map/mix_more/pallas_call | solution.py:243
  (63 shorter events, 1.2 us)
Async XLA Ops:
  0.0 18.6 %collective-permute-start.3 = (bf16[512,4096]{1,0:T(8,128)(2,1)}, bf16[512,4096]{1,0:T(8,128)(2,1)}, u32[]{:S(2)}, u32[]{:S(2)}) collective-permute-start(bf16[512,4096]{1,0:T(8,128)(2,1)} %bitcast.56), channel_id=1, source_target_pairs={{0,2},{2,0},{4,6},{6,4},{8,10},{10,8},{12,14},{14,12},{16,18},{18,... | collective-permute-start | bytes 12582920 | tf_op jit(solution)/shard_map/ppermute | solution.py:35
  3.5 9.8 %collective-permute-start.2 = (bf16[224,512]{1,0:T(8,128)(2,1)S(1)}, bf16[224,512]{1,0:T(8,128)(2,1)S(1)}, u32[]{:S(2)}, u32[]{:S(2)}) collective-permute-start(bf16[224,512]{1,0:T(8,128)(2,1)S(1)} %get-tuple-element.113), channel_id=1, source_target_pairs={{0,66},{2,64},{4,70},{6,68},{8,74},{10,72},{12,78},{14,76},{16,82}... | collective-permute-start | bytes 688136 | tf_op jit(solution)/shard_map/ppermute | solution.py:35
  7.2 11.0 %collective-permute-start.1 = (bf16[224,512]{1,0:T(8,128)(2,1)S(1)}, bf16[224,512]{1,0:T(8,128)(2,1)S(1)}, u32[]{:S(2)}, u32[]{:S(2)}) collective-permute-start(bf16[224,512]{1,0:T(8,128)(2,1)S(1)} %fusion.18), channel_id=1, source_target_pairs={{0,64},{2,66},{4,68},{6,70},{8,72},{10,74},{12,76},{14,78},{16,80}... | collective-permute-start | bytes 688136 | tf_op jit(solution)/shard_map/ppermute | solution.py:35
  7.4 10.8 %collective-permute-start = (bf16[224,512]{1,0:T(8,128)(2,1)S(1)}, bf16[224,512]{1,0:T(8,128)(2,1)S(1)}, u32[]{:S(2)}, u32[]{:S(2)}) collective-permute-start(bf16[224,512]{1,0:T(8,128)(2,1)S(1)} %get-tuple-element.112), channel_id=1, source_target_pairs={{0,2},{2,0},{4,6},{6,4},{8,10},{10,8},{12,14},{14,12},{16,18},{18,... | collective-permute-start | bytes 688136 | tf_op jit(solution)/shard_map/ppermute | solution.py:35
  18.6 29.5 %copy-start.11 = (s32[32]{0:T(128)S(1)}, s32[32]{0:T(128)}, u32[]{:S(2)}) copy-start(s32[32]{0:T(128)} %constant.203.clone) | copy-start | bytes 388
  18.6 29.4 %copy-start.12 = (s32[32]{0:T(128)S(1)}, s32[32]{0:T(128)}, u32[]{:S(2)}) copy-start(s32[32]{0:T(128)} %constant.202.clone) | copy-start | bytes 388
  18.6 29.4 %copy-start.13 = (s32[32]{0:T(128)S(1)}, s32[32]{0:T(128)}, u32[]{:S(2)}) copy-start(s32[32]{0:T(128)} %constant.201.clone) | copy-start | bytes 388
  18.6 11.9 %collective-permute-start.6 = (bf16[272,768]{1,0:T(8,128)(2,1)S(1)}, bf16[272,768]{1,0:T(8,128)(2,1)S(1)}, u32[]{:S(2)}, u32[]{:S(2)}) collective-permute-start(bf16[272,768]{1,0:T(8,128)(2,1)S(1)} %pad_maximum_fusion.3), channel_id=1, source_target_pairs={{0,4},{2,6},{4,8},{6,10},{8,12},{10,14},{12,0},{14,2},{16,20},{18,... | collective-permute-start | bytes 1253384 | tf_op jit(solution)/shard_map/ppermute | solution.py:35
  19.9 20.6 %collective-permute-start.5 = (bf16[272,768]{1,0:T(8,128)(2,1)S(1)}, bf16[272,768]{1,0:T(8,128)(2,1)S(1)}, u32[]{:S(2)}, u32[]{:S(2)}) collective-permute-start(bf16[272,768]{1,0:T(8,128)(2,1)S(1)} %pad_maximum_fusion.3), channel_id=1, source_target_pairs={{0,8},{2,10},{4,12},{6,14},{8,0},{10,2},{12,4},{14,6},{16,24},{18,... | collective-permute-start | bytes 1253384 | tf_op jit(solution)/shard_map/ppermute | solution.py:35
  22.4 18.1 %collective-permute-start.4 = (bf16[272,768]{1,0:T(8,128)(2,1)S(1)}, bf16[272,768]{1,0:T(8,128)(2,1)S(1)}, u32[]{:S(2)}, u32[]{:S(2)}) collective-permute-start(bf16[272,768]{1,0:T(8,128)(2,1)S(1)} %pad_maximum_fusion.3), channel_id=1, source_target_pairs={{0,12},{2,14},{4,0},{6,2},{8,4},{10,6},{12,8},{14,10},{16,28},{18,... | collective-permute-start | bytes 1253384 | tf_op jit(solution)/shard_map/ppermute | solution.py:35
  23.5 18.3 %collective-permute-start.9 = (bf16[272,768]{1,0:T(8,128)(2,1)S(1)}, bf16[272,768]{1,0:T(8,128)(2,1)S(1)}, u32[]{:S(2)}, u32[]{:S(2)}) collective-permute-start(bf16[272,768]{1,0:T(8,128)(2,1)S(1)} %pad_maximum_fusion.4), channel_id=1, source_target_pairs={{0,16},{2,18},{4,20},{6,22},{8,24},{10,26},{12,28},{14,30},{16,32}... | collective-permute-start | bytes 1253384 | tf_op jit(solution)/shard_map/ppermute | solution.py:35
  24.8 19.8 %collective-permute-start.8 = (bf16[272,768]{1,0:T(8,128)(2,1)S(1)}, bf16[272,768]{1,0:T(8,128)(2,1)S(1)}, u32[]{:S(2)}, u32[]{:S(2)}) collective-permute-start(bf16[272,768]{1,0:T(8,128)(2,1)S(1)} %pad_maximum_fusion.4), channel_id=1, source_target_pairs={{0,32},{2,34},{4,36},{6,38},{8,40},{10,42},{12,44},{14,46},{16,48}... | collective-permute-start | bytes 1253384 | tf_op jit(solution)/shard_map/ppermute | solution.py:35
  30.5 14.1 %collective-permute-start.7 = (bf16[272,768]{1,0:T(8,128)(2,1)S(1)}, bf16[272,768]{1,0:T(8,128)(2,1)S(1)}, u32[]{:S(2)}, u32[]{:S(2)}) collective-permute-start(bf16[272,768]{1,0:T(8,128)(2,1)S(1)} %pad_maximum_fusion.4), channel_id=1, source_target_pairs={{0,48},{2,50},{4,52},{6,54},{8,56},{10,58},{12,60},{14,62},{16,0},... | collective-permute-start | bytes 1253384 | tf_op jit(solution)/shard_map/ppermute | solution.py:35
  45.9 100.5 %collective-permute-start.18 = (bf16[512,4096]{1,0:T(8,128)(2,1)}, bf16[512,4096]{1,0:T(8,128)(2,1)}, u32[]{:S(2)}, u32[]{:S(2)}) collective-permute-start(bf16[512,4096]{1,0:T(8,128)(2,1)} %constant_dynamic-slice_fusion.3), channel_id=1, source_target_pairs={{0,1},{1,0},{2,67},{3,66},{4,5},{5,4},{6,71},{7,70},{8,9},{9,8},{1... | collective-permute-start | bytes 12582920 | tf_op jit(solution)/shard_map/ppermute | solution.py:560
  48.7 40.3 %collective-permute-start.10 = (bf16[1088,768]{1,0:T(8,128)(2,1)}, bf16[1088,768]{1,0:T(8,128)(2,1)S(1)}, u32[]{:S(2)}, u32[]{:S(2)}) collective-permute-start(bf16[1088,768]{1,0:T(8,128)(2,1)} %pad_maximum_fusion.key_line.refs_0_.refs_1_.refs_2_.refs_3_), channel_id=1, source_target_pairs={{0,48},{2,50},{4,52},{6,54},{8,56},{10,58},{12,60},{14,62},{16,0},... | collective-permute-start | bytes 5013512 | tf_op jit(solution)/shard_map/ppermute | solution.py:35
  51.4 39.3 %collective-permute-start.11 = (bf16[1088,768]{1,0:T(8,128)(2,1)}, bf16[1088,768]{1,0:T(8,128)(2,1)S(1)}, u32[]{:S(2)}, u32[]{:S(2)}) collective-permute-start(bf16[1088,768]{1,0:T(8,128)(2,1)} %pad_maximum_fusion.key_line.refs_0_.refs_1_.refs_2_.refs_3_), channel_id=1, source_target_pairs={{0,16},{2,18},{4,20},{6,22},{8,24},{10,26},{12,28},{14,30},{16,32}... | collective-permute-start | bytes 5013512 | tf_op jit(solution)/shard_map/ppermute | solution.py:35
  52.5 38.5 %collective-permute-start.12 = (bf16[1088,768]{1,0:T(8,128)(2,1)}, bf16[1088,768]{1,0:T(8,128)(2,1)}, u32[]{:S(2)}, u32[]{:S(2)}) collective-permute-start(bf16[1088,768]{1,0:T(8,128)(2,1)} %pad_maximum_fusion.1.value_line.refs_16_.refs_17_.refs_18_.refs_19_), channel_id=1, source_target_pairs={{0,12},{2,14},{4,0},{6,2},{8,4},{10,6},{12,8},{14,10},{16,28},{18,... | collective-permute-start | bytes 5013512 | tf_op jit(solution)/shard_map/ppermute | solution.py:35
  52.5 39.7 %collective-permute-start.13 = (bf16[1088,768]{1,0:T(8,128)(2,1)}, bf16[1088,768]{1,0:T(8,128)(2,1)}, u32[]{:S(2)}, u32[]{:S(2)}) collective-permute-start(bf16[1088,768]{1,0:T(8,128)(2,1)} %pad_maximum_fusion.1.value_line.refs_16_.refs_17_.refs_18_.refs_19_), channel_id=1, source_target_pairs={{0,4},{2,6},{4,8},{6,10},{8,12},{10,14},{12,0},{14,2},{16,20},{18,... | collective-permute-start | bytes 5013512 | tf_op jit(solution)/shard_map/ppermute | solution.py:35
  88.9 3.3 %copy-start = (bf16[1088,768]{1,0:T(8,128)(2,1)}, bf16[1088,768]{1,0:T(8,128)(2,1)S(1)}, u32[]{:S(2)}) copy-start(bf16[1088,768]{1,0:T(8,128)(2,1)S(1)} %collective-permute-done.10.k1.refs_0_.refs_4_.refs_5_.refs_6_.refs_7_) | copy-start | bytes 5013508
  90.6 1.6 copy-start.1
  95.5 20.1 %collective-permute-start.14 = (bf16[544,768]{1,0:T(8,128)(2,1)}, bf16[544,768]{1,0:T(8,128)(2,1)S(1)}, u32[]{:S(2)}, u32[]{:S(2)}) collective-permute-start(bf16[544,768]{1,0:T(8,128)(2,1)} %get-tuple-element.63), channel_id=1, source_target_pairs={{0,48},{2,50},{4,52},{6,54},{8,56},{10,58},{12,60},{14,62},{16,0},... | collective-permute-start | bytes 2506760 | tf_op jit(solution)/shard_map/ppermute | solution.py:35
  96.7 19.6 %collective-permute-start.15 = (bf16[544,768]{1,0:T(8,128)(2,1)}, bf16[544,768]{1,0:T(8,128)(2,1)S(1)}, u32[]{:S(2)}, u32[]{:S(2)}) collective-permute-start(bf16[544,768]{1,0:T(8,128)(2,1)} %get-tuple-element.64), channel_id=1, source_target_pairs={{0,16},{2,18},{4,20},{6,22},{8,24},{10,26},{12,28},{14,30},{16,32}... | collective-permute-start | bytes 2506760 | tf_op jit(solution)/shard_map/ppermute | solution.py:35
  97.2 19.1 %collective-permute-start.16 = (bf16[544,768]{1,0:T(8,128)(2,1)}, bf16[544,768]{1,0:T(8,128)(2,1)S(1)}, u32[]{:S(2)}, u32[]{:S(2)}) collective-permute-start(bf16[544,768]{1,0:T(8,128)(2,1)} %get-tuple-element.65), channel_id=1, source_target_pairs={{0,12},{2,14},{4,0},{6,2},{8,4},{10,6},{12,8},{14,10},{16,28},{18,... | collective-permute-start | bytes 2506760 | tf_op jit(solution)/shard_map/ppermute | solution.py:35
  97.3 19.8 %collective-permute-start.17 = (bf16[544,768]{1,0:T(8,128)(2,1)}, bf16[544,768]{1,0:T(8,128)(2,1)S(1)}, u32[]{:S(2)}, u32[]{:S(2)}) collective-permute-start(bf16[544,768]{1,0:T(8,128)(2,1)} %get-tuple-element.66), channel_id=1, source_target_pairs={{0,4},{2,6},{4,8},{6,10},{8,12},{10,14},{12,0},{14,2},{16,20},{18,... | collective-permute-start | bytes 2506760 | tf_op jit(solution)/shard_map/ppermute | solution.py:35
  115.6 1.6 copy-start.2
  116.3 0.9 copy-start.3
  116.4 1.2 copy-start.4
  117.1 0.9 copy-start.5
  127.1 19.3 %all-to-all-start = ((bf16[32,16,1024]{2,1,0:T(8,128)(2,1)}), bf16[32,16,1024]{2,1,0:T(8,128)(2,1)S(1)}, u32[]{:S(2)}, u32[]{:S(2)}) async-start(bf16[32,16,1024]{2,1,0:T(8,128)(2,1)} %bitcast.49), calls=%async_computation | async-start | bytes 2097152 | tf_op jit(solution)/shard_map/all_to_all | solution.py:564
  146.5 4.6 %copy-start.7 = (bf16[32,16,1024]{2,1,0:T(8,128)(2,1)}, bf16[32,16,1024]{2,1,0:T(8,128)(2,1)S(1)}, u32[]{:S(2)}) copy-start(bf16[32,16,1024]{2,1,0:T(8,128)(2,1)S(1)} %all-to-all-done.x_ref) | copy-start | bytes 3145732
  146.5 57.5 %collective-permute-start.22 = (bf16[512,4096]{1,0:T(8,128)(2,1)}, bf16[512,4096]{1,0:T(8,128)(2,1)}, u32[]{:S(2)}, u32[]{:S(2)}) collective-permute-start(bf16[512,4096]{1,0:T(8,128)(2,1)} %collective-permute-done.18.w_near), channel_id=1, source_target_pairs={{0,2},{2,0},{4,6},{6,4},{8,10},{10,8},{12,14},{14,12},{16,18},{18,... | collective-permute-start | bytes 12582920 | tf_op jit(solution)/shard_map/ppermute | solution.py:35
  151.0 17.9 %copy-start.10 = (f32[1024]{0:T(1024)S(1)}, f32[1024]{0:T(1024)}, u32[]{:S(2)}) copy-start(f32[1024]{0:T(1024)} %param.13) | copy-start | bytes 12292
  151.0 35.3 %copy-start.6 = (bf16[512,1024]{1,0:T(8,128)(2,1)S(1)}, bf16[512,1024]{1,0:T(8,128)(2,1)}, u32[]{:S(2)}) copy-start(bf16[512,1024]{1,0:T(8,128)(2,1)} %get-tuple-element.68) | copy-start | bytes 3145732
  164.5 21.8 %all-to-all-start.1 = ((bf16[32,16,1024]{2,1,0:T(8,128)(2,1)}), bf16[32,16,1024]{2,1,0:T(8,128)(2,1)S(1)}, u32[]{:S(2)}, u32[]{:S(2)}) async-start(bf16[32,16,1024]{2,1,0:T(8,128)(2,1)} %long_conv.1), calls=%async_computation.1 | async-start | bytes 2097152 | tf_op jit(solution)/shard_map/all_to_all | solution.py:581
  188.2 3.8 %collective-permute-start.19 = (bf16[512,256]{1,0:T(8,128)(2,1)S(1)}, bf16[512,256]{1,0:T(8,128)(2,1)S(1)}, u32[]{:S(2)}, u32[]{:S(2)}) collective-permute-start(bf16[512,256]{1,0:T(8,128)(2,1)S(1)} %get-tuple-element.87), channel_id=1, source_target_pairs={{0,2},{2,0},{4,6},{6,4},{8,10},{10,8},{12,14},{14,12},{16,18},{18,... | collective-permute-start | bytes 786440 | tf_op jit(solution)/shard_map/ppermute | solution.py:35
  190.2 10.1 %collective-permute-start.20 = (bf16[512,256]{1,0:T(8,128)(2,1)S(1)}, bf16[512,256]{1,0:T(8,128)(2,1)S(1)}, u32[]{:S(2)}, u32[]{:S(2)}) collective-permute-start(bf16[512,256]{1,0:T(8,128)(2,1)S(1)} %get-tuple-element.86), channel_id=1, source_target_pairs={{0,1},{1,0},{2,3},{3,2},{4,5},{5,4},{6,7},{7,6},{8,9},{9,8},{10,11... | collective-permute-start | bytes 786440 | tf_op jit(solution)/shard_map/ppermute | solution.py:594
  190.3 13.7 %collective-permute-start.21 = (bf16[512,256]{1,0:T(8,128)(2,1)S(1)}, bf16[512,256]{1,0:T(8,128)(2,1)S(1)}, u32[]{:S(2)}, u32[]{:S(2)}) collective-permute-start(bf16[512,256]{1,0:T(8,128)(2,1)S(1)} %get-tuple-element.85), channel_id=1, source_target_pairs={{0,3},{1,2},{2,1},{3,0},{4,7},{5,6},{6,5},{7,4},{8,11},{9,10},{10,... | collective-permute-start | bytes 786440 | tf_op jit(solution)/shard_map/ppermute | solution.py:599
  200.3 3.6 %copy-start.8 = (bf16[512,256]{1,0:T(8,128)(2,1)}, bf16[512,256]{1,0:T(8,128)(2,1)S(1)}, u32[]{:S(2)}) copy-start(bf16[512,256]{1,0:T(8,128)(2,1)S(1)} %collective-permute-done.20.near_h) | copy-start | bytes 786436
  203.9 0.7 copy-start.9

commit v12 on v11

--- a/solution.py
+++ b/solution.py
@@ -407,7 +407,7 @@
                     q_ref[col, blocks + k, pick, :] = out_im[part, k * 128 : (k + 1) * 128]
         return carry
 
-    lax.fori_loop(0, chans // 2, pair, 0, unroll=2)
+    lax.fori_loop(0, chans // 2, pair, 0, unroll=4)
     copies[2].wait()
     for col in range(2):
         q = jnp.concatenate([q_ref[col, k].astype(BF16) for k in range(2 * blocks)], axis=1)
@@ -575,8 +575,7 @@
     forward, inverse = row_tables(rows, padded)
     fwd = jnp.asarray(forward.astype(np.float32).astype(ml_dtypes.bfloat16))
     inv = jnp.asarray(inverse.astype(np.float32).astype(ml_dtypes.bfloat16))
-    mine_ch, ow_same, f, m = lax.optimization_barrier((mine_ch, ow_same, f, m))
-    ow_cross = send(ow_same, dc=1)
+    mine_ch, f, m = lax.optimization_barrier((mine_ch, f, m))
     conv = long_conv(mine_ch, fwd, inv, tw, a, ai, m, f)
     conv = lax.all_to_all(conv, "seq", 0, 0, axis_index_groups=SAME_CORE)
     conv = conv.reshape(chan, 2 * rows).astype(F32)
@@ -598,6 +597,8 @@
             perm2.append((t * 2 + th, (t ^ 1) * 2 + 1 - th))
     from_hc = lax.ppermute(oth_there, ("seq", "ch"), perm2)
     from_c = send(oth_here, dc=1)
+    from_c, ow_same = lax.optimization_barrier((from_c, ow_same))
+    ow_cross = send(ow_same, dc=1)
     here = ordered(own_here, from_c)
 
     mixed = mix_part(None, [here], [out_weight])

time: 213 us -> 220 us (1.033)
  starting transfers between devices: 44.1 us -> 61.3 us
  waiting for transfers between devices: 78.1 us -> 65.5 us
  local copies, waits for them, and re-layouts: 9.31 us -> 11.6 us
    ppermute x20, starting transfers between devices: 31.6 us -> 47.4 us  [send(): return lax.ppermute(value, 'seq', perm)]
    ppermute x20, waiting for transfers between devices: 45.5 us -> 40.6 us  [send(): return lax.ppermute(value, 'seq', perm)]
    all_to_all x1, waiting for transfers between devices: 17.3 us -> 12.5 us  [per_device(): conv = lax.all_to_all(conv, 'seq', 0, 0, axis_index_groups=SAME_CORE)]
    all_to_all x1, waiting for transfers between devices: 11.6 us -> 8.83 us  [per_device(): mine_ch = lax.all_to_all(packed, 'seq', 0, 0, axis_index_groups=SAME_CORE)]
    unnamed x28, local copies, waits for them, and re-layouts: 1.64 us -> 3.93 us
  transfers between devices with their start and end apart: 25 -> 25, of which waited for: 15 -> 13; matrix products, arithmetic and copies ran while one was open for 8% -> 7% of each run, Pallas kernels for 30% -> 27%
where the time goes in v12:
time: 220 us; the launch traced here: 219 us
  Pallas kernels  70.7 us (32%)
  waiting for transfers between devices  65.5 us (30%)
  starting transfers between devices  61.3 us (28%)
  local copies, waits for them, and re-layouts  11.6 us (5%)
  other arithmetic  9.63 us (4%)
    ppermute x20, starting transfers between devices, send(): return lax.ppermute(value, 'seq', perm)  47.4 us
    ppermute x20, waiting for transfers between devices, send(): return lax.ppermute(value, 'seq', perm)  40.6 us
    pallas_call x2, Pallas kernels, sum_part(): pl.pallas_call(kernel, grid_spec=pltpu.PrefetchScalarGridSpec(num_scalar_...  26.6 us
    pallas_call x2, Pallas kernels, mix_part(): pl.pallas_call(mix_kernel if total is None else mix_more_kernel, grid=(4,...  15.4 us
    pallas_call x1, Pallas kernels, long_conv(): pl.pallas_call(conv_kernel, in_specs=[vmem, hbm, hbm, hbm, vmem, vmem, vm...  13 us
    all_to_all x1, waiting for transfers between devices, per_device(): conv = lax.all_to_all(conv, 'seq', 0, 0, axis_index_groups=SAME_CORE)  12.5 us
    pallas_call x1, Pallas kernels, last_part(): pl.pallas_call(last_kernel, grid=(4,), in_specs=[pl.BlockSpec((tile, wide...  9.09 us
    all_to_all x1, waiting for transfers between devices, per_device(): mine_ch = lax.all_to_all(packed, 'seq', 0, 0, axis_index_groups=SAME_CORE)  8.83 us
  transfers between devices with their start and end apart: 25, of which 13 were waited for; matrix products, arithmetic and copies ran while one was open for 7% of the time, Pallas kernels for 27%

profile of v12, /device:TPU:1, one launch (start us, length us, event | category | flops | bytes accessed | tf_op | source)
XLA Modules:
  0.0 219.1 jit_solution(880999112167723785)
XLA Ops:
  0.0 1.4 collective-permute-start.3
  1.4 0.9 copy.11
  2.5 1.1 constant_dynamic-slice_fusion.5
  3.5 3.6 %collective-permute-start.2 = (bf16[224,512]{1,0:T(8,128)(2,1)S(1)}, bf16[224,512]{1,0:T(8,128)(2,1)S(1)}, u32[]{:S(2)}, u32[]{:S(2)}) collective-permute-start(bf16[224,512]{1,0:T(8,128)(2,1)S(1)} %get-tuple-element.115), channel_id=1, source_target_pairs={{0,66},{2,64},{4,70},{6,68},{8,74},{10,72},{12,78},{14,76},{16,82}... | collective-permute-start | bytes 688136 | tf_op jit(solution)/shard_map/ppermute | solution.py:35
  7.4 0.5 collective-permute-start
  7.9 4.7 %constant_dynamic-slice_fusion.3 = bf16[512,4096]{1,0:T(8,128)(2,1)} fusion(bf16[1024,4096]{1,0:T(8,128)(2,1)} %w_here.1, s32[]{:T(128)S(6)} %select_n.290), kind=kLoop, calls=%fused_computation.141 | loop fusion | bytes 8388612 | tf_op jit(solution)/shard_map/dynamic_slice | solution.py:529
  12.6 0.8 collective-permute-done.2
  13.4 4.8 %collective-permute-done.1 = bf16[224,512]{1,0:T(8,128)(2,1)S(1)} collective-permute-done((bf16[224,512]{1,0:T(8,128)(2,1)S(1)}, bf16[224,512]{1,0:T(8,128)(2,1)S(1)}, u32[]{:S(2)}, u32[]{:S(2)}) %collective-permute-start.1) | collective-permute-done | bytes 229408 | tf_op jit(solution)/shard_map/ppermute | solution.py:35
  18.6 1.3 collective-permute-start.6
  19.9 2.5 %collective-permute-start.5 = (bf16[272,768]{1,0:T(8,128)(2,1)S(1)}, bf16[272,768]{1,0:T(8,128)(2,1)S(1)}, u32[]{:S(2)}, u32[]{:S(2)}) collective-permute-start(bf16[272,768]{1,0:T(8,128)(2,1)S(1)} %pad_maximum_fusion.3), channel_id=1, source_target_pairs={{0,8},{2,10},{4,12},{6,14},{8,0},{10,2},{12,4},{14,6},{16,24},{18,... | collective-permute-start | bytes 1253384 | tf_op jit(solution)/shard_map/ppermute | solution.py:35
  22.3 1.2 collective-permute-start.4
  23.5 1.4 collective-permute-start.9
  24.9 2.6 %collective-permute-start.8 = (bf16[272,768]{1,0:T(8,128)(2,1)S(1)}, bf16[272,768]{1,0:T(8,128)(2,1)S(1)}, u32[]{:S(2)}, u32[]{:S(2)}) collective-permute-start(bf16[272,768]{1,0:T(8,128)(2,1)S(1)} %pad_maximum_fusion.4), channel_id=1, source_target_pairs={{0,32},{2,34},{4,36},{6,38},{8,40},{10,42},{12,44},{14,46},{16,48}... | collective-permute-start | bytes 1253384 | tf_op jit(solution)/shard_map/ppermute | solution.py:35
  27.5 3.0 %collective-permute-done.6 = bf16[272,768]{1,0:T(8,128)(2,1)S(1)} collective-permute-done((bf16[272,768]{1,0:T(8,128)(2,1)S(1)}, bf16[272,768]{1,0:T(8,128)(2,1)S(1)}, u32[]{:S(2)}, u32[]{:S(2)}) %collective-permute-start.6) | collective-permute-done | bytes 417824 | tf_op jit(solution)/shard_map/ppermute | solution.py:35
  30.5 2.7 %collective-permute-start.7 = (bf16[272,768]{1,0:T(8,128)(2,1)S(1)}, bf16[272,768]{1,0:T(8,128)(2,1)S(1)}, u32[]{:S(2)}, u32[]{:S(2)}) collective-permute-start(bf16[272,768]{1,0:T(8,128)(2,1)S(1)} %pad_maximum_fusion.4), channel_id=1, source_target_pairs={{0,48},{2,50},{4,52},{6,54},{8,56},{10,58},{12,60},{14,62},{16,0},... | collective-permute-start | bytes 1253384 | tf_op jit(solution)/shard_map/ppermute | solution.py:35
  33.2 0.6 pad_add_fusion.order_ref
  33.8 6.6 %collective-permute-done.5 = bf16[272,768]{1,0:T(8,128)(2,1)S(1)} collective-permute-done((bf16[272,768]{1,0:T(8,128)(2,1)S(1)}, bf16[272,768]{1,0:T(8,128)(2,1)S(1)}, u32[]{:S(2)}, u32[]{:S(2)}) %collective-permute-start.5) | collective-permute-done | bytes 417824 | tf_op jit(solution)/shard_map/ppermute | solution.py:35
  40.4 1.3 pad_maximum_fusion.key_line.refs_0_.refs_1_.refs_2_.refs_3_
  41.8 2.9 %collective-permute-done.8 = bf16[272,768]{1,0:T(8,128)(2,1)S(1)} collective-permute-done((bf16[272,768]{1,0:T(8,128)(2,1)S(1)}, bf16[272,768]{1,0:T(8,128)(2,1)S(1)}, u32[]{:S(2)}, u32[]{:S(2)}) %collective-permute-start.8) | collective-permute-done | bytes 417824 | tf_op jit(solution)/shard_map/ppermute | solution.py:35
  44.7 1.3 pad_maximum_fusion.1.value_line.refs_16_.refs_17_.refs_18_.refs_19_
  46.0 3.0 %collective-permute-start.10 = (bf16[1088,768]{1,0:T(8,128)(2,1)}, bf16[1088,768]{1,0:T(8,128)(2,1)S(1)}, u32[]{:S(2)}, u32[]{:S(2)}) collective-permute-start(bf16[1088,768]{1,0:T(8,128)(2,1)} %pad_maximum_fusion.key_line.refs_0_.refs_1_.refs_2_.refs_3_), channel_id=1, source_target_pairs={{0,48},{2,50},{4,52},{6,54},{8,56},{10,58},{12,60},{14,62},{16,0},... | collective-permute-start | bytes 5013512 | tf_op jit(solution)/shard_map/ppermute | solution.py:35
  49.0 0.5 collective-permute-start.11
  49.5 1.5 collective-permute-start.13
  51.0 0.2 fusion.56
  51.4 0.7 fusion.29.ai_ref
  52.0 0.3 fusion.53
  52.4 0.7 pad_maximum_fusion.6
  53.0 0.6 fusion.35
  53.6 0.7 pad_maximum_fusion.5.tw_hbm
  54.3 11.9 %first_part.1 = (f32[1024,768]{1,0:T(8,128)}, f32[1024,768]{1,0:T(8,128)}, bf16[1024,1024]{1,0:T(8,128)(2,1)}, bf16[1024,1024]{1,0:T(8,128)(2,1)}) custom-call(s32[2,32]{1,0:T(2,128)} %pad_add_fusion.order_ref, bf16[512,4096]{1,0:T(8,128)(2,1)} %bitcast.57, bf16[512,4096]{1,0:T(8,128)(2,1)} %collective-permute-done.3.other_ref, ...), custom_call_target="tpu_custom_call" | custom-call | flops 3221225472 | bytes 18874368 | tf_op jit(solution)/shard_map/first_part/pallas_call | solution.py:122
  66.2 19.9 %collective-permute-done.10.k1.refs_0_.refs_4_.refs_5_.refs_6_.refs_7_ = bf16[1088,768]{1,0:T(8,128)(2,1)S(1)} collective-permute-done((bf16[1088,768]{1,0:T(8,128)(2,1)}, bf16[1088,768]{1,0:T(8,128)(2,1)S(1)}, u32[]{:S(2)}, u32[]{:S(2)}) %collective-permute-start.10) | collective-permute-done | bytes 1671200 | tf_op jit(solution)/shard_map/ppermute | solution.py:35
  86.1 0.8 collective-permute-done.11.k3.refs_1_.refs_12_.refs_13_.refs_14_.refs_15_
  86.9 0.5 collective-permute-done.13.v3.refs_3_.refs_28_.refs_29_.refs_30_.refs_31_
  87.4 0.7 copy-done.1
  88.1 3.2 %cut_halves.1 = (bf16[544,768]{1,0:T(8,128)(2,1)}, bf16[544,768]{1,0:T(8,128)(2,1)}, bf16[544,768]{1,0:T(8,128)(2,1)}, bf16[544,768]{1,0:T(8,128)(2,1)}) custom-call(bf16[1088,768]{1,0:T(8,128)(2,1)} %copy-done, bf16[1088,768]{1,0:T(8,128)(2,1)} %copy-done.1, bf16[1088,768]{1,0:T(8,128)(2,1)} %collective-permute-done.12.v1.refs_2_.refs_20_.refs_21_.refs_22_.refs_23_, ...), custom_call_target="tpu_custom_call" | custom-call | bytes 6684672 | tf_op jit(solution)/shard_map/cut_halves/pallas_call | solution.py:154
  91.3 0.8 collective-permute-start.14
  92.2 0.6 collective-permute-start.15
  92.8 1.5 collective-permute-start.17
  94.3 2.1 collective-permute-start.19
  96.4 14.7 %second_part.1 = (f32[1024,768]{1,0:T(8,128)}, f32[1024,768]{1,0:T(8,128)}) custom-call(s32[2,32]{1,0:T(2,128)} %pad_add_fusion.order_ref, bf16[512,4096]{1,0:T(8,128)(2,1)} %bitcast.58, bf16[512,4096]{1,0:T(8,128)(2,1)} %collective-permute-done.3.other_ref, f32[1024,768]{1,0:T(8,128)} %get-tuple-element.54.key_in, f32[1024,768]{1,0:T(8,128)} %get-tuple-element.55.value_in, ...), custom_call_target="tpu_custom_call" | custom-call | flops 6442450944 | bytes 18874368 | tf_op jit(solution)/shard_map/second_part/pallas_call | solution.py:122
  111.3 0.7 copy-done.2
  112.0 0.3 copy-done.3
  112.3 0.2 copy-done.4
  112.6 0.2 copy-done.5
  112.8 9.1 %last_part.1 = (bf16[512,1024]{1,0:T(8,128)(2,1)}, bf16[512,1024]{1,0:T(8,128)(2,1)}) custom-call(f32[1024,768]{1,0:T(8,128)} %get-tuple-element.60.key_ref, f32[1024,768]{1,0:T(8,128)} %get-tuple-element.61.value_ref, bf16[1024,1024]{1,0:T(8,128)(2,1)} %get-tuple-element.62.key_tok_ref, bf16[1024,1024]{1,0:T(8,128)(2,1)} %get-tuple-element.63.value_tok_ref, ...), custom_call_target="tpu_custom_call" | custom-call | flops 3221225472 | bytes 16777216 | tf_op jit(solution)/shard_map/last_part/pallas_call | solution.py:188
  121.9 5.6 %all-to-all-start = ((bf16[32,16,1024]{2,1,0:T(8,128)(2,1)}), bf16[32,16,1024]{2,1,0:T(8,128)(2,1)S(1)}, u32[]{:S(2)}, u32[]{:S(2)}) async-start(bf16[32,16,1024]{2,1,0:T(8,128)(2,1)} %bitcast.49), calls=%async_computation | async-start | bytes 2097152 | tf_op jit(solution)/shard_map/all_to_all | solution.py:564
  127.5 0.8 copy.12.a_ref
  128.2 3.4 %filter_part.1 = (f32[64,1024]{1,0:T(8,128)}, bf16[256,256]{1,0:T(8,128)(2,1)}) custom-call(s32[2,32]{1,0:T(2,128)} %pad_add_fusion.order_ref, bf16[1088,768]{1,0:T(8,128)(2,1)} %pad_maximum_fusion.key_line.refs_0_.refs_1_.refs_2_.refs_3_, bf16[1088,768]{1,0:T(8,128)(2,1)} %pad_maximum_fusion.key_line.refs_0_.refs_1_.refs_2_.refs_3_, ...), custom_call_target="tpu_custom_call" | custom-call | flops 1000000000 | bytes 1048576 | tf_op jit(solution)/shard_map/filter_part/pallas_call | solution.py:319
  131.6 8.8 %all-to-all-done.x_ref = bf16[32,16,1024]{2,1,0:T(8,128)(2,1)S(1)} async-done(((bf16[32,16,1024]{2,1,0:T(8,128)(2,1)}), bf16[32,16,1024]{2,1,0:T(8,128)(2,1)S(1)}, u32[]{:S(2)}, u32[]{:S(2)}) %all-to-all-start) | async-done | bytes 1048608 | tf_op jit(solution)/shard_map/all_to_all | solution.py:564
  140.5 1.0 copy-done.7
  141.4 13.0 %long_conv.1 = bf16[32,16,1024]{2,1,0:T(8,128)(2,1)} custom-call(bf16[32,16,1024]{2,1,0:T(8,128)(2,1)} %copy-done.7, bf16[512,1024]{1,0:T(8,128)(2,1)} %constant.204.clone.fwd_hbm, bf16[1024,512]{1,0:T(8,128)(2,1)} %constant.205.clone.inv_hbm, f32[64,1024]{1,0:T(8,128)} %pad_maximum_fusion.5.tw_hbm, bf16[256,256]{1,0:T(8,128)(2,1)} %copy.12.a_ref, ...), custom_call_target="tpu_custom_call" | custom-call | flops 8000000000 | bytes 8388608 | tf_op jit(solution)/shard_map/long_conv/pallas_call | solution.py:422
  154.4 4.5 %all-to-all-start.1 = ((bf16[32,16,1024]{2,1,0:T(8,128)(2,1)}), bf16[32,16,1024]{2,1,0:T(8,128)(2,1)S(1)}, u32[]{:S(2)}, u32[]{:S(2)}) async-start(bf16[32,16,1024]{2,1,0:T(8,128)(2,1)} %long_conv.1), calls=%async_computation.1 | async-start | bytes 2097152 | tf_op jit(solution)/shard_map/all_to_all | solution.py:580
  159.0 12.5 %all-to-all-done.1 = bf16[32,16,1024]{2,1,0:T(8,128)(2,1)S(1)} async-done(((bf16[32,16,1024]{2,1,0:T(8,128)(2,1)}), bf16[32,16,1024]{2,1,0:T(8,128)(2,1)S(1)}, u32[]{:S(2)}, u32[]{:S(2)}) %all-to-all-start.1) | async-done | bytes 1048608 | tf_op jit(solution)/shard_map/all_to_all | solution.py:580
  171.5 1.7 fusion.1
  173.4 21.8 %collective-permute-start.18 = (bf16[512,256]{1,0:T(8,128)(2,1)S(1)}, bf16[512,256]{1,0:T(8,128)(2,1)S(1)}, u32[]{:S(2)}, u32[]{:S(2)}) collective-permute-start(bf16[512,256]{1,0:T(8,128)(2,1)S(1)} %get-tuple-element.89), channel_id=1, source_target_pairs={{0,2},{2,0},{4,6},{6,4},{8,10},{10,8},{12,14},{14,12},{16,18},{18,... | collective-permute-start | bytes 786440 | tf_op jit(solution)/shard_map/ppermute | solution.py:35
  195.2 1.2 collective-permute-done.18
  196.3 0.4 collective-permute-start.22
  196.7 0.6 collective-permute-start.20
  197.3 1.2 collective-permute-start.21
  198.6 0.8 pad_maximum_fusion.2.here
  199.5 7.4 %mix_part.1.total_ref = f32[256,4096]{1,0:T(8,128)} custom-call(bf16[1024,256]{1,0:T(8,128)(2,1)} %pad_maximum_fusion.2.here, bf16[1024,4096]{1,0:T(8,128)(2,1)} %w_here.1), custom_call_target="tpu_custom_call" | custom-call | flops 2147483648 | bytes 12582912 | tf_op jit(solution)/shard_map/mix_part/pallas_call | solution.py:243
  206.8 3.5 %collective-permute-done.21.far_h = bf16[512,256]{1,0:T(8,128)(2,1)S(1)} collective-permute-done((bf16[512,256]{1,0:T(8,128)(2,1)S(1)}, bf16[512,256]{1,0:T(8,128)(2,1)S(1)}, u32[]{:S(2)}, u32[]{:S(2)}) %collective-permute-start.21) | collective-permute-done | bytes 262176 | tf_op jit(solution)/shard_map/ppermute | solution.py:598
  210.4 0.7 copy-done.9
  211.0 8.0 %mix_more.1 = bf16[256,4096]{1,0:T(8,128)(2,1)} custom-call(f32[256,4096]{1,0:T(8,128)} %mix_part.1.total_ref, bf16[512,256]{1,0:T(8,128)(2,1)} %copy-done.8, bf16[512,256]{1,0:T(8,128)(2,1)} %copy-done.9, bf16[512,4096]{1,0:T(8,128)(2,1)} %collective-permute-done.19.w_near, bf16[512,4096]{1,0:T(8,128)(2,1)} %collective-permute-done.22.w_far), custom_call_target="tpu_custom_call" | custom-call | flops 2147483648 | bytes 12582912 | tf_op jit(solution)/shard_map/mix_more/pallas_call | solution.py:243
  (63 shorter events, 1.4 us)
Async XLA Ops:
  0.0 18.6 %collective-permute-start.3 = (bf16[512,4096]{1,0:T(8,128)(2,1)}, bf16[512,4096]{1,0:T(8,128)(2,1)}, u32[]{:S(2)}, u32[]{:S(2)}) collective-permute-start(bf16[512,4096]{1,0:T(8,128)(2,1)} %bitcast.56), channel_id=1, source_target_pairs={{0,2},{2,0},{4,6},{6,4},{8,10},{10,8},{12,14},{14,12},{16,18},{18,... | collective-permute-start | bytes 12582920 | tf_op jit(solution)/shard_map/ppermute | solution.py:35
  3.5 9.8 %collective-permute-start.2 = (bf16[224,512]{1,0:T(8,128)(2,1)S(1)}, bf16[224,512]{1,0:T(8,128)(2,1)S(1)}, u32[]{:S(2)}, u32[]{:S(2)}) collective-permute-start(bf16[224,512]{1,0:T(8,128)(2,1)S(1)} %get-tuple-element.115), channel_id=1, source_target_pairs={{0,66},{2,64},{4,70},{6,68},{8,74},{10,72},{12,78},{14,76},{16,82}... | collective-permute-start | bytes 688136 | tf_op jit(solution)/shard_map/ppermute | solution.py:35
  7.2 11.0 %collective-permute-start.1 = (bf16[224,512]{1,0:T(8,128)(2,1)S(1)}, bf16[224,512]{1,0:T(8,128)(2,1)S(1)}, u32[]{:S(2)}, u32[]{:S(2)}) collective-permute-start(bf16[224,512]{1,0:T(8,128)(2,1)S(1)} %fusion.18), channel_id=1, source_target_pairs={{0,64},{2,66},{4,68},{6,70},{8,72},{10,74},{12,76},{14,78},{16,80}... | collective-permute-start | bytes 688136 | tf_op jit(solution)/shard_map/ppermute | solution.py:35
  7.4 10.8 %collective-permute-start = (bf16[224,512]{1,0:T(8,128)(2,1)S(1)}, bf16[224,512]{1,0:T(8,128)(2,1)S(1)}, u32[]{:S(2)}, u32[]{:S(2)}) collective-permute-start(bf16[224,512]{1,0:T(8,128)(2,1)S(1)} %get-tuple-element.114), channel_id=1, source_target_pairs={{0,2},{2,0},{4,6},{6,4},{8,10},{10,8},{12,14},{14,12},{16,18},{18,... | collective-permute-start | bytes 688136 | tf_op jit(solution)/shard_map/ppermute | solution.py:35
  12.6 10.9 %copy-start.11 = (s32[32]{0:T(128)S(1)}, s32[32]{0:T(128)}, u32[]{:S(2)}) copy-start(s32[32]{0:T(128)} %constant.203.clone) | copy-start | bytes 388
  12.6 10.9 %copy-start.12 = (s32[32]{0:T(128)S(1)}, s32[32]{0:T(128)}, u32[]{:S(2)}) copy-start(s32[32]{0:T(128)} %constant.202.clone) | copy-start | bytes 388
  12.6 10.9 %copy-start.13 = (s32[32]{0:T(128)S(1)}, s32[32]{0:T(128)}, u32[]{:S(2)}) copy-start(s32[32]{0:T(128)} %constant.201.clone) | copy-start | bytes 388
  18.6 11.9 %collective-permute-start.6 = (bf16[272,768]{1,0:T(8,128)(2,1)S(1)}, bf16[272,768]{1,0:T(8,128)(2,1)S(1)}, u32[]{:S(2)}, u32[]{:S(2)}) collective-permute-start(bf16[272,768]{1,0:T(8,128)(2,1)S(1)} %pad_maximum_fusion.3), channel_id=1, source_target_pairs={{0,4},{2,6},{4,8},{6,10},{8,12},{10,14},{12,0},{14,2},{16,20},{18,... | collective-permute-start | bytes 1253384 | tf_op jit(solution)/shard_map/ppermute | solution.py:35
  19.9 20.6 %collective-permute-start.5 = (bf16[272,768]{1,0:T(8,128)(2,1)S(1)}, bf16[272,768]{1,0:T(8,128)(2,1)S(1)}, u32[]{:S(2)}, u32[]{:S(2)}) collective-permute-start(bf16[272,768]{1,0:T(8,128)(2,1)S(1)} %pad_maximum_fusion.3), channel_id=1, source_target_pairs={{0,8},{2,10},{4,12},{6,14},{8,0},{10,2},{12,4},{14,6},{16,24},{18,... | collective-permute-start | bytes 1253384 | tf_op jit(solution)/shard_map/ppermute | solution.py:35
  22.3 18.1 %collective-permute-start.4 = (bf16[272,768]{1,0:T(8,128)(2,1)S(1)}, bf16[272,768]{1,0:T(8,128)(2,1)S(1)}, u32[]{:S(2)}, u32[]{:S(2)}) collective-permute-start(bf16[272,768]{1,0:T(8,128)(2,1)S(1)} %pad_maximum_fusion.3), channel_id=1, source_target_pairs={{0,12},{2,14},{4,0},{6,2},{8,4},{10,6},{12,8},{14,10},{16,28},{18,... | collective-permute-start | bytes 1253384 | tf_op jit(solution)/shard_map/ppermute | solution.py:35
  23.5 18.3 %collective-permute-start.9 = (bf16[272,768]{1,0:T(8,128)(2,1)S(1)}, bf16[272,768]{1,0:T(8,128)(2,1)S(1)}, u32[]{:S(2)}, u32[]{:S(2)}) collective-permute-start(bf16[272,768]{1,0:T(8,128)(2,1)S(1)} %pad_maximum_fusion.4), channel_id=1, source_target_pairs={{0,16},{2,18},{4,20},{6,22},{8,24},{10,26},{12,28},{14,30},{16,32}... | collective-permute-start | bytes 1253384 | tf_op jit(solution)/shard_map/ppermute | solution.py:35
  24.9 19.8 %collective-permute-start.8 = (bf16[272,768]{1,0:T(8,128)(2,1)S(1)}, bf16[272,768]{1,0:T(8,128)(2,1)S(1)}, u32[]{:S(2)}, u32[]{:S(2)}) collective-permute-start(bf16[272,768]{1,0:T(8,128)(2,1)S(1)} %pad_maximum_fusion.4), channel_id=1, source_target_pairs={{0,32},{2,34},{4,36},{6,38},{8,40},{10,42},{12,44},{14,46},{16,48}... | collective-permute-start | bytes 1253384 | tf_op jit(solution)/shard_map/ppermute | solution.py:35
  30.5 14.2 %collective-permute-start.7 = (bf16[272,768]{1,0:T(8,128)(2,1)S(1)}, bf16[272,768]{1,0:T(8,128)(2,1)S(1)}, u32[]{:S(2)}, u32[]{:S(2)}) collective-permute-start(bf16[272,768]{1,0:T(8,128)(2,1)S(1)} %pad_maximum_fusion.4), channel_id=1, source_target_pairs={{0,48},{2,50},{4,52},{6,54},{8,56},{10,58},{12,60},{14,62},{16,0},... | collective-permute-start | bytes 1253384 | tf_op jit(solution)/shard_map/ppermute | solution.py:35
  46.0 40.1 %collective-permute-start.10 = (bf16[1088,768]{1,0:T(8,128)(2,1)}, bf16[1088,768]{1,0:T(8,128)(2,1)S(1)}, u32[]{:S(2)}, u32[]{:S(2)}) collective-permute-start(bf16[1088,768]{1,0:T(8,128)(2,1)} %pad_maximum_fusion.key_line.refs_0_.refs_1_.refs_2_.refs_3_), channel_id=1, source_target_pairs={{0,48},{2,50},{4,52},{6,54},{8,56},{10,58},{12,60},{14,62},{16,0},... | collective-permute-start | bytes 5013512 | tf_op jit(solution)/shard_map/ppermute | solution.py:35
  49.0 38.0 %collective-permute-start.11 = (bf16[1088,768]{1,0:T(8,128)(2,1)}, bf16[1088,768]{1,0:T(8,128)(2,1)S(1)}, u32[]{:S(2)}, u32[]{:S(2)}) collective-permute-start(bf16[1088,768]{1,0:T(8,128)(2,1)} %pad_maximum_fusion.key_line.refs_0_.refs_1_.refs_2_.refs_3_), channel_id=1, source_target_pairs={{0,16},{2,18},{4,20},{6,22},{8,24},{10,26},{12,28},{14,30},{16,32}... | collective-permute-start | bytes 5013512 | tf_op jit(solution)/shard_map/ppermute | solution.py:35
  49.5 37.4 %collective-permute-start.12 = (bf16[1088,768]{1,0:T(8,128)(2,1)}, bf16[1088,768]{1,0:T(8,128)(2,1)}, u32[]{:S(2)}, u32[]{:S(2)}) collective-permute-start(bf16[1088,768]{1,0:T(8,128)(2,1)} %pad_maximum_fusion.1.value_line.refs_16_.refs_17_.refs_18_.refs_19_), channel_id=1, source_target_pairs={{0,12},{2,14},{4,0},{6,2},{8,4},{10,6},{12,8},{14,10},{16,28},{18,... | collective-permute-start | bytes 5013512 | tf_op jit(solution)/shard_map/ppermute | solution.py:35
  49.5 37.9 %collective-permute-start.13 = (bf16[1088,768]{1,0:T(8,128)(2,1)}, bf16[1088,768]{1,0:T(8,128)(2,1)}, u32[]{:S(2)}, u32[]{:S(2)}) collective-permute-start(bf16[1088,768]{1,0:T(8,128)(2,1)} %pad_maximum_fusion.1.value_line.refs_16_.refs_17_.refs_18_.refs_19_), channel_id=1, source_target_pairs={{0,4},{2,6},{4,8},{6,10},{8,12},{10,14},{12,0},{14,2},{16,20},{18,... | collective-permute-start | bytes 5013512 | tf_op jit(solution)/shard_map/ppermute | solution.py:35
  86.1 1.3 copy-start
  86.9 1.2 copy-start.1
  91.3 19.8 %collective-permute-start.14 = (bf16[544,768]{1,0:T(8,128)(2,1)}, bf16[544,768]{1,0:T(8,128)(2,1)S(1)}, u32[]{:S(2)}, u32[]{:S(2)}) collective-permute-start(bf16[544,768]{1,0:T(8,128)(2,1)} %get-tuple-element.64), channel_id=1, source_target_pairs={{0,48},{2,50},{4,52},{6,54},{8,56},{10,58},{12,60},{14,62},{16,0},... | collective-permute-start | bytes 2506760 | tf_op jit(solution)/shard_map/ppermute | solution.py:35
  92.2 19.0 %collective-permute-start.15 = (bf16[544,768]{1,0:T(8,128)(2,1)}, bf16[544,768]{1,0:T(8,128)(2,1)S(1)}, u32[]{:S(2)}, u32[]{:S(2)}) collective-permute-start(bf16[544,768]{1,0:T(8,128)(2,1)} %get-tuple-element.65), channel_id=1, source_target_pairs={{0,16},{2,18},{4,20},{6,22},{8,24},{10,26},{12,28},{14,30},{16,32}... | collective-permute-start | bytes 2506760 | tf_op jit(solution)/shard_map/ppermute | solution.py:35
  92.8 18.3 %collective-permute-start.16 = (bf16[544,768]{1,0:T(8,128)(2,1)}, bf16[544,768]{1,0:T(8,128)(2,1)S(1)}, u32[]{:S(2)}, u32[]{:S(2)}) collective-permute-start(bf16[544,768]{1,0:T(8,128)(2,1)} %get-tuple-element.66), channel_id=1, source_target_pairs={{0,12},{2,14},{4,0},{6,2},{8,4},{10,6},{12,8},{14,10},{16,28},{18,... | collective-permute-start | bytes 2506760 | tf_op jit(solution)/shard_map/ppermute | solution.py:35
  92.8 18.4 %collective-permute-start.17 = (bf16[544,768]{1,0:T(8,128)(2,1)}, bf16[544,768]{1,0:T(8,128)(2,1)S(1)}, u32[]{:S(2)}, u32[]{:S(2)}) collective-permute-start(bf16[544,768]{1,0:T(8,128)(2,1)} %get-tuple-element.67), channel_id=1, source_target_pairs={{0,4},{2,6},{4,8},{6,10},{8,12},{10,14},{12,0},{14,2},{16,20},{18,... | collective-permute-start | bytes 2506760 | tf_op jit(solution)/shard_map/ppermute | solution.py:35
  94.3 100.9 %collective-permute-start.19 = (bf16[512,4096]{1,0:T(8,128)(2,1)}, bf16[512,4096]{1,0:T(8,128)(2,1)}, u32[]{:S(2)}, u32[]{:S(2)}) collective-permute-start(bf16[512,4096]{1,0:T(8,128)(2,1)} %constant_dynamic-slice_fusion.3), channel_id=1, source_target_pairs={{0,1},{1,0},{2,67},{3,66},{4,5},{5,4},{6,71},{7,70},{8,9},{9,8},{1... | collective-permute-start | bytes 12582920 | tf_op jit(solution)/shard_map/ppermute | solution.py:560
  111.1 0.9 copy-start.2
  111.1 1.2 copy-start.3
  111.1 1.4 copy-start.4
  111.2 1.5 copy-start.5
  121.9 18.6 %all-to-all-start = ((bf16[32,16,1024]{2,1,0:T(8,128)(2,1)}), bf16[32,16,1024]{2,1,0:T(8,128)(2,1)S(1)}, u32[]{:S(2)}, u32[]{:S(2)}) async-start(bf16[32,16,1024]{2,1,0:T(8,128)(2,1)} %bitcast.49), calls=%async_computation | async-start | bytes 2097152 | tf_op jit(solution)/shard_map/all_to_all | solution.py:564
  140.5 1.0 copy-start.7
  141.4 17.5 %copy-start.10 = (f32[1024]{0:T(1024)S(1)}, f32[1024]{0:T(1024)}, u32[]{:S(2)}) copy-start(f32[1024]{0:T(1024)} %param.13) | copy-start | bytes 12292
  141.4 30.1 %copy-start.6 = (bf16[512,1024]{1,0:T(8,128)(2,1)S(1)}, bf16[512,1024]{1,0:T(8,128)(2,1)}, u32[]{:S(2)}) copy-start(bf16[512,1024]{1,0:T(8,128)(2,1)} %get-tuple-element.69) | copy-start | bytes 3145732
  154.4 17.1 %all-to-all-start.1 = ((bf16[32,16,1024]{2,1,0:T(8,128)(2,1)}), bf16[32,16,1024]{2,1,0:T(8,128)(2,1)S(1)}, u32[]{:S(2)}, u32[]{:S(2)}) async-start(bf16[32,16,1024]{2,1,0:T(8,128)(2,1)} %long_conv.1), calls=%async_computation.1 | async-start | bytes 2097152 | tf_op jit(solution)/shard_map/all_to_all | solution.py:580
  173.4 23.0 %collective-permute-start.18 = (bf16[512,256]{1,0:T(8,128)(2,1)S(1)}, bf16[512,256]{1,0:T(8,128)(2,1)S(1)}, u32[]{:S(2)}, u32[]{:S(2)}) collective-permute-start(bf16[512,256]{1,0:T(8,128)(2,1)S(1)} %get-tuple-element.89), channel_id=1, source_target_pairs={{0,2},{2,0},{4,6},{6,4},{8,10},{10,8},{12,14},{14,12},{16,18},{18,... | collective-permute-start | bytes 786440 | tf_op jit(solution)/shard_map/ppermute | solution.py:35
  196.3 14.0 %collective-permute-start.22 = (bf16[512,4096]{1,0:T(8,128)(2,1)}, bf16[512,4096]{1,0:T(8,128)(2,1)}, u32[]{:S(2)}, u32[]{:S(2)}) collective-permute-start(bf16[512,4096]{1,0:T(8,128)(2,1)} %collective-permute-done.19.w_near), channel_id=1, source_target_pairs={{0,2},{2,0},{4,6},{6,4},{8,10},{10,8},{12,14},{14,12},{16,18},{18,... | collective-permute-start | bytes 12582920 | tf_op jit(solution)/shard_map/ppermute | solution.py:35
  196.7 10.1 %collective-permute-start.20 = (bf16[512,256]{1,0:T(8,128)(2,1)S(1)}, bf16[512,256]{1,0:T(8,128)(2,1)S(1)}, u32[]{:S(2)}, u32[]{:S(2)}) collective-permute-start(bf16[512,256]{1,0:T(8,128)(2,1)S(1)} %get-tuple-element.88), channel_id=1, source_target_pairs={{0,1},{1,0},{2,3},{3,2},{4,5},{5,4},{6,7},{7,6},{8,9},{9,8},{10,11... | collective-permute-start | bytes 786440 | tf_op jit(solution)/shard_map/ppermute | solution.py:593
  197.3 13.0 %collective-permute-start.21 = (bf16[512,256]{1,0:T(8,128)(2,1)S(1)}, bf16[512,256]{1,0:T(8,128)(2,1)S(1)}, u32[]{:S(2)}, u32[]{:S(2)}) collective-permute-start(bf16[512,256]{1,0:T(8,128)(2,1)S(1)} %get-tuple-element.87), channel_id=1, source_target_pairs={{0,3},{1,2},{2,1},{3,0},{4,7},{5,6},{6,5},{7,4},{8,11},{9,10},{10,... | collective-permute-start | bytes 786440 | tf_op jit(solution)/shard_map/ppermute | solution.py:598
  206.8 3.5 %copy-start.8 = (bf16[512,256]{1,0:T(8,128)(2,1)}, bf16[512,256]{1,0:T(8,128)(2,1)S(1)}, u32[]{:S(2)}) copy-start(bf16[512,256]{1,0:T(8,128)(2,1)S(1)} %collective-permute-done.20.near_h) | copy-start | bytes 786436
  210.4 0.7 copy-start.9

commit v13 on v12

--- a/solution.py
+++ b/solution.py
@@ -559,6 +559,7 @@
             perm.append((t * 2 + th, index_of(tz ^ tc, ty, tx, tc) * 2 + 1 - th))
     ow_same = lax.ppermute(ow_part, ("seq", "ch"), perm)
 
+    last_lines, ow_same = lax.optimization_barrier((last_lines, ow_same))
     source, gate = last_part(totals, first[2:], last_lines)
     packed = source.reshape(CHIPS, chan // CHIPS, 2 * rows)
     mine_ch = lax.all_to_all(packed, "seq", 0, 0, axis_index_groups=SAME_CORE)

time: 220 us -> 211 us (0.959)
  starting transfers between devices: 61.3 us -> 43.6 us
  waiting for transfers between devices: 65.5 us -> 75.7 us
    ppermute x20, starting transfers between devices: 47.4 us -> 30.5 us  [send(): return lax.ppermute(value, 'seq', perm)]
    ppermute x20, waiting for transfers between devices: 40.6 us -> 46.7 us  [send(): return lax.ppermute(value, 'seq', perm)]
  transfers between devices with their start and end apart: 25 -> 25, of which waited for: 13 -> 16; matrix products, arithmetic and copies ran while one was open for 7% -> 7% of each run, Pallas kernels for 27% -> 19%
where the time goes in v13:
time: 211 us; the launch traced here: 210 us
  waiting for transfers between devices  75.7 us (36%)
  Pallas kernels  70.7 us (34%)
  starting transfers between devices  43.6 us (21%)
  local copies, waits for them, and re-layouts  10.3 us (5%)
  other arithmetic  9.63 us (5%)
    ppermute x20, waiting for transfers between devices, send(): return lax.ppermute(value, 'seq', perm)  46.7 us
    ppermute x20, starting transfers between devices, send(): return lax.ppermute(value, 'seq', perm)  30.5 us
    pallas_call x2, Pallas kernels, sum_part(): pl.pallas_call(kernel, grid_spec=pltpu.PrefetchScalarGridSpec(num_scalar_...  26.6 us
    pallas_call x2, Pallas kernels, mix_part(): pl.pallas_call(mix_kernel if total is None else mix_more_kernel, grid=(4,...  15.4 us
    all_to_all x1, waiting for transfers between devices, per_device(): conv = lax.all_to_all(conv, 'seq', 0, 0, axis_index_groups=SAME_CORE)  14.5 us
    pallas_call x1, Pallas kernels, long_conv(): pl.pallas_call(conv_kernel, in_specs=[vmem, hbm, hbm, hbm, vmem, vmem, vm...  13 us
    all_to_all x1, waiting for transfers between devices, per_device(): mine_ch = lax.all_to_all(packed, 'seq', 0, 0, axis_index_groups=SAME_CORE)  10.9 us
    pallas_call x1, Pallas kernels, last_part(): pl.pallas_call(last_kernel, grid=(4,), in_specs=[pl.BlockSpec((tile, wide...  9.09 us
  transfers between devices with their start and end apart: 25, of which 16 were waited for; matrix products, arithmetic and copies ran while one was open for 7% of the time, Pallas kernels for 19%

profile of v13, /device:TPU:1, one launch (start us, length us, event | category | flops | bytes accessed | tf_op | source)
XLA Modules:
  0.0 210.2 jit_solution(10134259143103679586)
XLA Ops:
  0.0 1.4 collective-permute-start.3
  1.4 0.9 copy.11
  2.5 1.1 constant_dynamic-slice_fusion.5
  3.5 3.6 %collective-permute-start.2 = (bf16[224,512]{1,0:T(8,128)(2,1)S(1)}, bf16[224,512]{1,0:T(8,128)(2,1)S(1)}, u32[]{:S(2)}, u32[]{:S(2)}) collective-permute-start(bf16[224,512]{1,0:T(8,128)(2,1)S(1)} %get-tuple-element.125), channel_id=1, source_target_pairs={{0,66},{2,64},{4,70},{6,68},{8,74},{10,72},{12,78},{14,76},{16,82}... | collective-permute-start | bytes 688136 | tf_op jit(solution)/shard_map/ppermute | solution.py:35
  7.4 0.5 collective-permute-start
  7.9 4.7 %constant_dynamic-slice_fusion.3 = bf16[512,4096]{1,0:T(8,128)(2,1)} fusion(bf16[1024,4096]{1,0:T(8,128)(2,1)} %w_here.1, s32[]{:T(128)S(6)} %select_n.290), kind=kLoop, calls=%fused_computation.141 | loop fusion | bytes 8388612 | tf_op jit(solution)/shard_map/dynamic_slice | solution.py:529
  12.6 0.8 collective-permute-done.2
  13.4 4.8 %collective-permute-done.1 = bf16[224,512]{1,0:T(8,128)(2,1)S(1)} collective-permute-done((bf16[224,512]{1,0:T(8,128)(2,1)S(1)}, bf16[224,512]{1,0:T(8,128)(2,1)S(1)}, u32[]{:S(2)}, u32[]{:S(2)}) %collective-permute-start.1) | collective-permute-done | bytes 229408 | tf_op jit(solution)/shard_map/ppermute | solution.py:35
  18.6 1.3 collective-permute-start.6
  19.9 2.5 %collective-permute-start.5 = (bf16[272,768]{1,0:T(8,128)(2,1)S(1)}, bf16[272,768]{1,0:T(8,128)(2,1)S(1)}, u32[]{:S(2)}, u32[]{:S(2)}) collective-permute-start(bf16[272,768]{1,0:T(8,128)(2,1)S(1)} %pad_maximum_fusion.3), channel_id=1, source_target_pairs={{0,8},{2,10},{4,12},{6,14},{8,0},{10,2},{12,4},{14,6},{16,24},{18,... | collective-permute-start | bytes 1253384 | tf_op jit(solution)/shard_map/ppermute | solution.py:35
  22.4 1.2 collective-permute-start.4
  23.5 1.3 collective-permute-start.9
  24.8 2.6 %collective-permute-start.8 = (bf16[272,768]{1,0:T(8,128)(2,1)S(1)}, bf16[272,768]{1,0:T(8,128)(2,1)S(1)}, u32[]{:S(2)}, u32[]{:S(2)}) collective-permute-start(bf16[272,768]{1,0:T(8,128)(2,1)S(1)} %pad_maximum_fusion.4), channel_id=1, source_target_pairs={{0,32},{2,34},{4,36},{6,38},{8,40},{10,42},{12,44},{14,46},{16,48}... | collective-permute-start | bytes 1253384 | tf_op jit(solution)/shard_map/ppermute | solution.py:35
  27.4 3.1 %collective-permute-done.6 = bf16[272,768]{1,0:T(8,128)(2,1)S(1)} collective-permute-done((bf16[272,768]{1,0:T(8,128)(2,1)S(1)}, bf16[272,768]{1,0:T(8,128)(2,1)S(1)}, u32[]{:S(2)}, u32[]{:S(2)}) %collective-permute-start.6) | collective-permute-done | bytes 417824 | tf_op jit(solution)/shard_map/ppermute | solution.py:35
  30.5 2.7 %collective-permute-start.7 = (bf16[272,768]{1,0:T(8,128)(2,1)S(1)}, bf16[272,768]{1,0:T(8,128)(2,1)S(1)}, u32[]{:S(2)}, u32[]{:S(2)}) collective-permute-start(bf16[272,768]{1,0:T(8,128)(2,1)S(1)} %pad_maximum_fusion.4), channel_id=1, source_target_pairs={{0,48},{2,50},{4,52},{6,54},{8,56},{10,58},{12,60},{14,62},{16,0},... | collective-permute-start | bytes 1253384 | tf_op jit(solution)/shard_map/ppermute | solution.py:35
  33.3 7.2 %collective-permute-done.5 = bf16[272,768]{1,0:T(8,128)(2,1)S(1)} collective-permute-done((bf16[272,768]{1,0:T(8,128)(2,1)S(1)}, bf16[272,768]{1,0:T(8,128)(2,1)S(1)}, u32[]{:S(2)}, u32[]{:S(2)}) %collective-permute-start.5) | collective-permute-done | bytes 417824 | tf_op jit(solution)/shard_map/ppermute | solution.py:35
  40.5 1.3 pad_maximum_fusion.key_line.refs_0_.refs_1_.refs_2_.refs_3_
  41.8 2.8 %collective-permute-done.8 = bf16[272,768]{1,0:T(8,128)(2,1)S(1)} collective-permute-done((bf16[272,768]{1,0:T(8,128)(2,1)S(1)}, bf16[272,768]{1,0:T(8,128)(2,1)S(1)}, u32[]{:S(2)}, u32[]{:S(2)}) %collective-permute-start.8) | collective-permute-done | bytes 417824 | tf_op jit(solution)/shard_map/ppermute | solution.py:35
  44.6 1.3 pad_maximum_fusion.1.value_line.refs_16_.refs_17_.refs_18_.refs_19_
  45.9 2.1 collective-permute-start.18
  48.1 0.6 pad_add_fusion.order_ref
  48.7 2.7 %collective-permute-start.10 = (bf16[1088,768]{1,0:T(8,128)(2,1)}, bf16[1088,768]{1,0:T(8,128)(2,1)S(1)}, u32[]{:S(2)}, u32[]{:S(2)}) collective-permute-start(bf16[1088,768]{1,0:T(8,128)(2,1)} %pad_maximum_fusion.key_line.refs_0_.refs_1_.refs_2_.refs_3_), channel_id=1, source_target_pairs={{0,48},{2,50},{4,52},{6,54},{8,56},{10,58},{12,60},{14,62},{16,0},... | collective-permute-start | bytes 5013512 | tf_op jit(solution)/shard_map/ppermute | solution.py:35
  51.4 1.1 collective-permute-start.11
  52.5 1.5 collective-permute-start.13
  54.0 0.2 fusion.56
  54.4 0.7 fusion.29.ai_ref
  55.0 0.3 fusion.53
  55.4 0.7 pad_maximum_fusion.6
  56.0 0.6 fusion.35
  56.6 0.7 pad_maximum_fusion.5.tw_hbm
  57.3 11.9 %first_part.1 = (f32[1024,768]{1,0:T(8,128)}, f32[1024,768]{1,0:T(8,128)}, bf16[1024,1024]{1,0:T(8,128)(2,1)}, bf16[1024,1024]{1,0:T(8,128)(2,1)}) custom-call(s32[2,32]{1,0:T(2,128)} %pad_add_fusion.order_ref, bf16[512,4096]{1,0:T(8,128)(2,1)} %bitcast.57, bf16[512,4096]{1,0:T(8,128)(2,1)} %collective-permute-done.3.other_ref, ...), custom_call_target="tpu_custom_call" | custom-call | flops 3221225472 | bytes 18874368 | tf_op jit(solution)/shard_map/first_part/pallas_call | solution.py:122
  69.2 19.8 %collective-permute-done.10.k1.refs_0_.refs_4_.refs_5_.refs_6_.refs_7_ = bf16[1088,768]{1,0:T(8,128)(2,1)S(1)} collective-permute-done((bf16[1088,768]{1,0:T(8,128)(2,1)}, bf16[1088,768]{1,0:T(8,128)(2,1)S(1)}, u32[]{:S(2)}, u32[]{:S(2)}) %collective-permute-start.10) | collective-permute-done | bytes 1671200 | tf_op jit(solution)/shard_map/ppermute | solution.py:35
  88.9 1.7 collective-permute-done.11.k3.refs_1_.refs_12_.refs_13_.refs_14_.refs_15_
  90.6 0.4 collective-permute-done.12.v1.refs_2_.refs_20_.refs_21_.refs_22_.refs_23_
  91.0 1.2 collective-permute-done.13.v3.refs_3_.refs_28_.refs_29_.refs_30_.refs_31_
  92.2 3.2 %cut_halves.1 = (bf16[544,768]{1,0:T(8,128)(2,1)}, bf16[544,768]{1,0:T(8,128)(2,1)}, bf16[544,768]{1,0:T(8,128)(2,1)}, bf16[544,768]{1,0:T(8,128)(2,1)}) custom-call(bf16[1088,768]{1,0:T(8,128)(2,1)} %copy-done, bf16[1088,768]{1,0:T(8,128)(2,1)} %copy-done.1, bf16[1088,768]{1,0:T(8,128)(2,1)} %collective-permute-done.12.v1.refs_2_.refs_20_.refs_21_.refs_22_.refs_23_, ...), custom_call_target="tpu_custom_call" | custom-call | bytes 6684672 | tf_op jit(solution)/shard_map/cut_halves/pallas_call | solution.py:154
  95.5 1.3 collective-permute-start.14
  96.7 0.5 collective-permute-start.15
  97.3 1.4 collective-permute-start.17
  98.7 14.7 %second_part.1 = (f32[1024,768]{1,0:T(8,128)}, f32[1024,768]{1,0:T(8,128)}) custom-call(s32[2,32]{1,0:T(2,128)} %pad_add_fusion.order_ref, bf16[512,4096]{1,0:T(8,128)(2,1)} %bitcast.58, bf16[512,4096]{1,0:T(8,128)(2,1)} %collective-permute-done.3.other_ref, f32[1024,768]{1,0:T(8,128)} %get-tuple-element.59.key_in, f32[1024,768]{1,0:T(8,128)} %get-tuple-element.60.value_in, ...), custom_call_target="tpu_custom_call" | custom-call | flops 6442450944 | bytes 18874368 | tf_op jit(solution)/shard_map/second_part/pallas_call | solution.py:122
  113.4 2.2 %collective-permute-done.14.ka.refs_8_.refs_9_ = bf16[544,768]{1,0:T(8,128)(2,1)S(1)} collective-permute-done((bf16[544,768]{1,0:T(8,128)(2,1)}, bf16[544,768]{1,0:T(8,128)(2,1)S(1)}, u32[]{:S(2)}, u32[]{:S(2)}) %collective-permute-start.14) | collective-permute-done | bytes 835616 | tf_op jit(solution)/shard_map/ppermute | solution.py:35
  115.6 0.8 collective-permute-done.15.kb.refs_10_.refs_11_
  116.4 0.8 collective-permute-done.17.vb.refs_26_.refs_27_
  117.3 0.3 copy-done.4
  117.5 0.5 copy-done.5
  118.1 9.1 %last_part.1 = (bf16[512,1024]{1,0:T(8,128)(2,1)}, bf16[512,1024]{1,0:T(8,128)(2,1)}) custom-call(f32[1024,768]{1,0:T(8,128)} %get-tuple-element.65.key_ref, f32[1024,768]{1,0:T(8,128)} %get-tuple-element.66.value_ref, bf16[1024,1024]{1,0:T(8,128)(2,1)} %get-tuple-element.67.key_tok_ref, bf16[1024,1024]{1,0:T(8,128)(2,1)} %get-tuple-element.68.value_tok_ref, ...), custom_call_target="tpu_custom_call" | custom-call | flops 3221225472 | bytes 16777216 | tf_op jit(solution)/shard_map/last_part/pallas_call | solution.py:188
  127.2 4.2 %all-to-all-start = ((bf16[32,16,1024]{2,1,0:T(8,128)(2,1)}), bf16[32,16,1024]{2,1,0:T(8,128)(2,1)S(1)}, u32[]{:S(2)}, u32[]{:S(2)}) async-start(bf16[32,16,1024]{2,1,0:T(8,128)(2,1)} %bitcast.49), calls=%async_computation | async-start | bytes 2097152 | tf_op jit(solution)/shard_map/all_to_all | solution.py:565
  131.4 0.8 copy.12.a_ref
  132.1 3.4 %filter_part.1 = (f32[64,1024]{1,0:T(8,128)}, bf16[256,256]{1,0:T(8,128)(2,1)}) custom-call(s32[2,32]{1,0:T(2,128)} %pad_add_fusion.order_ref, bf16[1088,768]{1,0:T(8,128)(2,1)} %pad_maximum_fusion.key_line.refs_0_.refs_1_.refs_2_.refs_3_, bf16[1088,768]{1,0:T(8,128)(2,1)} %pad_maximum_fusion.key_line.refs_0_.refs_1_.refs_2_.refs_3_, ...), custom_call_target="tpu_custom_call" | custom-call | flops 1000000000 | bytes 1048576 | tf_op jit(solution)/shard_map/filter_part/pallas_call | solution.py:319
  135.5 10.9 %all-to-all-done.x_ref = bf16[32,16,1024]{2,1,0:T(8,128)(2,1)S(1)} async-done(((bf16[32,16,1024]{2,1,0:T(8,128)(2,1)}), bf16[32,16,1024]{2,1,0:T(8,128)(2,1)S(1)}, u32[]{:S(2)}, u32[]{:S(2)}) %all-to-all-start) | async-done | bytes 1048608 | tf_op jit(solution)/shard_map/all_to_all | solution.py:565
  146.5 1.0 copy-done.7
  147.5 13.0 %long_conv.1 = bf16[32,16,1024]{2,1,0:T(8,128)(2,1)} custom-call(bf16[32,16,1024]{2,1,0:T(8,128)(2,1)} %copy-done.7, bf16[512,1024]{1,0:T(8,128)(2,1)} %constant.204.clone.fwd_hbm, bf16[1024,512]{1,0:T(8,128)(2,1)} %constant.205.clone.inv_hbm, f32[64,1024]{1,0:T(8,128)} %pad_maximum_fusion.5.tw_hbm, bf16[256,256]{1,0:T(8,128)(2,1)} %copy.12.a_ref, ...), custom_call_target="tpu_custom_call" | custom-call | flops 8000000000 | bytes 8388608 | tf_op jit(solution)/shard_map/long_conv/pallas_call | solution.py:422
  160.5 4.9 %all-to-all-start.1 = ((bf16[32,16,1024]{2,1,0:T(8,128)(2,1)}), bf16[32,16,1024]{2,1,0:T(8,128)(2,1)S(1)}, u32[]{:S(2)}, u32[]{:S(2)}) async-start(bf16[32,16,1024]{2,1,0:T(8,128)(2,1)} %long_conv.1), calls=%async_computation.1 | async-start | bytes 2097152 | tf_op jit(solution)/shard_map/all_to_all | solution.py:581
  165.5 14.5 %all-to-all-done.1 = bf16[32,16,1024]{2,1,0:T(8,128)(2,1)S(1)} async-done(((bf16[32,16,1024]{2,1,0:T(8,128)(2,1)}), bf16[32,16,1024]{2,1,0:T(8,128)(2,1)S(1)}, u32[]{:S(2)}, u32[]{:S(2)}) %all-to-all-start.1) | async-done | bytes 1048608 | tf_op jit(solution)/shard_map/all_to_all | solution.py:581
  180.1 1.7 fusion.1
  181.9 4.4 %collective-permute-start.19 = (bf16[512,256]{1,0:T(8,128)(2,1)S(1)}, bf16[512,256]{1,0:T(8,128)(2,1)S(1)}, u32[]{:S(2)}, u32[]{:S(2)}) collective-permute-start(bf16[512,256]{1,0:T(8,128)(2,1)S(1)} %get-tuple-element.99), channel_id=1, source_target_pairs={{0,2},{2,0},{4,6},{6,4},{8,10},{10,8},{12,14},{14,12},{16,18},{18,... | collective-permute-start | bytes 786440 | tf_op jit(solution)/shard_map/ppermute | solution.py:35
  186.3 1.2 collective-permute-done.19
  187.5 0.4 collective-permute-start.22
  187.8 1.8 collective-permute-start.21
  189.8 0.8 pad_maximum_fusion.2.here
  190.6 7.4 %mix_part.1.total_ref = f32[256,4096]{1,0:T(8,128)} custom-call(bf16[1024,256]{1,0:T(8,128)(2,1)} %pad_maximum_fusion.2.here, bf16[1024,4096]{1,0:T(8,128)(2,1)} %w_here.1), custom_call_target="tpu_custom_call" | custom-call | flops 2147483648 | bytes 12582912 | tf_op jit(solution)/shard_map/mix_part/pallas_call | solution.py:243
  198.0 3.5 %collective-permute-done.21.far_h = bf16[512,256]{1,0:T(8,128)(2,1)S(1)} collective-permute-done((bf16[512,256]{1,0:T(8,128)(2,1)S(1)}, bf16[512,256]{1,0:T(8,128)(2,1)S(1)}, u32[]{:S(2)}, u32[]{:S(2)}) %collective-permute-start.21) | collective-permute-done | bytes 262176 | tf_op jit(solution)/shard_map/ppermute | solution.py:599
  201.5 0.7 copy-done.9
  202.2 8.0 %mix_more.1 = bf16[256,4096]{1,0:T(8,128)(2,1)} custom-call(f32[256,4096]{1,0:T(8,128)} %mix_part.1.total_ref, bf16[512,256]{1,0:T(8,128)(2,1)} %copy-done.8, bf16[512,256]{1,0:T(8,128)(2,1)} %copy-done.9, bf16[512,4096]{1,0:T(8,128)(2,1)} %collective-permute-done.18.w_near, bf16[512,4096]{1,0:T(8,128)(2,1)} %collective-permute-done.22.w_far), custom_call_target="tpu_custom_call" | custom-call | flops 2147483648 | bytes 12582912 | tf_op jit(solution)/shard_map/mix_more/pallas_call | solution.py:243
  (63 shorter events, 1.5 us)
Async XLA Ops:
  0.0 18.6 %collective-permute-start.3 = (bf16[512,4096]{1,0:T(8,128)(2,1)}, bf16[512,4096]{1,0:T(8,128)(2,1)}, u32[]{:S(2)}, u32[]{:S(2)}) collective-permute-start(bf16[512,4096]{1,0:T(8,128)(2,1)} %bitcast.56), channel_id=1, source_target_pairs={{0,2},{2,0},{4,6},{6,4},{8,10},{10,8},{12,14},{14,12},{16,18},{18,... | collective-permute-start | bytes 12582920 | tf_op jit(solution)/shard_map/ppermute | solution.py:35
  3.5 9.8 %collective-permute-start.2 = (bf16[224,512]{1,0:T(8,128)(2,1)S(1)}, bf16[224,512]{1,0:T(8,128)(2,1)S(1)}, u32[]{:S(2)}, u32[]{:S(2)}) collective-permute-start(bf16[224,512]{1,0:T(8,128)(2,1)S(1)} %get-tuple-element.125), channel_id=1, source_target_pairs={{0,66},{2,64},{4,70},{6,68},{8,74},{10,72},{12,78},{14,76},{16,82}... | collective-permute-start | bytes 688136 | tf_op jit(solution)/shard_map/ppermute | solution.py:35
  7.2 11.0 %collective-permute-start.1 = (bf16[224,512]{1,0:T(8,128)(2,1)S(1)}, bf16[224,512]{1,0:T(8,128)(2,1)S(1)}, u32[]{:S(2)}, u32[]{:S(2)}) collective-permute-start(bf16[224,512]{1,0:T(8,128)(2,1)S(1)} %fusion.18), channel_id=1, source_target_pairs={{0,64},{2,66},{4,68},{6,70},{8,72},{10,74},{12,76},{14,78},{16,80}... | collective-permute-start | bytes 688136 | tf_op jit(solution)/shard_map/ppermute | solution.py:35
  7.4 10.8 %collective-permute-start = (bf16[224,512]{1,0:T(8,128)(2,1)S(1)}, bf16[224,512]{1,0:T(8,128)(2,1)S(1)}, u32[]{:S(2)}, u32[]{:S(2)}) collective-permute-start(bf16[224,512]{1,0:T(8,128)(2,1)S(1)} %get-tuple-element.124), channel_id=1, source_target_pairs={{0,2},{2,0},{4,6},{6,4},{8,10},{10,8},{12,14},{14,12},{16,18},{18,... | collective-permute-start | bytes 688136 | tf_op jit(solution)/shard_map/ppermute | solution.py:35
  18.6 29.5 %copy-start.11 = (s32[32]{0:T(128)S(1)}, s32[32]{0:T(128)}, u32[]{:S(2)}) copy-start(s32[32]{0:T(128)} %constant.203.clone) | copy-start | bytes 388
  18.6 29.4 %copy-start.12 = (s32[32]{0:T(128)S(1)}, s32[32]{0:T(128)}, u32[]{:S(2)}) copy-start(s32[32]{0:T(128)} %constant.202.clone) | copy-start | bytes 388
  18.6 29.4 %copy-start.13 = (s32[32]{0:T(128)S(1)}, s32[32]{0:T(128)}, u32[]{:S(2)}) copy-start(s32[32]{0:T(128)} %constant.201.clone) | copy-start | bytes 388
  18.6 11.9 %collective-permute-start.6 = (bf16[272,768]{1,0:T(8,128)(2,1)S(1)}, bf16[272,768]{1,0:T(8,128)(2,1)S(1)}, u32[]{:S(2)}, u32[]{:S(2)}) collective-permute-start(bf16[272,768]{1,0:T(8,128)(2,1)S(1)} %pad_maximum_fusion.3), channel_id=1, source_target_pairs={{0,4},{2,6},{4,8},{6,10},{8,12},{10,14},{12,0},{14,2},{16,20},{18,... | collective-permute-start | bytes 1253384 | tf_op jit(solution)/shard_map/ppermute | solution.py:35
  19.9 20.6 %collective-permute-start.5 = (bf16[272,768]{1,0:T(8,128)(2,1)S(1)}, bf16[272,768]{1,0:T(8,128)(2,1)S(1)}, u32[]{:S(2)}, u32[]{:S(2)}) collective-permute-start(bf16[272,768]{1,0:T(8,128)(2,1)S(1)} %pad_maximum_fusion.3), channel_id=1, source_target_pairs={{0,8},{2,10},{4,12},{6,14},{8,0},{10,2},{12,4},{14,6},{16,24},{18,... | collective-permute-start | bytes 1253384 | tf_op jit(solution)/shard_map/ppermute | solution.py:35
  22.4 18.1 %collective-permute-start.4 = (bf16[272,768]{1,0:T(8,128)(2,1)S(1)}, bf16[272,768]{1,0:T(8,128)(2,1)S(1)}, u32[]{:S(2)}, u32[]{:S(2)}) collective-permute-start(bf16[272,768]{1,0:T(8,128)(2,1)S(1)} %pad_maximum_fusion.3), channel_id=1, source_target_pairs={{0,12},{2,14},{4,0},{6,2},{8,4},{10,6},{12,8},{14,10},{16,28},{18,... | collective-permute-start | bytes 1253384 | tf_op jit(solution)/shard_map/ppermute | solution.py:35
  23.5 18.3 %collective-permute-start.9 = (bf16[272,768]{1,0:T(8,128)(2,1)S(1)}, bf16[272,768]{1,0:T(8,128)(2,1)S(1)}, u32[]{:S(2)}, u32[]{:S(2)}) collective-permute-start(bf16[272,768]{1,0:T(8,128)(2,1)S(1)} %pad_maximum_fusion.4), channel_id=1, source_target_pairs={{0,16},{2,18},{4,20},{6,22},{8,24},{10,26},{12,28},{14,30},{16,32}... | collective-permute-start | bytes 1253384 | tf_op jit(solution)/shard_map/ppermute | solution.py:35
  24.8 19.8 %collective-permute-start.8 = (bf16[272,768]{1,0:T(8,128)(2,1)S(1)}, bf16[272,768]{1,0:T(8,128)(2,1)S(1)}, u32[]{:S(2)}, u32[]{:S(2)}) collective-permute-start(bf16[272,768]{1,0:T(8,128)(2,1)S(1)} %pad_maximum_fusion.4), channel_id=1, source_target_pairs={{0,32},{2,34},{4,36},{6,38},{8,40},{10,42},{12,44},{14,46},{16,48}... | collective-permute-start | bytes 1253384 | tf_op jit(solution)/shard_map/ppermute | solution.py:35
  30.5 14.1 %collective-permute-start.7 = (bf16[272,768]{1,0:T(8,128)(2,1)S(1)}, bf16[272,768]{1,0:T(8,128)(2,1)S(1)}, u32[]{:S(2)}, u32[]{:S(2)}) collective-permute-start(bf16[272,768]{1,0:T(8,128)(2,1)S(1)} %pad_maximum_fusion.4), channel_id=1, source_target_pairs={{0,48},{2,50},{4,52},{6,54},{8,56},{10,58},{12,60},{14,62},{16,0},... | collective-permute-start | bytes 1253384 | tf_op jit(solution)/shard_map/ppermute | solution.py:35
  45.9 71.2 %collective-permute-start.18 = (bf16[512,4096]{1,0:T(8,128)(2,1)}, bf16[512,4096]{1,0:T(8,128)(2,1)}, u32[]{:S(2)}, u32[]{:S(2)}) collective-permute-start(bf16[512,4096]{1,0:T(8,128)(2,1)} %constant_dynamic-slice_fusion.3), channel_id=1, source_target_pairs={{0,1},{1,0},{2,67},{3,66},{4,5},{5,4},{6,71},{7,70},{8,9},{9,8},{1... | collective-permute-start | bytes 12582920 | tf_op jit(solution)/shard_map/ppermute | solution.py:560
  48.7 40.3 %collective-permute-start.10 = (bf16[1088,768]{1,0:T(8,128)(2,1)}, bf16[1088,768]{1,0:T(8,128)(2,1)S(1)}, u32[]{:S(2)}, u32[]{:S(2)}) collective-permute-start(bf16[1088,768]{1,0:T(8,128)(2,1)} %pad_maximum_fusion.key_line.refs_0_.refs_1_.refs_2_.refs_3_), channel_id=1, source_target_pairs={{0,48},{2,50},{4,52},{6,54},{8,56},{10,58},{12,60},{14,62},{16,0},... | collective-permute-start | bytes 5013512 | tf_op jit(solution)/shard_map/ppermute | solution.py:35
  51.4 39.3 %collective-permute-start.11 = (bf16[1088,768]{1,0:T(8,128)(2,1)}, bf16[1088,768]{1,0:T(8,128)(2,1)S(1)}, u32[]{:S(2)}, u32[]{:S(2)}) collective-permute-start(bf16[1088,768]{1,0:T(8,128)(2,1)} %pad_maximum_fusion.key_line.refs_0_.refs_1_.refs_2_.refs_3_), channel_id=1, source_target_pairs={{0,16},{2,18},{4,20},{6,22},{8,24},{10,26},{12,28},{14,30},{16,32}... | collective-permute-start | bytes 5013512 | tf_op jit(solution)/shard_map/ppermute | solution.py:35
  52.5 38.5 %collective-permute-start.12 = (bf16[1088,768]{1,0:T(8,128)(2,1)}, bf16[1088,768]{1,0:T(8,128)(2,1)}, u32[]{:S(2)}, u32[]{:S(2)}) collective-permute-start(bf16[1088,768]{1,0:T(8,128)(2,1)} %pad_maximum_fusion.1.value_line.refs_16_.refs_17_.refs_18_.refs_19_), channel_id=1, source_target_pairs={{0,12},{2,14},{4,0},{6,2},{8,4},{10,6},{12,8},{14,10},{16,28},{18,... | collective-permute-start | bytes 5013512 | tf_op jit(solution)/shard_map/ppermute | solution.py:35
  52.5 39.7 %collective-permute-start.13 = (bf16[1088,768]{1,0:T(8,128)(2,1)}, bf16[1088,768]{1,0:T(8,128)(2,1)}, u32[]{:S(2)}, u32[]{:S(2)}) collective-permute-start(bf16[1088,768]{1,0:T(8,128)(2,1)} %pad_maximum_fusion.1.value_line.refs_16_.refs_17_.refs_18_.refs_19_), channel_id=1, source_target_pairs={{0,4},{2,6},{4,8},{6,10},{8,12},{10,14},{12,0},{14,2},{16,20},{18,... | collective-permute-start | bytes 5013512 | tf_op jit(solution)/shard_map/ppermute | solution.py:35
  88.9 3.3 %copy-start = (bf16[1088,768]{1,0:T(8,128)(2,1)}, bf16[1088,768]{1,0:T(8,128)(2,1)S(1)}, u32[]{:S(2)}) copy-start(bf16[1088,768]{1,0:T(8,128)(2,1)S(1)} %collective-permute-done.10.k1.refs_0_.refs_4_.refs_5_.refs_6_.refs_7_) | copy-start | bytes 5013508
  90.6 1.6 copy-start.1
  95.5 20.1 %collective-permute-start.14 = (bf16[544,768]{1,0:T(8,128)(2,1)}, bf16[544,768]{1,0:T(8,128)(2,1)S(1)}, u32[]{:S(2)}, u32[]{:S(2)}) collective-permute-start(bf16[544,768]{1,0:T(8,128)(2,1)} %get-tuple-element.69), channel_id=1, source_target_pairs={{0,48},{2,50},{4,52},{6,54},{8,56},{10,58},{12,60},{14,62},{16,0},... | collective-permute-start | bytes 2506760 | tf_op jit(solution)/shard_map/ppermute | solution.py:35
  96.7 19.6 %collective-permute-start.15 = (bf16[544,768]{1,0:T(8,128)(2,1)}, bf16[544,768]{1,0:T(8,128)(2,1)S(1)}, u32[]{:S(2)}, u32[]{:S(2)}) collective-permute-start(bf16[544,768]{1,0:T(8,128)(2,1)} %get-tuple-element.70), channel_id=1, source_target_pairs={{0,16},{2,18},{4,20},{6,22},{8,24},{10,26},{12,28},{14,30},{16,32}... | collective-permute-start | bytes 2506760 | tf_op jit(solution)/shard_map/ppermute | solution.py:35
  97.2 19.1 %collective-permute-start.16 = (bf16[544,768]{1,0:T(8,128)(2,1)}, bf16[544,768]{1,0:T(8,128)(2,1)S(1)}, u32[]{:S(2)}, u32[]{:S(2)}) collective-permute-start(bf16[544,768]{1,0:T(8,128)(2,1)} %get-tuple-element.71), channel_id=1, source_target_pairs={{0,12},{2,14},{4,0},{6,2},{8,4},{10,6},{12,8},{14,10},{16,28},{18,... | collective-permute-start | bytes 2506760 | tf_op jit(solution)/shard_map/ppermute | solution.py:35
  97.3 19.8 %collective-permute-start.17 = (bf16[544,768]{1,0:T(8,128)(2,1)}, bf16[544,768]{1,0:T(8,128)(2,1)S(1)}, u32[]{:S(2)}, u32[]{:S(2)}) collective-permute-start(bf16[544,768]{1,0:T(8,128)(2,1)} %get-tuple-element.72), channel_id=1, source_target_pairs={{0,4},{2,6},{4,8},{6,10},{8,12},{10,14},{12,0},{14,2},{16,20},{18,... | collective-permute-start | bytes 2506760 | tf_op jit(solution)/shard_map/ppermute | solution.py:35
  115.6 1.6 copy-start.2
  116.3 0.9 copy-start.3
  116.4 1.2 copy-start.4
  117.1 0.9 copy-start.5
  127.2 19.3 %all-to-all-start = ((bf16[32,16,1024]{2,1,0:T(8,128)(2,1)}), bf16[32,16,1024]{2,1,0:T(8,128)(2,1)S(1)}, u32[]{:S(2)}, u32[]{:S(2)}) async-start(bf16[32,16,1024]{2,1,0:T(8,128)(2,1)} %bitcast.49), calls=%async_computation | async-start | bytes 2097152 | tf_op jit(solution)/shard_map/all_to_all | solution.py:565
  146.5 1.0 copy-start.7
  147.5 18.0 %copy-start.10 = (f32[1024]{0:T(1024)S(1)}, f32[1024]{0:T(1024)}, u32[]{:S(2)}) copy-start(f32[1024]{0:T(1024)} %param.13) | copy-start | bytes 12292
  147.5 32.6 %copy-start.6 = (bf16[512,1024]{1,0:T(8,128)(2,1)S(1)}, bf16[512,1024]{1,0:T(8,128)(2,1)}, u32[]{:S(2)}) copy-start(bf16[512,1024]{1,0:T(8,128)(2,1)} %get-tuple-element.79) | copy-start | bytes 3145732
  160.5 19.6 %all-to-all-start.1 = ((bf16[32,16,1024]{2,1,0:T(8,128)(2,1)}), bf16[32,16,1024]{2,1,0:T(8,128)(2,1)S(1)}, u32[]{:S(2)}, u32[]{:S(2)}) async-start(bf16[32,16,1024]{2,1,0:T(8,128)(2,1)} %long_conv.1), calls=%async_computation.1 | async-start | bytes 2097152 | tf_op jit(solution)/shard_map/all_to_all | solution.py:581
  181.9 5.5 %collective-permute-start.19 = (bf16[512,256]{1,0:T(8,128)(2,1)S(1)}, bf16[512,256]{1,0:T(8,128)(2,1)S(1)}, u32[]{:S(2)}, u32[]{:S(2)}) collective-permute-start(bf16[512,256]{1,0:T(8,128)(2,1)S(1)} %get-tuple-element.99), channel_id=1, source_target_pairs={{0,2},{2,0},{4,6},{6,4},{8,10},{10,8},{12,14},{14,12},{16,18},{18,... | collective-permute-start | bytes 786440 | tf_op jit(solution)/shard_map/ppermute | solution.py:35
  187.5 14.0 %collective-permute-start.22 = (bf16[512,4096]{1,0:T(8,128)(2,1)}, bf16[512,4096]{1,0:T(8,128)(2,1)}, u32[]{:S(2)}, u32[]{:S(2)}) collective-permute-start(bf16[512,4096]{1,0:T(8,128)(2,1)} %collective-permute-done.18.w_near), channel_id=1, source_target_pairs={{0,2},{2,0},{4,6},{6,4},{8,10},{10,8},{12,14},{14,12},{16,18},{18,... | collective-permute-start | bytes 12582920 | tf_op jit(solution)/shard_map/ppermute | solution.py:35
  187.8 10.1 %collective-permute-start.20 = (bf16[512,256]{1,0:T(8,128)(2,1)S(1)}, bf16[512,256]{1,0:T(8,128)(2,1)S(1)}, u32[]{:S(2)}, u32[]{:S(2)}) collective-permute-start(bf16[512,256]{1,0:T(8,128)(2,1)S(1)} %get-tuple-element.98), channel_id=1, source_target_pairs={{0,1},{1,0},{2,3},{3,2},{4,5},{5,4},{6,7},{7,6},{8,9},{9,8},{10,11... | collective-permute-start | bytes 786440 | tf_op jit(solution)/shard_map/ppermute | solution.py:594
  187.8 13.6 %collective-permute-start.21 = (bf16[512,256]{1,0:T(8,128)(2,1)S(1)}, bf16[512,256]{1,0:T(8,128)(2,1)S(1)}, u32[]{:S(2)}, u32[]{:S(2)}) collective-permute-start(bf16[512,256]{1,0:T(8,128)(2,1)S(1)} %get-tuple-element.97), channel_id=1, source_target_pairs={{0,3},{1,2},{2,1},{3,0},{4,7},{5,6},{6,5},{7,4},{8,11},{9,10},{10,... | collective-permute-start | bytes 786440 | tf_op jit(solution)/shard_map/ppermute | solution.py:599
  198.0 3.5 %copy-start.8 = (bf16[512,256]{1,0:T(8,128)(2,1)}, bf16[512,256]{1,0:T(8,128)(2,1)S(1)}, u32[]{:S(2)}) copy-start(bf16[512,256]{1,0:T(8,128)(2,1)S(1)} %collective-permute-done.20.near_h) | copy-start | bytes 786436
  201.5 0.7 copy-start.9

commit v14 on v9

--- a/solution.py
+++ b/solution.py
@@ -420,7 +420,7 @@
                     q_ref[col, blocks + k, pick, :] = out_im[part, k * 128 : (k + 1) * 128]
         return carry
 
-    lax.fori_loop(0, chans // 2, pair, 0, unroll=2)
+    lax.fori_loop(0, chans // 2, pair, 0, unroll=4)
     copies[2].wait()
     for col in range(2):
         q = jnp.concatenate([q_ref[col, k].astype(BF16) for k in range(2 * blocks)], axis=1)
@@ -574,9 +574,8 @@
     forward, inverse = row_tables(rows, padded)
     fwd = jnp.asarray(forward.astype(np.float32).astype(ml_dtypes.bfloat16))
     inv = jnp.asarray(inverse.astype(np.float32).astype(ml_dtypes.bfloat16))
+    mine_ch, ow_same, f, m = lax.optimization_barrier((mine_ch, ow_same, f, m))
     conv = long_conv(mine_ch, fwd, inv, tw, a, ai, m, f)
-    conv, ow_same = lax.optimization_barrier((conv, ow_same))
-    ow_cross = send(ow_same, dc=1)
     conv = lax.all_to_all(conv, "seq", 0, 0, axis_index_groups=SAME_CORE)
     conv = conv.reshape(chan, 2 * rows).astype(F32)
 
@@ -597,6 +596,8 @@
             perm2.append((t * 2 + th, (t ^ 1) * 2 + 1 - th))
     from_hc = lax.ppermute(oth_there, ("seq", "ch"), perm2)
     from_c = send(oth_here, dc=1)
+    from_c, ow_same = lax.optimization_barrier((from_c, ow_same))
+    ow_cross = send(ow_same, dc=1)
     here = ordered(own_here, from_c)
 
     mixed = mix_part(None, [here], [out_weight])

time: 211 us -> 209 us (level)
    all_to_all x1, waiting for transfers between devices: 7.56 us -> 5.01 us  [per_device(): conv = lax.all_to_all(conv, 'seq', 0, 0, axis_index_groups=SAME_CORE)]
  transfers between devices with their start and end apart: 27 -> 27, of which waited for: 11 -> 12; matrix products, arithmetic and copies ran while one was open for 7% -> 7% of each run, Pallas kernels for 31% -> 25%
where the time goes in v14:
time: 209 us; the launch traced here: 208 us
  Pallas kernels  73.2 us (35%)
  waiting for transfers between devices  55.7 us (27%)
  starting transfers between devices  43.7 us (21%)
  between operations  13.7 us (7%)
  local copies, waits for them, and re-layouts  11.8 us (6%)
  other arithmetic  9.64 us (5%)
    ppermute x21, waiting for transfers between devices, send(): return lax.ppermute(value, 'seq', perm)  35.1 us
    ppermute x21, starting transfers between devices, send(): return lax.ppermute(value, 'seq', perm)  28.9 us
    pallas_call x2, Pallas kernels, sum_part(): pl.pallas_call(kernel, grid_spec=pltpu.PrefetchScalarGridSpec(num_scalar_...  22.1 us
    pallas_call x2, Pallas kernels, mix_part(): pl.pallas_call(mix_kernel if total is None else mix_more_kernel, grid=(4,...  15.5 us
    pallas_call x1, Pallas kernels, long_conv(): pl.pallas_call(conv_kernel, in_specs=[vmem, hbm, hbm, hbm, vmem, vmem, vm...  12.9 us
    all_to_all x1, waiting for transfers between devices, per_device(): mine_ch = lax.all_to_all(packed, 'seq', 0, 0, axis_index_groups=SAME_CORE)  12.1 us
    pallas_call x1, Pallas kernels, gate_part(): pl.pallas_call(gate_kernel, grid=(4,), in_specs=[pl.BlockSpec((tile, widt...  9.99 us
    pallas_call x1, Pallas kernels, last_part(): pl.pallas_call(last_kernel, grid=(4,), in_specs=[pl.BlockSpec((tile, chan...  7.55 us
  transfers between devices with their start and end apart: 27, of which 12 were waited for; matrix products, arithmetic and copies ran while one was open for 7% of the time, Pallas kernels for 25%

profile of v14, /device:TPU:1, one launch (start us, length us, event | category | flops | bytes accessed | tf_op | source)
XLA Modules:
  0.0 207.7 jit_solution(11090867203749641731)
XLA Ops:
  6.5 0.9 copy.11
  7.6 1.5 collective-permute-start.4
  9.1 1.0 dynamic-slice_bitcast_fusion
  10.3 1.4 collective-permute-done
  11.7 0.7 maximum_maximum_fusion
  12.4 0.2 collective-permute-start.3
  12.7 4.0 %collective-permute-start.2 = (bf16[128,512]{1,0:T(8,128)(2,1)S(1)}, bf16[128,512]{1,0:T(8,128)(2,1)S(1)}, u32[]{:S(2)}, u32[]{:S(2)}) collective-permute-start(bf16[128,512]{1,0:T(8,128)(2,1)S(1)} %bitcast.65), channel_id=1, source_target_pairs={{0,66},{2,64},{4,70},{6,68},{8,74},{10,72},{12,78},{14,76},{16,82}... | collective-permute-start | bytes 393224 | tf_op jit(solution)/shard_map/ppermute | solution.py:35
  16.8 3.4 %collective-permute-done.2 = bf16[128,512]{1,0:T(8,128)(2,1)S(1)} collective-permute-done((bf16[128,512]{1,0:T(8,128)(2,1)S(1)}, bf16[128,512]{1,0:T(8,128)(2,1)S(1)}, u32[]{:S(2)}, u32[]{:S(2)}) %collective-permute-start.2) | collective-permute-done | bytes 131104 | tf_op jit(solution)/shard_map/ppermute | solution.py:35
  20.2 3.0 %collective-permute-done.1 = bf16[128,512]{1,0:T(8,128)(2,1)S(1)} collective-permute-done((bf16[128,512]{1,0:T(8,128)(2,1)S(1)}, bf16[128,512]{1,0:T(8,128)(2,1)S(1)}, u32[]{:S(2)}, u32[]{:S(2)}) %collective-permute-start.1) | collective-permute-done | bytes 131104 | tf_op jit(solution)/shard_map/ppermute | solution.py:35
  23.3 1.3 collective-permute-start.7
  24.6 2.5 %collective-permute-start.6 = (bf16[256,512]{1,0:T(8,128)(2,1)S(1)}, bf16[256,512]{1,0:T(8,128)(2,1)S(1)}, u32[]{:S(2)}, u32[]{:S(2)}) collective-permute-start(bf16[256,512]{1,0:T(8,128)(2,1)S(1)} %get-tuple-element.43), channel_id=1, source_target_pairs={{0,8},{2,10},{4,12},{6,14},{8,0},{10,2},{12,4},{14,6},{16,24},{18,... | collective-permute-start | bytes 786440 | tf_op jit(solution)/shard_map/ppermute | solution.py:35
  27.0 1.2 collective-permute-start.5
  28.2 1.3 collective-permute-start.10
  29.5 2.6 %collective-permute-start.9 = (bf16[256,512]{1,0:T(8,128)(2,1)S(1)}, bf16[256,512]{1,0:T(8,128)(2,1)S(1)}, u32[]{:S(2)}, u32[]{:S(2)}) collective-permute-start(bf16[256,512]{1,0:T(8,128)(2,1)S(1)} %get-tuple-element.44), channel_id=1, source_target_pairs={{0,32},{2,34},{4,36},{6,38},{8,40},{10,42},{12,44},{14,46},{16,48}... | collective-permute-start | bytes 786440 | tf_op jit(solution)/shard_map/ppermute | solution.py:35
  32.1 2.7 %collective-permute-start.8 = (bf16[256,512]{1,0:T(8,128)(2,1)S(1)}, bf16[256,512]{1,0:T(8,128)(2,1)S(1)}, u32[]{:S(2)}, u32[]{:S(2)}) collective-permute-start(bf16[256,512]{1,0:T(8,128)(2,1)S(1)} %get-tuple-element.44), channel_id=1, source_target_pairs={{0,48},{2,50},{4,52},{6,54},{8,56},{10,58},{12,60},{14,62},{16,0},... | collective-permute-start | bytes 786440 | tf_op jit(solution)/shard_map/ppermute | solution.py:35
  34.9 4.7 %constant_dynamic-slice_fusion.3 = bf16[512,4096]{1,0:T(8,128)(2,1)} fusion(bf16[1024,4096]{1,0:T(8,128)(2,1)} %w_here.1, s32[]{:T(128)S(6)} %select_n.230), kind=kLoop, calls=%fused_computation.104 | loop fusion | bytes 8388612 | tf_op jit(solution)/shard_map/dynamic_slice | solution.py:538
  39.5 0.3 collective-permute-done.6
  39.8 1.1 pad_maximum_fusion.key_line
  40.9 3.1 %collective-permute-done.9 = bf16[256,512]{1,0:T(8,128)(2,1)S(1)} collective-permute-done((bf16[256,512]{1,0:T(8,128)(2,1)S(1)}, bf16[256,512]{1,0:T(8,128)(2,1)S(1)}, u32[]{:S(2)}, u32[]{:S(2)}) %collective-permute-start.9) | collective-permute-done | bytes 262176 | tf_op jit(solution)/shard_map/ppermute | solution.py:35
  44.0 1.1 pad_maximum_fusion.1.value_line
  45.0 3.3 %collective-permute-start.19 = (bf16[512,4096]{1,0:T(8,128)(2,1)}, bf16[512,4096]{1,0:T(8,128)(2,1)}, u32[]{:S(2)}, u32[]{:S(2)}) collective-permute-start(bf16[512,4096]{1,0:T(8,128)(2,1)} %constant_dynamic-slice_fusion.3), channel_id=1, source_target_pairs={{0,1},{1,0},{2,67},{3,66},{4,5},{5,4},{6,71},{7,70},{8,9},{9,8},{1... | collective-permute-start | bytes 12582920 | tf_op jit(solution)/shard_map/ppermute | solution.py:566
  48.3 0.2 fusion.38
  48.8 2.3 %collective-permute-start.11 = (bf16[1024,512]{1,0:T(8,128)(2,1)}, bf16[1024,512]{1,0:T(8,128)(2,1)S(1)}, u32[]{:S(2)}, u32[]{:S(2)}) collective-permute-start(bf16[1024,512]{1,0:T(8,128)(2,1)} %pad_maximum_fusion.key_line), channel_id=1, source_target_pairs={{0,48},{2,50},{4,52},{6,54},{8,56},{10,58},{12,60},{14,62},{16,0},... | collective-permute-start | bytes 3145736 | tf_op jit(solution)/shard_map/ppermute | solution.py:35
  51.1 0.4 collective-permute-start.12
  51.5 1.4 collective-permute-start.14
  53.0 0.6 pad_add_fusion.order_ref
  53.6 0.7 fusion.9.ai_ref
  54.2 0.3 fusion.35
  54.6 0.7 pad_maximum_fusion.6
  55.2 0.6 fusion.15
  55.8 0.7 pad_maximum_fusion.5.tw_hbm
  56.5 10.4 %first_part.1 = (f32[1024,512]{1,0:T(8,128)}, f32[1024,512]{1,0:T(8,128)}, bf16[1024,1024]{1,0:T(8,128)(2,1)}, bf16[1024,1024]{1,0:T(8,128)(2,1)}) custom-call(s32[2,32]{1,0:T(2,128)} %pad_add_fusion.order_ref, bf16[512,4096]{1,0:T(8,128)(2,1)} %bitcast.57, bf16[512,4096]{1,0:T(8,128)(2,1)} %collective-permute-done.3.other_ref, ...), custom_call_target="tpu_custom_call" | custom-call | flops 2147483648 | bytes 18874368 | tf_op jit(solution)/shard_map/first_part/pallas_call | solution.py:117
  66.9 18.4 %collective-permute-done.11.k1.refs_0_ = bf16[1024,512]{1,0:T(8,128)(2,1)S(1)} collective-permute-done((bf16[1024,512]{1,0:T(8,128)(2,1)}, bf16[1024,512]{1,0:T(8,128)(2,1)S(1)}, u32[]{:S(2)}, u32[]{:S(2)}) %collective-permute-start.11) | collective-permute-done | bytes 1048608 | tf_op jit(solution)/shard_map/ppermute | solution.py:35
  85.4 1.7 collective-permute-done.12.k3.refs_1_
  87.1 1.0 copy-done.2
  88.1 0.3 copy-done.3
  88.4 2.6 %cut_halves.1 = (bf16[512,512]{1,0:T(8,128)(2,1)}, bf16[512,512]{1,0:T(8,128)(2,1)}, bf16[512,512]{1,0:T(8,128)(2,1)}, bf16[512,512]{1,0:T(8,128)(2,1)}) custom-call(bf16[1024,512]{1,0:T(8,128)(2,1)} %copy-done.1, bf16[1024,512]{1,0:T(8,128)(2,1)} %copy-done.2, bf16[1024,512]{1,0:T(8,128)(2,1)} %copy-done.3, bf16[1024,512]{1,0:T(8,128)(2,1)} %collective-permute-done.14.v3.refs_3_), custom_call_target="tpu_custom_call" | custom-call | bytes 4194304 | tf_op jit(solution)/shard_map/cut_halves/pallas_call | solution.py:149
  91.0 0.7 collective-permute-start.15
  91.7 0.8 collective-permute-start.16
  92.5 1.5 collective-permute-start.18
  94.0 11.7 %second_part.1 = (f32[1024,512]{1,0:T(8,128)}, f32[1024,512]{1,0:T(8,128)}) custom-call(s32[2,32]{1,0:T(2,128)} %pad_add_fusion.order_ref, bf16[512,4096]{1,0:T(8,128)(2,1)} %bitcast.58, bf16[512,4096]{1,0:T(8,128)(2,1)} %collective-permute-done.3.other_ref, f32[1024,512]{1,0:T(8,128)} %get-tuple-element.51.key_in, f32[1024,512]{1,0:T(8,128)} %get-tuple-element.52.value_in, ...), custom_call_target="tpu_custom_call" | custom-call | flops 4294967296 | bytes 18874368 | tf_op jit(solution)/shard_map/second_part/pallas_call | solution.py:117
  105.7 2.6 %collective-permute-done.16.kb = bf16[512,512]{1,0:T(8,128)(2,1)S(1)} collective-permute-done((bf16[512,512]{1,0:T(8,128)(2,1)}, bf16[512,512]{1,0:T(8,128)(2,1)S(1)}, u32[]{:S(2)}, u32[]{:S(2)}) %collective-permute-start.16) | collective-permute-done | bytes 524320 | tf_op jit(solution)/shard_map/ppermute | solution.py:35
  108.4 0.8 copy-done.6
  109.1 0.2 copy-done.7
  109.5 7.5 %last_part.1 = bf16[512,1024]{1,0:T(8,128)(2,1)} custom-call(f32[1024,512]{1,0:T(8,128)} %get-tuple-element.57.key_ref, f32[1024,512]{1,0:T(8,128)} %get-tuple-element.58.value_ref, bf16[1024,1024]{1,0:T(8,128)(2,1)} %get-tuple-element.59.key_tok_ref, bf16[1024,1024]{1,0:T(8,128)(2,1)} %get-tuple-element.60.value_tok_ref, bf16[512,512]{1,0:T(8,128)(2,1)} %copy-done.5, ...), custom_call_target="tpu_custom_call" | custom-call | flops 2147483648 | bytes 13631488 | tf_op jit(solution)/shard_map/last_part/pallas_call | solution.py:178
  117.0 4.7 %all-to-all-start = ((bf16[32,16,1024]{2,1,0:T(8,128)(2,1)}), bf16[32,16,1024]{2,1,0:T(8,128)(2,1)S(1)}, u32[]{:S(2)}, u32[]{:S(2)}) async-start(bf16[32,16,1024]{2,1,0:T(8,128)(2,1)} %bitcast.60), calls=%async_computation | async-start | bytes 2097152 | tf_op jit(solution)/shard_map/all_to_all | solution.py:570
  121.7 0.8 copy.12.a_ref
  122.5 2.5 %filter_part.1 = (f32[64,1024]{1,0:T(8,128)}, bf16[256,256]{1,0:T(8,128)(2,1)}) custom-call(s32[1]{0:T(128)} %bitcast.19.z_ref, bf16[32,160,512]{2,1,0:T(8,128)(2,1)} %bitcast.61, f32[2,64,64]{2,1,0:T(8,128)} %get-tuple-element.66.cs_ref, f32[2,64,64]{2,1,0:T(8,128)} %get-tuple-element.67.twist_ref), custom_call_target="tpu_custom_call" | custom-call | flops 1000000000 | bytes 1048576 | tf_op jit(solution)/shard_map/filter_part/pallas_call | solution.py:333
  125.0 12.1 %all-to-all-done.x_ref = bf16[32,16,1024]{2,1,0:T(8,128)(2,1)S(1)} async-done(((bf16[32,16,1024]{2,1,0:T(8,128)(2,1)}), bf16[32,16,1024]{2,1,0:T(8,128)(2,1)S(1)}, u32[]{:S(2)}, u32[]{:S(2)}) %all-to-all-start) | async-done | bytes 1048608 | tf_op jit(solution)/shard_map/all_to_all | solution.py:570
  137.1 1.0 copy-done.4
  138.1 12.9 %long_conv.1 = bf16[32,16,1024]{2,1,0:T(8,128)(2,1)} custom-call(bf16[32,16,1024]{2,1,0:T(8,128)(2,1)} %copy-done.4, bf16[512,1024]{1,0:T(8,128)(2,1)} %constant.193.clone.fwd_hbm, bf16[1024,512]{1,0:T(8,128)(2,1)} %constant.194.clone.inv_hbm, f32[64,1024]{1,0:T(8,128)} %pad_maximum_fusion.5.tw_hbm, bf16[256,256]{1,0:T(8,128)(2,1)} %copy.12.a_ref, ...), custom_call_target="tpu_custom_call" | custom-call | flops 8000000000 | bytes 8388608 | tf_op jit(solution)/shard_map/long_conv/pallas_call | solution.py:435
  151.0 5.1 %all-to-all-start.1 = ((bf16[32,16,1024]{2,1,0:T(8,128)(2,1)}), bf16[32,16,1024]{2,1,0:T(8,128)(2,1)S(1)}, u32[]{:S(2)}, u32[]{:S(2)}) async-start(bf16[32,16,1024]{2,1,0:T(8,128)(2,1)} %long_conv.1), calls=%async_computation.1 | async-start | bytes 2097152 | tf_op jit(solution)/shard_map/all_to_all | solution.py:579
  156.2 10.0 %gate_part.1 = bf16[512,1024]{1,0:T(8,128)(2,1)} custom-call(bf16[512,4096]{1,0:T(8,128)(2,1)} %bitcast.59, bf16[512,4096]{1,0:T(8,128)(2,1)} %collective-permute-done.3.other_ref, bf16[32,160,512]{2,1,0:T(8,128)(2,1)} %bitcast.62), custom_call_target="tpu_custom_call" | custom-call | flops 4294967296 | bytes 13631488 | tf_op jit(solution)/shard_map/gate_part/pallas_call | solution.py:209
  166.1 5.0 %all-to-all-done.1 = bf16[32,16,1024]{2,1,0:T(8,128)(2,1)S(1)} async-done(((bf16[32,16,1024]{2,1,0:T(8,128)(2,1)}), bf16[32,16,1024]{2,1,0:T(8,128)(2,1)S(1)}, u32[]{:S(2)}, u32[]{:S(2)}) %all-to-all-start.1) | async-done | bytes 1048608 | tf_op jit(solution)/shard_map/all_to_all | solution.py:579
  171.2 1.7 fusion.1
  173.0 3.9 %collective-permute-start.20 = (bf16[512,256]{1,0:T(8,128)(2,1)S(1)}, bf16[512,256]{1,0:T(8,128)(2,1)S(1)}, u32[]{:S(2)}, u32[]{:S(2)}) collective-permute-start(bf16[512,256]{1,0:T(8,128)(2,1)S(1)} %get-tuple-element.85), channel_id=1, source_target_pairs={{0,2},{2,0},{4,6},{6,4},{8,10},{10,8},{12,14},{14,12},{16,18},{18,... | collective-permute-start | bytes 786440 | tf_op jit(solution)/shard_map/ppermute | solution.py:35
  176.9 1.2 collective-permute-done.20
  178.1 0.4 collective-permute-start.23
  178.5 1.8 collective-permute-start.22
  180.4 0.8 pad_maximum_fusion.2.here
  181.2 7.5 %mix_part.1.total_ref = f32[256,4096]{1,0:T(8,128)} custom-call(bf16[1024,256]{1,0:T(8,128)(2,1)} %pad_maximum_fusion.2.here, bf16[1024,4096]{1,0:T(8,128)(2,1)} %w_here.1), custom_call_target="tpu_custom_call" | custom-call | flops 2147483648 | bytes 12582912 | tf_op jit(solution)/shard_map/mix_part/pallas_call | solution.py:266
  188.7 3.4 %collective-permute-done.22.far_h = bf16[512,256]{1,0:T(8,128)(2,1)S(1)} collective-permute-done((bf16[512,256]{1,0:T(8,128)(2,1)S(1)}, bf16[512,256]{1,0:T(8,128)(2,1)S(1)}, u32[]{:S(2)}, u32[]{:S(2)}) %collective-permute-start.22) | collective-permute-done | bytes 262176 | tf_op jit(solution)/shard_map/ppermute | solution.py:597
  192.1 0.7 copy-done.10
  192.8 8.0 %mix_more.1 = bf16[256,4096]{1,0:T(8,128)(2,1)} custom-call(f32[256,4096]{1,0:T(8,128)} %mix_part.1.total_ref, bf16[512,256]{1,0:T(8,128)(2,1)} %copy-done.9, bf16[512,256]{1,0:T(8,128)(2,1)} %copy-done.10, bf16[512,4096]{1,0:T(8,128)(2,1)} %collective-permute-done.19.w_near, bf16[512,4096]{1,0:T(8,128)(2,1)} %collective-permute-done.23.w_far), custom_call_target="tpu_custom_call" | custom-call | flops 2147483648 | bytes 12582912 | tf_op jit(solution)/shard_map/mix_more/pallas_call | solution.py:266
  (65 shorter events, 1.3 us)
Async XLA Ops:
  6.5 115.9 %all-gather.3.cloned.1.call-start = ((), (), s32[]{:S(2)}) async-start(), calls=%async_computation.2 | async-start | bytes 5406720 | tf_op jit(solution)/shard_map/all_gather | solution.py:535
  7.6 2.7 %collective-permute-start.4 = (bf16[32,256]{1,0:T(8,128)(2,1)S(1)}, bf16[32,256]{1,0:T(8,128)(2,1)S(1)}, u32[]{:S(2)}, u32[]{:S(2)}) collective-permute-start(bf16[32,256]{1,0:T(8,128)(2,1)S(1)} %pad_maximum_fusion.8), channel_id=1, source_target_pairs={{0,2},{2,0},{4,6},{6,4},{8,10},{10,8},{12,14},{14,12},{16,18},{18,... | collective-permute-start | bytes 49160 | tf_op jit(solution)/shard_map/ppermute | solution.py:35
  10.1 1.5 collective-permute-start
  12.4 10.9 %collective-permute-start.3 = (bf16[512,4096]{1,0:T(8,128)(2,1)}, bf16[512,4096]{1,0:T(8,128)(2,1)}, u32[]{:S(2)}, u32[]{:S(2)}) collective-permute-start(bf16[512,4096]{1,0:T(8,128)(2,1)} %bitcast.56), channel_id=1, source_target_pairs={{0,2},{2,0},{4,6},{6,4},{8,10},{10,8},{12,14},{14,12},{16,18},{18,... | collective-permute-start | bytes 12582920 | tf_op jit(solution)/shard_map/ppermute | solution.py:35
  12.7 7.5 %collective-permute-start.2 = (bf16[128,512]{1,0:T(8,128)(2,1)S(1)}, bf16[128,512]{1,0:T(8,128)(2,1)S(1)}, u32[]{:S(2)}, u32[]{:S(2)}) collective-permute-start(bf16[128,512]{1,0:T(8,128)(2,1)S(1)} %bitcast.65), channel_id=1, source_target_pairs={{0,66},{2,64},{4,70},{6,68},{8,74},{10,72},{12,78},{14,76},{16,82}... | collective-permute-start | bytes 393224 | tf_op jit(solution)/shard_map/ppermute | solution.py:35
  16.7 6.5 %collective-permute-start.1 = (bf16[128,512]{1,0:T(8,128)(2,1)S(1)}, bf16[128,512]{1,0:T(8,128)(2,1)S(1)}, u32[]{:S(2)}, u32[]{:S(2)}) collective-permute-start(bf16[128,512]{1,0:T(8,128)(2,1)S(1)} %bitcast.66), channel_id=1, source_target_pairs={{0,64},{2,66},{4,68},{6,70},{8,72},{10,74},{12,76},{14,78},{16,80}... | collective-permute-start | bytes 393224 | tf_op jit(solution)/shard_map/ppermute | solution.py:35
  23.3 8.8 %collective-permute-start.7 = (bf16[256,512]{1,0:T(8,128)(2,1)S(1)}, bf16[256,512]{1,0:T(8,128)(2,1)S(1)}, u32[]{:S(2)}, u32[]{:S(2)}) collective-permute-start(bf16[256,512]{1,0:T(8,128)(2,1)S(1)} %get-tuple-element.43), channel_id=1, source_target_pairs={{0,4},{2,6},{4,8},{6,10},{8,12},{10,14},{12,0},{14,2},{16,20},{18,... | collective-permute-start | bytes 786440 | tf_op jit(solution)/shard_map/ppermute | solution.py:35
  24.6 15.2 %collective-permute-start.6 = (bf16[256,512]{1,0:T(8,128)(2,1)S(1)}, bf16[256,512]{1,0:T(8,128)(2,1)S(1)}, u32[]{:S(2)}, u32[]{:S(2)}) collective-permute-start(bf16[256,512]{1,0:T(8,128)(2,1)S(1)} %get-tuple-element.43), channel_id=1, source_target_pairs={{0,8},{2,10},{4,12},{6,14},{8,0},{10,2},{12,4},{14,6},{16,24},{18,... | collective-permute-start | bytes 786440 | tf_op jit(solution)/shard_map/ppermute | solution.py:35
  27.0 12.8 %collective-permute-start.5 = (bf16[256,512]{1,0:T(8,128)(2,1)S(1)}, bf16[256,512]{1,0:T(8,128)(2,1)S(1)}, u32[]{:S(2)}, u32[]{:S(2)}) collective-permute-start(bf16[256,512]{1,0:T(8,128)(2,1)S(1)} %get-tuple-element.43), channel_id=1, source_target_pairs={{0,12},{2,14},{4,0},{6,2},{8,4},{10,6},{12,8},{14,10},{16,28},{18,... | collective-permute-start | bytes 786440 | tf_op jit(solution)/shard_map/ppermute | solution.py:35
  28.2 12.7 %collective-permute-start.10 = (bf16[256,512]{1,0:T(8,128)(2,1)S(1)}, bf16[256,512]{1,0:T(8,128)(2,1)S(1)}, u32[]{:S(2)}, u32[]{:S(2)}) collective-permute-start(bf16[256,512]{1,0:T(8,128)(2,1)S(1)} %get-tuple-element.44), channel_id=1, source_target_pairs={{0,16},{2,18},{4,20},{6,22},{8,24},{10,26},{12,28},{14,30},{16,32}... | collective-permute-start | bytes 786440 | tf_op jit(solution)/shard_map/ppermute | solution.py:35
  29.5 14.5 %collective-permute-start.9 = (bf16[256,512]{1,0:T(8,128)(2,1)S(1)}, bf16[256,512]{1,0:T(8,128)(2,1)S(1)}, u32[]{:S(2)}, u32[]{:S(2)}) collective-permute-start(bf16[256,512]{1,0:T(8,128)(2,1)S(1)} %get-tuple-element.44), channel_id=1, source_target_pairs={{0,32},{2,34},{4,36},{6,38},{8,40},{10,42},{12,44},{14,46},{16,48}... | collective-permute-start | bytes 786440 | tf_op jit(solution)/shard_map/ppermute | solution.py:35
  32.1 11.8 %collective-permute-start.8 = (bf16[256,512]{1,0:T(8,128)(2,1)S(1)}, bf16[256,512]{1,0:T(8,128)(2,1)S(1)}, u32[]{:S(2)}, u32[]{:S(2)}) collective-permute-start(bf16[256,512]{1,0:T(8,128)(2,1)S(1)} %get-tuple-element.44), channel_id=1, source_target_pairs={{0,48},{2,50},{4,52},{6,54},{8,56},{10,58},{12,60},{14,62},{16,0},... | collective-permute-start | bytes 786440 | tf_op jit(solution)/shard_map/ppermute | solution.py:35
  39.5 9.2 %copy-start.12 = (s32[32]{0:T(128)S(1)}, s32[32]{0:T(128)}, u32[]{:S(2)}) copy-start(s32[32]{0:T(128)} %constant.192.clone) | copy-start | bytes 388
  39.5 9.2 %copy-start.13 = (s32[32]{0:T(128)S(1)}, s32[32]{0:T(128)}, u32[]{:S(2)}) copy-start(s32[32]{0:T(128)} %constant.191.clone) | copy-start | bytes 388
  39.5 9.2 %copy-start.14 = (s32[32]{0:T(128)S(1)}, s32[32]{0:T(128)}, u32[]{:S(2)}) copy-start(s32[32]{0:T(128)} %constant.190.clone) | copy-start | bytes 388
  45.0 92.1 %collective-permute-start.19 = (bf16[512,4096]{1,0:T(8,128)(2,1)}, bf16[512,4096]{1,0:T(8,128)(2,1)}, u32[]{:S(2)}, u32[]{:S(2)}) collective-permute-start(bf16[512,4096]{1,0:T(8,128)(2,1)} %constant_dynamic-slice_fusion.3), channel_id=1, source_target_pairs={{0,1},{1,0},{2,67},{3,66},{4,5},{5,4},{6,71},{7,70},{8,9},{9,8},{1... | collective-permute-start | bytes 12582920 | tf_op jit(solution)/shard_map/ppermute | solution.py:566
  48.8 36.6 %collective-permute-start.11 = (bf16[1024,512]{1,0:T(8,128)(2,1)}, bf16[1024,512]{1,0:T(8,128)(2,1)S(1)}, u32[]{:S(2)}, u32[]{:S(2)}) collective-permute-start(bf16[1024,512]{1,0:T(8,128)(2,1)} %pad_maximum_fusion.key_line), channel_id=1, source_target_pairs={{0,48},{2,50},{4,52},{6,54},{8,56},{10,58},{12,60},{14,62},{16,0},... | collective-permute-start | bytes 3145736 | tf_op jit(solution)/shard_map/ppermute | solution.py:35
  51.1 36.0 %collective-permute-start.12 = (bf16[1024,512]{1,0:T(8,128)(2,1)}, bf16[1024,512]{1,0:T(8,128)(2,1)S(1)}, u32[]{:S(2)}, u32[]{:S(2)}) collective-permute-start(bf16[1024,512]{1,0:T(8,128)(2,1)} %pad_maximum_fusion.key_line), channel_id=1, source_target_pairs={{0,16},{2,18},{4,20},{6,22},{8,24},{10,26},{12,28},{14,30},{16,32}... | collective-permute-start | bytes 3145736 | tf_op jit(solution)/shard_map/ppermute | solution.py:35
  51.5 35.6 %collective-permute-start.13 = (bf16[1024,512]{1,0:T(8,128)(2,1)}, bf16[1024,512]{1,0:T(8,128)(2,1)S(1)}, u32[]{:S(2)}, u32[]{:S(2)}) collective-permute-start(bf16[1024,512]{1,0:T(8,128)(2,1)} %pad_maximum_fusion.1.value_line), channel_id=1, source_target_pairs={{0,12},{2,14},{4,0},{6,2},{8,4},{10,6},{12,8},{14,10},{16,28},{18,... | collective-permute-start | bytes 3145736 | tf_op jit(solution)/shard_map/ppermute | solution.py:35
  51.5 35.6 %collective-permute-start.14 = (bf16[1024,512]{1,0:T(8,128)(2,1)}, bf16[1024,512]{1,0:T(8,128)(2,1)}, u32[]{:S(2)}, u32[]{:S(2)}) collective-permute-start(bf16[1024,512]{1,0:T(8,128)(2,1)} %pad_maximum_fusion.1.value_line), channel_id=1, source_target_pairs={{0,4},{2,6},{4,8},{6,10},{8,12},{10,14},{12,0},{14,2},{16,20},{18,... | collective-permute-start | bytes 3145736 | tf_op jit(solution)/shard_map/ppermute | solution.py:35
  85.4 1.8 copy-start.1
  87.1 1.0 copy-start.2
  87.1 1.3 copy-start.3
  91.0 14.7 %collective-permute-start.15 = (bf16[512,512]{1,0:T(8,128)(2,1)}, bf16[512,512]{1,0:T(8,128)(2,1)S(1)}, u32[]{:S(2)}, u32[]{:S(2)}) collective-permute-start(bf16[512,512]{1,0:T(8,128)(2,1)} %get-tuple-element.61), channel_id=1, source_target_pairs={{0,48},{2,50},{4,52},{6,54},{8,56},{10,58},{12,60},{14,62},{16,0},... | collective-permute-start | bytes 1572872 | tf_op jit(solution)/shard_map/ppermute | solution.py:35
  91.7 16.6 %collective-permute-start.16 = (bf16[512,512]{1,0:T(8,128)(2,1)}, bf16[512,512]{1,0:T(8,128)(2,1)S(1)}, u32[]{:S(2)}, u32[]{:S(2)}) collective-permute-start(bf16[512,512]{1,0:T(8,128)(2,1)} %get-tuple-element.62), channel_id=1, source_target_pairs={{0,16},{2,18},{4,20},{6,22},{8,24},{10,26},{12,28},{14,30},{16,32}... | collective-permute-start | bytes 1572872 | tf_op jit(solution)/shard_map/ppermute | solution.py:35
  92.5 15.8 %collective-permute-start.17 = (bf16[512,512]{1,0:T(8,128)(2,1)}, bf16[512,512]{1,0:T(8,128)(2,1)S(1)}, u32[]{:S(2)}, u32[]{:S(2)}) collective-permute-start(bf16[512,512]{1,0:T(8,128)(2,1)} %get-tuple-element.63), channel_id=1, source_target_pairs={{0,12},{2,14},{4,0},{6,2},{8,4},{10,6},{12,8},{14,10},{16,28},{18,... | collective-permute-start | bytes 1572872 | tf_op jit(solution)/shard_map/ppermute | solution.py:35
  92.5 15.8 %collective-permute-start.18 = (bf16[512,512]{1,0:T(8,128)(2,1)}, bf16[512,512]{1,0:T(8,128)(2,1)S(1)}, u32[]{:S(2)}, u32[]{:S(2)}) collective-permute-start(bf16[512,512]{1,0:T(8,128)(2,1)} %get-tuple-element.64), channel_id=1, source_target_pairs={{0,4},{2,6},{4,8},{6,10},{8,12},{10,14},{12,0},{14,2},{16,20},{18,... | collective-permute-start | bytes 1572872 | tf_op jit(solution)/shard_map/ppermute | solution.py:35
  105.7 2.6 %copy-start.5 = (bf16[512,512]{1,0:T(8,128)(2,1)}, bf16[512,512]{1,0:T(8,128)(2,1)S(1)}, u32[]{:S(2)}) copy-start(bf16[512,512]{1,0:T(8,128)(2,1)S(1)} %collective-permute-done.15.ka) | copy-start | bytes 1572868
  108.3 0.8 copy-start.6
  108.3 1.0 copy-start.7
  108.3 1.1 copy-start.8
  117.0 20.1 %all-to-all-start = ((bf16[32,16,1024]{2,1,0:T(8,128)(2,1)}), bf16[32,16,1024]{2,1,0:T(8,128)(2,1)S(1)}, u32[]{:S(2)}, u32[]{:S(2)}) async-start(bf16[32,16,1024]{2,1,0:T(8,128)(2,1)} %bitcast.60), calls=%async_computation | async-start | bytes 2097152 | tf_op jit(solution)/shard_map/all_to_all | solution.py:570
  137.1 1.0 copy-start.4
  151.0 5.1 %copy-start.11 = (f32[1024]{0:T(1024)S(1)}, f32[1024]{0:T(1024)}, u32[]{:S(2)}) copy-start(f32[1024]{0:T(1024)} %param.13) | copy-start | bytes 12292
  151.0 20.2 %all-to-all-start.1 = ((bf16[32,16,1024]{2,1,0:T(8,128)(2,1)}), bf16[32,16,1024]{2,1,0:T(8,128)(2,1)S(1)}, u32[]{:S(2)}, u32[]{:S(2)}) async-start(bf16[32,16,1024]{2,1,0:T(8,128)(2,1)} %long_conv.1), calls=%async_computation.1 | async-start | bytes 2097152 | tf_op jit(solution)/shard_map/all_to_all | solution.py:579
  156.2 15.0 %copy-start = (bf16[512,1024]{1,0:T(8,128)(2,1)S(1)}, bf16[512,1024]{1,0:T(8,128)(2,1)}, u32[]{:S(2)}) copy-start(bf16[512,1024]{1,0:T(8,128)(2,1)} %last_part.1) | copy-start | bytes 3145732
  173.0 5.1 %collective-permute-start.20 = (bf16[512,256]{1,0:T(8,128)(2,1)S(1)}, bf16[512,256]{1,0:T(8,128)(2,1)S(1)}, u32[]{:S(2)}, u32[]{:S(2)}) collective-permute-start(bf16[512,256]{1,0:T(8,128)(2,1)S(1)} %get-tuple-element.85), channel_id=1, source_target_pairs={{0,2},{2,0},{4,6},{6,4},{8,10},{10,8},{12,14},{14,12},{16,18},{18,... | collective-permute-start | bytes 786440 | tf_op jit(solution)/shard_map/ppermute | solution.py:35
  178.1 14.0 %collective-permute-start.23 = (bf16[512,4096]{1,0:T(8,128)(2,1)}, bf16[512,4096]{1,0:T(8,128)(2,1)}, u32[]{:S(2)}, u32[]{:S(2)}) collective-permute-start(bf16[512,4096]{1,0:T(8,128)(2,1)} %collective-permute-done.19.w_near), channel_id=1, source_target_pairs={{0,2},{2,0},{4,6},{6,4},{8,10},{10,8},{12,14},{14,12},{16,18},{18,... | collective-permute-start | bytes 12582920 | tf_op jit(solution)/shard_map/ppermute | solution.py:35
  178.5 10.2 %collective-permute-start.21 = (bf16[512,256]{1,0:T(8,128)(2,1)S(1)}, bf16[512,256]{1,0:T(8,128)(2,1)S(1)}, u32[]{:S(2)}, u32[]{:S(2)}) collective-permute-start(bf16[512,256]{1,0:T(8,128)(2,1)S(1)} %get-tuple-element.84), channel_id=1, source_target_pairs={{0,1},{1,0},{2,3},{3,2},{4,5},{5,4},{6,7},{7,6},{8,9},{9,8},{10,11... | collective-permute-start | bytes 786440 | tf_op jit(solution)/shard_map/ppermute | solution.py:592
  178.5 13.6 %collective-permute-start.22 = (bf16[512,256]{1,0:T(8,128)(2,1)S(1)}, bf16[512,256]{1,0:T(8,128)(2,1)S(1)}, u32[]{:S(2)}, u32[]{:S(2)}) collective-permute-start(bf16[512,256]{1,0:T(8,128)(2,1)S(1)} %get-tuple-element.83), channel_id=1, source_target_pairs={{0,3},{1,2},{2,1},{3,0},{4,7},{5,6},{6,5},{7,4},{8,11},{9,10},{10,... | collective-permute-start | bytes 786440 | tf_op jit(solution)/shard_map/ppermute | solution.py:597
  188.7 3.4 %copy-start.9 = (bf16[512,256]{1,0:T(8,128)(2,1)}, bf16[512,256]{1,0:T(8,128)(2,1)S(1)}, u32[]{:S(2)}) copy-start(bf16[512,256]{1,0:T(8,128)(2,1)S(1)} %collective-permute-done.21.near_h) | copy-start | bytes 786436
  192.1 0.7 copy-start.10
Sparse Core Ops, SparseCore 0:
  12.5 106.3 all-gather.2

commit v15 on v14

--- a/solution.py
+++ b/solution.py
@@ -174,10 +174,10 @@
 def last_part(totals, tokens, weights):
     total, chan = totals[0].shape
     quarter = tokens[0].shape[1]
-    tile = total // 4
+    tile = total // 8
     return pl.pallas_call(
         last_kernel,
-        grid=(4,),
+        grid=(8,),
         in_specs=[pl.BlockSpec((tile, chan), lambda i: (i, 0))] * 2
         + [pl.BlockSpec((tile, quarter), lambda i: (i, 0))] * 2
         + [pl.BlockSpec((quarter // 2, chan), lambda i: (0, 0))] * 4,
@@ -253,7 +253,7 @@
 def mix_part(total, parts, weights):
     rows = parts[0].shape[1]
     width = weights[0].shape[1]
-    tile = width // 4
+    tile = width // 8
     depth = sum(p.shape[0] for p in parts)
     totals = [] if total is None else [total]
 
@@ -265,7 +265,7 @@
 
     return pl.pallas_call(
         mix_kernel if total is None else mix_more_kernel,
-        grid=(4,),
+        grid=(8,),
         in_specs=[tiled(t) for t in totals] + [whole(p) for p in parts] + [tiled(w) for w in weights],
         out_specs=pl.BlockSpec((rows, tile), lambda i: (0, i)),
         out_shape=jax.ShapeDtypeStruct((rows, width), F32 if total is None else BF16),

time: 209 us -> 213 us (1.019)
  Pallas kernels: 73.2 us -> 78.7 us
    pallas_call x3, Pallas kernels: 23 us -> 28.6 us  [the longest x2 19 us: mix_part(): pl.pallas_call(mix_kernel if total is None else mix_more_kernel, grid=(8,...]
  transfers between devices with their start and end apart: 27 -> 27, of which waited for: 12 -> 12; matrix products, arithmetic and copies ran while one was open for 7% -> 6% of each run, Pallas kernels for 25% -> 27%
where the time goes in v15:
time: 213 us; the launch traced here: 211 us
  Pallas kernels  78.7 us (37%)
  waiting for transfers between devices  53.8 us (25%)
  starting transfers between devices  43.7 us (21%)
  between operations  13.7 us (6%)
  local copies, waits for them, and re-layouts  11.8 us (6%)
  other arithmetic  9.64 us (5%)
    ppermute x21, waiting for transfers between devices, send(): return lax.ppermute(value, 'seq', perm)  35.1 us
    ppermute x21, starting transfers between devices, send(): return lax.ppermute(value, 'seq', perm)  28.9 us
    pallas_call x2, Pallas kernels, sum_part(): pl.pallas_call(kernel, grid_spec=pltpu.PrefetchScalarGridSpec(num_scalar_...  22.1 us
    pallas_call x2, Pallas kernels, mix_part(): pl.pallas_call(mix_kernel if total is None else mix_more_kernel, grid=(8,...  19 us
    pallas_call x1, Pallas kernels, long_conv(): pl.pallas_call(conv_kernel, in_specs=[vmem, hbm, hbm, hbm, vmem, vmem, vm...  12.9 us
    all_to_all x1, waiting for transfers between devices, per_device(): mine_ch = lax.all_to_all(packed, 'seq', 0, 0, axis_index_groups=SAME_CORE)  12.1 us
    pallas_call x1, Pallas kernels, gate_part(): pl.pallas_call(gate_kernel, grid=(4,), in_specs=[pl.BlockSpec((tile, widt...  9.99 us
    pallas_call x1, Pallas kernels, last_part(): pl.pallas_call(last_kernel, grid=(8,), in_specs=[pl.BlockSpec((tile, chan...  9.56 us
  transfers between devices with their start and end apart: 27, of which 12 were waited for; matrix products, arithmetic and copies ran while one was open for 6% of the time, Pallas kernels for 27%

profile of v15, /device:TPU:1, one launch (start us, length us, event | category | flops | bytes accessed | tf_op | source)
XLA Modules:
  0.0 211.5 jit_solution(18057071231928492345)
XLA Ops:
  6.5 0.9 copy.11
  7.6 1.5 collective-permute-start.4
  9.1 1.0 dynamic-slice_bitcast_fusion
  10.3 1.4 collective-permute-done
  11.7 0.7 maximum_maximum_fusion
  12.4 0.2 collective-permute-start.3
  12.7 4.0 %collective-permute-start.2 = (bf16[128,512]{1,0:T(8,128)(2,1)S(1)}, bf16[128,512]{1,0:T(8,128)(2,1)S(1)}, u32[]{:S(2)}, u32[]{:S(2)}) collective-permute-start(bf16[128,512]{1,0:T(8,128)(2,1)S(1)} %bitcast.65), channel_id=1, source_target_pairs={{0,66},{2,64},{4,70},{6,68},{8,74},{10,72},{12,78},{14,76},{16,82}... | collective-permute-start | bytes 393224 | tf_op jit(solution)/shard_map/ppermute | solution.py:35
  16.8 3.4 %collective-permute-done.2 = bf16[128,512]{1,0:T(8,128)(2,1)S(1)} collective-permute-done((bf16[128,512]{1,0:T(8,128)(2,1)S(1)}, bf16[128,512]{1,0:T(8,128)(2,1)S(1)}, u32[]{:S(2)}, u32[]{:S(2)}) %collective-permute-start.2) | collective-permute-done | bytes 131104 | tf_op jit(solution)/shard_map/ppermute | solution.py:35
  20.2 3.0 %collective-permute-done.1 = bf16[128,512]{1,0:T(8,128)(2,1)S(1)} collective-permute-done((bf16[128,512]{1,0:T(8,128)(2,1)S(1)}, bf16[128,512]{1,0:T(8,128)(2,1)S(1)}, u32[]{:S(2)}, u32[]{:S(2)}) %collective-permute-start.1) | collective-permute-done | bytes 131104 | tf_op jit(solution)/shard_map/ppermute | solution.py:35
  23.3 1.3 collective-permute-start.7
  24.6 2.5 %collective-permute-start.6 = (bf16[256,512]{1,0:T(8,128)(2,1)S(1)}, bf16[256,512]{1,0:T(8,128)(2,1)S(1)}, u32[]{:S(2)}, u32[]{:S(2)}) collective-permute-start(bf16[256,512]{1,0:T(8,128)(2,1)S(1)} %get-tuple-element.43), channel_id=1, source_target_pairs={{0,8},{2,10},{4,12},{6,14},{8,0},{10,2},{12,4},{14,6},{16,24},{18,... | collective-permute-start | bytes 786440 | tf_op jit(solution)/shard_map/ppermute | solution.py:35
  27.0 1.2 collective-permute-start.5
  28.2 1.3 collective-permute-start.10
  29.5 2.6 %collective-permute-start.9 = (bf16[256,512]{1,0:T(8,128)(2,1)S(1)}, bf16[256,512]{1,0:T(8,128)(2,1)S(1)}, u32[]{:S(2)}, u32[]{:S(2)}) collective-permute-start(bf16[256,512]{1,0:T(8,128)(2,1)S(1)} %get-tuple-element.44), channel_id=1, source_target_pairs={{0,32},{2,34},{4,36},{6,38},{8,40},{10,42},{12,44},{14,46},{16,48}... | collective-permute-start | bytes 786440 | tf_op jit(solution)/shard_map/ppermute | solution.py:35
  32.1 2.7 %collective-permute-start.8 = (bf16[256,512]{1,0:T(8,128)(2,1)S(1)}, bf16[256,512]{1,0:T(8,128)(2,1)S(1)}, u32[]{:S(2)}, u32[]{:S(2)}) collective-permute-start(bf16[256,512]{1,0:T(8,128)(2,1)S(1)} %get-tuple-element.44), channel_id=1, source_target_pairs={{0,48},{2,50},{4,52},{6,54},{8,56},{10,58},{12,60},{14,62},{16,0},... | collective-permute-start | bytes 786440 | tf_op jit(solution)/shard_map/ppermute | solution.py:35
  34.9 4.7 %constant_dynamic-slice_fusion.3 = bf16[512,4096]{1,0:T(8,128)(2,1)} fusion(bf16[1024,4096]{1,0:T(8,128)(2,1)} %w_here.1, s32[]{:T(128)S(6)} %select_n.230), kind=kLoop, calls=%fused_computation.104 | loop fusion | bytes 8388612 | tf_op jit(solution)/shard_map/dynamic_slice | solution.py:538
  39.5 0.3 collective-permute-done.6
  39.8 1.1 pad_maximum_fusion.key_line
  40.9 3.1 %collective-permute-done.9 = bf16[256,512]{1,0:T(8,128)(2,1)S(1)} collective-permute-done((bf16[256,512]{1,0:T(8,128)(2,1)S(1)}, bf16[256,512]{1,0:T(8,128)(2,1)S(1)}, u32[]{:S(2)}, u32[]{:S(2)}) %collective-permute-start.9) | collective-permute-done | bytes 262176 | tf_op jit(solution)/shard_map/ppermute | solution.py:35
  44.0 1.1 pad_maximum_fusion.1.value_line
  45.0 3.3 %collective-permute-start.19 = (bf16[512,4096]{1,0:T(8,128)(2,1)}, bf16[512,4096]{1,0:T(8,128)(2,1)}, u32[]{:S(2)}, u32[]{:S(2)}) collective-permute-start(bf16[512,4096]{1,0:T(8,128)(2,1)} %constant_dynamic-slice_fusion.3), channel_id=1, source_target_pairs={{0,1},{1,0},{2,67},{3,66},{4,5},{5,4},{6,71},{7,70},{8,9},{9,8},{1... | collective-permute-start | bytes 12582920 | tf_op jit(solution)/shard_map/ppermute | solution.py:566
  48.3 0.2 fusion.38
  48.8 2.3 %collective-permute-start.11 = (bf16[1024,512]{1,0:T(8,128)(2,1)}, bf16[1024,512]{1,0:T(8,128)(2,1)S(1)}, u32[]{:S(2)}, u32[]{:S(2)}) collective-permute-start(bf16[1024,512]{1,0:T(8,128)(2,1)} %pad_maximum_fusion.key_line), channel_id=1, source_target_pairs={{0,48},{2,50},{4,52},{6,54},{8,56},{10,58},{12,60},{14,62},{16,0},... | collective-permute-start | bytes 3145736 | tf_op jit(solution)/shard_map/ppermute | solution.py:35
  51.1 0.4 collective-permute-start.12
  51.5 1.4 collective-permute-start.14
  53.0 0.6 pad_add_fusion.order_ref
  53.6 0.7 fusion.9.ai_ref
  54.2 0.3 fusion.35
  54.6 0.7 pad_maximum_fusion.6
  55.2 0.6 fusion.15
  55.8 0.7 pad_maximum_fusion.5.tw_hbm
  56.5 10.4 %first_part.1 = (f32[1024,512]{1,0:T(8,128)}, f32[1024,512]{1,0:T(8,128)}, bf16[1024,1024]{1,0:T(8,128)(2,1)}, bf16[1024,1024]{1,0:T(8,128)(2,1)}) custom-call(s32[2,32]{1,0:T(2,128)} %pad_add_fusion.order_ref, bf16[512,4096]{1,0:T(8,128)(2,1)} %bitcast.57, bf16[512,4096]{1,0:T(8,128)(2,1)} %collective-permute-done.3.other_ref, ...), custom_call_target="tpu_custom_call" | custom-call | flops 2147483648 | bytes 18874368 | tf_op jit(solution)/shard_map/first_part/pallas_call | solution.py:117
  66.9 18.4 %collective-permute-done.11.k1.refs_0_ = bf16[1024,512]{1,0:T(8,128)(2,1)S(1)} collective-permute-done((bf16[1024,512]{1,0:T(8,128)(2,1)}, bf16[1024,512]{1,0:T(8,128)(2,1)S(1)}, u32[]{:S(2)}, u32[]{:S(2)}) %collective-permute-start.11) | collective-permute-done | bytes 1048608 | tf_op jit(solution)/shard_map/ppermute | solution.py:35
  85.4 1.7 collective-permute-done.12.k3.refs_1_
  87.1 1.0 copy-done.2
  88.1 0.3 copy-done.3
  88.4 2.6 %cut_halves.1 = (bf16[512,512]{1,0:T(8,128)(2,1)}, bf16[512,512]{1,0:T(8,128)(2,1)}, bf16[512,512]{1,0:T(8,128)(2,1)}, bf16[512,512]{1,0:T(8,128)(2,1)}) custom-call(bf16[1024,512]{1,0:T(8,128)(2,1)} %copy-done.1, bf16[1024,512]{1,0:T(8,128)(2,1)} %copy-done.2, bf16[1024,512]{1,0:T(8,128)(2,1)} %copy-done.3, bf16[1024,512]{1,0:T(8,128)(2,1)} %collective-permute-done.14.v3.refs_3_), custom_call_target="tpu_custom_call" | custom-call | bytes 4194304 | tf_op jit(solution)/shard_map/cut_halves/pallas_call | solution.py:149
  91.0 0.7 collective-permute-start.15
  91.7 0.8 collective-permute-start.16
  92.5 1.5 collective-permute-start.18
  94.0 11.7 %second_part.1 = (f32[1024,512]{1,0:T(8,128)}, f32[1024,512]{1,0:T(8,128)}) custom-call(s32[2,32]{1,0:T(2,128)} %pad_add_fusion.order_ref, bf16[512,4096]{1,0:T(8,128)(2,1)} %bitcast.58, bf16[512,4096]{1,0:T(8,128)(2,1)} %collective-permute-done.3.other_ref, f32[1024,512]{1,0:T(8,128)} %get-tuple-element.51.key_in, f32[1024,512]{1,0:T(8,128)} %get-tuple-element.52.value_in, ...), custom_call_target="tpu_custom_call" | custom-call | flops 4294967296 | bytes 18874368 | tf_op jit(solution)/shard_map/second_part/pallas_call | solution.py:117
  105.7 2.6 %collective-permute-done.16.kb = bf16[512,512]{1,0:T(8,128)(2,1)S(1)} collective-permute-done((bf16[512,512]{1,0:T(8,128)(2,1)}, bf16[512,512]{1,0:T(8,128)(2,1)S(1)}, u32[]{:S(2)}, u32[]{:S(2)}) %collective-permute-start.16) | collective-permute-done | bytes 524320 | tf_op jit(solution)/shard_map/ppermute | solution.py:35
  108.4 0.8 copy-done.6
  109.1 0.2 copy-done.7
  109.5 9.6 %last_part.1 = bf16[512,1024]{1,0:T(8,128)(2,1)} custom-call(f32[1024,512]{1,0:T(8,128)} %get-tuple-element.57.key_ref, f32[1024,512]{1,0:T(8,128)} %get-tuple-element.58.value_ref, bf16[1024,1024]{1,0:T(8,128)(2,1)} %get-tuple-element.59.key_tok_ref, bf16[1024,1024]{1,0:T(8,128)(2,1)} %get-tuple-element.60.value_tok_ref, bf16[512,512]{1,0:T(8,128)(2,1)} %copy-done.5, ...), custom_call_target="tpu_custom_call" | custom-call | flops 2147483648 | bytes 13631488 | tf_op jit(solution)/shard_map/last_part/pallas_call | solution.py:178
  119.0 4.7 %all-to-all-start = ((bf16[32,16,1024]{2,1,0:T(8,128)(2,1)}), bf16[32,16,1024]{2,1,0:T(8,128)(2,1)S(1)}, u32[]{:S(2)}, u32[]{:S(2)}) async-start(bf16[32,16,1024]{2,1,0:T(8,128)(2,1)} %bitcast.60), calls=%async_computation | async-start | bytes 2097152 | tf_op jit(solution)/shard_map/all_to_all | solution.py:570
  123.8 0.8 copy.12.a_ref
  124.5 2.5 %filter_part.1 = (f32[64,1024]{1,0:T(8,128)}, bf16[256,256]{1,0:T(8,128)(2,1)}) custom-call(s32[1]{0:T(128)} %bitcast.19.z_ref, bf16[32,160,512]{2,1,0:T(8,128)(2,1)} %bitcast.61, f32[2,64,64]{2,1,0:T(8,128)} %get-tuple-element.66.cs_ref, f32[2,64,64]{2,1,0:T(8,128)} %get-tuple-element.67.twist_ref), custom_call_target="tpu_custom_call" | custom-call | flops 1000000000 | bytes 1048576 | tf_op jit(solution)/shard_map/filter_part/pallas_call | solution.py:333
  127.1 12.1 %all-to-all-done.x_ref = bf16[32,16,1024]{2,1,0:T(8,128)(2,1)S(1)} async-done(((bf16[32,16,1024]{2,1,0:T(8,128)(2,1)}), bf16[32,16,1024]{2,1,0:T(8,128)(2,1)S(1)}, u32[]{:S(2)}, u32[]{:S(2)}) %all-to-all-start) | async-done | bytes 1048608 | tf_op jit(solution)/shard_map/all_to_all | solution.py:570
  139.2 1.0 copy-done.4
  140.2 12.9 %long_conv.1 = bf16[32,16,1024]{2,1,0:T(8,128)(2,1)} custom-call(bf16[32,16,1024]{2,1,0:T(8,128)(2,1)} %copy-done.4, bf16[512,1024]{1,0:T(8,128)(2,1)} %constant.193.clone.fwd_hbm, bf16[1024,512]{1,0:T(8,128)(2,1)} %constant.194.clone.inv_hbm, f32[64,1024]{1,0:T(8,128)} %pad_maximum_fusion.5.tw_hbm, bf16[256,256]{1,0:T(8,128)(2,1)} %copy.12.a_ref, ...), custom_call_target="tpu_custom_call" | custom-call | flops 8000000000 | bytes 8388608 | tf_op jit(solution)/shard_map/long_conv/pallas_call | solution.py:435
  153.1 5.0 %all-to-all-start.1 = ((bf16[32,16,1024]{2,1,0:T(8,128)(2,1)}), bf16[32,16,1024]{2,1,0:T(8,128)(2,1)S(1)}, u32[]{:S(2)}, u32[]{:S(2)}) async-start(bf16[32,16,1024]{2,1,0:T(8,128)(2,1)} %long_conv.1), calls=%async_computation.1 | async-start | bytes 2097152 | tf_op jit(solution)/shard_map/all_to_all | solution.py:579
  158.2 10.0 %gate_part.1 = bf16[512,1024]{1,0:T(8,128)(2,1)} custom-call(bf16[512,4096]{1,0:T(8,128)(2,1)} %bitcast.59, bf16[512,4096]{1,0:T(8,128)(2,1)} %collective-permute-done.3.other_ref, bf16[32,160,512]{2,1,0:T(8,128)(2,1)} %bitcast.62), custom_call_target="tpu_custom_call" | custom-call | flops 4294967296 | bytes 13631488 | tf_op jit(solution)/shard_map/gate_part/pallas_call | solution.py:209
  168.2 5.0 %all-to-all-done.1 = bf16[32,16,1024]{2,1,0:T(8,128)(2,1)S(1)} async-done(((bf16[32,16,1024]{2,1,0:T(8,128)(2,1)}), bf16[32,16,1024]{2,1,0:T(8,128)(2,1)S(1)}, u32[]{:S(2)}, u32[]{:S(2)}) %all-to-all-start.1) | async-done | bytes 1048608 | tf_op jit(solution)/shard_map/all_to_all | solution.py:579
  173.2 1.7 fusion.1
  175.1 3.9 %collective-permute-start.20 = (bf16[512,256]{1,0:T(8,128)(2,1)S(1)}, bf16[512,256]{1,0:T(8,128)(2,1)S(1)}, u32[]{:S(2)}, u32[]{:S(2)}) collective-permute-start(bf16[512,256]{1,0:T(8,128)(2,1)S(1)} %get-tuple-element.85), channel_id=1, source_target_pairs={{0,2},{2,0},{4,6},{6,4},{8,10},{10,8},{12,14},{14,12},{16,18},{18,... | collective-permute-start | bytes 786440 | tf_op jit(solution)/shard_map/ppermute | solution.py:35
  179.0 1.2 collective-permute-done.20
  180.2 0.4 collective-permute-start.23
  180.5 1.8 collective-permute-start.22
  182.5 0.8 pad_maximum_fusion.2.here
  183.3 9.3 %mix_part.1.total_ref = f32[256,4096]{1,0:T(8,128)} custom-call(bf16[1024,256]{1,0:T(8,128)(2,1)} %pad_maximum_fusion.2.here, bf16[1024,4096]{1,0:T(8,128)(2,1)} %w_here.1), custom_call_target="tpu_custom_call" | custom-call | flops 2147483648 | bytes 12582912 | tf_op jit(solution)/shard_map/mix_part/pallas_call | solution.py:266
  192.6 1.6 collective-permute-done.22.far_h
  194.2 0.7 copy-done.10
  194.9 9.7 %mix_more.1 = bf16[256,4096]{1,0:T(8,128)(2,1)} custom-call(f32[256,4096]{1,0:T(8,128)} %mix_part.1.total_ref, bf16[512,256]{1,0:T(8,128)(2,1)} %copy-done.9, bf16[512,256]{1,0:T(8,128)(2,1)} %copy-done.10, bf16[512,4096]{1,0:T(8,128)(2,1)} %collective-permute-done.19.w_near, bf16[512,4096]{1,0:T(8,128)(2,1)} %collective-permute-done.23.w_far), custom_call_target="tpu_custom_call" | custom-call | flops 2147483648 | bytes 12582912 | tf_op jit(solution)/shard_map/mix_more/pallas_call | solution.py:266
  (65 shorter events, 1.3 us)
Async XLA Ops:
  6.5 118.0 %all-gather.3.cloned.1.call-start = ((), (), s32[]{:S(2)}) async-start(), calls=%async_computation.2 | async-start | bytes 5406720 | tf_op jit(solution)/shard_map/all_gather | solution.py:535
  7.6 2.7 %collective-permute-start.4 = (bf16[32,256]{1,0:T(8,128)(2,1)S(1)}, bf16[32,256]{1,0:T(8,128)(2,1)S(1)}, u32[]{:S(2)}, u32[]{:S(2)}) collective-permute-start(bf16[32,256]{1,0:T(8,128)(2,1)S(1)} %pad_maximum_fusion.8), channel_id=1, source_target_pairs={{0,2},{2,0},{4,6},{6,4},{8,10},{10,8},{12,14},{14,12},{16,18},{18,... | collective-permute-start | bytes 49160 | tf_op jit(solution)/shard_map/ppermute | solution.py:35
  10.1 1.5 collective-permute-start
  12.4 10.9 %collective-permute-start.3 = (bf16[512,4096]{1,0:T(8,128)(2,1)}, bf16[512,4096]{1,0:T(8,128)(2,1)}, u32[]{:S(2)}, u32[]{:S(2)}) collective-permute-start(bf16[512,4096]{1,0:T(8,128)(2,1)} %bitcast.56), channel_id=1, source_target_pairs={{0,2},{2,0},{4,6},{6,4},{8,10},{10,8},{12,14},{14,12},{16,18},{18,... | collective-permute-start | bytes 12582920 | tf_op jit(solution)/shard_map/ppermute | solution.py:35
  12.7 7.5 %collective-permute-start.2 = (bf16[128,512]{1,0:T(8,128)(2,1)S(1)}, bf16[128,512]{1,0:T(8,128)(2,1)S(1)}, u32[]{:S(2)}, u32[]{:S(2)}) collective-permute-start(bf16[128,512]{1,0:T(8,128)(2,1)S(1)} %bitcast.65), channel_id=1, source_target_pairs={{0,66},{2,64},{4,70},{6,68},{8,74},{10,72},{12,78},{14,76},{16,82}... | collective-permute-start | bytes 393224 | tf_op jit(solution)/shard_map/ppermute | solution.py:35
  16.7 6.5 %collective-permute-start.1 = (bf16[128,512]{1,0:T(8,128)(2,1)S(1)}, bf16[128,512]{1,0:T(8,128)(2,1)S(1)}, u32[]{:S(2)}, u32[]{:S(2)}) collective-permute-start(bf16[128,512]{1,0:T(8,128)(2,1)S(1)} %bitcast.66), channel_id=1, source_target_pairs={{0,64},{2,66},{4,68},{6,70},{8,72},{10,74},{12,76},{14,78},{16,80}... | collective-permute-start | bytes 393224 | tf_op jit(solution)/shard_map/ppermute | solution.py:35
  23.3 8.8 %collective-permute-start.7 = (bf16[256,512]{1,0:T(8,128)(2,1)S(1)}, bf16[256,512]{1,0:T(8,128)(2,1)S(1)}, u32[]{:S(2)}, u32[]{:S(2)}) collective-permute-start(bf16[256,512]{1,0:T(8,128)(2,1)S(1)} %get-tuple-element.43), channel_id=1, source_target_pairs={{0,4},{2,6},{4,8},{6,10},{8,12},{10,14},{12,0},{14,2},{16,20},{18,... | collective-permute-start | bytes 786440 | tf_op jit(solution)/shard_map/ppermute | solution.py:35
  24.6 15.2 %collective-permute-start.6 = (bf16[256,512]{1,0:T(8,128)(2,1)S(1)}, bf16[256,512]{1,0:T(8,128)(2,1)S(1)}, u32[]{:S(2)}, u32[]{:S(2)}) collective-permute-start(bf16[256,512]{1,0:T(8,128)(2,1)S(1)} %get-tuple-element.43), channel_id=1, source_target_pairs={{0,8},{2,10},{4,12},{6,14},{8,0},{10,2},{12,4},{14,6},{16,24},{18,... | collective-permute-start | bytes 786440 | tf_op jit(solution)/shard_map/ppermute | solution.py:35
  27.0 12.8 %collective-permute-start.5 = (bf16[256,512]{1,0:T(8,128)(2,1)S(1)}, bf16[256,512]{1,0:T(8,128)(2,1)S(1)}, u32[]{:S(2)}, u32[]{:S(2)}) collective-permute-start(bf16[256,512]{1,0:T(8,128)(2,1)S(1)} %get-tuple-element.43), channel_id=1, source_target_pairs={{0,12},{2,14},{4,0},{6,2},{8,4},{10,6},{12,8},{14,10},{16,28},{18,... | collective-permute-start | bytes 786440 | tf_op jit(solution)/shard_map/ppermute | solution.py:35
  28.2 12.7 %collective-permute-start.10 = (bf16[256,512]{1,0:T(8,128)(2,1)S(1)}, bf16[256,512]{1,0:T(8,128)(2,1)S(1)}, u32[]{:S(2)}, u32[]{:S(2)}) collective-permute-start(bf16[256,512]{1,0:T(8,128)(2,1)S(1)} %get-tuple-element.44), channel_id=1, source_target_pairs={{0,16},{2,18},{4,20},{6,22},{8,24},{10,26},{12,28},{14,30},{16,32}... | collective-permute-start | bytes 786440 | tf_op jit(solution)/shard_map/ppermute | solution.py:35
  29.5 14.5 %collective-permute-start.9 = (bf16[256,512]{1,0:T(8,128)(2,1)S(1)}, bf16[256,512]{1,0:T(8,128)(2,1)S(1)}, u32[]{:S(2)}, u32[]{:S(2)}) collective-permute-start(bf16[256,512]{1,0:T(8,128)(2,1)S(1)} %get-tuple-element.44), channel_id=1, source_target_pairs={{0,32},{2,34},{4,36},{6,38},{8,40},{10,42},{12,44},{14,46},{16,48}... | collective-permute-start | bytes 786440 | tf_op jit(solution)/shard_map/ppermute | solution.py:35
  32.1 11.8 %collective-permute-start.8 = (bf16[256,512]{1,0:T(8,128)(2,1)S(1)}, bf16[256,512]{1,0:T(8,128)(2,1)S(1)}, u32[]{:S(2)}, u32[]{:S(2)}) collective-permute-start(bf16[256,512]{1,0:T(8,128)(2,1)S(1)} %get-tuple-element.44), channel_id=1, source_target_pairs={{0,48},{2,50},{4,52},{6,54},{8,56},{10,58},{12,60},{14,62},{16,0},... | collective-permute-start | bytes 786440 | tf_op jit(solution)/shard_map/ppermute | solution.py:35
  39.5 9.2 %copy-start.12 = (s32[32]{0:T(128)S(1)}, s32[32]{0:T(128)}, u32[]{:S(2)}) copy-start(s32[32]{0:T(128)} %constant.192.clone) | copy-start | bytes 388
  39.5 9.2 %copy-start.13 = (s32[32]{0:T(128)S(1)}, s32[32]{0:T(128)}, u32[]{:S(2)}) copy-start(s32[32]{0:T(128)} %constant.191.clone) | copy-start | bytes 388
  39.5 9.2 %copy-start.14 = (s32[32]{0:T(128)S(1)}, s32[32]{0:T(128)}, u32[]{:S(2)}) copy-start(s32[32]{0:T(128)} %constant.190.clone) | copy-start | bytes 388
  45.0 94.1 %collective-permute-start.19 = (bf16[512,4096]{1,0:T(8,128)(2,1)}, bf16[512,4096]{1,0:T(8,128)(2,1)}, u32[]{:S(2)}, u32[]{:S(2)}) collective-permute-start(bf16[512,4096]{1,0:T(8,128)(2,1)} %constant_dynamic-slice_fusion.3), channel_id=1, source_target_pairs={{0,1},{1,0},{2,67},{3,66},{4,5},{5,4},{6,71},{7,70},{8,9},{9,8},{1... | collective-permute-start | bytes 12582920 | tf_op jit(solution)/shard_map/ppermute | solution.py:566
  48.8 36.6 %collective-permute-start.11 = (bf16[1024,512]{1,0:T(8,128)(2,1)}, bf16[1024,512]{1,0:T(8,128)(2,1)S(1)}, u32[]{:S(2)}, u32[]{:S(2)}) collective-permute-start(bf16[1024,512]{1,0:T(8,128)(2,1)} %pad_maximum_fusion.key_line), channel_id=1, source_target_pairs={{0,48},{2,50},{4,52},{6,54},{8,56},{10,58},{12,60},{14,62},{16,0},... | collective-permute-start | bytes 3145736 | tf_op jit(solution)/shard_map/ppermute | solution.py:35
  51.1 36.0 %collective-permute-start.12 = (bf16[1024,512]{1,0:T(8,128)(2,1)}, bf16[1024,512]{1,0:T(8,128)(2,1)S(1)}, u32[]{:S(2)}, u32[]{:S(2)}) collective-permute-start(bf16[1024,512]{1,0:T(8,128)(2,1)} %pad_maximum_fusion.key_line), channel_id=1, source_target_pairs={{0,16},{2,18},{4,20},{6,22},{8,24},{10,26},{12,28},{14,30},{16,32}... | collective-permute-start | bytes 3145736 | tf_op jit(solution)/shard_map/ppermute | solution.py:35
  51.5 35.6 %collective-permute-start.13 = (bf16[1024,512]{1,0:T(8,128)(2,1)}, bf16[1024,512]{1,0:T(8,128)(2,1)S(1)}, u32[]{:S(2)}, u32[]{:S(2)}) collective-permute-start(bf16[1024,512]{1,0:T(8,128)(2,1)} %pad_maximum_fusion.1.value_line), channel_id=1, source_target_pairs={{0,12},{2,14},{4,0},{6,2},{8,4},{10,6},{12,8},{14,10},{16,28},{18,... | collective-permute-start | bytes 3145736 | tf_op jit(solution)/shard_map/ppermute | solution.py:35
  51.5 35.6 %collective-permute-start.14 = (bf16[1024,512]{1,0:T(8,128)(2,1)}, bf16[1024,512]{1,0:T(8,128)(2,1)}, u32[]{:S(2)}, u32[]{:S(2)}) collective-permute-start(bf16[1024,512]{1,0:T(8,128)(2,1)} %pad_maximum_fusion.1.value_line), channel_id=1, source_target_pairs={{0,4},{2,6},{4,8},{6,10},{8,12},{10,14},{12,0},{14,2},{16,20},{18,... | collective-permute-start | bytes 3145736 | tf_op jit(solution)/shard_map/ppermute | solution.py:35
  85.4 1.8 copy-start.1
  87.1 1.0 copy-start.2
  87.1 1.3 copy-start.3
  91.0 14.7 %collective-permute-start.15 = (bf16[512,512]{1,0:T(8,128)(2,1)}, bf16[512,512]{1,0:T(8,128)(2,1)S(1)}, u32[]{:S(2)}, u32[]{:S(2)}) collective-permute-start(bf16[512,512]{1,0:T(8,128)(2,1)} %get-tuple-element.61), channel_id=1, source_target_pairs={{0,48},{2,50},{4,52},{6,54},{8,56},{10,58},{12,60},{14,62},{16,0},... | collective-permute-start | bytes 1572872 | tf_op jit(solution)/shard_map/ppermute | solution.py:35
  91.7 16.6 %collective-permute-start.16 = (bf16[512,512]{1,0:T(8,128)(2,1)}, bf16[512,512]{1,0:T(8,128)(2,1)S(1)}, u32[]{:S(2)}, u32[]{:S(2)}) collective-permute-start(bf16[512,512]{1,0:T(8,128)(2,1)} %get-tuple-element.62), channel_id=1, source_target_pairs={{0,16},{2,18},{4,20},{6,22},{8,24},{10,26},{12,28},{14,30},{16,32}... | collective-permute-start | bytes 1572872 | tf_op jit(solution)/shard_map/ppermute | solution.py:35
  92.5 15.8 %collective-permute-start.17 = (bf16[512,512]{1,0:T(8,128)(2,1)}, bf16[512,512]{1,0:T(8,128)(2,1)S(1)}, u32[]{:S(2)}, u32[]{:S(2)}) collective-permute-start(bf16[512,512]{1,0:T(8,128)(2,1)} %get-tuple-element.63), channel_id=1, source_target_pairs={{0,12},{2,14},{4,0},{6,2},{8,4},{10,6},{12,8},{14,10},{16,28},{18,... | collective-permute-start | bytes 1572872 | tf_op jit(solution)/shard_map/ppermute | solution.py:35
  92.5 15.8 %collective-permute-start.18 = (bf16[512,512]{1,0:T(8,128)(2,1)}, bf16[512,512]{1,0:T(8,128)(2,1)S(1)}, u32[]{:S(2)}, u32[]{:S(2)}) collective-permute-start(bf16[512,512]{1,0:T(8,128)(2,1)} %get-tuple-element.64), channel_id=1, source_target_pairs={{0,4},{2,6},{4,8},{6,10},{8,12},{10,14},{12,0},{14,2},{16,20},{18,... | collective-permute-start | bytes 1572872 | tf_op jit(solution)/shard_map/ppermute | solution.py:35
  105.7 2.6 %copy-start.5 = (bf16[512,512]{1,0:T(8,128)(2,1)}, bf16[512,512]{1,0:T(8,128)(2,1)S(1)}, u32[]{:S(2)}) copy-start(bf16[512,512]{1,0:T(8,128)(2,1)S(1)} %collective-permute-done.15.ka) | copy-start | bytes 1572868
  108.3 0.8 copy-start.6
  108.3 1.0 copy-start.7
  108.3 1.1 copy-start.8
  119.0 20.1 %all-to-all-start = ((bf16[32,16,1024]{2,1,0:T(8,128)(2,1)}), bf16[32,16,1024]{2,1,0:T(8,128)(2,1)S(1)}, u32[]{:S(2)}, u32[]{:S(2)}) async-start(bf16[32,16,1024]{2,1,0:T(8,128)(2,1)} %bitcast.60), calls=%async_computation | async-start | bytes 2097152 | tf_op jit(solution)/shard_map/all_to_all | solution.py:570
  139.2 1.0 copy-start.4
  153.1 5.1 %copy-start.11 = (f32[1024]{0:T(1024)S(1)}, f32[1024]{0:T(1024)}, u32[]{:S(2)}) copy-start(f32[1024]{0:T(1024)} %param.13) | copy-start | bytes 12292
  153.1 20.1 %all-to-all-start.1 = ((bf16[32,16,1024]{2,1,0:T(8,128)(2,1)}), bf16[32,16,1024]{2,1,0:T(8,128)(2,1)S(1)}, u32[]{:S(2)}, u32[]{:S(2)}) async-start(bf16[32,16,1024]{2,1,0:T(8,128)(2,1)} %long_conv.1), calls=%async_computation.1 | async-start | bytes 2097152 | tf_op jit(solution)/shard_map/all_to_all | solution.py:579
  158.2 15.0 %copy-start = (bf16[512,1024]{1,0:T(8,128)(2,1)S(1)}, bf16[512,1024]{1,0:T(8,128)(2,1)}, u32[]{:S(2)}) copy-start(bf16[512,1024]{1,0:T(8,128)(2,1)} %last_part.1) | copy-start | bytes 3145732
  175.1 5.1 %collective-permute-start.20 = (bf16[512,256]{1,0:T(8,128)(2,1)S(1)}, bf16[512,256]{1,0:T(8,128)(2,1)S(1)}, u32[]{:S(2)}, u32[]{:S(2)}) collective-permute-start(bf16[512,256]{1,0:T(8,128)(2,1)S(1)} %get-tuple-element.85), channel_id=1, source_target_pairs={{0,2},{2,0},{4,6},{6,4},{8,10},{10,8},{12,14},{14,12},{16,18},{18,... | collective-permute-start | bytes 786440 | tf_op jit(solution)/shard_map/ppermute | solution.py:35
  180.2 14.0 %collective-permute-start.23 = (bf16[512,4096]{1,0:T(8,128)(2,1)}, bf16[512,4096]{1,0:T(8,128)(2,1)}, u32[]{:S(2)}, u32[]{:S(2)}) collective-permute-start(bf16[512,4096]{1,0:T(8,128)(2,1)} %collective-permute-done.19.w_near), channel_id=1, source_target_pairs={{0,2},{2,0},{4,6},{6,4},{8,10},{10,8},{12,14},{14,12},{16,18},{18,... | collective-permute-start | bytes 12582920 | tf_op jit(solution)/shard_map/ppermute | solution.py:35
  180.5 12.1 %collective-permute-start.21 = (bf16[512,256]{1,0:T(8,128)(2,1)S(1)}, bf16[512,256]{1,0:T(8,128)(2,1)S(1)}, u32[]{:S(2)}, u32[]{:S(2)}) collective-permute-start(bf16[512,256]{1,0:T(8,128)(2,1)S(1)} %get-tuple-element.84), channel_id=1, source_target_pairs={{0,1},{1,0},{2,3},{3,2},{4,5},{5,4},{6,7},{7,6},{8,9},{9,8},{10,11... | collective-permute-start | bytes 786440 | tf_op jit(solution)/shard_map/ppermute | solution.py:592
  180.5 13.6 %collective-permute-start.22 = (bf16[512,256]{1,0:T(8,128)(2,1)S(1)}, bf16[512,256]{1,0:T(8,128)(2,1)S(1)}, u32[]{:S(2)}, u32[]{:S(2)}) collective-permute-start(bf16[512,256]{1,0:T(8,128)(2,1)S(1)} %get-tuple-element.83), channel_id=1, source_target_pairs={{0,3},{1,2},{2,1},{3,0},{4,7},{5,6},{6,5},{7,4},{8,11},{9,10},{10,... | collective-permute-start | bytes 786440 | tf_op jit(solution)/shard_map/ppermute | solution.py:597
  192.6 1.6 copy-start.9
  194.2 0.7 copy-start.10
Sparse Core Ops, SparseCore 0:
  12.5 106.5 all-gather.2

commit v16 on v14

--- a/solution.py
+++ b/solution.py
@@ -253,7 +253,7 @@
 def mix_part(total, parts, weights):
     rows = parts[0].shape[1]
     width = weights[0].shape[1]
-    tile = width // 4
+    tile = width // 2
     depth = sum(p.shape[0] for p in parts)
     totals = [] if total is None else [total]
 
@@ -265,7 +265,7 @@
 
     return pl.pallas_call(
         mix_kernel if total is None else mix_more_kernel,
-        grid=(4,),
+        grid=(2,),
         in_specs=[tiled(t) for t in totals] + [whole(p) for p in parts] + [tiled(w) for w in weights],
         out_specs=pl.BlockSpec((rows, tile), lambda i: (0, i)),
         out_shape=jax.ShapeDtypeStruct((rows, width), F32 if total is None else BF16),

time: 209 us -> 208 us (level)
  no operation moved by 1% of the time
where the time goes in v16:
time: 208 us; the launch traced here: 207 us
  Pallas kernels  71.4 us (34%)
  waiting for transfers between devices  56.7 us (27%)
  starting transfers between devices  43.7 us (21%)
  between operations  13.7 us (7%)
  local copies, waits for them, and re-layouts  11.8 us (6%)
  other arithmetic  9.64 us (5%)
    ppermute x21, waiting for transfers between devices, send(): return lax.ppermute(value, 'seq', perm)  35.1 us
    ppermute x21, starting transfers between devices, send(): return lax.ppermute(value, 'seq', perm)  28.9 us
    pallas_call x2, Pallas kernels, sum_part(): pl.pallas_call(kernel, grid_spec=pltpu.PrefetchScalarGridSpec(num_scalar_...  22.1 us
    pallas_call x2, Pallas kernels, mix_part(): pl.pallas_call(mix_kernel if total is None else mix_more_kernel, grid=(2,...  13.7 us
    pallas_call x1, Pallas kernels, long_conv(): pl.pallas_call(conv_kernel, in_specs=[vmem, hbm, hbm, hbm, vmem, vmem, vm...  12.9 us
    all_to_all x1, waiting for transfers between devices, per_device(): mine_ch = lax.all_to_all(packed, 'seq', 0, 0, axis_index_groups=SAME_CORE)  12.1 us
    pallas_call x1, Pallas kernels, gate_part(): pl.pallas_call(gate_kernel, grid=(4,), in_specs=[pl.BlockSpec((tile, widt...  9.99 us
    pallas_call x1, Pallas kernels, last_part(): pl.pallas_call(last_kernel, grid=(4,), in_specs=[pl.BlockSpec((tile, chan...  7.55 us
  transfers between devices with their start and end apart: 27, of which 12 were waited for; matrix products, arithmetic and copies ran while one was open for 7% of the time, Pallas kernels for 25%

profile of v16, /device:TPU:1, one launch (start us, length us, event | category | flops | bytes accessed | tf_op | source)
XLA Modules:
  0.0 206.9 jit_solution(4654339279363388668)
XLA Ops:
  6.5 0.9 copy.11
  7.6 1.5 collective-permute-start.4
  9.1 1.0 dynamic-slice_bitcast_fusion
  10.3 1.4 collective-permute-done
  11.7 0.7 maximum_maximum_fusion
  12.4 0.2 collective-permute-start.3
  12.7 4.0 %collective-permute-start.2 = (bf16[128,512]{1,0:T(8,128)(2,1)S(1)}, bf16[128,512]{1,0:T(8,128)(2,1)S(1)}, u32[]{:S(2)}, u32[]{:S(2)}) collective-permute-start(bf16[128,512]{1,0:T(8,128)(2,1)S(1)} %bitcast.65), channel_id=1, source_target_pairs={{0,66},{2,64},{4,70},{6,68},{8,74},{10,72},{12,78},{14,76},{16,82}... | collective-permute-start | bytes 393224 | tf_op jit(solution)/shard_map/ppermute | solution.py:35
  16.8 3.4 %collective-permute-done.2 = bf16[128,512]{1,0:T(8,128)(2,1)S(1)} collective-permute-done((bf16[128,512]{1,0:T(8,128)(2,1)S(1)}, bf16[128,512]{1,0:T(8,128)(2,1)S(1)}, u32[]{:S(2)}, u32[]{:S(2)}) %collective-permute-start.2) | collective-permute-done | bytes 131104 | tf_op jit(solution)/shard_map/ppermute | solution.py:35
  20.2 3.0 %collective-permute-done.1 = bf16[128,512]{1,0:T(8,128)(2,1)S(1)} collective-permute-done((bf16[128,512]{1,0:T(8,128)(2,1)S(1)}, bf16[128,512]{1,0:T(8,128)(2,1)S(1)}, u32[]{:S(2)}, u32[]{:S(2)}) %collective-permute-start.1) | collective-permute-done | bytes 131104 | tf_op jit(solution)/shard_map/ppermute | solution.py:35
  23.3 1.3 collective-permute-start.7
  24.6 2.5 %collective-permute-start.6 = (bf16[256,512]{1,0:T(8,128)(2,1)S(1)}, bf16[256,512]{1,0:T(8,128)(2,1)S(1)}, u32[]{:S(2)}, u32[]{:S(2)}) collective-permute-start(bf16[256,512]{1,0:T(8,128)(2,1)S(1)} %get-tuple-element.43), channel_id=1, source_target_pairs={{0,8},{2,10},{4,12},{6,14},{8,0},{10,2},{12,4},{14,6},{16,24},{18,... | collective-permute-start | bytes 786440 | tf_op jit(solution)/shard_map/ppermute | solution.py:35
  27.0 1.2 collective-permute-start.5
  28.2 1.3 collective-permute-start.10
  29.5 2.6 %collective-permute-start.9 = (bf16[256,512]{1,0:T(8,128)(2,1)S(1)}, bf16[256,512]{1,0:T(8,128)(2,1)S(1)}, u32[]{:S(2)}, u32[]{:S(2)}) collective-permute-start(bf16[256,512]{1,0:T(8,128)(2,1)S(1)} %get-tuple-element.44), channel_id=1, source_target_pairs={{0,32},{2,34},{4,36},{6,38},{8,40},{10,42},{12,44},{14,46},{16,48}... | collective-permute-start | bytes 786440 | tf_op jit(solution)/shard_map/ppermute | solution.py:35
  32.1 2.7 %collective-permute-start.8 = (bf16[256,512]{1,0:T(8,128)(2,1)S(1)}, bf16[256,512]{1,0:T(8,128)(2,1)S(1)}, u32[]{:S(2)}, u32[]{:S(2)}) collective-permute-start(bf16[256,512]{1,0:T(8,128)(2,1)S(1)} %get-tuple-element.44), channel_id=1, source_target_pairs={{0,48},{2,50},{4,52},{6,54},{8,56},{10,58},{12,60},{14,62},{16,0},... | collective-permute-start | bytes 786440 | tf_op jit(solution)/shard_map/ppermute | solution.py:35
  34.9 4.7 %constant_dynamic-slice_fusion.3 = bf16[512,4096]{1,0:T(8,128)(2,1)} fusion(bf16[1024,4096]{1,0:T(8,128)(2,1)} %w_here.1, s32[]{:T(128)S(6)} %select_n.230), kind=kLoop, calls=%fused_computation.104 | loop fusion | bytes 8388612 | tf_op jit(solution)/shard_map/dynamic_slice | solution.py:538
  39.5 0.3 collective-permute-done.6
  39.8 1.1 pad_maximum_fusion.key_line
  40.9 3.1 %collective-permute-done.9 = bf16[256,512]{1,0:T(8,128)(2,1)S(1)} collective-permute-done((bf16[256,512]{1,0:T(8,128)(2,1)S(1)}, bf16[256,512]{1,0:T(8,128)(2,1)S(1)}, u32[]{:S(2)}, u32[]{:S(2)}) %collective-permute-start.9) | collective-permute-done | bytes 262176 | tf_op jit(solution)/shard_map/ppermute | solution.py:35
  44.0 1.1 pad_maximum_fusion.1.value_line
  45.0 3.3 %collective-permute-start.19 = (bf16[512,4096]{1,0:T(8,128)(2,1)}, bf16[512,4096]{1,0:T(8,128)(2,1)}, u32[]{:S(2)}, u32[]{:S(2)}) collective-permute-start(bf16[512,4096]{1,0:T(8,128)(2,1)} %constant_dynamic-slice_fusion.3), channel_id=1, source_target_pairs={{0,1},{1,0},{2,67},{3,66},{4,5},{5,4},{6,71},{7,70},{8,9},{9,8},{1... | collective-permute-start | bytes 12582920 | tf_op jit(solution)/shard_map/ppermute | solution.py:566
  48.3 0.2 fusion.38
  48.8 2.3 %collective-permute-start.11 = (bf16[1024,512]{1,0:T(8,128)(2,1)}, bf16[1024,512]{1,0:T(8,128)(2,1)S(1)}, u32[]{:S(2)}, u32[]{:S(2)}) collective-permute-start(bf16[1024,512]{1,0:T(8,128)(2,1)} %pad_maximum_fusion.key_line), channel_id=1, source_target_pairs={{0,48},{2,50},{4,52},{6,54},{8,56},{10,58},{12,60},{14,62},{16,0},... | collective-permute-start | bytes 3145736 | tf_op jit(solution)/shard_map/ppermute | solution.py:35
  51.1 0.4 collective-permute-start.12
  51.5 1.4 collective-permute-start.14
  53.0 0.6 pad_add_fusion.order_ref
  53.6 0.7 fusion.9.ai_ref
  54.2 0.3 fusion.35
  54.6 0.7 pad_maximum_fusion.6
  55.2 0.6 fusion.15
  55.8 0.7 pad_maximum_fusion.5.tw_hbm
  56.5 10.4 %first_part.1 = (f32[1024,512]{1,0:T(8,128)}, f32[1024,512]{1,0:T(8,128)}, bf16[1024,1024]{1,0:T(8,128)(2,1)}, bf16[1024,1024]{1,0:T(8,128)(2,1)}) custom-call(s32[2,32]{1,0:T(2,128)} %pad_add_fusion.order_ref, bf16[512,4096]{1,0:T(8,128)(2,1)} %bitcast.57, bf16[512,4096]{1,0:T(8,128)(2,1)} %collective-permute-done.3.other_ref, ...), custom_call_target="tpu_custom_call" | custom-call | flops 2147483648 | bytes 18874368 | tf_op jit(solution)/shard_map/first_part/pallas_call | solution.py:117
  66.9 18.4 %collective-permute-done.11.k1.refs_0_ = bf16[1024,512]{1,0:T(8,128)(2,1)S(1)} collective-permute-done((bf16[1024,512]{1,0:T(8,128)(2,1)}, bf16[1024,512]{1,0:T(8,128)(2,1)S(1)}, u32[]{:S(2)}, u32[]{:S(2)}) %collective-permute-start.11) | collective-permute-done | bytes 1048608 | tf_op jit(solution)/shard_map/ppermute | solution.py:35
  85.4 1.7 collective-permute-done.12.k3.refs_1_
  87.1 1.0 copy-done.2
  88.1 0.3 copy-done.3
  88.4 2.6 %cut_halves.1 = (bf16[512,512]{1,0:T(8,128)(2,1)}, bf16[512,512]{1,0:T(8,128)(2,1)}, bf16[512,512]{1,0:T(8,128)(2,1)}, bf16[512,512]{1,0:T(8,128)(2,1)}) custom-call(bf16[1024,512]{1,0:T(8,128)(2,1)} %copy-done.1, bf16[1024,512]{1,0:T(8,128)(2,1)} %copy-done.2, bf16[1024,512]{1,0:T(8,128)(2,1)} %copy-done.3, bf16[1024,512]{1,0:T(8,128)(2,1)} %collective-permute-done.14.v3.refs_3_), custom_call_target="tpu_custom_call" | custom-call | bytes 4194304 | tf_op jit(solution)/shard_map/cut_halves/pallas_call | solution.py:149
  91.0 0.7 collective-permute-start.15
  91.7 0.8 collective-permute-start.16
  92.5 1.5 collective-permute-start.18
  94.0 11.7 %second_part.1 = (f32[1024,512]{1,0:T(8,128)}, f32[1024,512]{1,0:T(8,128)}) custom-call(s32[2,32]{1,0:T(2,128)} %pad_add_fusion.order_ref, bf16[512,4096]{1,0:T(8,128)(2,1)} %bitcast.58, bf16[512,4096]{1,0:T(8,128)(2,1)} %collective-permute-done.3.other_ref, f32[1024,512]{1,0:T(8,128)} %get-tuple-element.51.key_in, f32[1024,512]{1,0:T(8,128)} %get-tuple-element.52.value_in, ...), custom_call_target="tpu_custom_call" | custom-call | flops 4294967296 | bytes 18874368 | tf_op jit(solution)/shard_map/second_part/pallas_call | solution.py:117
  105.7 2.6 %collective-permute-done.16.kb = bf16[512,512]{1,0:T(8,128)(2,1)S(1)} collective-permute-done((bf16[512,512]{1,0:T(8,128)(2,1)}, bf16[512,512]{1,0:T(8,128)(2,1)S(1)}, u32[]{:S(2)}, u32[]{:S(2)}) %collective-permute-start.16) | collective-permute-done | bytes 524320 | tf_op jit(solution)/shard_map/ppermute | solution.py:35
  108.4 0.8 copy-done.6
  109.1 0.2 copy-done.7
  109.5 7.5 %last_part.1 = bf16[512,1024]{1,0:T(8,128)(2,1)} custom-call(f32[1024,512]{1,0:T(8,128)} %get-tuple-element.57.key_ref, f32[1024,512]{1,0:T(8,128)} %get-tuple-element.58.value_ref, bf16[1024,1024]{1,0:T(8,128)(2,1)} %get-tuple-element.59.key_tok_ref, bf16[1024,1024]{1,0:T(8,128)(2,1)} %get-tuple-element.60.value_tok_ref, bf16[512,512]{1,0:T(8,128)(2,1)} %copy-done.5, ...), custom_call_target="tpu_custom_call" | custom-call | flops 2147483648 | bytes 13631488 | tf_op jit(solution)/shard_map/last_part/pallas_call | solution.py:178
  117.0 4.7 %all-to-all-start = ((bf16[32,16,1024]{2,1,0:T(8,128)(2,1)}), bf16[32,16,1024]{2,1,0:T(8,128)(2,1)S(1)}, u32[]{:S(2)}, u32[]{:S(2)}) async-start(bf16[32,16,1024]{2,1,0:T(8,128)(2,1)} %bitcast.60), calls=%async_computation | async-start | bytes 2097152 | tf_op jit(solution)/shard_map/all_to_all | solution.py:570
  121.7 0.8 copy.12.a_ref
  122.5 2.5 %filter_part.1 = (f32[64,1024]{1,0:T(8,128)}, bf16[256,256]{1,0:T(8,128)(2,1)}) custom-call(s32[1]{0:T(128)} %bitcast.19.z_ref, bf16[32,160,512]{2,1,0:T(8,128)(2,1)} %bitcast.61, f32[2,64,64]{2,1,0:T(8,128)} %get-tuple-element.66.cs_ref, f32[2,64,64]{2,1,0:T(8,128)} %get-tuple-element.67.twist_ref), custom_call_target="tpu_custom_call" | custom-call | flops 1000000000 | bytes 1048576 | tf_op jit(solution)/shard_map/filter_part/pallas_call | solution.py:333
  125.0 12.1 %all-to-all-done.x_ref = bf16[32,16,1024]{2,1,0:T(8,128)(2,1)S(1)} async-done(((bf16[32,16,1024]{2,1,0:T(8,128)(2,1)}), bf16[32,16,1024]{2,1,0:T(8,128)(2,1)S(1)}, u32[]{:S(2)}, u32[]{:S(2)}) %all-to-all-start) | async-done | bytes 1048608 | tf_op jit(solution)/shard_map/all_to_all | solution.py:570
  137.1 1.0 copy-done.4
  138.1 12.9 %long_conv.1 = bf16[32,16,1024]{2,1,0:T(8,128)(2,1)} custom-call(bf16[32,16,1024]{2,1,0:T(8,128)(2,1)} %copy-done.4, bf16[512,1024]{1,0:T(8,128)(2,1)} %constant.193.clone.fwd_hbm, bf16[1024,512]{1,0:T(8,128)(2,1)} %constant.194.clone.inv_hbm, f32[64,1024]{1,0:T(8,128)} %pad_maximum_fusion.5.tw_hbm, bf16[256,256]{1,0:T(8,128)(2,1)} %copy.12.a_ref, ...), custom_call_target="tpu_custom_call" | custom-call | flops 8000000000 | bytes 8388608 | tf_op jit(solution)/shard_map/long_conv/pallas_call | solution.py:435
  151.0 5.1 %all-to-all-start.1 = ((bf16[32,16,1024]{2,1,0:T(8,128)(2,1)}), bf16[32,16,1024]{2,1,0:T(8,128)(2,1)S(1)}, u32[]{:S(2)}, u32[]{:S(2)}) async-start(bf16[32,16,1024]{2,1,0:T(8,128)(2,1)} %long_conv.1), calls=%async_computation.1 | async-start | bytes 2097152 | tf_op jit(solution)/shard_map/all_to_all | solution.py:579
  156.2 10.0 %gate_part.1 = bf16[512,1024]{1,0:T(8,128)(2,1)} custom-call(bf16[512,4096]{1,0:T(8,128)(2,1)} %bitcast.59, bf16[512,4096]{1,0:T(8,128)(2,1)} %collective-permute-done.3.other_ref, bf16[32,160,512]{2,1,0:T(8,128)(2,1)} %bitcast.62), custom_call_target="tpu_custom_call" | custom-call | flops 4294967296 | bytes 13631488 | tf_op jit(solution)/shard_map/gate_part/pallas_call | solution.py:209
  166.1 5.0 %all-to-all-done.1 = bf16[32,16,1024]{2,1,0:T(8,128)(2,1)S(1)} async-done(((bf16[32,16,1024]{2,1,0:T(8,128)(2,1)}), bf16[32,16,1024]{2,1,0:T(8,128)(2,1)S(1)}, u32[]{:S(2)}, u32[]{:S(2)}) %all-to-all-start.1) | async-done | bytes 1048608 | tf_op jit(solution)/shard_map/all_to_all | solution.py:579
  171.2 1.7 fusion.1
  173.0 3.9 %collective-permute-start.20 = (bf16[512,256]{1,0:T(8,128)(2,1)S(1)}, bf16[512,256]{1,0:T(8,128)(2,1)S(1)}, u32[]{:S(2)}, u32[]{:S(2)}) collective-permute-start(bf16[512,256]{1,0:T(8,128)(2,1)S(1)} %get-tuple-element.85), channel_id=1, source_target_pairs={{0,2},{2,0},{4,6},{6,4},{8,10},{10,8},{12,14},{14,12},{16,18},{18,... | collective-permute-start | bytes 786440 | tf_op jit(solution)/shard_map/ppermute | solution.py:35
  176.9 1.2 collective-permute-done.20
  178.1 0.4 collective-permute-start.23
  178.5 1.8 collective-permute-start.22
  180.4 0.8 pad_maximum_fusion.2.here
  181.2 6.4 %mix_part.1.total_ref = f32[256,4096]{1,0:T(8,128)} custom-call(bf16[1024,256]{1,0:T(8,128)(2,1)} %pad_maximum_fusion.2.here, bf16[1024,4096]{1,0:T(8,128)(2,1)} %w_here.1), custom_call_target="tpu_custom_call" | custom-call | flops 2147483648 | bytes 12582912 | tf_op jit(solution)/shard_map/mix_part/pallas_call | solution.py:266
  187.7 4.4 %collective-permute-done.22.far_h = bf16[512,256]{1,0:T(8,128)(2,1)S(1)} collective-permute-done((bf16[512,256]{1,0:T(8,128)(2,1)S(1)}, bf16[512,256]{1,0:T(8,128)(2,1)S(1)}, u32[]{:S(2)}, u32[]{:S(2)}) %collective-permute-start.22) | collective-permute-done | bytes 262176 | tf_op jit(solution)/shard_map/ppermute | solution.py:597
  192.1 0.7 copy-done.10
  192.8 7.2 %mix_more.1 = bf16[256,4096]{1,0:T(8,128)(2,1)} custom-call(f32[256,4096]{1,0:T(8,128)} %mix_part.1.total_ref, bf16[512,256]{1,0:T(8,128)(2,1)} %copy-done.9, bf16[512,256]{1,0:T(8,128)(2,1)} %copy-done.10, bf16[512,4096]{1,0:T(8,128)(2,1)} %collective-permute-done.19.w_near, bf16[512,4096]{1,0:T(8,128)(2,1)} %collective-permute-done.23.w_far), custom_call_target="tpu_custom_call" | custom-call | flops 2147483648 | bytes 12582912 | tf_op jit(solution)/shard_map/mix_more/pallas_call | solution.py:266
  (65 shorter events, 1.3 us)
Async XLA Ops:
  6.5 115.9 %all-gather.3.cloned.1.call-start = ((), (), s32[]{:S(2)}) async-start(), calls=%async_computation.2 | async-start | bytes 5406720 | tf_op jit(solution)/shard_map/all_gather | solution.py:535
  7.6 2.7 %collective-permute-start.4 = (bf16[32,256]{1,0:T(8,128)(2,1)S(1)}, bf16[32,256]{1,0:T(8,128)(2,1)S(1)}, u32[]{:S(2)}, u32[]{:S(2)}) collective-permute-start(bf16[32,256]{1,0:T(8,128)(2,1)S(1)} %pad_maximum_fusion.8), channel_id=1, source_target_pairs={{0,2},{2,0},{4,6},{6,4},{8,10},{10,8},{12,14},{14,12},{16,18},{18,... | collective-permute-start | bytes 49160 | tf_op jit(solution)/shard_map/ppermute | solution.py:35
  10.1 1.5 collective-permute-start
  12.4 10.9 %collective-permute-start.3 = (bf16[512,4096]{1,0:T(8,128)(2,1)}, bf16[512,4096]{1,0:T(8,128)(2,1)}, u32[]{:S(2)}, u32[]{:S(2)}) collective-permute-start(bf16[512,4096]{1,0:T(8,128)(2,1)} %bitcast.56), channel_id=1, source_target_pairs={{0,2},{2,0},{4,6},{6,4},{8,10},{10,8},{12,14},{14,12},{16,18},{18,... | collective-permute-start | bytes 12582920 | tf_op jit(solution)/shard_map/ppermute | solution.py:35
  12.7 7.5 %collective-permute-start.2 = (bf16[128,512]{1,0:T(8,128)(2,1)S(1)}, bf16[128,512]{1,0:T(8,128)(2,1)S(1)}, u32[]{:S(2)}, u32[]{:S(2)}) collective-permute-start(bf16[128,512]{1,0:T(8,128)(2,1)S(1)} %bitcast.65), channel_id=1, source_target_pairs={{0,66},{2,64},{4,70},{6,68},{8,74},{10,72},{12,78},{14,76},{16,82}... | collective-permute-start | bytes 393224 | tf_op jit(solution)/shard_map/ppermute | solution.py:35
  16.7 6.5 %collective-permute-start.1 = (bf16[128,512]{1,0:T(8,128)(2,1)S(1)}, bf16[128,512]{1,0:T(8,128)(2,1)S(1)}, u32[]{:S(2)}, u32[]{:S(2)}) collective-permute-start(bf16[128,512]{1,0:T(8,128)(2,1)S(1)} %bitcast.66), channel_id=1, source_target_pairs={{0,64},{2,66},{4,68},{6,70},{8,72},{10,74},{12,76},{14,78},{16,80}... | collective-permute-start | bytes 393224 | tf_op jit(solution)/shard_map/ppermute | solution.py:35
  23.3 8.8 %collective-permute-start.7 = (bf16[256,512]{1,0:T(8,128)(2,1)S(1)}, bf16[256,512]{1,0:T(8,128)(2,1)S(1)}, u32[]{:S(2)}, u32[]{:S(2)}) collective-permute-start(bf16[256,512]{1,0:T(8,128)(2,1)S(1)} %get-tuple-element.43), channel_id=1, source_target_pairs={{0,4},{2,6},{4,8},{6,10},{8,12},{10,14},{12,0},{14,2},{16,20},{18,... | collective-permute-start | bytes 786440 | tf_op jit(solution)/shard_map/ppermute | solution.py:35
  24.6 15.2 %collective-permute-start.6 = (bf16[256,512]{1,0:T(8,128)(2,1)S(1)}, bf16[256,512]{1,0:T(8,128)(2,1)S(1)}, u32[]{:S(2)}, u32[]{:S(2)}) collective-permute-start(bf16[256,512]{1,0:T(8,128)(2,1)S(1)} %get-tuple-element.43), channel_id=1, source_target_pairs={{0,8},{2,10},{4,12},{6,14},{8,0},{10,2},{12,4},{14,6},{16,24},{18,... | collective-permute-start | bytes 786440 | tf_op jit(solution)/shard_map/ppermute | solution.py:35
  27.0 12.8 %collective-permute-start.5 = (bf16[256,512]{1,0:T(8,128)(2,1)S(1)}, bf16[256,512]{1,0:T(8,128)(2,1)S(1)}, u32[]{:S(2)}, u32[]{:S(2)}) collective-permute-start(bf16[256,512]{1,0:T(8,128)(2,1)S(1)} %get-tuple-element.43), channel_id=1, source_target_pairs={{0,12},{2,14},{4,0},{6,2},{8,4},{10,6},{12,8},{14,10},{16,28},{18,... | collective-permute-start | bytes 786440 | tf_op jit(solution)/shard_map/ppermute | solution.py:35
  28.2 12.7 %collective-permute-start.10 = (bf16[256,512]{1,0:T(8,128)(2,1)S(1)}, bf16[256,512]{1,0:T(8,128)(2,1)S(1)}, u32[]{:S(2)}, u32[]{:S(2)}) collective-permute-start(bf16[256,512]{1,0:T(8,128)(2,1)S(1)} %get-tuple-element.44), channel_id=1, source_target_pairs={{0,16},{2,18},{4,20},{6,22},{8,24},{10,26},{12,28},{14,30},{16,32}... | collective-permute-start | bytes 786440 | tf_op jit(solution)/shard_map/ppermute | solution.py:35
  29.5 14.5 %collective-permute-start.9 = (bf16[256,512]{1,0:T(8,128)(2,1)S(1)}, bf16[256,512]{1,0:T(8,128)(2,1)S(1)}, u32[]{:S(2)}, u32[]{:S(2)}) collective-permute-start(bf16[256,512]{1,0:T(8,128)(2,1)S(1)} %get-tuple-element.44), channel_id=1, source_target_pairs={{0,32},{2,34},{4,36},{6,38},{8,40},{10,42},{12,44},{14,46},{16,48}... | collective-permute-start | bytes 786440 | tf_op jit(solution)/shard_map/ppermute | solution.py:35
  32.1 11.8 %collective-permute-start.8 = (bf16[256,512]{1,0:T(8,128)(2,1)S(1)}, bf16[256,512]{1,0:T(8,128)(2,1)S(1)}, u32[]{:S(2)}, u32[]{:S(2)}) collective-permute-start(bf16[256,512]{1,0:T(8,128)(2,1)S(1)} %get-tuple-element.44), channel_id=1, source_target_pairs={{0,48},{2,50},{4,52},{6,54},{8,56},{10,58},{12,60},{14,62},{16,0},... | collective-permute-start | bytes 786440 | tf_op jit(solution)/shard_map/ppermute | solution.py:35
  39.5 9.2 %copy-start.12 = (s32[32]{0:T(128)S(1)}, s32[32]{0:T(128)}, u32[]{:S(2)}) copy-start(s32[32]{0:T(128)} %constant.192.clone) | copy-start | bytes 388
  39.5 9.2 %copy-start.13 = (s32[32]{0:T(128)S(1)}, s32[32]{0:T(128)}, u32[]{:S(2)}) copy-start(s32[32]{0:T(128)} %constant.191.clone) | copy-start | bytes 388
  39.5 9.2 %copy-start.14 = (s32[32]{0:T(128)S(1)}, s32[32]{0:T(128)}, u32[]{:S(2)}) copy-start(s32[32]{0:T(128)} %constant.190.clone) | copy-start | bytes 388
  45.0 92.1 %collective-permute-start.19 = (bf16[512,4096]{1,0:T(8,128)(2,1)}, bf16[512,4096]{1,0:T(8,128)(2,1)}, u32[]{:S(2)}, u32[]{:S(2)}) collective-permute-start(bf16[512,4096]{1,0:T(8,128)(2,1)} %constant_dynamic-slice_fusion.3), channel_id=1, source_target_pairs={{0,1},{1,0},{2,67},{3,66},{4,5},{5,4},{6,71},{7,70},{8,9},{9,8},{1... | collective-permute-start | bytes 12582920 | tf_op jit(solution)/shard_map/ppermute | solution.py:566
  48.8 36.6 %collective-permute-start.11 = (bf16[1024,512]{1,0:T(8,128)(2,1)}, bf16[1024,512]{1,0:T(8,128)(2,1)S(1)}, u32[]{:S(2)}, u32[]{:S(2)}) collective-permute-start(bf16[1024,512]{1,0:T(8,128)(2,1)} %pad_maximum_fusion.key_line), channel_id=1, source_target_pairs={{0,48},{2,50},{4,52},{6,54},{8,56},{10,58},{12,60},{14,62},{16,0},... | collective-permute-start | bytes 3145736 | tf_op jit(solution)/shard_map/ppermute | solution.py:35
  51.1 36.0 %collective-permute-start.12 = (bf16[1024,512]{1,0:T(8,128)(2,1)}, bf16[1024,512]{1,0:T(8,128)(2,1)S(1)}, u32[]{:S(2)}, u32[]{:S(2)}) collective-permute-start(bf16[1024,512]{1,0:T(8,128)(2,1)} %pad_maximum_fusion.key_line), channel_id=1, source_target_pairs={{0,16},{2,18},{4,20},{6,22},{8,24},{10,26},{12,28},{14,30},{16,32}... | collective-permute-start | bytes 3145736 | tf_op jit(solution)/shard_map/ppermute | solution.py:35
  51.5 35.6 %collective-permute-start.13 = (bf16[1024,512]{1,0:T(8,128)(2,1)}, bf16[1024,512]{1,0:T(8,128)(2,1)S(1)}, u32[]{:S(2)}, u32[]{:S(2)}) collective-permute-start(bf16[1024,512]{1,0:T(8,128)(2,1)} %pad_maximum_fusion.1.value_line), channel_id=1, source_target_pairs={{0,12},{2,14},{4,0},{6,2},{8,4},{10,6},{12,8},{14,10},{16,28},{18,... | collective-permute-start | bytes 3145736 | tf_op jit(solution)/shard_map/ppermute | solution.py:35
  51.5 35.6 %collective-permute-start.14 = (bf16[1024,512]{1,0:T(8,128)(2,1)}, bf16[1024,512]{1,0:T(8,128)(2,1)}, u32[]{:S(2)}, u32[]{:S(2)}) collective-permute-start(bf16[1024,512]{1,0:T(8,128)(2,1)} %pad_maximum_fusion.1.value_line), channel_id=1, source_target_pairs={{0,4},{2,6},{4,8},{6,10},{8,12},{10,14},{12,0},{14,2},{16,20},{18,... | collective-permute-start | bytes 3145736 | tf_op jit(solution)/shard_map/ppermute | solution.py:35
  85.4 1.8 copy-start.1
  87.1 1.0 copy-start.2
  87.1 1.3 copy-start.3
  91.0 14.7 %collective-permute-start.15 = (bf16[512,512]{1,0:T(8,128)(2,1)}, bf16[512,512]{1,0:T(8,128)(2,1)S(1)}, u32[]{:S(2)}, u32[]{:S(2)}) collective-permute-start(bf16[512,512]{1,0:T(8,128)(2,1)} %get-tuple-element.61), channel_id=1, source_target_pairs={{0,48},{2,50},{4,52},{6,54},{8,56},{10,58},{12,60},{14,62},{16,0},... | collective-permute-start | bytes 1572872 | tf_op jit(solution)/shard_map/ppermute | solution.py:35
  91.7 16.6 %collective-permute-start.16 = (bf16[512,512]{1,0:T(8,128)(2,1)}, bf16[512,512]{1,0:T(8,128)(2,1)S(1)}, u32[]{:S(2)}, u32[]{:S(2)}) collective-permute-start(bf16[512,512]{1,0:T(8,128)(2,1)} %get-tuple-element.62), channel_id=1, source_target_pairs={{0,16},{2,18},{4,20},{6,22},{8,24},{10,26},{12,28},{14,30},{16,32}... | collective-permute-start | bytes 1572872 | tf_op jit(solution)/shard_map/ppermute | solution.py:35
  92.5 15.8 %collective-permute-start.17 = (bf16[512,512]{1,0:T(8,128)(2,1)}, bf16[512,512]{1,0:T(8,128)(2,1)S(1)}, u32[]{:S(2)}, u32[]{:S(2)}) collective-permute-start(bf16[512,512]{1,0:T(8,128)(2,1)} %get-tuple-element.63), channel_id=1, source_target_pairs={{0,12},{2,14},{4,0},{6,2},{8,4},{10,6},{12,8},{14,10},{16,28},{18,... | collective-permute-start | bytes 1572872 | tf_op jit(solution)/shard_map/ppermute | solution.py:35
  92.5 15.8 %collective-permute-start.18 = (bf16[512,512]{1,0:T(8,128)(2,1)}, bf16[512,512]{1,0:T(8,128)(2,1)S(1)}, u32[]{:S(2)}, u32[]{:S(2)}) collective-permute-start(bf16[512,512]{1,0:T(8,128)(2,1)} %get-tuple-element.64), channel_id=1, source_target_pairs={{0,4},{2,6},{4,8},{6,10},{8,12},{10,14},{12,0},{14,2},{16,20},{18,... | collective-permute-start | bytes 1572872 | tf_op jit(solution)/shard_map/ppermute | solution.py:35
  105.7 2.6 %copy-start.5 = (bf16[512,512]{1,0:T(8,128)(2,1)}, bf16[512,512]{1,0:T(8,128)(2,1)S(1)}, u32[]{:S(2)}) copy-start(bf16[512,512]{1,0:T(8,128)(2,1)S(1)} %collective-permute-done.15.ka) | copy-start | bytes 1572868
  108.3 0.8 copy-start.6
  108.3 1.0 copy-start.7
  108.3 1.1 copy-start.8
  117.0 20.1 %all-to-all-start = ((bf16[32,16,1024]{2,1,0:T(8,128)(2,1)}), bf16[32,16,1024]{2,1,0:T(8,128)(2,1)S(1)}, u32[]{:S(2)}, u32[]{:S(2)}) async-start(bf16[32,16,1024]{2,1,0:T(8,128)(2,1)} %bitcast.60), calls=%async_computation | async-start | bytes 2097152 | tf_op jit(solution)/shard_map/all_to_all | solution.py:570
  137.1 1.0 copy-start.4
  151.0 5.1 %copy-start.11 = (f32[1024]{0:T(1024)S(1)}, f32[1024]{0:T(1024)}, u32[]{:S(2)}) copy-start(f32[1024]{0:T(1024)} %param.13) | copy-start | bytes 12292
  151.0 20.2 %all-to-all-start.1 = ((bf16[32,16,1024]{2,1,0:T(8,128)(2,1)}), bf16[32,16,1024]{2,1,0:T(8,128)(2,1)S(1)}, u32[]{:S(2)}, u32[]{:S(2)}) async-start(bf16[32,16,1024]{2,1,0:T(8,128)(2,1)} %long_conv.1), calls=%async_computation.1 | async-start | bytes 2097152 | tf_op jit(solution)/shard_map/all_to_all | solution.py:579
  156.2 15.0 %copy-start = (bf16[512,1024]{1,0:T(8,128)(2,1)S(1)}, bf16[512,1024]{1,0:T(8,128)(2,1)}, u32[]{:S(2)}) copy-start(bf16[512,1024]{1,0:T(8,128)(2,1)} %last_part.1) | copy-start | bytes 3145732
  173.0 5.1 %collective-permute-start.20 = (bf16[512,256]{1,0:T(8,128)(2,1)S(1)}, bf16[512,256]{1,0:T(8,128)(2,1)S(1)}, u32[]{:S(2)}, u32[]{:S(2)}) collective-permute-start(bf16[512,256]{1,0:T(8,128)(2,1)S(1)} %get-tuple-element.85), channel_id=1, source_target_pairs={{0,2},{2,0},{4,6},{6,4},{8,10},{10,8},{12,14},{14,12},{16,18},{18,... | collective-permute-start | bytes 786440 | tf_op jit(solution)/shard_map/ppermute | solution.py:35
  178.1 14.0 %collective-permute-start.23 = (bf16[512,4096]{1,0:T(8,128)(2,1)}, bf16[512,4096]{1,0:T(8,128)(2,1)}, u32[]{:S(2)}, u32[]{:S(2)}) collective-permute-start(bf16[512,4096]{1,0:T(8,128)(2,1)} %collective-permute-done.19.w_near), channel_id=1, source_target_pairs={{0,2},{2,0},{4,6},{6,4},{8,10},{10,8},{12,14},{14,12},{16,18},{18,... | collective-permute-start | bytes 12582920 | tf_op jit(solution)/shard_map/ppermute | solution.py:35
  178.5 9.2 %collective-permute-start.21 = (bf16[512,256]{1,0:T(8,128)(2,1)S(1)}, bf16[512,256]{1,0:T(8,128)(2,1)S(1)}, u32[]{:S(2)}, u32[]{:S(2)}) collective-permute-start(bf16[512,256]{1,0:T(8,128)(2,1)S(1)} %get-tuple-element.84), channel_id=1, source_target_pairs={{0,1},{1,0},{2,3},{3,2},{4,5},{5,4},{6,7},{7,6},{8,9},{9,8},{10,11... | collective-permute-start | bytes 786440 | tf_op jit(solution)/shard_map/ppermute | solution.py:592
  178.5 13.6 %collective-permute-start.22 = (bf16[512,256]{1,0:T(8,128)(2,1)S(1)}, bf16[512,256]{1,0:T(8,128)(2,1)S(1)}, u32[]{:S(2)}, u32[]{:S(2)}) collective-permute-start(bf16[512,256]{1,0:T(8,128)(2,1)S(1)} %get-tuple-element.83), channel_id=1, source_target_pairs={{0,3},{1,2},{2,1},{3,0},{4,7},{5,6},{6,5},{7,4},{8,11},{9,10},{10,... | collective-permute-start | bytes 786440 | tf_op jit(solution)/shard_map/ppermute | solution.py:597
  187.7 4.4 %copy-start.9 = (bf16[512,256]{1,0:T(8,128)(2,1)}, bf16[512,256]{1,0:T(8,128)(2,1)S(1)}, u32[]{:S(2)}) copy-start(bf16[512,256]{1,0:T(8,128)(2,1)S(1)} %collective-permute-done.21.near_h) | copy-start | bytes 786436
  192.1 0.7 copy-start.10
Sparse Core Ops, SparseCore 0:
  12.5 106.3 all-gather.2
